TPU v7x, 32 devices: a whole 2x2x4 slice. The times are simulated.
32 devices in a mesh: tile: 16 (over z, y, core), sub: 2 (over x).
Axes of the slice: x: 2, y: 2, z: 4, core: 2. Of those that a mesh axis runs over, the one named last changes fastest.
Arguments:
- up_check: bfloat16 [888, 2048], P('sub', 'tile'), may hold values from -6 to 6
- up_inverse: bfloat16 [888, 888], P('sub'), may hold values from -0.1875 to 0.1875
- translate: bfloat16 [8, 888, 888], P(None, 'sub'), may hold values from -0.1875 to 0.1875
- down_inverse: bfloat16 [888, 888], P('sub'), may hold values from -0.09375 to 0.09375
- list_slot: int32 [2048, 8], P('tile'), may hold values from 0 to 639
- list_class: int32 [2048, 8], P('tile'), may hold values from 0 to 7
- list_count: int32 [2048], P('tile'), may hold values from 2 to 8, as said below
Outputs:
- local_density: bfloat16 [888, 2048], P('sub', 'tile')
Inputs may be any that keep to these rules, and one draw needn't show every extreme that they name: Entries at and after list_count of a cell are padding and are not used.
All inputs are finite; a program needn't handle non-finite values.
Results may differ from a plain program's by a relative error of at most 0.0061.
Values may be sent and summed in bfloat16 or wider, within the bound.
No kernel may reach another device: no remote copies, remote signals or barrier semaphores. Data moves between devices by JAX's collectives and lax.ppermute only.
A program may use at most 64 MiB of HBM per device.

v0:
```python
import jax
import jax.numpy as jnp
from jax import lax
from jax.sharding import PartitionSpec as P

REACH = 2


def passed_along(value, axis, steps):
    count = lax.axis_size(axis)
    leading, last = (max(0, -steps), min(count, count - steps))
    return lax.ppermute(value, axis, [(source, source + steps) for source in range(leading, last)])


def fold_product(matrix, shard_rows):
    return jnp.dot(matrix, shard_rows, preferred_element_type=jnp.float32)


def shards(up_check, up_inverse, translate, down_inverse, list_slot, list_class, list_count):
    radius = REACH
    equivalent = fold_product(
        up_inverse, lax.all_gather(up_check, "sub", axis=0, tiled=True)
    ).astype(jnp.bfloat16)
    whole_rows = lax.all_gather(equivalent, "sub", axis=0, tiled=True)
    blocks = []
    for offset in range(-radius, radius + 1):
        if offset == 0:
            blocks.append(whole_rows)
        else:
            blocks.append(passed_along(whole_rows, "tile", -offset))
    window = jnp.concatenate(blocks, axis=1)
    class_count = translate.shape[0]
    picked = jnp.take(window, list_slot, axis=1)
    active = lax.broadcasted_iota(jnp.int32, list_slot.shape, 1) < list_count[:, None]
    class_ids = lax.broadcasted_iota(jnp.int32, (1, 1, class_count), 2)
    weights = jnp.where(
        (list_class[:, :, None] == class_ids) & active[:, :, None], 1.0, 0.0
    ).astype(jnp.bfloat16)
    grouped = jnp.einsum("ecj,cjk->kec", picked, weights, preferred_element_type=jnp.float32)
    grouped_half = grouped.astype(jnp.bfloat16)
    down_check = jnp.einsum(
        "kre,kec->rc", translate, grouped_half, preferred_element_type=jnp.float32
    ).astype(jnp.bfloat16)
    local = fold_product(down_inverse, lax.all_gather(down_check, "sub", axis=0, tiled=True))
    return local.astype(jnp.bfloat16)


def solution(mesh):
    in_specs = (
        P("sub", "tile"),
        P("sub", None),
        P(None, "sub", None),
        P("sub", None),
        P("tile", None),
        P("tile", None),
        P("tile"),
    )
    out_specs = P("sub", "tile")
    return jax.shard_map(shards, mesh=mesh, in_specs=in_specs, out_specs=out_specs, check_vma=False)
```

profile of v0, /device:TPU:8, one launch (start us, length us, event | category | flops | bytes accessed | tf_op | source)
XLA Modules:
  0.0 49.5 jit_solution(9499310050268292307)
XLA Ops:
  0.0 0.0 copy-start
  0.0 0.0 copy-start.2
  0.0 0.0 copy-start.4
  0.0 0.0 copy-start.3
  0.0 5.9 %all-gather = bf16[2,444,128]{2,1,0:T(8,128)(2,1)S(1)} all-gather(bf16[1,444,128]{2,1,0:T(8,128)(2,1)} %bitcast.33), channel_id=1, replica_groups=mesh['tile'=16,'sub'=2] {'sub'}, dimensions={0}, use_global_device_ids=true | all-gather | bytes 340992 | tf_op jit(solution)/shard_map/all_gather | solution.py:22
  6.0 0.0 copy-done
  6.0 0.4 fusion.18
  6.4 5.5 %all-gather.1 = bf16[2,444,128]{2,1,0:T(8,128)(2,1)S(1)} all-gather(bf16[1,444,128]{2,1,0:T(8,128)(2,1)S(1)} %fusion.18), channel_id=1, replica_groups=mesh['tile'=16,'sub'=2] {'sub'}, dimensions={0}, use_global_device_ids=true | all-gather | bytes 340992 | tf_op jit(solution)/shard_map/all_gather | solution.py:24
  11.9 0.2 copy.27
  12.1 3.3 %collective-permute-start.3 = (bf16[888,128]{0,1:T(8,128)(2,1)S(1)}, bf16[888,128]{0,1:T(8,128)(2,1)S(1)}, u32[]{:S(2)}, u32[]{:S(2)}) collective-permute-start(bf16[888,128]{0,1:T(8,128)(2,1)S(1)} %copy.27), channel_id=1, source_target_pairs={{4,0},{6,2},{8,4},{10,6},{12,8},{14,10},{16,12},{18,14},{20,16},{2... | collective-permute-start | bytes 681992 | tf_op jit(solution)/shard_map/ppermute | solution.py:12
  15.4 1.9 %collective-permute-start.2 = (bf16[888,128]{0,1:T(8,128)(2,1)S(1)}, bf16[888,128]{0,1:T(8,128)(2,1)S(1)}, u32[]{:S(2)}, u32[]{:S(2)}) collective-permute-start(bf16[888,128]{0,1:T(8,128)(2,1)S(1)} %copy.27), channel_id=1, source_target_pairs={{2,0},{4,2},{6,4},{8,6},{10,8},{12,10},{14,12},{16,14},{18,16},{20... | collective-permute-start | bytes 681992 | tf_op jit(solution)/shard_map/ppermute | solution.py:12
  17.3 2.4 %collective-permute-start.1 = (bf16[888,128]{0,1:T(8,128)(2,1)S(1)}, bf16[888,128]{0,1:T(8,128)(2,1)S(1)}, u32[]{:S(2)}, u32[]{:S(2)}) collective-permute-start(bf16[888,128]{0,1:T(8,128)(2,1)S(1)} %copy.27), channel_id=1, source_target_pairs={{0,2},{2,4},{4,6},{6,8},{8,10},{10,12},{12,14},{14,16},{16,18},{18... | collective-permute-start | bytes 681992 | tf_op jit(solution)/shard_map/ppermute | solution.py:12
  19.7 2.5 %collective-permute-start = (bf16[888,128]{0,1:T(8,128)(2,1)S(1)}, bf16[888,128]{0,1:T(8,128)(2,1)S(1)}, u32[]{:S(2)}, u32[]{:S(2)}) collective-permute-start(bf16[888,128]{0,1:T(8,128)(2,1)S(1)} %copy.27), channel_id=1, source_target_pairs={{0,4},{2,6},{4,8},{6,10},{8,12},{10,14},{12,16},{14,18},{16,20},{1... | collective-permute-start | bytes 681992 | tf_op jit(solution)/shard_map/ppermute | solution.py:12
  22.3 0.0 copy-done.2
  22.3 0.0 copy-done.4
  22.3 0.1 iota_compare_fusion.1
  22.4 0.1 copy.32
  22.5 0.1 reshape.27
  22.6 0.1 copy.26
  22.7 0.0 copy-done.3
  22.7 0.1 copy.25
  22.8 7.6 %collective-permute-done = bf16[888,128]{0,1:T(8,128)(2,1)S(1)} collective-permute-done((bf16[888,128]{0,1:T(8,128)(2,1)S(1)}, bf16[888,128]{0,1:T(8,128)(2,1)S(1)}, u32[]{:S(2)}, u32[]{:S(2)}) %collective-permute-start) | collective-permute-done | bytes 227360 | tf_op jit(solution)/shard_map/ppermute | solution.py:12
  30.5 0.0 collective-permute-done.1
  30.6 0.0 collective-permute-done.2
  30.6 0.0 collective-permute-done.3
  30.7 5.3 %gather_fusion = bf16[1024,888]{1,0:T(8,128)(2,1)} fusion(bf16[888,640]{0,1:T(8,128)(2,1)S(1)} %constant_dynamic-update-slice_fusion, s32[1024]{0:T(1024)S(1)} %broadcast_clamp_fusion), kind=kCustom, calls=%fused_computation | custom fusion | bytes 3641344 | tf_op jit(solution)/shard_map/jit(_take)/gather | solution.py:33
  35.9 2.3 %convert_bitcast_fusion = bf16[8,888,128]{1,0,2:T(8,128)(2,1)S(1)} fusion(bf16[1024,888]{1,0:T(8,128)(2,1)} %gather_fusion, pred[128,8]{1,0:T(8,128)(4,1)S(1)} %copy.26, s32[128,8]{1,0:T(8,128)S(1)} %copy.25, pred[128,8]{1,0:T(8,128)(4,1)S(1)} %iota_compare_fusion.1), kind=kOutput, calls=%fused_computation.7 | convolution fusion | flops 16400384 | bytes 3643392 | tf_op jit(solution)/shard_map/ecj,cjk->kec/dot_general | solution.py:39
  38.2 0.0 copy-start.1
  38.2 4.7 %fusion.20 = bf16[1,444,128]{2,1,0:T(8,128)(2,1)S(1)} fusion(bf16[8,444,888]{2,0,1:T(8,128)(2,1)} %param.9, bf16[8,888,128]{1,0,2:T(8,128)(2,1)S(1)} %convert_bitcast_fusion), kind=kOutput, calls=%fused_computation.15 | convolution fusion | flops 807525888 | bytes 8240640 | tf_op jit(solution)/shard_map/kre,kec->rc/dot_general | solution.py:41
  42.9 5.5 %all-gather.2 = bf16[2,444,128]{2,1,0:T(8,128)(2,1)S(1)} all-gather(bf16[1,444,128]{2,1,0:T(8,128)(2,1)S(1)} %fusion.20), channel_id=1, replica_groups=mesh['tile'=16,'sub'=2] {'sub'}, dimensions={0}, use_global_device_ids=true | all-gather | bytes 340992 | tf_op jit(solution)/shard_map/all_gather | solution.py:44
  48.5 0.0 copy-done.1
  48.5 1.0 %fusion.19 = bf16[444,128]{1,0:T(8,128)(2,1)} fusion(bf16[888,128]{1,0:T(8,128)(2,1)S(1)} %reshape.40, bf16[444,888]{1,0:T(8,128)(2,1)S(1)} %copy-done.1), kind=kOutput, calls=%fused_computation.14 | convolution fusion | flops 100990464 | bytes 1129536 | tf_op jit(solution)/shard_map/dot_general | solution.py:16
  (11 shorter events, 0.3 us)
Async XLA Ops:
  0.0 6.0 %copy-start = (bf16[444,888]{1,0:T(8,128)(2,1)S(1)}, bf16[444,888]{1,0:T(8,128)(2,1)}, u32[]{:S(2)}) copy-start(bf16[444,888]{1,0:T(8,128)(2,1)} %param.8) | copy-start | bytes 2365636
  0.0 22.3 %copy-start.2 = (s32[128,8]{0,1:T(8,128)S(1)}, s32[128,8]{0,1:T(8,128)}, u32[]{:S(2)}) copy-start(s32[128,8]{0,1:T(8,128)} %param.11) | copy-start | bytes 12292
  0.0 22.3 %copy-start.4 = (s32[128]{0:T(128)S(1)}, s32[128]{0:T(128)}, u32[]{:S(2)}) copy-start(s32[128]{0:T(128)} %param.13) | copy-start | bytes 1540
  0.0 22.7 %copy-start.3 = (s32[128,8]{0,1:T(8,128)S(1)}, s32[128,8]{0,1:T(8,128)}, u32[]{:S(2)}) copy-start(s32[128,8]{0,1:T(8,128)} %param.12) | copy-start | bytes 12292
  12.1 18.6 %collective-permute-start.3 = (bf16[888,128]{0,1:T(8,128)(2,1)S(1)}, bf16[888,128]{0,1:T(8,128)(2,1)S(1)}, u32[]{:S(2)}, u32[]{:S(2)}) collective-permute-start(bf16[888,128]{0,1:T(8,128)(2,1)S(1)} %copy.27), channel_id=1, source_target_pairs={{4,0},{6,2},{8,4},{10,6},{12,8},{14,10},{16,12},{18,14},{20,16},{2... | collective-permute-start | bytes 681992 | tf_op jit(solution)/shard_map/ppermute | solution.py:12
  15.4 15.2 %collective-permute-start.2 = (bf16[888,128]{0,1:T(8,128)(2,1)S(1)}, bf16[888,128]{0,1:T(8,128)(2,1)S(1)}, u32[]{:S(2)}, u32[]{:S(2)}) collective-permute-start(bf16[888,128]{0,1:T(8,128)(2,1)S(1)} %copy.27), channel_id=1, source_target_pairs={{2,0},{4,2},{6,4},{8,6},{10,8},{12,10},{14,12},{16,14},{18,16},{20... | collective-permute-start | bytes 681992 | tf_op jit(solution)/shard_map/ppermute | solution.py:12
  17.3 13.2 %collective-permute-start.1 = (bf16[888,128]{0,1:T(8,128)(2,1)S(1)}, bf16[888,128]{0,1:T(8,128)(2,1)S(1)}, u32[]{:S(2)}, u32[]{:S(2)}) collective-permute-start(bf16[888,128]{0,1:T(8,128)(2,1)S(1)} %copy.27), channel_id=1, source_target_pairs={{0,2},{2,4},{4,6},{6,8},{8,10},{10,12},{12,14},{14,16},{16,18},{18... | collective-permute-start | bytes 681992 | tf_op jit(solution)/shard_map/ppermute | solution.py:12
  19.7 10.7 %collective-permute-start = (bf16[888,128]{0,1:T(8,128)(2,1)S(1)}, bf16[888,128]{0,1:T(8,128)(2,1)S(1)}, u32[]{:S(2)}, u32[]{:S(2)}) collective-permute-start(bf16[888,128]{0,1:T(8,128)(2,1)S(1)} %copy.27), channel_id=1, source_target_pairs={{0,4},{2,6},{4,8},{6,10},{8,12},{10,14},{12,16},{14,18},{16,20},{1... | collective-permute-start | bytes 681992 | tf_op jit(solution)/shard_map/ppermute | solution.py:12
  38.2 10.2 %copy-start.1 = (bf16[444,888]{1,0:T(8,128)(2,1)S(1)}, bf16[444,888]{1,0:T(8,128)(2,1)}, u32[]{:S(2)}) copy-start(bf16[444,888]{1,0:T(8,128)(2,1)} %param.10) | copy-start | bytes 2365636
where the time goes:
time: 49.8 us; the launch traced here: 49.5 us
  blocking collectives  16.8 us (34%)
  starting transfers between devices  10.2 us (20%)
  matrix products  8.38 us (17%)
  waiting for transfers between devices  7.63 us (15%)
  local copies, waits for them, and re-layouts  6.16 us (12%)
    ppermute x4, starting transfers between devices, passed_along(): lax.ppermute(value, axis, [(source, source + steps) for source in range(l...  10.2 us
    ppermute x4, waiting for transfers between devices, passed_along(): lax.ppermute(value, axis, [(source, source + steps) for source in range(l...  7.63 us
    all_gather x1, blocking collectives, shards(): lax.all_gather(up_check, 'sub', axis=0, tiled=True)  5.91 us
    all_gather x1, blocking collectives, shards(): whole_rows = lax.all_gather(equivalent, 'sub', axis=0, tiled=True)  5.47 us
    all_gather x1, blocking collectives, shards(): lax.all_gather(down_check, 'sub', axis=0, tiled=True)  5.47 us
    gather x1, local copies, waits for them, and re-layouts, shards(): picked = jnp.take(window, list_slot, axis=1)  5.28 us
    dot_general x1, matrix products, shards(): jnp.einsum('kre,kec->rc', translate, grouped_half, preferred_element_type...  4.7 us
    dot_general x1, matrix products, shards(): jnp.einsum('ecj,cjk->kec', picked, weights, preferred_element_type=jnp.fl...  2.28 us
  transfers between devices with their start and end apart: 4, of which 1 were waited for; matrix products, arithmetic and copies ran while one was open for 1% of the time, Pallas kernels for 0%

commit v1 on v0

v1 whole, which is shorter than its diff:
```python
import functools

import jax
import jax.numpy as jnp
from jax import lax
from jax.experimental import pallas as pl
from jax.experimental.pallas import tpu as pltpu
from jax.sharding import PartitionSpec as P

REACH = 2
CLASS_STRIDE = 1024
CHUNK = 112


def gathered_rows(shard):
    if lax.axis_size("sub") != 2:
        return lax.all_gather(shard, "sub", axis=0, tiled=True)
    other = lax.ppermute(shard, "sub", [(0, 1), (1, 0)])
    first = lax.axis_index("sub") == 0
    return jnp.where(
        first, jnp.concatenate([shard, other], 0), jnp.concatenate([other, shard], 0)
    )


def moved(value, step):
    count = lax.axis_size("tile")
    pairs = []
    for tile in range(count):
        target = tile + (step if tile % 2 else -step)
        if 0 <= target < count:
            pairs.append((tile, target))
    return lax.ppermute(value, "tile", pairs)


def select_kernel(codes_ref, base_ref, out_ref):
    blocks, entries, cells = codes_ref.shape
    classes = out_ref.shape[1] // cells
    for block in range(blocks):
        codes = codes_ref[block] - base_ref[block]
        source = lax.broadcasted_iota(jnp.int32, (cells, cells), 0)
        for k in range(classes):
            row = source + k * CLASS_STRIDE
            total = jnp.zeros((cells, cells), jnp.float32)
            for entry in range(entries):
                total += jnp.where(codes[entry : entry + 1, :] == row, 1.0, 0.0)
            out_ref[block, k * cells : (k + 1) * cells, :] = total.astype(jnp.bfloat16)


def push_kernel(
    translate_ref, equivalent_ref, select_ref, own_ref, near_ref, far_ref, mate_ref,
    held, product, sems,
):
    rows, classes, _ = translate_ref.shape
    cells = equivalent_ref.shape[1]
    starts = list(range(0, rows, CHUNK))
    copies = []
    for i, start in enumerate(starts):
        part = pl.ds(start, min(CHUNK, rows - start))
        copy = pltpu.make_async_copy(translate_ref.at[part], held.at[part], sems.at[i])
        copy.start()
        copies.append(copy)
    equivalent = equivalent_ref[...]
    for copy, start in zip(copies, starts):
        size = min(CHUNK, rows - start)
        copy.wait()
        left = held[start : start + size].reshape(size * classes, held.shape[2])
        product[: size * classes, :] = jnp.dot(
            left, equivalent, preferred_element_type=jnp.float32
        )
        terms = [
            product[pl.ds(k, size, stride=classes), :].astype(jnp.bfloat16)
            for k in range(classes)
        ]
        terms = jnp.concatenate(terms, axis=1)
        part = pl.ds(start, size)
        for block, ref in enumerate((own_ref, near_ref, far_ref, mate_ref, mate_ref)):
            value = jnp.dot(terms, select_ref[block], preferred_element_type=jnp.float32)
            if block < 3:
                ref[part, :] = value.astype(ref.dtype)
            else:
                column = (block - 3) * cells
                ref[part, column : column + cells] = value.astype(ref.dtype)


def shards(up_check, up_inverse, translate, down_inverse, list_slot, list_class, list_count):
    classes, rows, depth = translate.shape
    cells, entries = list_slot.shape

    slots = list_slot.T
    active = lax.broadcasted_iota(jnp.int32, slots.shape, 0) < list_count[None, :]
    code = jnp.where(active, list_class.T * CLASS_STRIDE + slots, -CLASS_STRIDE)
    codes = jnp.stack([code, moved(code, 1), moved(code, -2), moved(code, -1), moved(code, 2)])
    away = 2 * (lax.axis_index("tile") % 2) - 1
    offsets = jnp.array([0, 1, 2, -1, -2], jnp.int32) * away
    base = (REACH - offsets) * cells

    select = pl.pallas_call(
        select_kernel,
        out_shape=jax.ShapeDtypeStruct((5, classes * cells, cells), jnp.bfloat16),
        in_specs=[
            pl.BlockSpec(memory_space=pltpu.VMEM),
            pl.BlockSpec(memory_space=pltpu.SMEM),
        ],
        out_specs=pl.BlockSpec(memory_space=pltpu.VMEM),
        cost_estimate=pl.CostEstimate(
            flops=5 * 2 * entries * classes * cells * cells, bytes_accessed=2 << 20,
            transcendentals=0,
        ),
        compiler_params=pltpu.CompilerParams(vmem_limit_bytes=8 << 20),
        name="select",
    )(codes, base)

    whole_check = gathered_rows(up_check)
    equivalent = jnp.dot(up_inverse, whole_check, preferred_element_type=jnp.float32)
    whole = gathered_rows(equivalent.astype(jnp.bfloat16))

    operators = jnp.transpose(translate, (1, 0, 2))
    own, near, far, mate = pl.pallas_call(
        push_kernel,
        out_shape=[
            jax.ShapeDtypeStruct((rows, cells), jnp.float32),
            jax.ShapeDtypeStruct((rows, cells), jnp.float32),
            jax.ShapeDtypeStruct((rows, cells), jnp.bfloat16),
            jax.ShapeDtypeStruct((rows, 2 * cells), jnp.bfloat16),
        ],
        in_specs=[
            pl.BlockSpec(memory_space=pl.ANY),
            pl.BlockSpec(memory_space=pltpu.VMEM),
            pl.BlockSpec(memory_space=pltpu.VMEM),
        ],
        out_specs=[pl.BlockSpec(memory_space=pltpu.VMEM)] * 4,
        scratch_shapes=[
            pltpu.VMEM((rows, classes, depth), jnp.bfloat16),
            pltpu.VMEM((CHUNK * classes, cells), jnp.float32),
            pltpu.SemaphoreType.DMA((pl.cdiv(rows, CHUNK),)),
        ],
        cost_estimate=pl.CostEstimate(
            flops=2 * rows * classes * cells * (depth + 5 * cells),
            bytes_accessed=2 * rows * classes * depth,
            transcendentals=0,
        ),
        compiler_params=pltpu.CompilerParams(vmem_limit_bytes=24 << 20),
        name="push",
    )(operators, whole, select)

    from_far = moved(far, 2)
    from_mate = moved(mate, -1).astype(jnp.float32)
    from_near = moved((near + from_mate[:, cells:]).astype(jnp.bfloat16), 1)
    down_check = (
        (own + from_mate[:, :cells])
        + (from_far.astype(jnp.float32) + from_near.astype(jnp.float32))
    ).astype(jnp.bfloat16)
    local = jnp.dot(
        down_inverse, gathered_rows(down_check), preferred_element_type=jnp.float32
    )
    return local.astype(jnp.bfloat16)


def solution(mesh):
    in_specs = (
        P("sub", "tile"),
        P("sub", None),
        P(None, "sub", None),
        P("sub", None),
        P("tile", None),
        P("tile", None),
        P("tile"),
    )
    out_specs = P("sub", "tile")
    return jax.shard_map(shards, mesh=mesh, in_specs=in_specs, out_specs=out_specs, check_vma=False)
```

time: 49.8 us -> 49.4 us (level)
  blocking collectives: 16.8 us -> 0 us
  Pallas kernels: 0 us -> 9.84 us
  starting transfers between devices: 10.2 us -> 19.9 us
  matrix products: 8.38 us -> 2.38 us
  waiting for transfers between devices: 7.63 us -> 11.8 us
  local copies, waits for them, and re-layouts: 6.16 us -> 2.82 us
  other arithmetic: 0.1 us -> 1.66 us
    all_gather x3 -> x0, blocking collectives: 16.8 us -> none  [the longest x1 5.91 us: shards(): lax.all_gather(up_check, 'sub', axis=0, tiled=True)]
    pallas_call x0 -> x2, Pallas kernels: none -> 9.84 us  [the longest x1 7.17 us: shards(): pl.pallas_call(push_kernel, out_shape=[jax.ShapeDtypeStruct((rows, cells)...]
    ppermute x4 -> x10, starting transfers between devices: 10.2 us -> 19.9 us  [the longest x7 15.3 us: moved(): return lax.ppermute(value, 'tile', pairs)]
    dot_general x4 -> x2, matrix products: 8.38 us -> 2.38 us  [the longest x1 1.36 us: shards(): jnp.dot(up_inverse, whole_check, preferred_element_type=jnp.float32)]
    gather x1 -> x0, local copies, waits for them, and re-layouts: 5.28 us -> none  [shards(): picked = jnp.take(window, list_slot, axis=1)]
    ppermute x4 -> x10, waiting for transfers between devices: 7.63 us -> 11.8 us  [the longest x3 9.26 us: gathered_rows(): other = lax.ppermute(shard, 'sub', [(0, 1), (1, 0)])]
    unnamed x19 -> x9, local copies, waits for them, and re-layouts: 0.53 us -> 2.82 us
    unnamed x0 -> x1, other arithmetic: none -> 0.78 us
  transfers between devices with their start and end apart: 4 -> 10, of which waited for: 1 -> 5; matrix products, arithmetic and copies ran while one was open for 1% -> 4% of each run, Pallas kernels for 0% -> 5%
where the time goes in v1:
time: 49.4 us; the launch traced here: 48.6 us
  starting transfers between devices  19.9 us (40%)
  waiting for transfers between devices  11.8 us (24%)
  Pallas kernels  9.84 us (20%)
  local copies, waits for them, and re-layouts  2.82 us (6%)
  matrix products  2.38 us (5%)
  other arithmetic  1.66 us (3%)
    ppermute x7, starting transfers between devices, moved(): return lax.ppermute(value, 'tile', pairs)  15.3 us
    ppermute x3, waiting for transfers between devices, gathered_rows(): other = lax.ppermute(shard, 'sub', [(0, 1), (1, 0)])  9.26 us
    pallas_call x1, Pallas kernels, shards(): pl.pallas_call(push_kernel, out_shape=[jax.ShapeDtypeStruct((rows, cells)...  7.17 us
    ppermute x3, starting transfers between devices, gathered_rows(): other = lax.ppermute(shard, 'sub', [(0, 1), (1, 0)])  4.66 us
    unnamed x9, local copies, waits for them, and re-layouts  2.82 us
    pallas_call x1, Pallas kernels, shards(): pl.pallas_call(select_kernel, out_shape=jax.ShapeDtypeStruct((5, classes...  2.67 us
    ppermute x7, waiting for transfers between devices, moved(): return lax.ppermute(value, 'tile', pairs)  2.58 us
    dot_general x1, matrix products, shards(): jnp.dot(up_inverse, whole_check, preferred_element_type=jnp.float32)  1.36 us
  transfers between devices with their start and end apart: 10, of which 5 were waited for; matrix products, arithmetic and copies ran while one was open for 4% of the time, Pallas kernels for 5%

profile of v1, /device:TPU:8, one launch (start us, length us, event | category | flops | bytes accessed | tf_op | source)
XLA Modules:
  0.0 48.6 jit_solution(3108196357444894276)
XLA Ops:
  0.0 0.0 copy-start
  0.0 0.8 %constant_dynamic-update-slice_fusion.4 = (s32[5,8,128]{2,1,0:T(8,128)S(1)}, s32[8,128]{1,0:T(8,128)S(1)}) fusion(s32[128,8]{0,1:T(8,128)} %param.12, s32[128,8]{0,1:T(8,128)} %param.13, s32[128]{0:T(128)} %param.14), kind=kLoop, calls=%fused_computation.28 | loop fusion | flops 4095 | bytes 16896
  0.8 0.0 collective-permute-start.4
  0.8 3.4 %collective-permute-start.3 = (s32[8,128]{1,0:T(8,128)S(1)}, s32[8,128]{1,0:T(8,128)S(1)}, u32[]{:S(2)}, u32[]{:S(2)}) collective-permute-start(s32[8,128]{1,0:T(8,128)S(1)} %get-tuple-element.14), channel_id=1, source_target_pairs={{0,4},{4,8},{6,2},{8,12},{10,6},{12,16},{14,10},{16,20},{18,14},{2... | collective-permute-start | bytes 12296 | tf_op jit(solution)/shard_map/ppermute | solution.py:32
  4.2 1.9 %collective-permute-start.2 = (s32[8,128]{1,0:T(8,128)S(1)}, s32[8,128]{1,0:T(8,128)S(1)}, u32[]{:S(2)}, u32[]{:S(2)}) collective-permute-start(s32[8,128]{1,0:T(8,128)S(1)} %get-tuple-element.14), channel_id=1, source_target_pairs={{2,4},{4,2},{6,8},{8,6},{10,12},{12,10},{14,16},{16,14},{18,20},{2... | collective-permute-start | bytes 12296 | tf_op jit(solution)/shard_map/ppermute | solution.py:32
  6.1 3.3 %collective-permute-start.5 = (s32[8,128]{1,0:T(8,128)S(1)}, s32[8,128]{1,0:T(8,128)S(1)}, u32[]{:S(2)}, u32[]{:S(2)}) collective-permute-start(s32[8,128]{1,0:T(8,128)S(1)} %get-tuple-element.14), channel_id=1, source_target_pairs={{2,6},{4,0},{6,10},{8,4},{10,14},{12,8},{14,18},{16,12},{18,22},{2... | collective-permute-start | bytes 12296 | tf_op jit(solution)/shard_map/ppermute | solution.py:32
  9.5 1.6 %collective-permute-start = (bf16[444,128]{1,0:T(8,128)(2,1)}, bf16[444,128]{1,0:T(8,128)(2,1)S(1)}, u32[]{:S(2)}, u32[]{:S(2)}) collective-permute-start(bf16[444,128]{1,0:T(8,128)(2,1)} %param.8), channel_id=1, source_target_pairs={{0,1},{1,0},{2,3},{3,2},{4,5},{5,4},{6,7},{7,6},{8,9},{9,8},{10,11... | collective-permute-start | bytes 341000 | tf_op jit(solution)/shard_map/ppermute | solution.py:18
  11.0 0.7 %subtract_multiply_fusion.base_ref = s32[5]{0:T(128)S(1)} fusion(s32[5]{0:T(128)} %constant.34.clone, s32[]{:T(128)S(6)} %sub.6), kind=kLoop, calls=%fused_computation.31 | loop fusion | flops 15 | bytes 44 | tf_op jit(solution)/shard_map/mul | solution.py:95
  11.7 0.0 collective-permute-done.2
  11.7 0.0 collective-permute-done.3
  11.7 0.0 collective-permute-done.4
  11.7 0.0 copy-start.2
  11.7 3.6 %collective-permute-done = bf16[444,128]{1,0:T(8,128)(2,1)S(1)} collective-permute-done((bf16[444,128]{1,0:T(8,128)(2,1)}, bf16[444,128]{1,0:T(8,128)(2,1)S(1)}, u32[]{:S(2)}, u32[]{:S(2)}) %collective-permute-start) | collective-permute-done | bytes 113696 | tf_op jit(solution)/shard_map/ppermute | solution.py:18
  15.4 0.0 copy-done
  15.4 1.4 %fusion = bf16[444,128]{1,0:T(8,128)(2,1)S(1)} fusion(bf16[444,888]{1,0:T(8,128)(2,1)S(1)} %copy-done, bf16[444,128]{1,0:T(8,128)(2,1)S(1)} %collective-permute-done, bf16[444,128]{1,0:T(8,128)(2,1)} %param.8, pred[]{:T(512)S(6)} %eq.4), kind=kOutput, calls=%fused_computation.2 | convolution fusion | flops 102013440 | bytes 1129537 | tf_op jit(solution)/shard_map/dot_general | solution.py:114
  16.7 1.6 %collective-permute-start.1 = (bf16[444,128]{1,0:T(8,128)(2,1)S(1)}, bf16[444,128]{1,0:T(8,128)(2,1)S(1)}, u32[]{:S(2)}, u32[]{:S(2)}) collective-permute-start(bf16[444,128]{1,0:T(8,128)(2,1)S(1)} %fusion), channel_id=1, source_target_pairs={{0,1},{1,0},{2,3},{3,2},{4,5},{5,4},{6,7},{7,6},{8,9},{9,8},{10,11... | collective-permute-start | bytes 341000 | tf_op jit(solution)/shard_map/ppermute | solution.py:18
  18.3 0.0 collective-permute-done.5
  18.3 2.7 %select.3.select_ref = bf16[5,1024,128]{2,1,0:T(8,128)(2,1)S(1)} custom-call(s32[5,8,128]{2,1,0:T(8,128)S(1)} %constant_dynamic-update-slice_fusion.codes_ref, s32[5]{0:T(128)S(1)} %subtract_multiply_fusion.base_ref), custom_call_target="tpu_custom_call" | custom-call | flops 10485760 | bytes 2097152 | tf_op jit(solution)/shard_map/select/pallas_call | solution.py:97
  21.0 1.1 %collective-permute-done.1 = bf16[444,128]{1,0:T(8,128)(2,1)S(1)} collective-permute-done((bf16[444,128]{1,0:T(8,128)(2,1)S(1)}, bf16[444,128]{1,0:T(8,128)(2,1)S(1)}, u32[]{:S(2)}, u32[]{:S(2)}) %collective-permute-start.1) | collective-permute-done | bytes 113696 | tf_op jit(solution)/shard_map/ppermute | solution.py:18
  22.1 0.1 maximum_select_fusion.2.equivalent_ref
  22.2 0.0 copy-start.1
  22.2 2.8 %copy-done.1 = bf16[8,444,888]{2,0,1:T(8,128)(2,1)S(1)} copy-done((bf16[8,444,888]{2,0,1:T(8,128)(2,1)S(1)}, bf16[8,444,888]{2,0,1:T(8,128)(2,1)}, u32[]{:S(2)}) %copy-start.1) | copy-done | bytes 6308376
  25.0 7.2 %push.1 = (f32[444,128]{1,0:T(8,128)S(1)}, f32[444,128]{1,0:T(8,128)S(1)}, bf16[444,128]{1,0:T(8,128)(2,1)S(1)}, bf16[444,256]{1,0:T(8,128)(2,1)S(1)}) custom-call(bf16[444,8,888]{2,1,0:T(8,128)(2,1)S(1)} %bitcast.20, bf16[888,128]{1,0:T(8,128)(2,1)S(1)} %maximum_select_fusion.2.equivalent_ref, bf16[5,1024,128]{2,1,0:T(8,128)(2,1)S(1)} %select.3.select_ref), custom_call_target="tpu_custom_call" | custom-call | flops 1389428736 | bytes 6308352 | tf_op jit(solution)/shard_map/push/pallas_call | solution.py:118
  32.1 0.1 collective-permute-start.6
  32.2 1.9 %collective-permute-start.7 = (bf16[444,128]{1,0:T(8,128)(2,1)S(1)}, bf16[444,128]{1,0:T(8,128)(2,1)S(1)}, u32[]{:S(2)}, u32[]{:S(2)}) collective-permute-start(bf16[444,128]{1,0:T(8,128)(2,1)S(1)} %get-tuple-element.11), channel_id=1, source_target_pairs={{2,6},{4,0},{6,10},{8,4},{10,14},{12,8},{14,18},{16,12},{18,22},{2... | collective-permute-start | bytes 341000 | tf_op jit(solution)/shard_map/ppermute | solution.py:32
  34.2 0.0 collective-permute-done.6
  34.2 4.6 %collective-permute-start.8 = (bf16[444,128]{1,0:T(8,128)(2,1)S(1)}, bf16[444,128]{1,0:T(8,128)(2,1)S(1)}, u32[]{:S(2)}, u32[]{:S(2)}) collective-permute-start(bf16[444,128]{1,0:T(8,128)(2,1)S(1)} %fusion.2), channel_id=1, source_target_pairs={{2,4},{4,2},{6,8},{8,6},{10,12},{12,10},{14,16},{16,14},{18,20},{2... | collective-permute-start | bytes 341000 | tf_op jit(solution)/shard_map/ppermute | solution.py:32
  38.9 1.3 %collective-permute-done.7 = bf16[444,128]{1,0:T(8,128)(2,1)S(1)} collective-permute-done((bf16[444,128]{1,0:T(8,128)(2,1)S(1)}, bf16[444,128]{1,0:T(8,128)(2,1)S(1)}, u32[]{:S(2)}, u32[]{:S(2)}) %collective-permute-start.7) | collective-permute-done | bytes 113696 | tf_op jit(solution)/shard_map/ppermute | solution.py:32
  40.2 1.3 %collective-permute-done.8 = bf16[444,128]{1,0:T(8,128)(2,1)S(1)} collective-permute-done((bf16[444,128]{1,0:T(8,128)(2,1)S(1)}, bf16[444,128]{1,0:T(8,128)(2,1)S(1)}, u32[]{:S(2)}, u32[]{:S(2)}) %collective-permute-start.8) | collective-permute-done | bytes 113696 | tf_op jit(solution)/shard_map/ppermute | solution.py:32
  41.5 0.1 fusion.4
  41.5 1.6 %collective-permute-start.9 = (bf16[444,128]{1,0:T(8,128)(2,1)S(1)}, bf16[444,128]{1,0:T(8,128)(2,1)S(1)}, u32[]{:S(2)}, u32[]{:S(2)}) collective-permute-start(bf16[444,128]{1,0:T(8,128)(2,1)S(1)} %fusion.4), channel_id=1, source_target_pairs={{0,1},{1,0},{2,3},{3,2},{4,5},{5,4},{6,7},{7,6},{8,9},{9,8},{10,11... | collective-permute-start | bytes 341000 | tf_op jit(solution)/shard_map/ppermute | solution.py:18
  43.1 4.5 %collective-permute-done.9 = bf16[444,128]{1,0:T(8,128)(2,1)S(1)} collective-permute-done((bf16[444,128]{1,0:T(8,128)(2,1)S(1)}, bf16[444,128]{1,0:T(8,128)(2,1)S(1)}, u32[]{:S(2)}, u32[]{:S(2)}) %collective-permute-start.9) | collective-permute-done | bytes 113696 | tf_op jit(solution)/shard_map/ppermute | solution.py:18
  47.6 0.0 copy-done.2
  47.6 1.0 %fusion.1 = bf16[444,128]{1,0:T(8,128)(2,1)} fusion(bf16[444,888]{1,0:T(8,128)(2,1)S(1)} %copy-done.2, bf16[444,128]{1,0:T(8,128)(2,1)S(1)} %collective-permute-done.9, bf16[444,128]{1,0:T(8,128)(2,1)S(1)} %fusion.4, pred[]{:T(512)S(6)} %eq.4), kind=kOutput, calls=%fused_computation.3 | convolution fusion | flops 102013440 | bytes 1129537 | tf_op jit(solution)/shard_map/dot_general | solution.py:153
  (6 shorter events, 0.1 us)
Async XLA Ops:
  0.0 15.4 %copy-start = (bf16[444,888]{1,0:T(8,128)(2,1)S(1)}, bf16[444,888]{1,0:T(8,128)(2,1)}, u32[]{:S(2)}) copy-start(bf16[444,888]{1,0:T(8,128)(2,1)} %param.9) | copy-start | bytes 2365636
  0.8 10.9 %collective-permute-start.4 = (s32[8,128]{1,0:T(8,128)S(1)}, s32[8,128]{1,0:T(8,128)S(1)}, u32[]{:S(2)}, u32[]{:S(2)}) collective-permute-start(s32[8,128]{1,0:T(8,128)S(1)} %get-tuple-element.14), channel_id=1, source_target_pairs={{0,2},{2,0},{4,6},{6,4},{8,10},{10,8},{12,14},{14,12},{16,18},{18,... | collective-permute-start | bytes 12296 | tf_op jit(solution)/shard_map/ppermute | solution.py:32
  0.8 10.9 %collective-permute-start.3 = (s32[8,128]{1,0:T(8,128)S(1)}, s32[8,128]{1,0:T(8,128)S(1)}, u32[]{:S(2)}, u32[]{:S(2)}) collective-permute-start(s32[8,128]{1,0:T(8,128)S(1)} %get-tuple-element.14), channel_id=1, source_target_pairs={{0,4},{4,8},{6,2},{8,12},{10,6},{12,16},{14,10},{16,20},{18,14},{2... | collective-permute-start | bytes 12296 | tf_op jit(solution)/shard_map/ppermute | solution.py:32
  4.2 7.5 %collective-permute-start.2 = (s32[8,128]{1,0:T(8,128)S(1)}, s32[8,128]{1,0:T(8,128)S(1)}, u32[]{:S(2)}, u32[]{:S(2)}) collective-permute-start(s32[8,128]{1,0:T(8,128)S(1)} %get-tuple-element.14), channel_id=1, source_target_pairs={{2,4},{4,2},{6,8},{8,6},{10,12},{12,10},{14,16},{16,14},{18,20},{2... | collective-permute-start | bytes 12296 | tf_op jit(solution)/shard_map/ppermute | solution.py:32
  6.1 12.1 %collective-permute-start.5 = (s32[8,128]{1,0:T(8,128)S(1)}, s32[8,128]{1,0:T(8,128)S(1)}, u32[]{:S(2)}, u32[]{:S(2)}) collective-permute-start(s32[8,128]{1,0:T(8,128)S(1)} %get-tuple-element.14), channel_id=1, source_target_pairs={{2,6},{4,0},{6,10},{8,4},{10,14},{12,8},{14,18},{16,12},{18,22},{2... | collective-permute-start | bytes 12296 | tf_op jit(solution)/shard_map/ppermute | solution.py:32
  9.5 5.9 %collective-permute-start = (bf16[444,128]{1,0:T(8,128)(2,1)}, bf16[444,128]{1,0:T(8,128)(2,1)S(1)}, u32[]{:S(2)}, u32[]{:S(2)}) collective-permute-start(bf16[444,128]{1,0:T(8,128)(2,1)} %param.8), channel_id=1, source_target_pairs={{0,1},{1,0},{2,3},{3,2},{4,5},{5,4},{6,7},{7,6},{8,9},{9,8},{10,11... | collective-permute-start | bytes 341000 | tf_op jit(solution)/shard_map/ppermute | solution.py:18
  11.7 35.9 %copy-start.2 = (bf16[444,888]{1,0:T(8,128)(2,1)S(1)}, bf16[444,888]{1,0:T(8,128)(2,1)}, u32[]{:S(2)}) copy-start(bf16[444,888]{1,0:T(8,128)(2,1)} %param.11) | copy-start | bytes 2365636
  16.7 5.3 %collective-permute-start.1 = (bf16[444,128]{1,0:T(8,128)(2,1)S(1)}, bf16[444,128]{1,0:T(8,128)(2,1)S(1)}, u32[]{:S(2)}, u32[]{:S(2)}) collective-permute-start(bf16[444,128]{1,0:T(8,128)(2,1)S(1)} %fusion), channel_id=1, source_target_pairs={{0,1},{1,0},{2,3},{3,2},{4,5},{5,4},{6,7},{7,6},{8,9},{9,8},{10,11... | collective-permute-start | bytes 341000 | tf_op jit(solution)/shard_map/ppermute | solution.py:18
  22.2 2.8 %copy-start.1 = (bf16[8,444,888]{2,0,1:T(8,128)(2,1)S(1)}, bf16[8,444,888]{2,0,1:T(8,128)(2,1)}, u32[]{:S(2)}) copy-start(bf16[8,444,888]{2,0,1:T(8,128)(2,1)} %param.10) | copy-start | bytes 18925060
  32.1 2.0 %collective-permute-start.6 = (bf16[444,256]{1,0:T(8,128)(2,1)S(1)}, bf16[444,256]{1,0:T(8,128)(2,1)S(1)}, u32[]{:S(2)}, u32[]{:S(2)}) collective-permute-start(bf16[444,256]{1,0:T(8,128)(2,1)S(1)} %get-tuple-element.10), channel_id=1, source_target_pairs={{0,2},{2,0},{4,6},{6,4},{8,10},{10,8},{12,14},{14,12},{16,18},{18,... | collective-permute-start | bytes 681992 | tf_op jit(solution)/shard_map/ppermute | solution.py:32
  32.2 7.9 %collective-permute-start.7 = (bf16[444,128]{1,0:T(8,128)(2,1)S(1)}, bf16[444,128]{1,0:T(8,128)(2,1)S(1)}, u32[]{:S(2)}, u32[]{:S(2)}) collective-permute-start(bf16[444,128]{1,0:T(8,128)(2,1)S(1)} %get-tuple-element.11), channel_id=1, source_target_pairs={{2,6},{4,0},{6,10},{8,4},{10,14},{12,8},{14,18},{16,12},{18,22},{2... | collective-permute-start | bytes 341000 | tf_op jit(solution)/shard_map/ppermute | solution.py:32
  34.2 7.2 %collective-permute-start.8 = (bf16[444,128]{1,0:T(8,128)(2,1)S(1)}, bf16[444,128]{1,0:T(8,128)(2,1)S(1)}, u32[]{:S(2)}, u32[]{:S(2)}) collective-permute-start(bf16[444,128]{1,0:T(8,128)(2,1)S(1)} %fusion.2), channel_id=1, source_target_pairs={{2,4},{4,2},{6,8},{8,6},{10,12},{12,10},{14,16},{16,14},{18,20},{2... | collective-permute-start | bytes 341000 | tf_op jit(solution)/shard_map/ppermute | solution.py:32
  41.5 6.1 %collective-permute-start.9 = (bf16[444,128]{1,0:T(8,128)(2,1)S(1)}, bf16[444,128]{1,0:T(8,128)(2,1)S(1)}, u32[]{:S(2)}, u32[]{:S(2)}) collective-permute-start(bf16[444,128]{1,0:T(8,128)(2,1)S(1)} %fusion.4), channel_id=1, source_target_pairs={{0,1},{1,0},{2,3},{3,2},{4,5},{5,4},{6,7},{7,6},{8,9},{9,8},{10,11... | collective-permute-start | bytes 341000 | tf_op jit(solution)/shard_map/ppermute | solution.py:18

commit v2 on v0

v2 whole, which is shorter than its diff:
```python
import functools

import jax
import jax.numpy as jnp
from jax import lax
from jax.experimental import pallas as pl
from jax.experimental.pallas import tpu as pltpu
from jax.sharding import PartitionSpec as P

REACH = 2
CLASS_SHIFT = 10
CHUNK = 112
LANES = 128
WHOLE = pl.BlockSpec(memory_space=pltpu.VMEM)


def across_sub(shard):
    return lax.ppermute(shard, "sub", [(0, 1), (1, 0)])


def to_mate(value):
    count = lax.axis_size("tile")
    pairs = [(t, t ^ 1) for t in range(count) if t ^ 1 < count]
    return lax.ppermute(value, "tile", pairs)


def to_near(value):
    count = lax.axis_size("tile")
    pairs = [(t, t + 2 * (t % 2) - 1) for t in range(count)]
    return lax.ppermute(value, "tile", [(a, b) for a, b in pairs if 0 <= b < count])


def away():
    return 2 * lax.rem(lax.axis_index("tile"), 2) - 1


def half_windows(shard_rows, depth, count):
    windows = []
    for index in range(count):
        low, high = index * shard_rows, (index + 1) * shard_rows
        start = low // LANES * LANES
        stop = min(pl.cdiv(high, LANES) * LANES, depth)
        windows.append((start, stop, low - start))
    return windows


def chunks(rows):
    return [(start, min(CHUNK, rows - start)) for start in range(0, rows, CHUNK)]


def pad_into(padded, offset, *refs):
    padded[...] = jnp.zeros(padded.shape, padded.dtype)
    for i, ref in enumerate(refs):
        rows, cells = ref.shape
        padded[offset : offset + rows, i * cells : (i + 1) * cells] = ref[...].astype(padded.dtype)


def first_kernel(windows, matrix_ref, own_ref, out_ref, padded):
    for index, (low, high, offset) in enumerate(windows):
        def run(low=low, high=high, offset=offset):
            pad_into(padded, offset, own_ref)
            out_ref[...] = jnp.dot(
                matrix_ref[:, low:high], padded[: high - low, :].astype(jnp.bfloat16),
                preferred_element_type=jnp.float32,
            )
        pl.when(lax.axis_index("sub") == index)(run)


def first(matrix, own, windows):
    rows, depth = matrix.shape
    cells = own.shape[1]
    span = max(high - low for low, high, _ in windows)
    return pl.pallas_call(
        functools.partial(first_kernel, windows),
        out_shape=jax.ShapeDtypeStruct((rows, cells), jnp.float32),
        in_specs=[WHOLE] * 2,
        out_specs=WHOLE,
        scratch_shapes=[pltpu.VMEM((span, cells), jnp.float32)],
        cost_estimate=pl.CostEstimate(
            flops=2 * rows * depth * cells, bytes_accessed=4 * rows * depth, transcendentals=0
        ),
        compiler_params=pltpu.CompilerParams(vmem_limit_bytes=16 << 20),
        name="first",
    )(matrix, own)


def rest_kernel(windows, matrix_ref, part_ref, other_ref, out_ref, padded):
    for index, (low, high, offset) in enumerate(windows):
        def run(low=low, high=high, offset=offset):
            pad_into(padded, offset, other_ref)
            out_ref[...] = (
                part_ref[...]
                + jnp.dot(
                    matrix_ref[:, low:high], padded[: high - low, :].astype(jnp.bfloat16),
                    preferred_element_type=jnp.float32,
                )
            ).astype(jnp.bfloat16)
        pl.when(lax.axis_index("sub") != index)(run)


def rest(matrix, part, other, windows):
    rows, depth = matrix.shape
    cells = other.shape[1]
    span = max(high - low for low, high, _ in windows)
    return pl.pallas_call(
        functools.partial(rest_kernel, windows),
        out_shape=jax.ShapeDtypeStruct((rows, cells), jnp.bfloat16),
        in_specs=[WHOLE] * 3,
        out_specs=WHOLE,
        scratch_shapes=[pltpu.VMEM((span, cells), jnp.float32)],
        cost_estimate=pl.CostEstimate(
            flops=2 * rows * span * cells, bytes_accessed=2 * rows * span, transcendentals=0
        ),
        compiler_params=pltpu.CompilerParams(vmem_limit_bytes=16 << 20),
        name="rest",
    )(matrix, part, other)


def build_select(code, base, out_ref, column, classes):
    entries, cells = code.shape
    slots = (code & ((1 << CLASS_SHIFT) - 1)) - base
    kinds = code >> CLASS_SHIFT
    band = 32
    for low in range(0, cells, band):
        source = lax.broadcasted_iota(jnp.int32, (band, cells), 0) + low
        totals = [jnp.zeros((band, cells), jnp.bfloat16)] * classes
        for entry in range(entries):
            hit = jnp.where(slots[entry : entry + 1, :] == source, 1.0, 0.0).astype(jnp.bfloat16)
            for k in range(classes):
                used = jnp.where(kinds[entry : entry + 1, :] == k, 1.0, 0.0).astype(jnp.bfloat16)
                totals[k] = totals[k] + hit * used
        for k in range(classes):
            out_ref[k * cells + low : k * cells + low + band, column : column + cells] = totals[k]


def prepare_kernel(
    windows, translate_ref, own_ref, mate_ref, code_ref, near_ref,
    held_ref, product_ref, select_own_ref, select_mate_ref, padded, sems,
):
    rows, classes, _ = translate_ref.shape
    entries, cells = code_ref.shape
    copies = []
    for i, (start, size) in enumerate(chunks(rows)):
        part = pl.ds(start, size)
        copy = pltpu.make_async_copy(translate_ref.at[part], held_ref.at[part], sems.at[i])
        copy.start()
        copies.append(copy)

    step = away()
    codes = [code_ref[...], near_ref[:entries, :], near_ref[entries:, :]]
    for block, code in enumerate(codes):
        base = (REACH - block * step) * cells
        build_select(code, base, select_own_ref, block * cells, classes)
        if block < 2:
            base = (REACH - (1 + block) * step) * cells
            build_select(code, base, select_mate_ref, block * cells, classes)

    for copy in copies:
        copy.wait()

    for index, (low, high, offset) in enumerate(windows):
        def run(low=low, high=high, offset=offset):
            pad_into(padded, offset, own_ref, mate_ref)
            right = padded[: high - low, :].astype(jnp.bfloat16)
            for start, size in chunks(rows):
                left = held_ref[start : start + size, :, low:high]
                product_ref[start * classes : (start + size) * classes, :] = jnp.dot(
                    left.reshape(size * classes, high - low), right,
                    preferred_element_type=jnp.float32,
                )
        if len(windows) == 1:
            run()
        else:
            pl.when(lax.axis_index("sub") == index)(run)


def push_kernel(
    windows, held_ref, product_ref, own_ref, mate_ref, select_own_ref, select_mate_ref,
    out_ref, sent_ref, padded, own_terms_ref, mate_terms_ref,
):
    rows, classes, _ = held_ref.shape
    cells = own_ref.shape[1]

    def keep(size, value):
        own_terms_ref[: size * classes, :] = value[:, :cells]
        mate_terms_ref[: size * classes, :] = value[:, cells:]

    def finish(start, size):
        def by_class(ref):
            parts = [ref[pl.ds(k, size, stride=classes), :] for k in range(classes)]
            return jnp.concatenate([part.astype(jnp.bfloat16) for part in parts], axis=1)

        total = jnp.dot(
            by_class(own_terms_ref), select_own_ref[...], preferred_element_type=jnp.float32
        )
        extra = jnp.dot(
            by_class(mate_terms_ref), select_mate_ref[...], preferred_element_type=jnp.float32
        )
        part = slice(start, start + size)
        out_ref[part, :] = total[:, :cells] + extra[:, :cells]
        sent_ref[part, :cells] = (total[:, cells : 2 * cells] + extra[:, cells:]).astype(
            jnp.bfloat16
        )
        sent_ref[part, cells:] = total[:, 2 * cells :].astype(jnp.bfloat16)

    for index, (low, high, offset) in enumerate(windows):
        def run(low=low, high=high, offset=offset):
            pad_into(padded, offset, own_ref, mate_ref)
            right = padded[: high - low, :].astype(jnp.bfloat16)
            for start, size in chunks(rows):
                left = held_ref[start : start + size, :, low:high]
                part = pl.ds(start * classes, size * classes)
                keep(size, product_ref[part, :] + jnp.dot(
                    left.reshape(size * classes, high - low), right,
                    preferred_element_type=jnp.float32,
                ))
                finish(start, size)
        pl.when(lax.axis_index("sub") != index)(run)

    if not windows:
        for start, size in chunks(rows):
            keep(size, product_ref[pl.ds(start * classes, size * classes), :])
            finish(start, size)


def prepare(operators, own, mate, code, near_codes, windows):
    rows, classes, depth = operators.shape
    cells = code.shape[1]
    span = max(high - low for low, high, _ in windows)
    return pl.pallas_call(
        functools.partial(prepare_kernel, windows),
        out_shape=[
            jax.ShapeDtypeStruct((rows, classes, depth), jnp.bfloat16),
            jax.ShapeDtypeStruct((rows * classes, 2 * cells), jnp.float32),
            jax.ShapeDtypeStruct((classes * cells, 3 * cells), jnp.bfloat16),
            jax.ShapeDtypeStruct((classes * cells, 2 * cells), jnp.bfloat16),
        ],
        in_specs=[pl.BlockSpec(memory_space=pl.ANY)] + [WHOLE] * 4,
        out_specs=[WHOLE] * 4,
        scratch_shapes=[
            pltpu.VMEM((span, 2 * cells), jnp.float32),
            pltpu.SemaphoreType.DMA((len(chunks(rows)),)),
        ],
        cost_estimate=pl.CostEstimate(
            flops=4 * rows * classes * cells * span,
            bytes_accessed=2 * rows * classes * depth,
            transcendentals=0,
        ),
        compiler_params=pltpu.CompilerParams(vmem_limit_bytes=40 << 20),
        name="prepare",
    )(operators, own, mate, code, near_codes)


def push(held, product, own, mate, select_own, select_mate, windows):
    rows, classes, depth = held.shape
    cells = own.shape[1]
    span = max([high - low for low, high, _ in windows], default=LANES)
    return pl.pallas_call(
        functools.partial(push_kernel, windows),
        out_shape=[
            jax.ShapeDtypeStruct((rows, cells), jnp.float32),
            jax.ShapeDtypeStruct((rows, 2 * cells), jnp.bfloat16),
        ],
        in_specs=[WHOLE] * 6,
        out_specs=[WHOLE] * 2,
        scratch_shapes=[
            pltpu.VMEM((span, 2 * cells), jnp.float32),
            pltpu.VMEM((CHUNK * classes, cells), jnp.float32),
            pltpu.VMEM((CHUNK * classes, cells), jnp.float32),
        ],
        cost_estimate=pl.CostEstimate(
            flops=2 * rows * classes * cells * (2 * span + 5 * cells),
            bytes_accessed=2 * rows * classes * depth,
            transcendentals=0,
        ),
        compiler_params=pltpu.CompilerParams(vmem_limit_bytes=40 << 20),
        name="push",
    )(held, product, own, mate, select_own, select_mate)


def shards(up_check, up_inverse, translate, down_inverse, list_slot, list_class, list_count):
    classes, rows, depth = translate.shape
    cells, entries = list_slot.shape
    halves = lax.axis_size("sub") == 2

    active = lax.broadcasted_iota(jnp.int32, (entries, cells), 0) < list_count[None, :]
    code = jnp.where(active, (list_class.T << CLASS_SHIFT) + list_slot.T, -1)
    chip_codes = jnp.concatenate([code, to_mate(code)], axis=0)
    near_codes = to_near(chip_codes)

    operators = jnp.transpose(translate, (1, 0, 2))
    if halves:
        windows = half_windows(rows, depth, 2)
        other_check = across_sub(up_check)
        part = first(up_inverse, up_check, windows)
        part, near_codes = lax.optimization_barrier((part, near_codes))
        equivalent = rest(up_inverse, part, other_check, windows)
        other = across_sub(equivalent)
    else:
        equivalent = lax.all_gather(
            jnp.dot(
                up_inverse, lax.all_gather(up_check, "sub", axis=0, tiled=True),
                preferred_element_type=jnp.float32,
            ).astype(jnp.bfloat16),
            "sub", axis=0, tiled=True,
        )
        windows = [(0, depth, 0)]
        other = equivalent
    held, product, select_own, select_mate = prepare(
        operators, equivalent, to_mate(equivalent), code, near_codes, windows
    )
    if halves:
        other, product = lax.optimization_barrier((other, product))
    other_mate = to_mate(other) if halves else other
    own_sum, sent = push(
        held, product, other, other_mate, select_own, select_mate, windows if halves else []
    )

    came = to_near(sent)
    came_far = to_mate(came[:, cells:])
    down_check = (
        own_sum + (came[:, :cells].astype(jnp.float32) + came_far.astype(jnp.float32))
    ).astype(jnp.bfloat16)
    if halves:
        other_down = across_sub(down_check)
        return rest(down_inverse, first(down_inverse, down_check, windows), other_down, windows)
    return jnp.dot(
        down_inverse, lax.all_gather(down_check, "sub", axis=0, tiled=True),
        preferred_element_type=jnp.float32,
    ).astype(jnp.bfloat16)


def solution(mesh):
    in_specs = (
        P("sub", "tile"),
        P("sub", None),
        P(None, "sub", None),
        P("sub", None),
        P("tile", None),
        P("tile", None),
        P("tile"),
    )
    out_specs = P("sub", "tile")
    return jax.shard_map(shards, mesh=mesh, in_specs=in_specs, out_specs=out_specs, check_vma=False)
```

time: 49.8 us -> 37.4 us (0.75)
  blocking collectives: 16.8 us -> 0 us
  Pallas kernels: 0 us -> 9.85 us
  matrix products: 8.38 us -> 0 us
  waiting for transfers between devices: 7.63 us -> 12.5 us
  local copies, waits for them, and re-layouts: 6.16 us -> 2.05 us
  starting transfers between devices: 10.2 us -> 11.7 us
  other arithmetic: 0.1 us -> 0.76 us
    all_gather x3 -> x0, blocking collectives: 16.8 us -> none  [the longest x1 5.91 us: shards(): lax.all_gather(up_check, 'sub', axis=0, tiled=True)]
    pallas_call x0 -> x6, Pallas kernels: none -> 9.85 us  [the longest x1 4.02 us: push(): pl.pallas_call(functools.partial(push_kernel, windows), out_shape=[jax.Sh...]
    dot_general x4 -> x0, matrix products: 8.38 us -> none  [the longest x1 4.7 us: shards(): jnp.einsum('kre,kec->rc', translate, grouped_half, preferred_element_type...]
    gather x1 -> x0, local copies, waits for them, and re-layouts: 5.28 us -> none  [shards(): picked = jnp.take(window, list_slot, axis=1)]
    ppermute x4 -> x9, waiting for transfers between devices: 7.63 us -> 12.5 us  [the longest x2 5.84 us: to_near(): lax.ppermute(value, 'tile', [(a, b) for a, b in pairs if 0 <= b < count])]
    unnamed x19 -> x6, local copies, waits for them, and re-layouts: 0.53 us -> 2.04 us
    ppermute x4 -> x9, starting transfers between devices: 10.2 us -> 11.7 us  [the longest x2 6.01 us: to_near(): lax.ppermute(value, 'tile', [(a, b) for a, b in pairs if 0 <= b < count])]
    select_n x1, other arithmetic: 0.01 us -> 0.71 us  [shards(): code = jnp.where(active, (list_class.T << CLASS_SHIFT) + list_slot.T, -1)]
  transfers between devices with their start and end apart: 4 -> 9, of which waited for: 1 -> 7; matrix products, arithmetic and copies ran while one was open for 1% -> 0% of each run, Pallas kernels for 0% -> 12%
where the time goes in v2:
time: 37.4 us; the launch traced here: 36.9 us
  waiting for transfers between devices  12.5 us (33%)
  starting transfers between devices  11.7 us (31%)
  Pallas kernels  9.85 us (26%)
  local copies, waits for them, and re-layouts  2.05 us (5%)
  other arithmetic  0.76 us (2%)
    ppermute x2, starting transfers between devices, to_near(): lax.ppermute(value, 'tile', [(a, b) for a, b in pairs if 0 <= b < count])  6.01 us
    ppermute x2, waiting for transfers between devices, to_near(): lax.ppermute(value, 'tile', [(a, b) for a, b in pairs if 0 <= b < count])  5.84 us
    ppermute x3, waiting for transfers between devices, across_sub(): return lax.ppermute(shard, 'sub', [(0, 1), (1, 0)])  4.2 us
    pallas_call x1, Pallas kernels, push(): pl.pallas_call(functools.partial(push_kernel, windows), out_shape=[jax.Sh...  4.02 us
    pallas_call x1, Pallas kernels, prepare(): pl.pallas_call(functools.partial(prepare_kernel, windows), out_shape=[jax...  4 us
    ppermute x3, starting transfers between devices, across_sub(): return lax.ppermute(shard, 'sub', [(0, 1), (1, 0)])  3.87 us
    ppermute x4, waiting for transfers between devices, to_mate(): return lax.ppermute(value, 'tile', pairs)  2.46 us
    unnamed x6, local copies, waits for them, and re-layouts  2.04 us
  transfers between devices with their start and end apart: 9, of which 7 were waited for; matrix products, arithmetic and copies ran while one was open for 0% of the time, Pallas kernels for 12%

profile of v2, /device:TPU:8, one launch (start us, length us, event | category | flops | bytes accessed | tf_op | source)
XLA Modules:
  0.0 36.9 jit_solution(2973893406880936399)
XLA Ops:
  0.0 0.7 %bitcast_select_fusion.code_ref = s32[8,128]{1,0:T(8,128)S(1)} fusion(s32[128,8]{0,1:T(8,128)} %param.11, s32[128,8]{0,1:T(8,128)} %param.12, s32[128]{0:T(128)} %param.13), kind=kLoop, calls=%fused_computation.2 | loop fusion | flops 4096 | bytes 12800 | tf_op jit(solution)/shard_map/jit(_where)/select_n | solution.py:287
  0.7 0.0 collective-permute-start
  0.7 1.6 %collective-permute-start.2 = (bf16[444,128]{1,0:T(8,128)(2,1)}, bf16[444,128]{1,0:T(8,128)(2,1)S(1)}, u32[]{:S(2)}, u32[]{:S(2)}) collective-permute-start(bf16[444,128]{1,0:T(8,128)(2,1)} %own_ref.1), channel_id=1, source_target_pairs={{0,1},{1,0},{2,3},{3,2},{4,5},{5,4},{6,7},{7,6},{8,9},{9,8},{10,11... | collective-permute-start | bytes 341000 | tf_op jit(solution)/shard_map/ppermute | solution.py:18
  2.3 0.0 collective-permute-done
  2.3 3.1 %collective-permute-start.1 = (s32[16,128]{1,0:T(8,128)S(1)}, s32[16,128]{1,0:T(8,128)S(1)}, u32[]{:S(2)}, u32[]{:S(2)}) collective-permute-start(s32[16,128]{1,0:T(8,128)S(1)} %pad_add_fusion), channel_id=1, source_target_pairs={{2,4},{4,2},{6,8},{8,6},{10,12},{12,10},{14,16},{16,14},{18,20},{2... | collective-permute-start | bytes 24584 | tf_op jit(solution)/shard_map/ppermute | solution.py:30
  5.4 0.0 copy-start
  5.4 1.1 %copy-done = bf16[444,888]{1,0:T(8,128)(2,1)S(1)} copy-done((bf16[444,888]{1,0:T(8,128)(2,1)S(1)}, bf16[444,888]{1,0:T(8,128)(2,1)}, u32[]{:S(2)}) %copy-start) | copy-done | bytes 788568
  6.5 0.0 copy-start.2
  6.5 0.9 %copy-done.2 = bf16[444,128]{1,0:T(8,128)(2,1)S(1)} copy-done((bf16[444,128]{1,0:T(8,128)(2,1)S(1)}, bf16[444,128]{1,0:T(8,128)(2,1)}, u32[]{:S(2)}) %copy-start.2) | copy-done | bytes 113688
  7.4 0.3 first.2.part_ref
  7.7 0.4 %collective-permute-done.1.near_ref = s32[16,128]{1,0:T(8,128)S(1)} collective-permute-done((s32[16,128]{1,0:T(8,128)S(1)}, s32[16,128]{1,0:T(8,128)S(1)}, u32[]{:S(2)}, u32[]{:S(2)}) %collective-permute-start.1) | collective-permute-done | bytes 8224 | tf_op jit(solution)/shard_map/ppermute | solution.py:30
  8.1 0.0 collective-permute-done.2.other_ref
  8.1 0.3 rest.2.own_ref
  8.4 0.1 collective-permute-start.3
  8.6 1.1 %collective-permute-start.4 = (bf16[444,128]{1,0:T(8,128)(2,1)S(1)}, bf16[444,128]{1,0:T(8,128)(2,1)S(1)}, u32[]{:S(2)}, u32[]{:S(2)}) collective-permute-start(bf16[444,128]{1,0:T(8,128)(2,1)S(1)} %rest.2.own_ref), channel_id=1, source_target_pairs={{0,1},{1,0},{2,3},{3,2},{4,5},{5,4},{6,7},{7,6},{8,9},{9,8},{10,11... | collective-permute-start | bytes 341000 | tf_op jit(solution)/shard_map/ppermute | solution.py:18
  9.7 0.2 collective-permute-done.3.mate_ref
  9.8 4.0 %prepare.1 = (bf16[444,8,888]{2,1,0:T(8,128)(2,1)S(1)}, f32[3552,256]{1,0:T(8,128)S(1)}, bf16[1024,384]{1,0:T(8,128)(2,1)S(1)}, bf16[1024,256]{1,0:T(8,128)(2,1)S(1)}) custom-call(bf16[444,8,888]{2,1,0:T(8,128)(2,1)} %bitcast.3, bf16[444,128]{1,0:T(8,128)(2,1)S(1)} %rest.2.own_ref, bf16[444,128]{1,0:T(8,128)(2,1)S(1)} %collective-permute-done.3.mate_ref, ...), custom_call_target="tpu_custom_call" | custom-call | flops 931135488 | bytes 6308352 | tf_op jit(solution)/shard_map/prepare/pallas_call | solution.py:230
  13.8 0.0 copy-start.1
  13.9 0.2 collective-permute-done.4.own_ref
  14.1 0.0 collective-permute-start.5
  14.1 1.3 %collective-permute-done.5.mate_ref = bf16[444,128]{1,0:T(8,128)(2,1)S(1)} collective-permute-done((bf16[444,128]{1,0:T(8,128)(2,1)S(1)}, bf16[444,128]{1,0:T(8,128)(2,1)S(1)}, u32[]{:S(2)}, u32[]{:S(2)}) %collective-permute-start.5) | collective-permute-done | bytes 113696 | tf_op jit(solution)/shard_map/ppermute | solution.py:24
  15.4 4.0 %push.1 = (f32[444,128]{1,0:T(8,128)S(1)}, bf16[444,256]{1,0:T(8,128)(2,1)S(1)}) custom-call(bf16[444,8,888]{2,1,0:T(8,128)(2,1)S(1)} %get-tuple-element.17.held_ref, f32[3552,256]{1,0:T(8,128)S(1)} %get-tuple-element.19.product_ref, bf16[444,128]{1,0:T(8,128)(2,1)S(1)} %collective-permute-done.4.own_ref, ...), custom_call_target="tpu_custom_call" | custom-call | flops 1513095168 | bytes 6308352 | tf_op jit(solution)/shard_map/push/pallas_call | solution.py:258
  19.4 2.9 %collective-permute-start.6 = (bf16[444,256]{1,0:T(8,128)(2,1)S(1)}, bf16[444,256]{1,0:T(8,128)(2,1)S(1)}, u32[]{:S(2)}, u32[]{:S(2)}) collective-permute-start(bf16[444,256]{1,0:T(8,128)(2,1)S(1)} %get-tuple-element.24), channel_id=1, source_target_pairs={{2,4},{4,2},{6,8},{8,6},{10,12},{12,10},{14,16},{16,14},{18,20},{2... | collective-permute-start | bytes 681992 | tf_op jit(solution)/shard_map/ppermute | solution.py:30
  22.4 5.4 %collective-permute-done.6 = bf16[444,256]{1,0:T(8,128)(2,1)S(1)} collective-permute-done((bf16[444,256]{1,0:T(8,128)(2,1)S(1)}, bf16[444,256]{1,0:T(8,128)(2,1)S(1)}, u32[]{:S(2)}, u32[]{:S(2)}) %collective-permute-start.6) | collective-permute-done | bytes 227360 | tf_op jit(solution)/shard_map/ppermute | solution.py:30
  27.8 1.7 %collective-permute-start.7 = (bf16[444,128]{1,0:T(8,128)(2,1)S(1)}, bf16[444,128]{1,0:T(8,128)(2,1)S(1)}, u32[]{:S(2)}, u32[]{:S(2)}) collective-permute-start(bf16[444,128]{1,0:T(8,128)(2,1)S(1)} %slice.9), channel_id=1, source_target_pairs={{0,2},{2,0},{4,6},{6,4},{8,10},{10,8},{12,14},{14,12},{16,18},{18,... | collective-permute-start | bytes 341000 | tf_op jit(solution)/shard_map/ppermute | solution.py:24
  29.5 1.0 %collective-permute-done.7 = bf16[444,128]{1,0:T(8,128)(2,1)S(1)} collective-permute-done((bf16[444,128]{1,0:T(8,128)(2,1)S(1)}, bf16[444,128]{1,0:T(8,128)(2,1)S(1)}, u32[]{:S(2)}, u32[]{:S(2)}) %collective-permute-start.7) | collective-permute-done | bytes 113696 | tf_op jit(solution)/shard_map/ppermute | solution.py:24
  30.5 1.2 %collective-permute-start.8 = (bf16[444,128]{1,0:T(8,128)(2,1)S(1)}, bf16[444,128]{1,0:T(8,128)(2,1)S(1)}, u32[]{:S(2)}, u32[]{:S(2)}) collective-permute-start(bf16[444,128]{1,0:T(8,128)(2,1)S(1)} %add_convert_fusion.own_ref), channel_id=1, source_target_pairs={{0,1},{1,0},{2,3},{3,2},{4,5},{5,4},{6,7},{7,6},{8,9},{9,8},{10,11... | collective-permute-start | bytes 341000 | tf_op jit(solution)/shard_map/ppermute | solution.py:18
  31.7 0.0 copy-done.1
  31.7 0.3 first.3.part_ref
  32.0 4.0 %collective-permute-done.8.other_ref = bf16[444,128]{1,0:T(8,128)(2,1)S(1)} collective-permute-done((bf16[444,128]{1,0:T(8,128)(2,1)S(1)}, bf16[444,128]{1,0:T(8,128)(2,1)S(1)}, u32[]{:S(2)}, u32[]{:S(2)}) %collective-permute-start.8) | collective-permute-done | bytes 113696 | tf_op jit(solution)/shard_map/ppermute | solution.py:18
  36.0 1.0 %rest.3 = bf16[444,128]{1,0:T(8,128)(2,1)} custom-call(bf16[444,888]{1,0:T(8,128)(2,1)S(1)} %copy-done.1, f32[444,128]{1,0:T(8,128)S(1)} %first.3.part_ref, bf16[444,128]{1,0:T(8,128)(2,1)S(1)} %collective-permute-done.8.other_ref), custom_call_target="tpu_custom_call" | custom-call | flops 58195968 | bytes 454656 | tf_op jit(solution)/shard_map/rest/pallas_call | solution.py:105
  (3 shorter events, 0.1 us)
Async XLA Ops:
  0.7 1.6 %collective-permute-start = (s32[8,128]{1,0:T(8,128)S(1)}, s32[8,128]{1,0:T(8,128)S(1)}, u32[]{:S(2)}, u32[]{:S(2)}) collective-permute-start(s32[8,128]{1,0:T(8,128)S(1)} %bitcast_select_fusion.code_ref), channel_id=1, source_target_pairs={{0,2},{2,0},{4,6},{6,4},{8,10},{10,8},{12,14},{14,12},{16,18},{18,... | collective-permute-start | bytes 12296 | tf_op jit(solution)/shard_map/ppermute | solution.py:24
  0.7 7.4 %collective-permute-start.2 = (bf16[444,128]{1,0:T(8,128)(2,1)}, bf16[444,128]{1,0:T(8,128)(2,1)S(1)}, u32[]{:S(2)}, u32[]{:S(2)}) collective-permute-start(bf16[444,128]{1,0:T(8,128)(2,1)} %own_ref.1), channel_id=1, source_target_pairs={{0,1},{1,0},{2,3},{3,2},{4,5},{5,4},{6,7},{7,6},{8,9},{9,8},{10,11... | collective-permute-start | bytes 341000 | tf_op jit(solution)/shard_map/ppermute | solution.py:18
  2.3 5.9 %collective-permute-start.1 = (s32[16,128]{1,0:T(8,128)S(1)}, s32[16,128]{1,0:T(8,128)S(1)}, u32[]{:S(2)}, u32[]{:S(2)}) collective-permute-start(s32[16,128]{1,0:T(8,128)S(1)} %pad_add_fusion), channel_id=1, source_target_pairs={{2,4},{4,2},{6,8},{8,6},{10,12},{12,10},{14,16},{16,14},{18,20},{2... | collective-permute-start | bytes 24584 | tf_op jit(solution)/shard_map/ppermute | solution.py:30
  5.4 1.1 %copy-start = (bf16[444,888]{1,0:T(8,128)(2,1)S(1)}, bf16[444,888]{1,0:T(8,128)(2,1)}, u32[]{:S(2)}) copy-start(bf16[444,888]{1,0:T(8,128)(2,1)} %matrix_ref.5) | copy-start | bytes 2365636
  6.5 0.9 %copy-start.2 = (bf16[444,128]{1,0:T(8,128)(2,1)S(1)}, bf16[444,128]{1,0:T(8,128)(2,1)}, u32[]{:S(2)}) copy-start(bf16[444,128]{1,0:T(8,128)(2,1)} %own_ref.1) | copy-start | bytes 340996
  8.4 1.4 %collective-permute-start.3 = (bf16[444,128]{1,0:T(8,128)(2,1)S(1)}, bf16[444,128]{1,0:T(8,128)(2,1)S(1)}, u32[]{:S(2)}, u32[]{:S(2)}) collective-permute-start(bf16[444,128]{1,0:T(8,128)(2,1)S(1)} %rest.2.own_ref), channel_id=1, source_target_pairs={{0,2},{2,0},{4,6},{6,4},{8,10},{10,8},{12,14},{14,12},{16,18},{18,... | collective-permute-start | bytes 341000 | tf_op jit(solution)/shard_map/ppermute | solution.py:24
  8.6 5.5 %collective-permute-start.4 = (bf16[444,128]{1,0:T(8,128)(2,1)S(1)}, bf16[444,128]{1,0:T(8,128)(2,1)S(1)}, u32[]{:S(2)}, u32[]{:S(2)}) collective-permute-start(bf16[444,128]{1,0:T(8,128)(2,1)S(1)} %rest.2.own_ref), channel_id=1, source_target_pairs={{0,1},{1,0},{2,3},{3,2},{4,5},{5,4},{6,7},{7,6},{8,9},{9,8},{10,11... | collective-permute-start | bytes 341000 | tf_op jit(solution)/shard_map/ppermute | solution.py:18
  13.8 17.9 %copy-start.1 = (bf16[444,888]{1,0:T(8,128)(2,1)S(1)}, bf16[444,888]{1,0:T(8,128)(2,1)}, u32[]{:S(2)}) copy-start(bf16[444,888]{1,0:T(8,128)(2,1)} %matrix_ref.7) | copy-start | bytes 2365636
  14.1 1.3 %collective-permute-start.5 = (bf16[444,128]{1,0:T(8,128)(2,1)S(1)}, bf16[444,128]{1,0:T(8,128)(2,1)S(1)}, u32[]{:S(2)}, u32[]{:S(2)}) collective-permute-start(bf16[444,128]{1,0:T(8,128)(2,1)S(1)} %collective-permute-done.4.own_ref), channel_id=1, source_target_pairs={{0,2},{2,0},{4,6},{6,4},{8,10},{10,8},{12,14},{14,12},{16,18},{18,... | collective-permute-start | bytes 341000 | tf_op jit(solution)/shard_map/ppermute | solution.py:24
  19.4 8.3 %collective-permute-start.6 = (bf16[444,256]{1,0:T(8,128)(2,1)S(1)}, bf16[444,256]{1,0:T(8,128)(2,1)S(1)}, u32[]{:S(2)}, u32[]{:S(2)}) collective-permute-start(bf16[444,256]{1,0:T(8,128)(2,1)S(1)} %get-tuple-element.24), channel_id=1, source_target_pairs={{2,4},{4,2},{6,8},{8,6},{10,12},{12,10},{14,16},{16,14},{18,20},{2... | collective-permute-start | bytes 681992 | tf_op jit(solution)/shard_map/ppermute | solution.py:30
  27.8 2.6 %collective-permute-start.7 = (bf16[444,128]{1,0:T(8,128)(2,1)S(1)}, bf16[444,128]{1,0:T(8,128)(2,1)S(1)}, u32[]{:S(2)}, u32[]{:S(2)}) collective-permute-start(bf16[444,128]{1,0:T(8,128)(2,1)S(1)} %slice.9), channel_id=1, source_target_pairs={{0,2},{2,0},{4,6},{6,4},{8,10},{10,8},{12,14},{14,12},{16,18},{18,... | collective-permute-start | bytes 341000 | tf_op jit(solution)/shard_map/ppermute | solution.py:24
  30.5 5.5 %collective-permute-start.8 = (bf16[444,128]{1,0:T(8,128)(2,1)S(1)}, bf16[444,128]{1,0:T(8,128)(2,1)S(1)}, u32[]{:S(2)}, u32[]{:S(2)}) collective-permute-start(bf16[444,128]{1,0:T(8,128)(2,1)S(1)} %add_convert_fusion.own_ref), channel_id=1, source_target_pairs={{0,1},{1,0},{2,3},{3,2},{4,5},{5,4},{6,7},{7,6},{8,9},{9,8},{10,11... | collective-permute-start | bytes 341000 | tf_op jit(solution)/shard_map/ppermute | solution.py:18

commit v3 on v2

--- a/solution.py
+++ b/solution.py
@@ -53,6 +53,50 @@
     for i, ref in enumerate(refs):
         rows, cells = ref.shape
         padded[offset : offset + rows, i * cells : (i + 1) * cells] = ref[...].astype(padded.dtype)
+
+
+def stage_kernel(
+    windows, matrix_ref, own_ref, translate_ref, matrix_held, translate_held, part_ref,
+    own_held, padded, sems,
+):
+    copies = [
+        pltpu.make_async_copy(own_ref, own_held, sems.at[0]),
+        pltpu.make_async_copy(matrix_ref, matrix_held, sems.at[1]),
+        pltpu.make_async_copy(translate_ref, translate_held, sems.at[2]),
+    ]
+    for copy in copies:
+        copy.start()
+    copies[0].wait()
+    copies[1].wait()
+    first_kernel(windows, matrix_held, own_held, part_ref, padded)
+    copies[2].wait()
+
+
+def stage(matrix, own, operators, windows):
+    rows, depth = matrix.shape
+    cells = own.shape[1]
+    span = max(high - low for low, high, _ in windows)
+    return pl.pallas_call(
+        functools.partial(stage_kernel, windows),
+        out_shape=[
+            jax.ShapeDtypeStruct(matrix.shape, matrix.dtype),
+            jax.ShapeDtypeStruct(operators.shape, operators.dtype),
+            jax.ShapeDtypeStruct((rows, cells), jnp.float32),
+        ],
+        in_specs=[pl.BlockSpec(memory_space=pltpu.HBM)] * 3,
+        out_specs=[WHOLE] * 3,
+        scratch_shapes=[
+            pltpu.VMEM(own.shape, own.dtype),
+            pltpu.VMEM((span, cells), jnp.float32),
+            pltpu.SemaphoreType.DMA((3,)),
+        ],
+        cost_estimate=pl.CostEstimate(
+            flops=2 * rows * depth * cells, bytes_accessed=2 * operators.size,
+            transcendentals=0,
+        ),
+        compiler_params=pltpu.CompilerParams(vmem_limit_bytes=24 << 20),
+        name="stage",
+    )(*[pltpu.with_memory_space_constraint(x, pltpu.HBM) for x in (matrix, own, operators)])
 
 
 def first_kernel(windows, matrix_ref, own_ref, out_ref, padded):
@@ -134,29 +178,20 @@
 
 
 def prepare_kernel(
-    windows, translate_ref, own_ref, mate_ref, code_ref, near_ref,
-    held_ref, product_ref, select_own_ref, select_mate_ref, padded, sems,
+    windows, held_ref, own_ref, mate_ref, codes_ref,
+    product_ref, select_own_ref, select_mate_ref, padded,
 ):
-    rows, classes, _ = translate_ref.shape
-    entries, cells = code_ref.shape
-    copies = []
-    for i, (start, size) in enumerate(chunks(rows)):
-        part = pl.ds(start, size)
-        copy = pltpu.make_async_copy(translate_ref.at[part], held_ref.at[part], sems.at[i])
-        copy.start()
-        copies.append(copy)
-
+    rows, classes, _ = held_ref.shape
+    tiles, _, cells = codes_ref.shape
     step = away()
-    codes = [code_ref[...], near_ref[:entries, :], near_ref[entries:, :]]
-    for block, code in enumerate(codes):
+    tile = lax.axis_index("tile")
+    for block in range(3):
+        code = codes_ref[jnp.clip(tile + block * step, 0, tiles - 1)]
         base = (REACH - block * step) * cells
         build_select(code, base, select_own_ref, block * cells, classes)
         if block < 2:
             base = (REACH - (1 + block) * step) * cells
             build_select(code, base, select_mate_ref, block * cells, classes)
-
-    for copy in copies:
-        copy.wait()
 
     for index, (low, high, offset) in enumerate(windows):
         def run(low=low, high=high, offset=offset):
@@ -176,85 +211,82 @@
 
 def push_kernel(
     windows, held_ref, product_ref, own_ref, mate_ref, select_own_ref, select_mate_ref,
-    out_ref, sent_ref, padded, own_terms_ref, mate_terms_ref,
+    out_ref, sent_ref, padded, own_terms, mate_terms,
 ):
     rows, classes, _ = held_ref.shape
     cells = own_ref.shape[1]
-
-    def keep(size, value):
-        own_terms_ref[: size * classes, :] = value[:, :cells]
-        mate_terms_ref[: size * classes, :] = value[:, cells:]
-
-    def finish(start, size):
-        def by_class(ref):
-            parts = [ref[pl.ds(k, size, stride=classes), :] for k in range(classes)]
-            return jnp.concatenate([part.astype(jnp.bfloat16) for part in parts], axis=1)
-
-        total = jnp.dot(
-            by_class(own_terms_ref), select_own_ref[...], preferred_element_type=jnp.float32
-        )
-        extra = jnp.dot(
-            by_class(mate_terms_ref), select_mate_ref[...], preferred_element_type=jnp.float32
-        )
-        part = slice(start, start + size)
-        out_ref[part, :] = total[:, :cells] + extra[:, :cells]
-        sent_ref[part, :cells] = (total[:, cells : 2 * cells] + extra[:, cells:]).astype(
-            jnp.bfloat16
-        )
-        sent_ref[part, cells:] = total[:, 2 * cells :].astype(jnp.bfloat16)
-
+    band = 256 // classes
+    line = lax.broadcasted_iota(jnp.int32, (256, 256), 0)
+    column = lax.broadcasted_iota(jnp.int32, (256, 256), 1)
+    apart = (column == (line % band) * classes + line // band).astype(jnp.bfloat16)
+
+    def keep(start, size, value):
+        value = value.astype(jnp.bfloat16)
+        if size < band:
+            value = jnp.concatenate(
+                [value, jnp.zeros(((band - size) * classes, 2 * cells), jnp.bfloat16)], axis=0
+            )
+        value = jnp.dot(apart, value, preferred_element_type=jnp.float32).astype(jnp.bfloat16)
+        for k in range(classes):
+            part = value[k * band : (k + 1) * band, :]
+            own_terms[start : start + band, k * cells : (k + 1) * cells] = part[:, :cells]
+            mate_terms[start : start + band, k * cells : (k + 1) * cells] = part[:, cells:]
+
+    bands = [(start, min(band, rows - start)) for start in range(0, rows, band)]
     for index, (low, high, offset) in enumerate(windows):
         def run(low=low, high=high, offset=offset):
             pad_into(padded, offset, own_ref, mate_ref)
             right = padded[: high - low, :].astype(jnp.bfloat16)
-            for start, size in chunks(rows):
+            for start, size in bands:
                 left = held_ref[start : start + size, :, low:high]
                 part = pl.ds(start * classes, size * classes)
-                keep(size, product_ref[part, :] + jnp.dot(
+                keep(start, size, product_ref[part, :] + jnp.dot(
                     left.reshape(size * classes, high - low), right,
                     preferred_element_type=jnp.float32,
                 ))
-                finish(start, size)
         pl.when(lax.axis_index("sub") != index)(run)
 
     if not windows:
-        for start, size in chunks(rows):
-            keep(size, product_ref[pl.ds(start * classes, size * classes), :])
-            finish(start, size)
-
-
-def prepare(operators, own, mate, code, near_codes, windows):
-    rows, classes, depth = operators.shape
-    cells = code.shape[1]
+        for start, size in bands:
+            keep(start, size, product_ref[pl.ds(start * classes, size * classes), :])
+
+    total = jnp.dot(own_terms[...], select_own_ref[...], preferred_element_type=jnp.float32)
+    extra = jnp.dot(mate_terms[...], select_mate_ref[...], preferred_element_type=jnp.float32)
+    total, extra = total[:rows], extra[:rows]
+    out_ref[...] = total[:, :cells] + extra[:, :cells]
+    sent_ref[:, :cells] = (total[:, cells : 2 * cells] + extra[:, cells:]).astype(jnp.bfloat16)
+    sent_ref[:, cells:] = total[:, 2 * cells :].astype(jnp.bfloat16)
+
+
+def prepare(held, own, mate, codes, windows):
+    rows, classes, depth = held.shape
+    cells = codes.shape[2]
     span = max(high - low for low, high, _ in windows)
     return pl.pallas_call(
         functools.partial(prepare_kernel, windows),
         out_shape=[
-            jax.ShapeDtypeStruct((rows, classes, depth), jnp.bfloat16),
             jax.ShapeDtypeStruct((rows * classes, 2 * cells), jnp.float32),
             jax.ShapeDtypeStruct((classes * cells, 3 * cells), jnp.bfloat16),
             jax.ShapeDtypeStruct((classes * cells, 2 * cells), jnp.bfloat16),
         ],
-        in_specs=[pl.BlockSpec(memory_space=pl.ANY)] + [WHOLE] * 4,
-        out_specs=[WHOLE] * 4,
-        scratch_shapes=[
-            pltpu.VMEM((span, 2 * cells), jnp.float32),
-            pltpu.SemaphoreType.DMA((len(chunks(rows)),)),
-        ],
+        in_specs=[WHOLE] * 4,
+        out_specs=[WHOLE] * 3,
+        scratch_shapes=[pltpu.VMEM((span, 2 * cells), jnp.float32)],
         cost_estimate=pl.CostEstimate(
             flops=4 * rows * classes * cells * span,
             bytes_accessed=2 * rows * classes * depth,
             transcendentals=0,
         ),
-        compiler_params=pltpu.CompilerParams(vmem_limit_bytes=40 << 20),
+        compiler_params=pltpu.CompilerParams(vmem_limit_bytes=32 << 20),
         name="prepare",
-    )(operators, own, mate, code, near_codes)
+    )(held, own, mate, codes)
 
 
 def push(held, product, own, mate, select_own, select_mate, windows):
     rows, classes, depth = held.shape
     cells = own.shape[1]
     span = max([high - low for low, high, _ in windows], default=LANES)
+    padded_rows = pl.cdiv(rows * classes, 256) * 256 // classes
     return pl.pallas_call(
         functools.partial(push_kernel, windows),
         out_shape=[
@@ -265,8 +297,8 @@
         out_specs=[WHOLE] * 2,
         scratch_shapes=[
             pltpu.VMEM((span, 2 * cells), jnp.float32),
-            pltpu.VMEM((CHUNK * classes, cells), jnp.float32),
-            pltpu.VMEM((CHUNK * classes, cells), jnp.float32),
+            pltpu.VMEM((padded_rows, classes * cells), jnp.bfloat16),
+            pltpu.VMEM((padded_rows, classes * cells), jnp.bfloat16),
         ],
         cost_estimate=pl.CostEstimate(
             flops=2 * rows * classes * cells * (2 * span + 5 * cells),
@@ -285,16 +317,15 @@
 
     active = lax.broadcasted_iota(jnp.int32, (entries, cells), 0) < list_count[None, :]
     code = jnp.where(active, (list_class.T << CLASS_SHIFT) + list_slot.T, -1)
-    chip_codes = jnp.concatenate([code, to_mate(code)], axis=0)
-    near_codes = to_near(chip_codes)
-
     operators = jnp.transpose(translate, (1, 0, 2))
+    codes = lax.all_gather(code, "tile")
     if halves:
         windows = half_windows(rows, depth, 2)
         other_check = across_sub(up_check)
-        part = first(up_inverse, up_check, windows)
-        part, near_codes = lax.optimization_barrier((part, near_codes))
-        equivalent = rest(up_inverse, part, other_check, windows)
+        operators, code = lax.optimization_barrier((operators, code))
+        up_held, held, part = stage(up_inverse, up_check, operators, windows)
+        part, codes = lax.optimization_barrier((part, codes))
+        equivalent = rest(up_held, part, other_check, windows)
         other = across_sub(equivalent)
     else:
         equivalent = lax.all_gather(
@@ -306,8 +337,9 @@
         )
         windows = [(0, depth, 0)]
         other = equivalent
-    held, product, select_own, select_mate = prepare(
-        operators, equivalent, to_mate(equivalent), code, near_codes, windows
+        held = operators
+    product, select_own, select_mate = prepare(
+        held, equivalent, to_mate(equivalent), codes, windows
     )
     if halves:
         other, product = lax.optimization_barrier((other, product))

time: 37.4 us -> 56.7 us (1.52)
  the two profiles are of different devices: /device:TPU:8 before, /device:TPU:0 now
where the time goes in v3:
time: 56.7 us; the launch traced here: 56.5 us
  blocking collectives  21.8 us (38%)
  Pallas kernels  12.5 us (22%)
  starting transfers between devices  12 us (21%)
  waiting for transfers between devices  9.39 us (17%)
  other arithmetic  0.75 us (1%)
    all_gather x1, blocking collectives, shards(): codes = lax.all_gather(code, 'tile')  21.8 us
    ppermute x3, starting transfers between devices, to_mate(): return lax.ppermute(value, 'tile', pairs)  7.27 us
    ppermute x3, waiting for transfers between devices, across_sub(): return lax.ppermute(shard, 'sub', [(0, 1), (1, 0)])  6.63 us
    pallas_call x1, Pallas kernels, push(): pl.pallas_call(functools.partial(push_kernel, windows), out_shape=[jax.Sh...  5.57 us
    ppermute x3, starting transfers between devices, across_sub(): return lax.ppermute(shard, 'sub', [(0, 1), (1, 0)])  4.03 us
    pallas_call x1, Pallas kernels, stage(): pl.pallas_call(functools.partial(stage_kernel, windows), out_shape=[jax.S...  3.15 us
    ppermute x3, waiting for transfers between devices, to_mate(): return lax.ppermute(value, 'tile', pairs)  2.75 us
    pallas_call x1, Pallas kernels, prepare(): pl.pallas_call(functools.partial(prepare_kernel, windows), out_shape=[jax...  2.19 us
  transfers between devices with their start and end apart: 7, of which 5 were waited for; matrix products, arithmetic and copies ran while one was open for 1% of the time, Pallas kernels for 10%

profile of v3, /device:TPU:0, one launch (start us, length us, event | category | flops | bytes accessed | tf_op | source)
XLA Modules:
  0.0 56.5 jit_solution(7791918616976477662)
XLA Ops:
  0.0 2.9 %collective-permute-start = (bf16[444,128]{1,0:T(8,128)(2,1)}, bf16[444,128]{1,0:T(8,128)(2,1)S(1)}, u32[]{:S(2)}, u32[]{:S(2)}) collective-permute-start(bf16[444,128]{1,0:T(8,128)(2,1)} %own_ref.1), channel_id=1, source_target_pairs={{0,1},{1,0},{2,3},{3,2},{4,5},{5,4},{6,7},{7,6},{8,9},{9,8},{10,11... | collective-permute-start | bytes 341000 | tf_op jit(solution)/shard_map/ppermute | solution.py:18
  2.9 0.7 %bitcast_select_fusion = s32[8,128]{1,0:T(8,128)S(1)} fusion(s32[128,8]{0,1:T(8,128)} %param.11, s32[128,8]{0,1:T(8,128)} %param.12, s32[128]{0:T(128)} %param.13), kind=kLoop, calls=%fused_computation.1 | loop fusion | flops 4096 | bytes 12800 | tf_op jit(solution)/shard_map/jit(_where)/select_n | solution.py:319
  3.6 3.1 %stage.1 = (bf16[444,888]{1,0:T(8,128)(2,1)S(1)}, bf16[444,8,888]{2,1,0:T(8,128)(2,1)S(1)}, f32[444,128]{1,0:T(8,128)S(1)}) custom-call(bf16[444,888]{1,0:T(8,128)(2,1)} %matrix_ref.3, bf16[444,128]{1,0:T(8,128)(2,1)} %own_ref.1, bf16[444,8,888]{2,1,0:T(8,128)(2,1)} %bitcast.5), custom_call_target="tpu_custom_call" | custom-call | flops 100933632 | bytes 6308352 | tf_op jit(solution)/shard_map/stage/pallas_call | solution.py:79
  6.8 21.8 %all-gather = s32[128,128]{1,0:T(8,128)S(1)} all-gather(s32[8,128]{1,0:T(8,128)S(1)} %bitcast_select_fusion), channel_id=2, replica_groups=mesh['tile'=16,'sub'=2] {'tile'}, dimensions={0}, use_global_device_ids=true | all-gather | bytes 69632 | tf_op jit(solution)/shard_map/all_gather | solution.py:321
  28.6 0.0 collective-permute-done.other_ref
  28.6 0.3 rest.2.own_ref
  28.9 0.4 collective-permute-start.2
  29.3 0.5 collective-permute-start.1
  29.9 0.5 collective-permute-done.2.mate_ref
  30.3 2.2 %prepare.1 = (f32[3552,256]{1,0:T(8,128)S(1)}, bf16[1024,384]{1,0:T(8,128)(2,1)S(1)}, bf16[1024,256]{1,0:T(8,128)(2,1)S(1)}) custom-call(bf16[444,8,888]{2,1,0:T(8,128)(2,1)S(1)} %get-tuple-element.19.held_ref, bf16[444,128]{1,0:T(8,128)(2,1)S(1)} %rest.2.own_ref, bf16[444,128]{1,0:T(8,128)(2,1)S(1)} %collective-permute-done.2.mate_ref, ...), custom_call_target="tpu_custom_call" | custom-call | flops 931135488 | bytes 6308352 | tf_op jit(solution)/shard_map/prepare/pallas_call | solution.py:265
  32.5 0.0 copy-start
  32.5 2.0 %collective-permute-done.1.own_ref = bf16[444,128]{1,0:T(8,128)(2,1)S(1)} collective-permute-done((bf16[444,128]{1,0:T(8,128)(2,1)S(1)}, bf16[444,128]{1,0:T(8,128)(2,1)S(1)}, u32[]{:S(2)}, u32[]{:S(2)}) %collective-permute-start.1) | collective-permute-done | bytes 113696 | tf_op jit(solution)/shard_map/ppermute | solution.py:18
  34.6 0.0 collective-permute-start.3
  34.6 1.3 %collective-permute-done.3.mate_ref = bf16[444,128]{1,0:T(8,128)(2,1)S(1)} collective-permute-done((bf16[444,128]{1,0:T(8,128)(2,1)S(1)}, bf16[444,128]{1,0:T(8,128)(2,1)S(1)}, u32[]{:S(2)}, u32[]{:S(2)}) %collective-permute-start.3) | collective-permute-done | bytes 113696 | tf_op jit(solution)/shard_map/ppermute | solution.py:24
  35.9 5.6 %push.1 = (f32[444,128]{1,0:T(8,128)S(1)}, bf16[444,256]{1,0:T(8,128)(2,1)S(1)}) custom-call(bf16[444,8,888]{2,1,0:T(8,128)(2,1)S(1)} %get-tuple-element.19.held_ref, f32[3552,256]{1,0:T(8,128)S(1)} %get-tuple-element.25.product_ref, bf16[444,128]{1,0:T(8,128)(2,1)S(1)} %collective-permute-done.1.own_ref, ...), custom_call_target="tpu_custom_call" | custom-call | flops 1513095168 | bytes 6308352 | tf_op jit(solution)/shard_map/push/pallas_call | solution.py:290
  41.5 0.7 %collective-permute-start.4 = (bf16[444,256]{1,0:T(8,128)(2,1)S(1)}, bf16[444,256]{1,0:T(8,128)(2,1)S(1)}, u32[]{:S(2)}, u32[]{:S(2)}) collective-permute-start(bf16[444,256]{1,0:T(8,128)(2,1)S(1)} %get-tuple-element.30), channel_id=1, source_target_pairs={{2,4},{4,2},{6,8},{8,6},{10,12},{12,10},{14,16},{16,14},{18,20},{2... | collective-permute-start | bytes 681992 | tf_op jit(solution)/shard_map/ppermute | solution.py:30
  42.1 0.0 collective-permute-done.4
  42.2 6.9 %collective-permute-start.5 = (bf16[444,128]{1,0:T(8,128)(2,1)S(1)}, bf16[444,128]{1,0:T(8,128)(2,1)S(1)}, u32[]{:S(2)}, u32[]{:S(2)}) collective-permute-start(bf16[444,128]{1,0:T(8,128)(2,1)S(1)} %slice.9), channel_id=1, source_target_pairs={{0,2},{2,0},{4,6},{6,4},{8,10},{10,8},{12,14},{14,12},{16,18},{18,... | collective-permute-start | bytes 341000 | tf_op jit(solution)/shard_map/ppermute | solution.py:24
  49.0 1.0 %collective-permute-done.5 = bf16[444,128]{1,0:T(8,128)(2,1)S(1)} collective-permute-done((bf16[444,128]{1,0:T(8,128)(2,1)S(1)}, bf16[444,128]{1,0:T(8,128)(2,1)S(1)}, u32[]{:S(2)}, u32[]{:S(2)}) %collective-permute-start.5) | collective-permute-done | bytes 113696 | tf_op jit(solution)/shard_map/ppermute | solution.py:24
  50.0 0.6 %collective-permute-start.6 = (bf16[444,128]{1,0:T(8,128)(2,1)S(1)}, bf16[444,128]{1,0:T(8,128)(2,1)S(1)}, u32[]{:S(2)}, u32[]{:S(2)}) collective-permute-start(bf16[444,128]{1,0:T(8,128)(2,1)S(1)} %add_convert_fusion.own_ref), channel_id=1, source_target_pairs={{0,1},{1,0},{2,3},{3,2},{4,5},{5,4},{6,7},{7,6},{8,9},{9,8},{10,11... | collective-permute-start | bytes 341000 | tf_op jit(solution)/shard_map/ppermute | solution.py:18
  50.6 0.0 copy-done
  50.6 0.3 first.1.part_ref
  50.9 4.6 %collective-permute-done.6.other_ref = bf16[444,128]{1,0:T(8,128)(2,1)S(1)} collective-permute-done((bf16[444,128]{1,0:T(8,128)(2,1)S(1)}, bf16[444,128]{1,0:T(8,128)(2,1)S(1)}, u32[]{:S(2)}, u32[]{:S(2)}) %collective-permute-start.6) | collective-permute-done | bytes 113696 | tf_op jit(solution)/shard_map/ppermute | solution.py:18
  55.5 1.0 %rest.3 = bf16[444,128]{1,0:T(8,128)(2,1)} custom-call(bf16[444,888]{1,0:T(8,128)(2,1)S(1)} %copy-done, f32[444,128]{1,0:T(8,128)S(1)} %first.1.part_ref, bf16[444,128]{1,0:T(8,128)(2,1)S(1)} %collective-permute-done.6.other_ref), custom_call_target="tpu_custom_call" | custom-call | flops 58195968 | bytes 454656 | tf_op jit(solution)/shard_map/rest/pallas_call | solution.py:149
  (2 shorter events, 0.1 us)
Async XLA Ops:
  0.0 28.6 %collective-permute-start = (bf16[444,128]{1,0:T(8,128)(2,1)}, bf16[444,128]{1,0:T(8,128)(2,1)S(1)}, u32[]{:S(2)}, u32[]{:S(2)}) collective-permute-start(bf16[444,128]{1,0:T(8,128)(2,1)} %own_ref.1), channel_id=1, source_target_pairs={{0,1},{1,0},{2,3},{3,2},{4,5},{5,4},{6,7},{7,6},{8,9},{9,8},{10,11... | collective-permute-start | bytes 341000 | tf_op jit(solution)/shard_map/ppermute | solution.py:18
  28.9 1.4 %collective-permute-start.2 = (bf16[444,128]{1,0:T(8,128)(2,1)S(1)}, bf16[444,128]{1,0:T(8,128)(2,1)S(1)}, u32[]{:S(2)}, u32[]{:S(2)}) collective-permute-start(bf16[444,128]{1,0:T(8,128)(2,1)S(1)} %rest.2.own_ref), channel_id=1, source_target_pairs={{0,2},{2,0},{4,6},{6,4},{8,10},{10,8},{12,14},{14,12},{16,18},{18,... | collective-permute-start | bytes 341000 | tf_op jit(solution)/shard_map/ppermute | solution.py:24
  29.3 5.2 %collective-permute-start.1 = (bf16[444,128]{1,0:T(8,128)(2,1)S(1)}, bf16[444,128]{1,0:T(8,128)(2,1)S(1)}, u32[]{:S(2)}, u32[]{:S(2)}) collective-permute-start(bf16[444,128]{1,0:T(8,128)(2,1)S(1)} %rest.2.own_ref), channel_id=1, source_target_pairs={{0,1},{1,0},{2,3},{3,2},{4,5},{5,4},{6,7},{7,6},{8,9},{9,8},{10,11... | collective-permute-start | bytes 341000 | tf_op jit(solution)/shard_map/ppermute | solution.py:18
  32.5 18.1 %copy-start = (bf16[444,888]{1,0:T(8,128)(2,1)S(1)}, bf16[444,888]{1,0:T(8,128)(2,1)}, u32[]{:S(2)}) copy-start(bf16[444,888]{1,0:T(8,128)(2,1)} %matrix_ref.5) | copy-start | bytes 2365636
  34.6 1.3 %collective-permute-start.3 = (bf16[444,128]{1,0:T(8,128)(2,1)S(1)}, bf16[444,128]{1,0:T(8,128)(2,1)S(1)}, u32[]{:S(2)}, u32[]{:S(2)}) collective-permute-start(bf16[444,128]{1,0:T(8,128)(2,1)S(1)} %collective-permute-done.1.own_ref), channel_id=1, source_target_pairs={{0,2},{2,0},{4,6},{6,4},{8,10},{10,8},{12,14},{14,12},{16,18},{18,... | collective-permute-start | bytes 341000 | tf_op jit(solution)/shard_map/ppermute | solution.py:24
  41.5 0.7 %collective-permute-start.4 = (bf16[444,256]{1,0:T(8,128)(2,1)S(1)}, bf16[444,256]{1,0:T(8,128)(2,1)S(1)}, u32[]{:S(2)}, u32[]{:S(2)}) collective-permute-start(bf16[444,256]{1,0:T(8,128)(2,1)S(1)} %get-tuple-element.30), channel_id=1, source_target_pairs={{2,4},{4,2},{6,8},{8,6},{10,12},{12,10},{14,16},{16,14},{18,20},{2... | collective-permute-start | bytes 681992 | tf_op jit(solution)/shard_map/ppermute | solution.py:30
  42.2 7.8 %collective-permute-start.5 = (bf16[444,128]{1,0:T(8,128)(2,1)S(1)}, bf16[444,128]{1,0:T(8,128)(2,1)S(1)}, u32[]{:S(2)}, u32[]{:S(2)}) collective-permute-start(bf16[444,128]{1,0:T(8,128)(2,1)S(1)} %slice.9), channel_id=1, source_target_pairs={{0,2},{2,0},{4,6},{6,4},{8,10},{10,8},{12,14},{14,12},{16,18},{18,... | collective-permute-start | bytes 341000 | tf_op jit(solution)/shard_map/ppermute | solution.py:24
  50.0 5.5 %collective-permute-start.6 = (bf16[444,128]{1,0:T(8,128)(2,1)S(1)}, bf16[444,128]{1,0:T(8,128)(2,1)S(1)}, u32[]{:S(2)}, u32[]{:S(2)}) collective-permute-start(bf16[444,128]{1,0:T(8,128)(2,1)S(1)} %add_convert_fusion.own_ref), channel_id=1, source_target_pairs={{0,1},{1,0},{2,3},{3,2},{4,5},{5,4},{6,7},{7,6},{8,9},{9,8},{10,11... | collective-permute-start | bytes 341000 | tf_op jit(solution)/shard_map/ppermute | solution.py:18

commit v4 on v2

--- a/solution.py
+++ b/solution.py
@@ -27,6 +27,12 @@
 def to_near(value):
     count = lax.axis_size("tile")
     pairs = [(t, t + 2 * (t % 2) - 1) for t in range(count)]
+    return lax.ppermute(value, "tile", [(a, b) for a, b in pairs if 0 <= b < count])
+
+
+def to_far(value):
+    count = lax.axis_size("tile")
+    pairs = [(t, t + 4 * (t % 2) - 2) for t in range(count)]
     return lax.ppermute(value, "tile", [(a, b) for a, b in pairs if 0 <= b < count])
 
 
@@ -53,6 +59,43 @@
     for i, ref in enumerate(refs):
         rows, cells = ref.shape
         padded[offset : offset + rows, i * cells : (i + 1) * cells] = ref[...].astype(padded.dtype)
+
+
+def stage_kernel(windows, matrix_ref, own_ref, held_ref, part_ref, own_held, padded, sems):
+    copies = [
+        pltpu.make_async_copy(own_ref, own_held, sems.at[0]),
+        pltpu.make_async_copy(matrix_ref, held_ref, sems.at[1]),
+    ]
+    for copy in copies:
+        copy.start()
+    for copy in copies:
+        copy.wait()
+    first_kernel(windows, held_ref, own_held, part_ref, padded)
+
+
+def stage(matrix, own, windows):
+    rows, depth = matrix.shape
+    cells = own.shape[1]
+    span = max(high - low for low, high, _ in windows)
+    return pl.pallas_call(
+        functools.partial(stage_kernel, windows),
+        out_shape=[
+            jax.ShapeDtypeStruct(matrix.shape, matrix.dtype),
+            jax.ShapeDtypeStruct((rows, cells), jnp.float32),
+        ],
+        in_specs=[pl.BlockSpec(memory_space=pltpu.HBM)] * 2,
+        out_specs=[WHOLE] * 2,
+        scratch_shapes=[
+            pltpu.VMEM(own.shape, own.dtype),
+            pltpu.VMEM((span, cells), jnp.float32),
+            pltpu.SemaphoreType.DMA((2,)),
+        ],
+        cost_estimate=pl.CostEstimate(
+            flops=2 * rows * depth * cells, bytes_accessed=4 * matrix.size, transcendentals=0
+        ),
+        compiler_params=pltpu.CompilerParams(vmem_limit_bytes=24 << 20),
+        name="stage",
+    )(*[pltpu.with_memory_space_constraint(x, pltpu.HBM) for x in (matrix, own)])
 
 
 def first_kernel(windows, matrix_ref, own_ref, out_ref, padded):
@@ -134,8 +177,8 @@
 
 
 def prepare_kernel(
-    windows, translate_ref, own_ref, mate_ref, code_ref, near_ref,
-    held_ref, product_ref, select_own_ref, select_mate_ref, padded, sems,
+    windows, translate_ref, own_ref, code_ref, near_ref, mate_ref, mate_near_ref,
+    held_ref, product_ref, away_select_ref, home_select_ref, padded, sems,
 ):
     rows, classes, _ = translate_ref.shape
     entries, cells = code_ref.shape
@@ -147,22 +190,21 @@
         copies.append(copy)
 
     step = away()
-    codes = [code_ref[...], near_ref[:entries, :], near_ref[entries:, :]]
-    for block, code in enumerate(codes):
-        base = (REACH - block * step) * cells
-        build_select(code, base, select_own_ref, block * cells, classes)
-        if block < 2:
-            base = (REACH - (1 + block) * step) * cells
-            build_select(code, base, select_mate_ref, block * cells, classes)
-
-    for copy in copies:
-        copy.wait()
+    for block, (code, offset) in enumerate(
+        [(mate_ref[...], -step), (mate_near_ref[...], -2 * step), (near_ref[entries:], 2 * step)]
+    ):
+        base = (REACH - offset) * cells
+        build_select(code, base, away_select_ref, block * cells, classes)
+    for block, (code, offset) in enumerate([(code_ref[...], 0), (near_ref[:entries], step)]):
+        base = (REACH - offset) * cells
+        build_select(code, base, home_select_ref, block * cells, classes)
 
     for index, (low, high, offset) in enumerate(windows):
         def run(low=low, high=high, offset=offset):
-            pad_into(padded, offset, own_ref, mate_ref)
+            pad_into(padded, offset, own_ref)
             right = padded[: high - low, :].astype(jnp.bfloat16)
-            for start, size in chunks(rows):
+            for copy, (start, size) in zip(copies, chunks(rows)):
+                copy.wait()
                 left = held_ref[start : start + size, :, low:high]
                 product_ref[start * classes : (start + size) * classes, :] = jnp.dot(
                     left.reshape(size * classes, high - low), right,
@@ -174,108 +216,124 @@
             pl.when(lax.axis_index("sub") == index)(run)
 
 
-def push_kernel(
-    windows, held_ref, product_ref, own_ref, mate_ref, select_own_ref, select_mate_ref,
-    out_ref, sent_ref, padded, own_terms_ref, mate_terms_ref,
+def prepare(operators, own, code, near_codes, mate_code, mate_near_code, windows):
+    rows, classes, depth = operators.shape
+    cells = code.shape[1]
+    span = max(high - low for low, high, _ in windows)
+    return pl.pallas_call(
+        functools.partial(prepare_kernel, windows),
+        out_shape=[
+            jax.ShapeDtypeStruct((rows, classes, depth), jnp.bfloat16),
+            jax.ShapeDtypeStruct((rows * classes, cells), jnp.float32),
+            jax.ShapeDtypeStruct((classes * cells, 3 * cells), jnp.bfloat16),
+            jax.ShapeDtypeStruct((classes * cells, 2 * cells), jnp.bfloat16),
+        ],
+        in_specs=[pl.BlockSpec(memory_space=pltpu.HBM)] + [WHOLE] * 5,
+        out_specs=[WHOLE] * 4,
+        scratch_shapes=[
+            pltpu.VMEM((span, cells), jnp.float32),
+            pltpu.SemaphoreType.DMA((len(chunks(rows)),)),
+        ],
+        cost_estimate=pl.CostEstimate(
+            flops=4 * rows * classes * cells * span,
+            bytes_accessed=2 * rows * classes * depth,
+            transcendentals=0,
+        ),
+        compiler_params=pltpu.CompilerParams(vmem_limit_bytes=32 << 20),
+        name="prepare",
+    )(
+        pltpu.with_memory_space_constraint(operators, pltpu.HBM),
+        own, code, near_codes, mate_code, mate_near_code,
+    )
+
+
+def push_away_kernel(
+    windows, held_ref, product_ref, other_ref, select_ref,
+    terms_ref, mate_ref, far_ref, padded, product,
 ):
     rows, classes, _ = held_ref.shape
-    cells = own_ref.shape[1]
-
-    def keep(size, value):
-        own_terms_ref[: size * classes, :] = value[:, :cells]
-        mate_terms_ref[: size * classes, :] = value[:, cells:]
-
-    def finish(start, size):
-        def by_class(ref):
-            parts = [ref[pl.ds(k, size, stride=classes), :] for k in range(classes)]
-            return jnp.concatenate([part.astype(jnp.bfloat16) for part in parts], axis=1)
-
-        total = jnp.dot(
-            by_class(own_terms_ref), select_own_ref[...], preferred_element_type=jnp.float32
-        )
-        extra = jnp.dot(
-            by_class(mate_terms_ref), select_mate_ref[...], preferred_element_type=jnp.float32
-        )
-        part = slice(start, start + size)
-        out_ref[part, :] = total[:, :cells] + extra[:, :cells]
-        sent_ref[part, :cells] = (total[:, cells : 2 * cells] + extra[:, cells:]).astype(
-            jnp.bfloat16
-        )
-        sent_ref[part, cells:] = total[:, 2 * cells :].astype(jnp.bfloat16)
+    cells = far_ref.shape[1]
+
+    def part_classes(source, start, size):
+        for k in range(classes):
+            term = source[pl.ds(start * classes + k, size, stride=classes), :]
+            terms_ref[start : start + size, k * cells : (k + 1) * cells] = term.astype(jnp.bfloat16)
 
     for index, (low, high, offset) in enumerate(windows):
         def run(low=low, high=high, offset=offset):
-            pad_into(padded, offset, own_ref, mate_ref)
+            pad_into(padded, offset, other_ref)
             right = padded[: high - low, :].astype(jnp.bfloat16)
             for start, size in chunks(rows):
                 left = held_ref[start : start + size, :, low:high]
-                part = pl.ds(start * classes, size * classes)
-                keep(size, product_ref[part, :] + jnp.dot(
+                part = slice(start * classes, (start + size) * classes)
+                product[part, :] = product_ref[part, :] + jnp.dot(
                     left.reshape(size * classes, high - low), right,
                     preferred_element_type=jnp.float32,
-                ))
-                finish(start, size)
+                )
+                part_classes(product, start, size)
         pl.when(lax.axis_index("sub") != index)(run)
 
     if not windows:
         for start, size in chunks(rows):
-            keep(size, product_ref[pl.ds(start * classes, size * classes), :])
-            finish(start, size)
-
-
-def prepare(operators, own, mate, code, near_codes, windows):
-    rows, classes, depth = operators.shape
-    cells = code.shape[1]
-    span = max(high - low for low, high, _ in windows)
-    return pl.pallas_call(
-        functools.partial(prepare_kernel, windows),
+            part_classes(product_ref, start, size)
+
+    total = jnp.dot(terms_ref[...], select_ref[...], preferred_element_type=jnp.float32)
+    mate_ref[...] = total[:, : 2 * cells].astype(jnp.bfloat16)
+    far_ref[...] = total[:, 2 * cells :].astype(jnp.bfloat16)
+
+
+def push_away(held, product, other, select, windows):
+    rows, classes, depth = held.shape
+    cells = other.shape[1]
+    span = max([high - low for low, high, _ in windows], default=LANES)
+    return pl.pallas_call(
+        functools.partial(push_away_kernel, windows),
         out_shape=[
-            jax.ShapeDtypeStruct((rows, classes, depth), jnp.bfloat16),
-            jax.ShapeDtypeStruct((rows * classes, 2 * cells), jnp.float32),
-            jax.ShapeDtypeStruct((classes * cells, 3 * cells), jnp.bfloat16),
-            jax.ShapeDtypeStruct((classes * cells, 2 * cells), jnp.bfloat16),
-        ],
-        in_specs=[pl.BlockSpec(memory_space=pl.ANY)] + [WHOLE] * 4,
-        out_specs=[WHOLE] * 4,
+            jax.ShapeDtypeStruct((rows, classes * cells), jnp.bfloat16),
+            jax.ShapeDtypeStruct((rows, 2 * cells), jnp.bfloat16),
+            jax.ShapeDtypeStruct((rows, cells), jnp.bfloat16),
+        ],
+        in_specs=[WHOLE] * 4,
+        out_specs=[WHOLE] * 3,
         scratch_shapes=[
-            pltpu.VMEM((span, 2 * cells), jnp.float32),
-            pltpu.SemaphoreType.DMA((len(chunks(rows)),)),
-        ],
-        cost_estimate=pl.CostEstimate(
-            flops=4 * rows * classes * cells * span,
+            pltpu.VMEM((span, cells), jnp.float32),
+            pltpu.VMEM((rows * classes, cells), jnp.float32),
+        ],
+        cost_estimate=pl.CostEstimate(
+            flops=2 * rows * classes * cells * (span + 3 * cells),
             bytes_accessed=2 * rows * classes * depth,
             transcendentals=0,
         ),
-        compiler_params=pltpu.CompilerParams(vmem_limit_bytes=40 << 20),
-        name="prepare",
-    )(operators, own, mate, code, near_codes)
-
-
-def push(held, product, own, mate, select_own, select_mate, windows):
-    rows, classes, depth = held.shape
-    cells = own.shape[1]
-    span = max([high - low for low, high, _ in windows], default=LANES)
-    return pl.pallas_call(
-        functools.partial(push_kernel, windows),
+        compiler_params=pltpu.CompilerParams(vmem_limit_bytes=32 << 20),
+        name="push_away",
+    )(held, product, other, select)
+
+
+def push_home_kernel(terms_ref, select_ref, came_ref, own_ref, near_ref):
+    cells = near_ref.shape[1]
+    total = jnp.dot(terms_ref[...], select_ref[...], preferred_element_type=jnp.float32)
+    total = total + came_ref[...].astype(jnp.float32)
+    own_ref[...] = total[:, :cells]
+    near_ref[...] = total[:, cells:].astype(jnp.bfloat16)
+
+
+def push_home(terms, select, came):
+    rows = terms.shape[0]
+    cells = select.shape[1] // 2
+    return pl.pallas_call(
+        push_home_kernel,
         out_shape=[
             jax.ShapeDtypeStruct((rows, cells), jnp.float32),
-            jax.ShapeDtypeStruct((rows, 2 * cells), jnp.bfloat16),
-        ],
-        in_specs=[WHOLE] * 6,
+            jax.ShapeDtypeStruct((rows, cells), jnp.bfloat16),
+        ],
+        in_specs=[WHOLE] * 3,
         out_specs=[WHOLE] * 2,
-        scratch_shapes=[
-            pltpu.VMEM((span, 2 * cells), jnp.float32),
-            pltpu.VMEM((CHUNK * classes, cells), jnp.float32),
-            pltpu.VMEM((CHUNK * classes, cells), jnp.float32),
-        ],
-        cost_estimate=pl.CostEstimate(
-            flops=2 * rows * classes * cells * (2 * span + 5 * cells),
-            bytes_accessed=2 * rows * classes * depth,
-            transcendentals=0,
-        ),
-        compiler_params=pltpu.CompilerParams(vmem_limit_bytes=40 << 20),
-        name="push",
-    )(held, product, own, mate, select_own, select_mate)
+        cost_estimate=pl.CostEstimate(
+            flops=2 * terms.size * 2 * cells, bytes_accessed=4 * terms.size, transcendentals=0
+        ),
+        compiler_params=pltpu.CompilerParams(vmem_limit_bytes=16 << 20),
+        name="push_home",
+    )(terms, select, came)
 
 
 def shards(up_check, up_inverse, translate, down_inverse, list_slot, list_class, list_count):
@@ -285,16 +343,19 @@
 
     active = lax.broadcasted_iota(jnp.int32, (entries, cells), 0) < list_count[None, :]
     code = jnp.where(active, (list_class.T << CLASS_SHIFT) + list_slot.T, -1)
-    chip_codes = jnp.concatenate([code, to_mate(code)], axis=0)
-    near_codes = to_near(chip_codes)
+    operators = jnp.transpose(translate, (1, 0, 2))
+    mate_code = to_mate(code)
+    near_codes = to_near(jnp.concatenate([code, mate_code], axis=0))
+    mate_near_code = to_mate(near_codes[:entries])
 
     operators = jnp.transpose(translate, (1, 0, 2))
     if halves:
         windows = half_windows(rows, depth, 2)
         other_check = across_sub(up_check)
-        part = first(up_inverse, up_check, windows)
+        staged, code = lax.optimization_barrier((up_inverse, code))
+        up_held, part = stage(staged, up_check, windows)
         part, near_codes = lax.optimization_barrier((part, near_codes))
-        equivalent = rest(up_inverse, part, other_check, windows)
+        equivalent = rest(up_held, part, other_check, windows)
         other = across_sub(equivalent)
     else:
         equivalent = lax.all_gather(
@@ -306,20 +367,18 @@
         )
         windows = [(0, depth, 0)]
         other = equivalent
-    held, product, select_own, select_mate = prepare(
-        operators, equivalent, to_mate(equivalent), code, near_codes, windows
+    held, product, away_select, home_select = prepare(
+        operators, equivalent, code, near_codes, mate_code, mate_near_code, windows
     )
-    if halves:
-        other, product = lax.optimization_barrier((other, product))
-    other_mate = to_mate(other) if halves else other
-    own_sum, sent = push(
-        held, product, other, other_mate, select_own, select_mate, windows if halves else []
+    terms, mate_sum, far_sum = push_away(
+        held, product, other, away_select, windows if halves else []
     )
-
-    came = to_near(sent)
-    came_far = to_mate(came[:, cells:])
+    mate_came = to_mate(mate_sum)
+    far_came = to_far(far_sum)
+    own_sum, near_sum = push_home(terms, home_select, mate_came)
+    near_came = to_near(near_sum)
     down_check = (
-        own_sum + (came[:, :cells].astype(jnp.float32) + came_far.astype(jnp.float32))
+        own_sum + (far_came.astype(jnp.float32) + near_came.astype(jnp.float32))
     ).astype(jnp.bfloat16)
     if halves:
         other_down = across_sub(down_check)

time: 37.4 us -> 34 us (0.909)
  waiting for transfers between devices: 12.5 us -> 10.2 us
  local copies, waits for them, and re-layouts: 2.05 us -> 0.01 us
  starting transfers between devices: 11.7 us -> 13.4 us
  Pallas kernels: 9.85 us -> 9.36 us
    ppermute x0 -> x1, starting transfers between devices: none -> 3.03 us  [to_far(): lax.ppermute(value, 'tile', [(a, b) for a, b in pairs if 0 <= b < count])]
    unnamed x6 -> x2, local copies, waits for them, and re-layouts: 2.04 us -> 0.01 us
    ppermute x2, waiting for transfers between devices: 5.84 us -> 3.94 us  [to_near(): lax.ppermute(value, 'tile', [(a, b) for a, b in pairs if 0 <= b < count])]
    ppermute x4 -> x3, starting transfers between devices: 1.79 us -> 0.24 us  [to_mate(): return lax.ppermute(value, 'tile', pairs)]
    ppermute x4 -> x3, waiting for transfers between devices: 2.46 us -> 1.17 us  [to_mate(): return lax.ppermute(value, 'tile', pairs)]
    ppermute x0 -> x1, waiting for transfers between devices: none -> 1.05 us  [to_far(): lax.ppermute(value, 'tile', [(a, b) for a, b in pairs if 0 <= b < count])]
    ppermute x2, starting transfers between devices: 6.01 us -> 6.44 us  [to_near(): lax.ppermute(value, 'tile', [(a, b) for a, b in pairs if 0 <= b < count])]
    pallas_call x1 -> x3, Pallas kernels: 4.02 us -> 3.89 us  [the longest x1 1.96 us: push_away(): pl.pallas_call(functools.partial(push_away_kernel, windows), out_shape=[j...]
  transfers between devices with their start and end apart: 9 -> 9, of which waited for: 7 -> 5; matrix products, arithmetic and copies ran while one was open for 0% -> 0% of each run, Pallas kernels for 12% -> 18%
where the time goes in v4:
time: 34 us; the launch traced here: 33.8 us
  starting transfers between devices  13.4 us (39%)
  waiting for transfers between devices  10.2 us (30%)
  Pallas kernels  9.36 us (28%)
  other arithmetic  0.75 us (2%)
    ppermute x2, starting transfers between devices, to_near(): lax.ppermute(value, 'tile', [(a, b) for a, b in pairs if 0 <= b < count])  6.44 us
    ppermute x3, waiting for transfers between devices, across_sub(): return lax.ppermute(shard, 'sub', [(0, 1), (1, 0)])  4.04 us
    ppermute x2, waiting for transfers between devices, to_near(): lax.ppermute(value, 'tile', [(a, b) for a, b in pairs if 0 <= b < count])  3.94 us
    pallas_call x1, Pallas kernels, prepare(): pl.pallas_call(functools.partial(prepare_kernel, windows), out_shape=[jax...  3.92 us
    ppermute x3, starting transfers between devices, across_sub(): return lax.ppermute(shard, 'sub', [(0, 1), (1, 0)])  3.7 us
    ppermute x1, starting transfers between devices, to_far(): lax.ppermute(value, 'tile', [(a, b) for a, b in pairs if 0 <= b < count])  3.03 us
    pallas_call x1, Pallas kernels, push_away(): pl.pallas_call(functools.partial(push_away_kernel, windows), out_shape=[j...  1.96 us
    pallas_call x1, Pallas kernels, stage(): pl.pallas_call(functools.partial(stage_kernel, windows), out_shape=[jax.S...  1.51 us
  transfers between devices with their start and end apart: 9, of which 5 were waited for; matrix products, arithmetic and copies ran while one was open for 0% of the time, Pallas kernels for 18%

profile of v4, /device:TPU:8, one launch (start us, length us, event | category | flops | bytes accessed | tf_op | source)
XLA Modules:
  0.0 33.8 jit_solution(8216576618482293789)
XLA Ops:
  0.0 0.7 %bitcast_select_fusion.code_ref = s32[8,128]{1,0:T(8,128)S(1)} fusion(s32[128,8]{0,1:T(8,128)} %param.11, s32[128,8]{0,1:T(8,128)} %param.12, s32[128]{0:T(128)} %param.13), kind=kLoop, calls=%fused_computation.2 | loop fusion | flops 4096 | bytes 12800 | tf_op jit(solution)/shard_map/jit(_where)/select_n | solution.py:345
  0.7 0.0 collective-permute-start
  0.7 1.6 %collective-permute-start.2 = (bf16[444,128]{1,0:T(8,128)(2,1)}, bf16[444,128]{1,0:T(8,128)(2,1)S(1)}, u32[]{:S(2)}, u32[]{:S(2)}) collective-permute-start(bf16[444,128]{1,0:T(8,128)(2,1)} %own_ref.1), channel_id=1, source_target_pairs={{0,1},{1,0},{2,3},{3,2},{4,5},{5,4},{6,7},{7,6},{8,9},{9,8},{10,11... | collective-permute-start | bytes 341000 | tf_op jit(solution)/shard_map/ppermute | solution.py:18
  2.3 0.0 collective-permute-done.mate_ref
  2.3 3.1 %collective-permute-start.1 = (s32[16,128]{1,0:T(8,128)S(1)}, s32[16,128]{1,0:T(8,128)S(1)}, u32[]{:S(2)}, u32[]{:S(2)}) collective-permute-start(s32[16,128]{1,0:T(8,128)S(1)} %pad_add_fusion), channel_id=1, source_target_pairs={{2,4},{4,2},{6,8},{8,6},{10,12},{12,10},{14,16},{16,14},{18,20},{2... | collective-permute-start | bytes 24584 | tf_op jit(solution)/shard_map/ppermute | solution.py:30
  5.4 1.5 %stage.1 = (bf16[444,888]{1,0:T(8,128)(2,1)S(1)}, f32[444,128]{1,0:T(8,128)S(1)}) custom-call(bf16[444,888]{1,0:T(8,128)(2,1)} %matrix_ref.2, bf16[444,128]{1,0:T(8,128)(2,1)} %own_ref.1), custom_call_target="tpu_custom_call" | custom-call | flops 100933632 | bytes 1577088 | tf_op jit(solution)/shard_map/stage/pallas_call | solution.py:80
  6.9 1.3 %collective-permute-done.1.near_ref = s32[16,128]{1,0:T(8,128)S(1)} collective-permute-done((s32[16,128]{1,0:T(8,128)S(1)}, s32[16,128]{1,0:T(8,128)S(1)}, u32[]{:S(2)}, u32[]{:S(2)}) %collective-permute-start.1) | collective-permute-done | bytes 8224 | tf_op jit(solution)/shard_map/ppermute | solution.py:30
  8.1 0.0 collective-permute-done.2.other_ref
  8.1 0.3 rest.2.own_ref
  8.4 1.1 %collective-permute-start.4 = (bf16[444,128]{1,0:T(8,128)(2,1)S(1)}, bf16[444,128]{1,0:T(8,128)(2,1)S(1)}, u32[]{:S(2)}, u32[]{:S(2)}) collective-permute-start(bf16[444,128]{1,0:T(8,128)(2,1)S(1)} %rest.2.own_ref), channel_id=1, source_target_pairs={{0,1},{1,0},{2,3},{3,2},{4,5},{5,4},{6,7},{7,6},{8,9},{9,8},{10,11... | collective-permute-start | bytes 341000 | tf_op jit(solution)/shard_map/ppermute | solution.py:18
  9.6 0.0 collective-permute-start.3
  9.6 1.2 %collective-permute-done.3.mate_near_ref = s32[8,128]{1,0:T(8,128)S(1)} collective-permute-done((s32[8,128]{1,0:T(8,128)S(1)}, s32[8,128]{1,0:T(8,128)S(1)}, u32[]{:S(2)}, u32[]{:S(2)}) %collective-permute-start.3) | collective-permute-done | bytes 4128 | tf_op jit(solution)/shard_map/ppermute | solution.py:24
  10.8 3.9 %prepare.1 = (bf16[444,8,888]{2,1,0:T(8,128)(2,1)S(1)}, f32[3552,128]{1,0:T(8,128)S(1)}, bf16[1024,384]{1,0:T(8,128)(2,1)S(1)}, bf16[1024,256]{1,0:T(8,128)(2,1)S(1)}) custom-call(bf16[444,8,888]{2,1,0:T(8,128)(2,1)} %bitcast.3, bf16[444,128]{1,0:T(8,128)(2,1)S(1)} %rest.2.own_ref, s32[8,128]{1,0:T(8,128)S(1)} %bitcast_select_fusion.code_ref, ...), custom_call_target="tpu_custom_call" | custom-call | flops 931135488 | bytes 6308352 | tf_op jit(solution)/shard_map/prepare/pallas_call | solution.py:223
  14.7 0.0 copy-start
  14.7 0.0 collective-permute-done.4.other_ref
  14.7 2.0 %push_away.1 = (bf16[444,1024]{1,0:T(8,128)(2,1)S(1)}, bf16[444,256]{1,0:T(8,128)(2,1)S(1)}, bf16[444,128]{1,0:T(8,128)(2,1)S(1)}) custom-call(bf16[444,8,888]{2,1,0:T(8,128)(2,1)S(1)} %get-tuple-element.26.held_ref, f32[3552,128]{1,0:T(8,128)S(1)} %get-tuple-element.27.product_ref, bf16[444,128]{1,0:T(8,128)(2,1)S(1)} %collective-permute-done.4.other_ref, ...), custom_call_target="tpu_custom_call" | custom-call | flops 814743552 | bytes 6308352 | tf_op jit(solution)/shard_map/push_away/pallas_call | solution.py:289
  16.7 0.2 collective-permute-start.5
  16.9 3.0 %collective-permute-start.6 = (bf16[444,128]{1,0:T(8,128)(2,1)S(1)}, bf16[444,128]{1,0:T(8,128)(2,1)S(1)}, u32[]{:S(2)}, u32[]{:S(2)}) collective-permute-start(bf16[444,128]{1,0:T(8,128)(2,1)S(1)} %get-tuple-element.33), channel_id=1, source_target_pairs={{2,6},{4,0},{6,10},{8,4},{10,14},{12,8},{14,18},{16,12},{18,22},{2... | collective-permute-start | bytes 341000 | tf_op jit(solution)/shard_map/ppermute | solution.py:36
  19.9 0.0 collective-permute-done.5.came_ref
  20.0 0.4 %push_home.1 = (f32[444,128]{1,0:T(8,128)S(1)}, bf16[444,128]{1,0:T(8,128)(2,1)S(1)}) custom-call(bf16[444,1024]{1,0:T(8,128)(2,1)S(1)} %get-tuple-element.29.terms_ref, bf16[1024,256]{1,0:T(8,128)(2,1)S(1)} %get-tuple-element.30.select_ref, bf16[444,256]{1,0:T(8,128)(2,1)S(1)} %collective-permute-done.5.came_ref), custom_call_target="tpu_custom_call" | custom-call | flops 232783872 | bytes 1818624 | tf_op jit(solution)/shard_map/push_home/pallas_call | solution.py:323
  20.4 3.4 %collective-permute-start.7 = (bf16[444,128]{1,0:T(8,128)(2,1)S(1)}, bf16[444,128]{1,0:T(8,128)(2,1)S(1)}, u32[]{:S(2)}, u32[]{:S(2)}) collective-permute-start(bf16[444,128]{1,0:T(8,128)(2,1)S(1)} %get-tuple-element.34), channel_id=1, source_target_pairs={{2,4},{4,2},{6,8},{8,6},{10,12},{12,10},{14,16},{16,14},{18,20},{2... | collective-permute-start | bytes 341000 | tf_op jit(solution)/shard_map/ppermute | solution.py:30
  23.8 1.1 %collective-permute-done.6 = bf16[444,128]{1,0:T(8,128)(2,1)S(1)} collective-permute-done((bf16[444,128]{1,0:T(8,128)(2,1)S(1)}, bf16[444,128]{1,0:T(8,128)(2,1)S(1)}, u32[]{:S(2)}, u32[]{:S(2)}) %collective-permute-start.6) | collective-permute-done | bytes 113696 | tf_op jit(solution)/shard_map/ppermute | solution.py:36
  24.8 2.7 %collective-permute-done.7 = bf16[444,128]{1,0:T(8,128)(2,1)S(1)} collective-permute-done((bf16[444,128]{1,0:T(8,128)(2,1)S(1)}, bf16[444,128]{1,0:T(8,128)(2,1)S(1)}, u32[]{:S(2)}, u32[]{:S(2)}) %collective-permute-start.7) | collective-permute-done | bytes 113696 | tf_op jit(solution)/shard_map/ppermute | solution.py:30
  27.5 1.0 %collective-permute-start.8 = (bf16[444,128]{1,0:T(8,128)(2,1)S(1)}, bf16[444,128]{1,0:T(8,128)(2,1)S(1)}, u32[]{:S(2)}, u32[]{:S(2)}) collective-permute-start(bf16[444,128]{1,0:T(8,128)(2,1)S(1)} %add_convert_fusion.own_ref), channel_id=1, source_target_pairs={{0,1},{1,0},{2,3},{3,2},{4,5},{5,4},{6,7},{7,6},{8,9},{9,8},{10,11... | collective-permute-start | bytes 341000 | tf_op jit(solution)/shard_map/ppermute | solution.py:18
  28.6 0.0 copy-done
  28.6 0.3 first.1.part_ref
  28.8 4.0 %collective-permute-done.8.other_ref = bf16[444,128]{1,0:T(8,128)(2,1)S(1)} collective-permute-done((bf16[444,128]{1,0:T(8,128)(2,1)S(1)}, bf16[444,128]{1,0:T(8,128)(2,1)S(1)}, u32[]{:S(2)}, u32[]{:S(2)}) %collective-permute-start.8) | collective-permute-done | bytes 113696 | tf_op jit(solution)/shard_map/ppermute | solution.py:18
  32.9 1.0 %rest.3 = bf16[444,128]{1,0:T(8,128)(2,1)} custom-call(bf16[444,888]{1,0:T(8,128)(2,1)S(1)} %copy-done, f32[444,128]{1,0:T(8,128)S(1)} %first.1.part_ref, bf16[444,128]{1,0:T(8,128)(2,1)S(1)} %collective-permute-done.8.other_ref), custom_call_target="tpu_custom_call" | custom-call | flops 58195968 | bytes 454656 | tf_op jit(solution)/shard_map/rest/pallas_call | solution.py:148
  (3 shorter events, 0.0 us)
Async XLA Ops:
  0.7 1.6 %collective-permute-start = (s32[8,128]{1,0:T(8,128)S(1)}, s32[8,128]{1,0:T(8,128)S(1)}, u32[]{:S(2)}, u32[]{:S(2)}) collective-permute-start(s32[8,128]{1,0:T(8,128)S(1)} %bitcast_select_fusion.code_ref), channel_id=1, source_target_pairs={{0,2},{2,0},{4,6},{6,4},{8,10},{10,8},{12,14},{14,12},{16,18},{18,... | collective-permute-start | bytes 12296 | tf_op jit(solution)/shard_map/ppermute | solution.py:24
  0.7 7.4 %collective-permute-start.2 = (bf16[444,128]{1,0:T(8,128)(2,1)}, bf16[444,128]{1,0:T(8,128)(2,1)S(1)}, u32[]{:S(2)}, u32[]{:S(2)}) collective-permute-start(bf16[444,128]{1,0:T(8,128)(2,1)} %own_ref.1), channel_id=1, source_target_pairs={{0,1},{1,0},{2,3},{3,2},{4,5},{5,4},{6,7},{7,6},{8,9},{9,8},{10,11... | collective-permute-start | bytes 341000 | tf_op jit(solution)/shard_map/ppermute | solution.py:18
  2.3 5.9 %collective-permute-start.1 = (s32[16,128]{1,0:T(8,128)S(1)}, s32[16,128]{1,0:T(8,128)S(1)}, u32[]{:S(2)}, u32[]{:S(2)}) collective-permute-start(s32[16,128]{1,0:T(8,128)S(1)} %pad_add_fusion), channel_id=1, source_target_pairs={{2,4},{4,2},{6,8},{8,6},{10,12},{12,10},{14,16},{16,14},{18,20},{2... | collective-permute-start | bytes 24584 | tf_op jit(solution)/shard_map/ppermute | solution.py:30
  8.4 6.3 %collective-permute-start.4 = (bf16[444,128]{1,0:T(8,128)(2,1)S(1)}, bf16[444,128]{1,0:T(8,128)(2,1)S(1)}, u32[]{:S(2)}, u32[]{:S(2)}) collective-permute-start(bf16[444,128]{1,0:T(8,128)(2,1)S(1)} %rest.2.own_ref), channel_id=1, source_target_pairs={{0,1},{1,0},{2,3},{3,2},{4,5},{5,4},{6,7},{7,6},{8,9},{9,8},{10,11... | collective-permute-start | bytes 341000 | tf_op jit(solution)/shard_map/ppermute | solution.py:18
  9.6 1.2 %collective-permute-start.3 = (s32[8,128]{1,0:T(8,128)S(1)}, s32[8,128]{1,0:T(8,128)S(1)}, u32[]{:S(2)}, u32[]{:S(2)}) collective-permute-start(s32[8,128]{1,0:T(8,128)S(1)} %slice.4), channel_id=1, source_target_pairs={{0,2},{2,0},{4,6},{6,4},{8,10},{10,8},{12,14},{14,12},{16,18},{18,... | collective-permute-start | bytes 12296 | tf_op jit(solution)/shard_map/ppermute | solution.py:24
  14.7 13.9 %copy-start = (bf16[444,888]{1,0:T(8,128)(2,1)S(1)}, bf16[444,888]{1,0:T(8,128)(2,1)}, u32[]{:S(2)}) copy-start(bf16[444,888]{1,0:T(8,128)(2,1)} %matrix_ref.4) | copy-start | bytes 2365636
  16.7 3.3 %collective-permute-start.5 = (bf16[444,256]{1,0:T(8,128)(2,1)S(1)}, bf16[444,256]{1,0:T(8,128)(2,1)S(1)}, u32[]{:S(2)}, u32[]{:S(2)}) collective-permute-start(bf16[444,256]{1,0:T(8,128)(2,1)S(1)} %get-tuple-element.31), channel_id=1, source_target_pairs={{0,2},{2,0},{4,6},{6,4},{8,10},{10,8},{12,14},{14,12},{16,18},{18,... | collective-permute-start | bytes 681992 | tf_op jit(solution)/shard_map/ppermute | solution.py:24
  16.9 7.9 %collective-permute-start.6 = (bf16[444,128]{1,0:T(8,128)(2,1)S(1)}, bf16[444,128]{1,0:T(8,128)(2,1)S(1)}, u32[]{:S(2)}, u32[]{:S(2)}) collective-permute-start(bf16[444,128]{1,0:T(8,128)(2,1)S(1)} %get-tuple-element.33), channel_id=1, source_target_pairs={{2,6},{4,0},{6,10},{8,4},{10,14},{12,8},{14,18},{16,12},{18,22},{2... | collective-permute-start | bytes 341000 | tf_op jit(solution)/shard_map/ppermute | solution.py:36
  20.4 7.1 %collective-permute-start.7 = (bf16[444,128]{1,0:T(8,128)(2,1)S(1)}, bf16[444,128]{1,0:T(8,128)(2,1)S(1)}, u32[]{:S(2)}, u32[]{:S(2)}) collective-permute-start(bf16[444,128]{1,0:T(8,128)(2,1)S(1)} %get-tuple-element.34), channel_id=1, source_target_pairs={{2,4},{4,2},{6,8},{8,6},{10,12},{12,10},{14,16},{16,14},{18,20},{2... | collective-permute-start | bytes 341000 | tf_op jit(solution)/shard_map/ppermute | solution.py:30
  27.5 5.3 %collective-permute-start.8 = (bf16[444,128]{1,0:T(8,128)(2,1)S(1)}, bf16[444,128]{1,0:T(8,128)(2,1)S(1)}, u32[]{:S(2)}, u32[]{:S(2)}) collective-permute-start(bf16[444,128]{1,0:T(8,128)(2,1)S(1)} %add_convert_fusion.own_ref), channel_id=1, source_target_pairs={{0,1},{1,0},{2,3},{3,2},{4,5},{5,4},{6,7},{7,6},{8,9},{9,8},{10,11... | collective-permute-start | bytes 341000 | tf_op jit(solution)/shard_map/ppermute | solution.py:18

commit v5 on v4

--- a/solution.py
+++ b/solution.py
@@ -11,6 +11,7 @@
 CLASS_SHIFT = 10
 CHUNK = 112
 LANES = 128
+PREPARE = 1 << 32
 WHOLE = pl.BlockSpec(memory_space=pltpu.VMEM)
 
 
@@ -59,43 +60,6 @@
     for i, ref in enumerate(refs):
         rows, cells = ref.shape
         padded[offset : offset + rows, i * cells : (i + 1) * cells] = ref[...].astype(padded.dtype)
-
-
-def stage_kernel(windows, matrix_ref, own_ref, held_ref, part_ref, own_held, padded, sems):
-    copies = [
-        pltpu.make_async_copy(own_ref, own_held, sems.at[0]),
-        pltpu.make_async_copy(matrix_ref, held_ref, sems.at[1]),
-    ]
-    for copy in copies:
-        copy.start()
-    for copy in copies:
-        copy.wait()
-    first_kernel(windows, held_ref, own_held, part_ref, padded)
-
-
-def stage(matrix, own, windows):
-    rows, depth = matrix.shape
-    cells = own.shape[1]
-    span = max(high - low for low, high, _ in windows)
-    return pl.pallas_call(
-        functools.partial(stage_kernel, windows),
-        out_shape=[
-            jax.ShapeDtypeStruct(matrix.shape, matrix.dtype),
-            jax.ShapeDtypeStruct((rows, cells), jnp.float32),
-        ],
-        in_specs=[pl.BlockSpec(memory_space=pltpu.HBM)] * 2,
-        out_specs=[WHOLE] * 2,
-        scratch_shapes=[
-            pltpu.VMEM(own.shape, own.dtype),
-            pltpu.VMEM((span, cells), jnp.float32),
-            pltpu.SemaphoreType.DMA((2,)),
-        ],
-        cost_estimate=pl.CostEstimate(
-            flops=2 * rows * depth * cells, bytes_accessed=4 * matrix.size, transcendentals=0
-        ),
-        compiler_params=pltpu.CompilerParams(vmem_limit_bytes=24 << 20),
-        name="stage",
-    )(*[pltpu.with_memory_space_constraint(x, pltpu.HBM) for x in (matrix, own)])
 
 
 def first_kernel(windows, matrix_ref, own_ref, out_ref, padded):
@@ -159,7 +123,7 @@
     )(matrix, part, other)
 
 
-def build_select(code, base, out_ref, column, classes):
+def build_select(code, base, out_ref, classes):
     entries, cells = code.shape
     slots = (code & ((1 << CLASS_SHIFT) - 1)) - base
     kinds = code >> CLASS_SHIFT
@@ -173,15 +137,15 @@
                 used = jnp.where(kinds[entry : entry + 1, :] == k, 1.0, 0.0).astype(jnp.bfloat16)
                 totals[k] = totals[k] + hit * used
         for k in range(classes):
-            out_ref[k * cells + low : k * cells + low + band, column : column + cells] = totals[k]
+            out_ref[k * cells + low : k * cells + low + band, :] = totals[k]
 
 
 def prepare_kernel(
-    windows, translate_ref, own_ref, code_ref, near_ref, mate_ref, mate_near_ref,
-    held_ref, product_ref, away_select_ref, home_select_ref, padded, sems,
+    windows, translate_ref, own_ref, code_ref, mate_ref,
+    held_ref, product_ref, home_ref, mate_select_ref, padded, sems,
 ):
     rows, classes, _ = translate_ref.shape
-    entries, cells = code_ref.shape
+    cells = code_ref.shape[1]
     copies = []
     for i, (start, size) in enumerate(chunks(rows)):
         part = pl.ds(start, size)
@@ -189,15 +153,8 @@
         copy.start()
         copies.append(copy)
 
-    step = away()
-    for block, (code, offset) in enumerate(
-        [(mate_ref[...], -step), (mate_near_ref[...], -2 * step), (near_ref[entries:], 2 * step)]
-    ):
-        base = (REACH - offset) * cells
-        build_select(code, base, away_select_ref, block * cells, classes)
-    for block, (code, offset) in enumerate([(code_ref[...], 0), (near_ref[:entries], step)]):
-        base = (REACH - offset) * cells
-        build_select(code, base, home_select_ref, block * cells, classes)
+    build_select(code_ref[...], REACH * cells, home_ref, classes)
+    build_select(mate_ref[...], (REACH + away()) * cells, mate_select_ref, classes)
 
     for index, (low, high, offset) in enumerate(windows):
         def run(low=low, high=high, offset=offset):
@@ -216,43 +173,60 @@
             pl.when(lax.axis_index("sub") == index)(run)
 
 
-def prepare(operators, own, code, near_codes, mate_code, mate_near_code, windows):
+def prepare(operators, own, code, mate_code, windows):
     rows, classes, depth = operators.shape
     cells = code.shape[1]
     span = max(high - low for low, high, _ in windows)
+    select = jax.ShapeDtypeStruct((classes * cells, cells), jnp.bfloat16)
     return pl.pallas_call(
         functools.partial(prepare_kernel, windows),
         out_shape=[
             jax.ShapeDtypeStruct((rows, classes, depth), jnp.bfloat16),
             jax.ShapeDtypeStruct((rows * classes, cells), jnp.float32),
-            jax.ShapeDtypeStruct((classes * cells, 3 * cells), jnp.bfloat16),
-            jax.ShapeDtypeStruct((classes * cells, 2 * cells), jnp.bfloat16),
-        ],
-        in_specs=[pl.BlockSpec(memory_space=pltpu.HBM)] + [WHOLE] * 5,
+            select,
+            select,
+        ],
+        in_specs=[pl.BlockSpec(memory_space=pltpu.HBM)] + [WHOLE] * 3,
         out_specs=[WHOLE] * 4,
         scratch_shapes=[
             pltpu.VMEM((span, cells), jnp.float32),
             pltpu.SemaphoreType.DMA((len(chunks(rows)),)),
         ],
-        cost_estimate=pl.CostEstimate(
-            flops=4 * rows * classes * cells * span,
-            bytes_accessed=2 * rows * classes * depth,
-            transcendentals=0,
-        ),
+        cost_estimate=pl.CostEstimate(flops=PREPARE, bytes_accessed=0, transcendentals=0),
         compiler_params=pltpu.CompilerParams(vmem_limit_bytes=32 << 20),
         name="prepare",
-    )(
-        pltpu.with_memory_space_constraint(operators, pltpu.HBM),
-        own, code, near_codes, mate_code, mate_near_code,
-    )
+    )(pltpu.with_memory_space_constraint(operators, pltpu.HBM), own, code, mate_code)
+
+
+def select_kernel(near_ref, near_select_ref, far_select_ref):
+    entries, cells = near_ref.shape[0] // 2, near_ref.shape[1]
+    classes = near_select_ref.shape[0] // cells
+    step = away()
+    build_select(near_ref[:entries, :], (REACH - step) * cells, near_select_ref, classes)
+    build_select(near_ref[entries:, :], (REACH - 2 * step) * cells, far_select_ref, classes)
+
+
+def selections(near_codes, classes):
+    cells = near_codes.shape[1]
+    select = jax.ShapeDtypeStruct((classes * cells, cells), jnp.bfloat16)
+    return pl.pallas_call(
+        select_kernel,
+        out_shape=[select, select],
+        in_specs=[WHOLE],
+        out_specs=[WHOLE] * 2,
+        cost_estimate=pl.CostEstimate(flops=PREPARE, bytes_accessed=0, transcendentals=0),
+        compiler_params=pltpu.CompilerParams(vmem_limit_bytes=8 << 20),
+        name="selections",
+    )(near_codes)
 
 
 def push_away_kernel(
-    windows, held_ref, product_ref, other_ref, select_ref,
-    terms_ref, mate_ref, far_ref, padded, product,
+    windows, held_ref, product_ref, other_ref, mate_select_ref, far_select_ref, code_ref,
+    terms_ref, mate_ref, far_ref, padded, product, select,
 ):
     rows, classes, _ = held_ref.shape
     cells = far_ref.shape[1]
+    build_select(code_ref[...], (REACH + 2 * away()) * cells, select, classes)
 
     def part_classes(source, start, size):
         for k in range(classes):
@@ -277,12 +251,15 @@
         for start, size in chunks(rows):
             part_classes(product_ref, start, size)
 
-    total = jnp.dot(terms_ref[...], select_ref[...], preferred_element_type=jnp.float32)
-    mate_ref[...] = total[:, : 2 * cells].astype(jnp.bfloat16)
-    far_ref[...] = total[:, 2 * cells :].astype(jnp.bfloat16)
-
-
-def push_away(held, product, other, select, windows):
+    for ref, column, chosen in (
+        (mate_ref, 0, mate_select_ref), (far_ref, 0, far_select_ref), (mate_ref, cells, select)
+    ):
+        ref[:, column : column + cells] = jnp.dot(
+            terms_ref[...], chosen[...], preferred_element_type=jnp.float32
+        ).astype(jnp.bfloat16)
+
+
+def push_away(held, product, other, mate_select, far_select, code, windows):
     rows, classes, depth = held.shape
     cells = other.shape[1]
     span = max([high - low for low, high, _ in windows], default=LANES)
@@ -293,11 +270,12 @@
             jax.ShapeDtypeStruct((rows, 2 * cells), jnp.bfloat16),
             jax.ShapeDtypeStruct((rows, cells), jnp.bfloat16),
         ],
-        in_specs=[WHOLE] * 4,
+        in_specs=[WHOLE] * 6,
         out_specs=[WHOLE] * 3,
         scratch_shapes=[
             pltpu.VMEM((span, cells), jnp.float32),
             pltpu.VMEM((rows * classes, cells), jnp.float32),
+            pltpu.VMEM((classes * cells, cells), jnp.bfloat16),
         ],
         cost_estimate=pl.CostEstimate(
             flops=2 * rows * classes * cells * (span + 3 * cells),
@@ -306,34 +284,38 @@
         ),
         compiler_params=pltpu.CompilerParams(vmem_limit_bytes=32 << 20),
         name="push_away",
-    )(held, product, other, select)
-
-
-def push_home_kernel(terms_ref, select_ref, came_ref, own_ref, near_ref):
+    )(held, product, other, mate_select, far_select, code)
+
+
+def push_home_kernel(terms_ref, home_ref, near_select_ref, came_ref, own_ref, near_ref):
     cells = near_ref.shape[1]
-    total = jnp.dot(terms_ref[...], select_ref[...], preferred_element_type=jnp.float32)
-    total = total + came_ref[...].astype(jnp.float32)
-    own_ref[...] = total[:, :cells]
-    near_ref[...] = total[:, cells:].astype(jnp.bfloat16)
-
-
-def push_home(terms, select, came):
+    terms = terms_ref[...]
+    near_ref[...] = (
+        jnp.dot(terms, near_select_ref[...], preferred_element_type=jnp.float32)
+        + came_ref[:, cells:].astype(jnp.float32)
+    ).astype(jnp.bfloat16)
+    own_ref[...] = jnp.dot(
+        terms, home_ref[...], preferred_element_type=jnp.float32
+    ) + came_ref[:, :cells].astype(jnp.float32)
+
+
+def push_home(terms, home, near_select, came):
     rows = terms.shape[0]
-    cells = select.shape[1] // 2
+    cells = home.shape[1]
     return pl.pallas_call(
         push_home_kernel,
         out_shape=[
             jax.ShapeDtypeStruct((rows, cells), jnp.float32),
             jax.ShapeDtypeStruct((rows, cells), jnp.bfloat16),
         ],
-        in_specs=[WHOLE] * 3,
+        in_specs=[WHOLE] * 4,
         out_specs=[WHOLE] * 2,
         cost_estimate=pl.CostEstimate(
             flops=2 * terms.size * 2 * cells, bytes_accessed=4 * terms.size, transcendentals=0
         ),
         compiler_params=pltpu.CompilerParams(vmem_limit_bytes=16 << 20),
         name="push_home",
-    )(terms, select, came)
+    )(terms, home, near_select, came)
 
 
 def shards(up_check, up_inverse, translate, down_inverse, list_slot, list_class, list_count):
@@ -346,36 +328,36 @@
     operators = jnp.transpose(translate, (1, 0, 2))
     mate_code = to_mate(code)
     near_codes = to_near(jnp.concatenate([code, mate_code], axis=0))
-    mate_near_code = to_mate(near_codes[:entries])
 
     operators = jnp.transpose(translate, (1, 0, 2))
     if halves:
         windows = half_windows(rows, depth, 2)
-        other_check = across_sub(up_check)
-        staged, code = lax.optimization_barrier((up_inverse, code))
-        up_held, part = stage(staged, up_check, windows)
-        part, near_codes = lax.optimization_barrier((part, near_codes))
-        equivalent = rest(up_held, part, other_check, windows)
+        mine = lax.axis_index("sub") * rows
+        check = lax.dynamic_update_slice(
+            jnp.zeros((depth, cells), up_check.dtype), up_check, (mine, 0)
+        )
+        check, mate_code = lax.optimization_barrier((check, mate_code))
+        check = lax.dynamic_update_slice(check, across_sub(up_check), (rows - mine, 0))
+    else:
+        windows = [(0, depth, 0)]
+        check = lax.all_gather(up_check, "sub", axis=0, tiled=True)
+    equivalent = jnp.dot(up_inverse, check, preferred_element_type=jnp.float32)
+    equivalent = equivalent.astype(jnp.bfloat16)
+    if halves:
         other = across_sub(equivalent)
     else:
-        equivalent = lax.all_gather(
-            jnp.dot(
-                up_inverse, lax.all_gather(up_check, "sub", axis=0, tiled=True),
-                preferred_element_type=jnp.float32,
-            ).astype(jnp.bfloat16),
-            "sub", axis=0, tiled=True,
-        )
-        windows = [(0, depth, 0)]
+        equivalent = lax.all_gather(equivalent, "sub", axis=0, tiled=True)
         other = equivalent
-    held, product, away_select, home_select = prepare(
-        operators, equivalent, code, near_codes, mate_code, mate_near_code, windows
-    )
+    held, product, home, mate_select = prepare(operators, equivalent, code, mate_code, windows)
+    near_codes, product = lax.optimization_barrier((near_codes, product))
+    near_select, far_select = selections(near_codes, classes)
+    mate_near_code = to_mate(near_codes[:entries])
     terms, mate_sum, far_sum = push_away(
-        held, product, other, away_select, windows if halves else []
+        held, product, other, mate_select, far_select, mate_near_code, windows if halves else []
     )
     mate_came = to_mate(mate_sum)
     far_came = to_far(far_sum)
-    own_sum, near_sum = push_home(terms, home_select, mate_came)
+    own_sum, near_sum = push_home(terms, home, near_select, mate_came)
     near_came = to_near(near_sum)
     down_check = (
         own_sum + (far_came.astype(jnp.float32) + near_came.astype(jnp.float32))

time: 34 us -> 35.2 us (1.035)
  local copies, waits for them, and re-layouts: 0.01 us -> 1.95 us
  waiting for transfers between devices: 10.2 us -> 9.47 us
  Pallas kernels: 9.36 us -> 8.68 us
  matrix products: 0 us -> 0.38 us
    dynamic_update_slice x0 -> x2, local copies, waits for them, and re-layouts: none -> 1.9 us  [the longest x1 1.5 us: shards(): lax.dynamic_update_slice(jnp.zeros((depth, cells), up_check.dtype), up_ch...]
    pallas_call x1, Pallas kernels: 1.51 us -> 0.46 us  [selections(): pl.pallas_call(select_kernel, out_shape=[select, select], in_specs=[WHOLE...]
    ppermute x2, waiting for transfers between devices: 3.94 us -> 3.19 us  [to_near(): lax.ppermute(value, 'tile', [(a, b) for a, b in pairs if 0 <= b < count])]
    ppermute x3, waiting for transfers between devices: 4.04 us -> 4.77 us  [across_sub(): return lax.ppermute(shard, 'sub', [(0, 1), (1, 0)])]
    ppermute x3, waiting for transfers between devices: 1.17 us -> 0.68 us  [to_mate(): return lax.ppermute(value, 'tile', pairs)]
    pallas_call x1, Pallas kernels: 1.96 us -> 2.41 us  [push_away(): pl.pallas_call(functools.partial(push_away_kernel, windows), out_shape=[j...]
    dot_general x0 -> x1, matrix products: none -> 0.38 us  [shards(): equivalent = jnp.dot(up_inverse, check, preferred_element_type=jnp.float32)]
    pallas_call x2 -> x1, Pallas kernels: 1.26 us -> 0.95 us  [rest(): pl.pallas_call(functools.partial(rest_kernel, windows), out_shape=jax.Sha...]
  transfers between devices with their start and end apart: 9 -> 9, of which waited for: 5 -> 4; matrix products, arithmetic and copies ran while one was open for 0% -> 7% of each run, Pallas kernels for 18% -> 15%
where the time goes in v5:
time: 35.2 us; the launch traced here: 35 us
  starting transfers between devices  13.5 us (38%)
  waiting for transfers between devices  9.47 us (27%)
  Pallas kernels  8.68 us (25%)
  local copies, waits for them, and re-layouts  1.95 us (6%)
  other arithmetic  0.83 us (2%)
  matrix products  0.38 us (1%)
    ppermute x2, starting transfers between devices, to_near(): lax.ppermute(value, 'tile', [(a, b) for a, b in pairs if 0 <= b < count])  6.18 us
    ppermute x3, waiting for transfers between devices, across_sub(): return lax.ppermute(shard, 'sub', [(0, 1), (1, 0)])  4.77 us
    pallas_call x1, Pallas kernels, prepare(): pl.pallas_call(functools.partial(prepare_kernel, windows), out_shape=[jax...  3.92 us
    ppermute x3, starting transfers between devices, across_sub(): return lax.ppermute(shard, 'sub', [(0, 1), (1, 0)])  3.71 us
    ppermute x1, starting transfers between devices, to_far(): lax.ppermute(value, 'tile', [(a, b) for a, b in pairs if 0 <= b < count])  3.3 us
    ppermute x2, waiting for transfers between devices, to_near(): lax.ppermute(value, 'tile', [(a, b) for a, b in pairs if 0 <= b < count])  3.19 us
    pallas_call x1, Pallas kernels, push_away(): pl.pallas_call(functools.partial(push_away_kernel, windows), out_shape=[j...  2.41 us
    dynamic_update_slice x1, local copies, waits for them, and re-layouts, shards(): lax.dynamic_update_slice(jnp.zeros((depth, cells), up_check.dtype), up_ch...  1.5 us
  transfers between devices with their start and end apart: 9, of which 4 were waited for; matrix products, arithmetic and copies ran while one was open for 7% of the time, Pallas kernels for 15%

profile of v5, /device:TPU:8, one launch (start us, length us, event | category | flops | bytes accessed | tf_op | source)
XLA Modules:
  0.0 35.0 jit_solution(3759877943136891510)
XLA Ops:
  0.0 0.0 copy-start
  0.0 0.8 %bitcast_select_fusion.code_ref = s32[8,128]{1,0:T(8,128)S(1)} fusion(s32[128,8]{0,1:T(8,128)} %param.11, s32[128,8]{0,1:T(8,128)} %param.12, s32[128]{0:T(128)} %param.13), kind=kLoop, calls=%fused_computation.4 | loop fusion | flops 4096 | bytes 12800 | tf_op jit(solution)/shard_map/jit(_where)/select_n | solution.py:327
  0.8 0.0 collective-permute-start
  0.8 1.6 %collective-permute-start.1 = (bf16[444,128]{1,0:T(8,128)(2,1)}, bf16[444,128]{1,0:T(8,128)(2,1)S(1)}, u32[]{:S(2)}, u32[]{:S(2)}) collective-permute-start(bf16[444,128]{1,0:T(8,128)(2,1)} %param.7), channel_id=1, source_target_pairs={{0,1},{1,0},{2,3},{3,2},{4,5},{5,4},{6,7},{7,6},{8,9},{9,8},{10,11... | collective-permute-start | bytes 341000 | tf_op jit(solution)/shard_map/ppermute | solution.py:19
  2.4 1.5 %dynamic_update_slice.6 = bf16[888,128]{1,0:T(8,128)(2,1)S(1)} dynamic-update-slice(bf16[888,128]{1,0:T(8,128)(2,1)S(1)} %broadcast_in_dim.8, bf16[444,128]{1,0:T(8,128)(2,1)} %param.7, s32[]{:T(128)S(6)} %select_n.10, s32[]{:T(128)} %constant.5.clone.1) | dynamic-update-slice | bytes 227332 | tf_op jit(solution)/shard_map/dynamic_update_slice | solution.py:336
  3.9 0.0 collective-permute-done.mate_ref
  3.9 3.1 %collective-permute-start.2 = (s32[16,128]{1,0:T(8,128)S(1)}, s32[16,128]{1,0:T(8,128)S(1)}, u32[]{:S(2)}, u32[]{:S(2)}) collective-permute-start(s32[16,128]{1,0:T(8,128)S(1)} %pad_add_fusion), channel_id=1, source_target_pairs={{2,4},{4,2},{6,8},{8,6},{10,12},{12,10},{14,16},{16,14},{18,20},{2... | collective-permute-start | bytes 24584 | tf_op jit(solution)/shard_map/ppermute | solution.py:31
  7.0 0.0 collective-permute-done.1
  7.0 0.4 %dynamic_update_slice.7 = bf16[888,128]{1,0:T(8,128)(2,1)S(1)} dynamic-update-slice(bf16[888,128]{1,0:T(8,128)(2,1)S(1)} %dynamic_update_slice.6, bf16[444,128]{1,0:T(8,128)(2,1)S(1)} %collective-permute-done.1, s32[]{:T(128)S(6)} %select_n.12, s32[]{:T(128)} %constant.5.clone.1) | dynamic-update-slice | bytes 227332 | tf_op jit(solution)/shard_map/dynamic_update_slice | solution.py:340
  7.4 0.0 copy-done
  7.4 0.4 %fusion.own_ref = bf16[444,128]{1,0:T(8,128)(2,1)S(1)} fusion(bf16[888,128]{1,0:T(8,128)(2,1)S(1)} %dynamic_update_slice.7, bf16[444,888]{1,0:T(8,128)(2,1)S(1)} %copy-done), kind=kOutput, calls=%fused_computation.1 | convolution fusion | flops 100990464 | bytes 1129536 | tf_op jit(solution)/shard_map/dot_general | solution.py:344
  7.8 1.7 %collective-permute-start.3 = (bf16[444,128]{1,0:T(8,128)(2,1)S(1)}, bf16[444,128]{1,0:T(8,128)(2,1)S(1)}, u32[]{:S(2)}, u32[]{:S(2)}) collective-permute-start(bf16[444,128]{1,0:T(8,128)(2,1)S(1)} %fusion.own_ref), channel_id=1, source_target_pairs={{0,1},{1,0},{2,3},{3,2},{4,5},{5,4},{6,7},{7,6},{8,9},{9,8},{10,11... | collective-permute-start | bytes 341000 | tf_op jit(solution)/shard_map/ppermute | solution.py:19
  9.5 3.9 %prepare.1 = (bf16[444,8,888]{2,1,0:T(8,128)(2,1)S(1)}, f32[3552,128]{1,0:T(8,128)S(1)}, bf16[1024,128]{1,0:T(8,128)(2,1)S(1)}, bf16[1024,128]{1,0:T(8,128)(2,1)S(1)}) custom-call(bf16[444,8,888]{2,1,0:T(8,128)(2,1)} %bitcast.7, bf16[444,128]{1,0:T(8,128)(2,1)S(1)} %fusion.own_ref, s32[8,128]{1,0:T(8,128)S(1)} %bitcast_select_fusion.code_ref, ...), custom_call_target="tpu_custom_call" | custom-call | flops 4294967296 | tf_op jit(solution)/shard_map/prepare/pallas_call | solution.py:181
  13.4 0.0 collective-permute-done.2.near_ref
  13.4 0.1 collective-permute-start.4
  13.5 0.5 %selections.1 = (bf16[1024,128]{1,0:T(8,128)(2,1)S(1)}, bf16[1024,128]{1,0:T(8,128)(2,1)S(1)}) custom-call(s32[16,128]{1,0:T(8,128)S(1)} %collective-permute-done.2.near_ref), custom_call_target="tpu_custom_call" | custom-call | flops 4294967296 | tf_op jit(solution)/shard_map/selections/pallas_call | solution.py:212
  14.0 0.0 copy-start.1
  14.0 0.7 %collective-permute-done.4.code_ref = s32[8,128]{1,0:T(8,128)S(1)} collective-permute-done((s32[8,128]{1,0:T(8,128)S(1)}, s32[8,128]{1,0:T(8,128)S(1)}, u32[]{:S(2)}, u32[]{:S(2)}) %collective-permute-start.4) | collective-permute-done | bytes 4128 | tf_op jit(solution)/shard_map/ppermute | solution.py:25
  14.7 0.0 collective-permute-done.3.other_ref
  14.7 2.4 %push_away.1 = (bf16[444,1024]{1,0:T(8,128)(2,1)S(1)}, bf16[444,256]{1,0:T(8,128)(2,1)S(1)}, bf16[444,128]{1,0:T(8,128)(2,1)S(1)}) custom-call(bf16[444,8,888]{2,1,0:T(8,128)(2,1)S(1)} %get-tuple-element.22.held_ref, f32[3552,128]{1,0:T(8,128)S(1)} %get-tuple-element.24.product_ref, bf16[444,128]{1,0:T(8,128)(2,1)S(1)} %collective-permute-done.3.other_ref, ...), custom_call_target="tpu_custom_call" | custom-call | flops 814743552 | bytes 6308352 | tf_op jit(solution)/shard_map/push_away/pallas_call | solution.py:266
  17.1 0.2 collective-permute-start.5
  17.3 3.3 %collective-permute-start.6 = (bf16[444,128]{1,0:T(8,128)(2,1)S(1)}, bf16[444,128]{1,0:T(8,128)(2,1)S(1)}, u32[]{:S(2)}, u32[]{:S(2)}) collective-permute-start(bf16[444,128]{1,0:T(8,128)(2,1)S(1)} %get-tuple-element.33), channel_id=1, source_target_pairs={{2,6},{4,0},{6,10},{8,4},{10,14},{12,8},{14,18},{16,12},{18,22},{2... | collective-permute-start | bytes 341000 | tf_op jit(solution)/shard_map/ppermute | solution.py:37
  20.6 0.0 collective-permute-done.5.came_ref
  20.6 0.6 %push_home.1 = (f32[444,128]{1,0:T(8,128)S(1)}, bf16[444,128]{1,0:T(8,128)(2,1)S(1)}) custom-call(bf16[444,1024]{1,0:T(8,128)(2,1)S(1)} %get-tuple-element.28.terms_ref, bf16[1024,128]{1,0:T(8,128)(2,1)S(1)} %get-tuple-element.29.home_ref, bf16[1024,128]{1,0:T(8,128)(2,1)S(1)} %get-tuple-element.30.near_select_ref, ...), custom_call_target="tpu_custom_call" | custom-call | flops 232783872 | bytes 1818624 | tf_op jit(solution)/shard_map/push_home/pallas_call | solution.py:305
  21.3 3.1 %collective-permute-start.7 = (bf16[444,128]{1,0:T(8,128)(2,1)S(1)}, bf16[444,128]{1,0:T(8,128)(2,1)S(1)}, u32[]{:S(2)}, u32[]{:S(2)}) collective-permute-start(bf16[444,128]{1,0:T(8,128)(2,1)S(1)} %get-tuple-element.34), channel_id=1, source_target_pairs={{2,4},{4,2},{6,8},{8,6},{10,12},{12,10},{14,16},{16,14},{18,20},{2... | collective-permute-start | bytes 341000 | tf_op jit(solution)/shard_map/ppermute | solution.py:31
  24.4 0.8 %collective-permute-done.6 = bf16[444,128]{1,0:T(8,128)(2,1)S(1)} collective-permute-done((bf16[444,128]{1,0:T(8,128)(2,1)S(1)}, bf16[444,128]{1,0:T(8,128)(2,1)S(1)}, u32[]{:S(2)}, u32[]{:S(2)}) %collective-permute-start.6) | collective-permute-done | bytes 113696 | tf_op jit(solution)/shard_map/ppermute | solution.py:37
  25.2 3.2 %collective-permute-done.7 = bf16[444,128]{1,0:T(8,128)(2,1)S(1)} collective-permute-done((bf16[444,128]{1,0:T(8,128)(2,1)S(1)}, bf16[444,128]{1,0:T(8,128)(2,1)S(1)}, u32[]{:S(2)}, u32[]{:S(2)}) %collective-permute-start.7) | collective-permute-done | bytes 113696 | tf_op jit(solution)/shard_map/ppermute | solution.py:31
  28.5 0.5 %collective-permute-start.8 = (bf16[444,128]{1,0:T(8,128)(2,1)S(1)}, bf16[444,128]{1,0:T(8,128)(2,1)S(1)}, u32[]{:S(2)}, u32[]{:S(2)}) collective-permute-start(bf16[444,128]{1,0:T(8,128)(2,1)S(1)} %add_convert_fusion.own_ref), channel_id=1, source_target_pairs={{0,1},{1,0},{2,3},{3,2},{4,5},{5,4},{6,7},{7,6},{8,9},{9,8},{10,11... | collective-permute-start | bytes 341000 | tf_op jit(solution)/shard_map/ppermute | solution.py:19
  28.9 0.0 copy-done.1
  29.0 0.3 first.1.part_ref
  29.2 4.8 %collective-permute-done.8.other_ref = bf16[444,128]{1,0:T(8,128)(2,1)S(1)} collective-permute-done((bf16[444,128]{1,0:T(8,128)(2,1)S(1)}, bf16[444,128]{1,0:T(8,128)(2,1)S(1)}, u32[]{:S(2)}, u32[]{:S(2)}) %collective-permute-start.8) | collective-permute-done | bytes 113696 | tf_op jit(solution)/shard_map/ppermute | solution.py:19
  34.0 1.0 %rest.1 = bf16[444,128]{1,0:T(8,128)(2,1)} custom-call(bf16[444,888]{1,0:T(8,128)(2,1)S(1)} %copy-done.1, f32[444,128]{1,0:T(8,128)S(1)} %first.1.part_ref, bf16[444,128]{1,0:T(8,128)(2,1)S(1)} %collective-permute-done.8.other_ref), custom_call_target="tpu_custom_call" | custom-call | flops 58195968 | bytes 454656 | tf_op jit(solution)/shard_map/rest/pallas_call | solution.py:112
  (4 shorter events, 0.1 us)
Async XLA Ops:
  0.0 7.4 %copy-start = (bf16[444,888]{1,0:T(8,128)(2,1)S(1)}, bf16[444,888]{1,0:T(8,128)(2,1)}, u32[]{:S(2)}) copy-start(bf16[444,888]{1,0:T(8,128)(2,1)} %param.8) | copy-start | bytes 2365636
  0.8 3.1 %collective-permute-start = (s32[8,128]{1,0:T(8,128)S(1)}, s32[8,128]{1,0:T(8,128)S(1)}, u32[]{:S(2)}, u32[]{:S(2)}) collective-permute-start(s32[8,128]{1,0:T(8,128)S(1)} %bitcast_select_fusion.code_ref), channel_id=1, source_target_pairs={{0,2},{2,0},{4,6},{6,4},{8,10},{10,8},{12,14},{14,12},{16,18},{18,... | collective-permute-start | bytes 12296 | tf_op jit(solution)/shard_map/ppermute | solution.py:25
  0.8 6.2 %collective-permute-start.1 = (bf16[444,128]{1,0:T(8,128)(2,1)}, bf16[444,128]{1,0:T(8,128)(2,1)S(1)}, u32[]{:S(2)}, u32[]{:S(2)}) collective-permute-start(bf16[444,128]{1,0:T(8,128)(2,1)} %param.7), channel_id=1, source_target_pairs={{0,1},{1,0},{2,3},{3,2},{4,5},{5,4},{6,7},{7,6},{8,9},{9,8},{10,11... | collective-permute-start | bytes 341000 | tf_op jit(solution)/shard_map/ppermute | solution.py:19
  3.9 9.5 %collective-permute-start.2 = (s32[16,128]{1,0:T(8,128)S(1)}, s32[16,128]{1,0:T(8,128)S(1)}, u32[]{:S(2)}, u32[]{:S(2)}) collective-permute-start(s32[16,128]{1,0:T(8,128)S(1)} %pad_add_fusion), channel_id=1, source_target_pairs={{2,4},{4,2},{6,8},{8,6},{10,12},{12,10},{14,16},{16,14},{18,20},{2... | collective-permute-start | bytes 24584 | tf_op jit(solution)/shard_map/ppermute | solution.py:31
  7.8 6.9 %collective-permute-start.3 = (bf16[444,128]{1,0:T(8,128)(2,1)S(1)}, bf16[444,128]{1,0:T(8,128)(2,1)S(1)}, u32[]{:S(2)}, u32[]{:S(2)}) collective-permute-start(bf16[444,128]{1,0:T(8,128)(2,1)S(1)} %fusion.own_ref), channel_id=1, source_target_pairs={{0,1},{1,0},{2,3},{3,2},{4,5},{5,4},{6,7},{7,6},{8,9},{9,8},{10,11... | collective-permute-start | bytes 341000 | tf_op jit(solution)/shard_map/ppermute | solution.py:19
  13.4 1.2 %collective-permute-start.4 = (s32[8,128]{1,0:T(8,128)S(1)}, s32[8,128]{1,0:T(8,128)S(1)}, u32[]{:S(2)}, u32[]{:S(2)}) collective-permute-start(s32[8,128]{1,0:T(8,128)S(1)} %slice.3), channel_id=1, source_target_pairs={{0,2},{2,0},{4,6},{6,4},{8,10},{10,8},{12,14},{14,12},{16,18},{18,... | collective-permute-start | bytes 12296 | tf_op jit(solution)/shard_map/ppermute | solution.py:25
  14.0 15.0 %copy-start.1 = (bf16[444,888]{1,0:T(8,128)(2,1)S(1)}, bf16[444,888]{1,0:T(8,128)(2,1)}, u32[]{:S(2)}) copy-start(bf16[444,888]{1,0:T(8,128)(2,1)} %matrix_ref.3) | copy-start | bytes 2365636
  17.1 3.5 %collective-permute-start.5 = (bf16[444,256]{1,0:T(8,128)(2,1)S(1)}, bf16[444,256]{1,0:T(8,128)(2,1)S(1)}, u32[]{:S(2)}, u32[]{:S(2)}) collective-permute-start(bf16[444,256]{1,0:T(8,128)(2,1)S(1)} %get-tuple-element.31), channel_id=1, source_target_pairs={{0,2},{2,0},{4,6},{6,4},{8,10},{10,8},{12,14},{14,12},{16,18},{18,... | collective-permute-start | bytes 681992 | tf_op jit(solution)/shard_map/ppermute | solution.py:25
  17.3 7.9 %collective-permute-start.6 = (bf16[444,128]{1,0:T(8,128)(2,1)S(1)}, bf16[444,128]{1,0:T(8,128)(2,1)S(1)}, u32[]{:S(2)}, u32[]{:S(2)}) collective-permute-start(bf16[444,128]{1,0:T(8,128)(2,1)S(1)} %get-tuple-element.33), channel_id=1, source_target_pairs={{2,6},{4,0},{6,10},{8,4},{10,14},{12,8},{14,18},{16,12},{18,22},{2... | collective-permute-start | bytes 341000 | tf_op jit(solution)/shard_map/ppermute | solution.py:37
  21.3 7.1 %collective-permute-start.7 = (bf16[444,128]{1,0:T(8,128)(2,1)S(1)}, bf16[444,128]{1,0:T(8,128)(2,1)S(1)}, u32[]{:S(2)}, u32[]{:S(2)}) collective-permute-start(bf16[444,128]{1,0:T(8,128)(2,1)S(1)} %get-tuple-element.34), channel_id=1, source_target_pairs={{2,4},{4,2},{6,8},{8,6},{10,12},{12,10},{14,16},{16,14},{18,20},{2... | collective-permute-start | bytes 341000 | tf_op jit(solution)/shard_map/ppermute | solution.py:31
  28.5 5.5 %collective-permute-start.8 = (bf16[444,128]{1,0:T(8,128)(2,1)S(1)}, bf16[444,128]{1,0:T(8,128)(2,1)S(1)}, u32[]{:S(2)}, u32[]{:S(2)}) collective-permute-start(bf16[444,128]{1,0:T(8,128)(2,1)S(1)} %add_convert_fusion.own_ref), channel_id=1, source_target_pairs={{0,1},{1,0},{2,3},{3,2},{4,5},{5,4},{6,7},{7,6},{8,9},{9,8},{10,11... | collective-permute-start | bytes 341000 | tf_op jit(solution)/shard_map/ppermute | solution.py:19

commit v6 on v4

--- a/solution.py
+++ b/solution.py
@@ -11,6 +11,8 @@
 CLASS_SHIFT = 10
 CHUNK = 112
 LANES = 128
+LOAD = 56
+IN_FLIGHT = 3
 WHOLE = pl.BlockSpec(memory_space=pltpu.VMEM)
 
 
@@ -50,8 +52,8 @@
     return windows
 
 
-def chunks(rows):
-    return [(start, min(CHUNK, rows - start)) for start in range(0, rows, CHUNK)]
+def chunks(rows, size):
+    return [(start, min(size, rows - start)) for start in range(0, rows, size)]
 
 
 def pad_into(padded, offset, *refs):
@@ -173,38 +175,40 @@
                 used = jnp.where(kinds[entry : entry + 1, :] == k, 1.0, 0.0).astype(jnp.bfloat16)
                 totals[k] = totals[k] + hit * used
         for k in range(classes):
-            out_ref[k * cells + low : k * cells + low + band, column : column + cells] = totals[k]
+            row = k * cells + low
+            out_ref[row : row + band, column : column + cells] = totals[k]
 
 
 def prepare_kernel(
-    windows, translate_ref, own_ref, code_ref, near_ref, mate_ref, mate_near_ref,
-    held_ref, product_ref, away_select_ref, home_select_ref, padded, sems,
+    windows, translate_ref, own_ref, code_ref, mate_ref, near_ref,
+    held_ref, product_ref, home_ref, away_ref, padded, sems,
 ):
     rows, classes, _ = translate_ref.shape
     entries, cells = code_ref.shape
+    parts = chunks(rows, LOAD)
     copies = []
-    for i, (start, size) in enumerate(chunks(rows)):
+    for i, (start, size) in enumerate(parts):
         part = pl.ds(start, size)
-        copy = pltpu.make_async_copy(translate_ref.at[part], held_ref.at[part], sems.at[i])
+        copies.append(
+            pltpu.make_async_copy(translate_ref.at[part], held_ref.at[part], sems.at[i])
+        )
+    for copy in copies[:IN_FLIGHT]:
         copy.start()
-        copies.append(copy)
 
     step = away()
-    for block, (code, offset) in enumerate(
-        [(mate_ref[...], -step), (mate_near_ref[...], -2 * step), (near_ref[entries:], 2 * step)]
-    ):
-        base = (REACH - offset) * cells
-        build_select(code, base, away_select_ref, block * cells, classes)
-    for block, (code, offset) in enumerate([(code_ref[...], 0), (near_ref[:entries], step)]):
-        base = (REACH - offset) * cells
-        build_select(code, base, home_select_ref, block * cells, classes)
+    build_select(code_ref[...], REACH * cells, home_ref, 0, classes)
+    build_select(near_ref[:entries, :], (REACH - step) * cells, home_ref, cells, classes)
+    build_select(mate_ref[...], (REACH + step) * cells, away_ref, 0, classes)
+    build_select(near_ref[entries:, :], (REACH - 2 * step) * cells, away_ref, cells, classes)
 
     for index, (low, high, offset) in enumerate(windows):
         def run(low=low, high=high, offset=offset):
             pad_into(padded, offset, own_ref)
             right = padded[: high - low, :].astype(jnp.bfloat16)
-            for copy, (start, size) in zip(copies, chunks(rows)):
-                copy.wait()
+            for i, (start, size) in enumerate(parts):
+                copies[i].wait()
+                if i + IN_FLIGHT < len(parts):
+                    copies[i + IN_FLIGHT].start()
                 left = held_ref[start : start + size, :, low:high]
                 product_ref[start * classes : (start + size) * classes, :] = jnp.dot(
                     left.reshape(size * classes, high - low), right,
@@ -216,43 +220,41 @@
             pl.when(lax.axis_index("sub") == index)(run)
 
 
-def prepare(operators, own, code, near_codes, mate_code, mate_near_code, windows):
+def prepare(operators, own, code, mate_code, near_codes, windows):
     rows, classes, depth = operators.shape
     cells = code.shape[1]
     span = max(high - low for low, high, _ in windows)
+    select = jax.ShapeDtypeStruct((classes * cells, 2 * cells), jnp.bfloat16)
     return pl.pallas_call(
         functools.partial(prepare_kernel, windows),
         out_shape=[
             jax.ShapeDtypeStruct((rows, classes, depth), jnp.bfloat16),
             jax.ShapeDtypeStruct((rows * classes, cells), jnp.float32),
-            jax.ShapeDtypeStruct((classes * cells, 3 * cells), jnp.bfloat16),
-            jax.ShapeDtypeStruct((classes * cells, 2 * cells), jnp.bfloat16),
-        ],
-        in_specs=[pl.BlockSpec(memory_space=pltpu.HBM)] + [WHOLE] * 5,
+            select,
+            select,
+        ],
+        in_specs=[pl.BlockSpec(memory_space=pltpu.HBM)] + [WHOLE] * 4,
         out_specs=[WHOLE] * 4,
         scratch_shapes=[
             pltpu.VMEM((span, cells), jnp.float32),
-            pltpu.SemaphoreType.DMA((len(chunks(rows)),)),
-        ],
-        cost_estimate=pl.CostEstimate(
-            flops=4 * rows * classes * cells * span,
-            bytes_accessed=2 * rows * classes * depth,
-            transcendentals=0,
-        ),
+            pltpu.SemaphoreType.DMA((len(chunks(rows, LOAD)),)),
+        ],
+        cost_estimate=pl.CostEstimate(flops=1 << 32, bytes_accessed=0, transcendentals=0),
         compiler_params=pltpu.CompilerParams(vmem_limit_bytes=32 << 20),
         name="prepare",
     )(
         pltpu.with_memory_space_constraint(operators, pltpu.HBM),
-        own, code, near_codes, mate_code, mate_near_code,
+        own, code, mate_code, near_codes,
     )
 
 
 def push_away_kernel(
-    windows, held_ref, product_ref, other_ref, select_ref,
-    terms_ref, mate_ref, far_ref, padded, product,
+    windows, held_ref, product_ref, other_ref, away_ref, code_ref,
+    terms_ref, mate_ref, far_ref, padded, product, select,
 ):
     rows, classes, _ = held_ref.shape
     cells = far_ref.shape[1]
+    build_select(code_ref[...], (REACH + 2 * away()) * cells, select, 0, classes)
 
     def part_classes(source, start, size):
         for k in range(classes):
@@ -263,7 +265,7 @@
         def run(low=low, high=high, offset=offset):
             pad_into(padded, offset, other_ref)
             right = padded[: high - low, :].astype(jnp.bfloat16)
-            for start, size in chunks(rows):
+            for start, size in chunks(rows, CHUNK):
                 left = held_ref[start : start + size, :, low:high]
                 part = slice(start * classes, (start + size) * classes)
                 product[part, :] = product_ref[part, :] + jnp.dot(
@@ -274,15 +276,19 @@
         pl.when(lax.axis_index("sub") != index)(run)
 
     if not windows:
-        for start, size in chunks(rows):
+        for start, size in chunks(rows, CHUNK):
             part_classes(product_ref, start, size)
 
-    total = jnp.dot(terms_ref[...], select_ref[...], preferred_element_type=jnp.float32)
-    mate_ref[...] = total[:, : 2 * cells].astype(jnp.bfloat16)
-    far_ref[...] = total[:, 2 * cells :].astype(jnp.bfloat16)
-
-
-def push_away(held, product, other, select, windows):
+    terms = terms_ref[...]
+    total = jnp.dot(terms, away_ref[...], preferred_element_type=jnp.float32)
+    mate_ref[:, :cells] = total[:, :cells].astype(jnp.bfloat16)
+    far_ref[...] = total[:, cells:].astype(jnp.bfloat16)
+    mate_ref[:, cells:] = jnp.dot(
+        terms, select[...], preferred_element_type=jnp.float32
+    ).astype(jnp.bfloat16)
+
+
+def push_away(held, product, other, away_select, code, windows):
     rows, classes, depth = held.shape
     cells = other.shape[1]
     span = max([high - low for low, high, _ in windows], default=LANES)
@@ -293,11 +299,12 @@
             jax.ShapeDtypeStruct((rows, 2 * cells), jnp.bfloat16),
             jax.ShapeDtypeStruct((rows, cells), jnp.bfloat16),
         ],
-        in_specs=[WHOLE] * 4,
+        in_specs=[WHOLE] * 5,
         out_specs=[WHOLE] * 3,
         scratch_shapes=[
             pltpu.VMEM((span, cells), jnp.float32),
             pltpu.VMEM((rows * classes, cells), jnp.float32),
+            pltpu.VMEM((classes * cells, cells), jnp.bfloat16),
         ],
         cost_estimate=pl.CostEstimate(
             flops=2 * rows * classes * cells * (span + 3 * cells),
@@ -306,7 +313,7 @@
         ),
         compiler_params=pltpu.CompilerParams(vmem_limit_bytes=32 << 20),
         name="push_away",
-    )(held, product, other, select)
+    )(held, product, other, away_select, code)
 
 
 def push_home_kernel(terms_ref, select_ref, came_ref, own_ref, near_ref):
@@ -346,18 +353,17 @@
     operators = jnp.transpose(translate, (1, 0, 2))
     mate_code = to_mate(code)
     near_codes = to_near(jnp.concatenate([code, mate_code], axis=0))
-    mate_near_code = to_mate(near_codes[:entries])
 
     operators = jnp.transpose(translate, (1, 0, 2))
     if halves:
         windows = half_windows(rows, depth, 2)
         other_check = across_sub(up_check)
-        staged, code = lax.optimization_barrier((up_inverse, code))
+        staged, mate_code = lax.optimization_barrier((up_inverse, mate_code))
         up_held, part = stage(staged, up_check, windows)
-        part, near_codes = lax.optimization_barrier((part, near_codes))
         equivalent = rest(up_held, part, other_check, windows)
         other = across_sub(equivalent)
     else:
+        windows = [(0, depth, 0)]
         equivalent = lax.all_gather(
             jnp.dot(
                 up_inverse, lax.all_gather(up_check, "sub", axis=0, tiled=True),
@@ -365,17 +371,19 @@
             ).astype(jnp.bfloat16),
             "sub", axis=0, tiled=True,
         )
-        windows = [(0, depth, 0)]
         other = equivalent
-    held, product, away_select, home_select = prepare(
-        operators, equivalent, code, near_codes, mate_code, mate_near_code, windows
+    near_codes, _ = lax.optimization_barrier((near_codes, equivalent))
+    mate_near_code = to_mate(near_codes[:entries])
+    held, product, home, away_select = prepare(
+        operators, equivalent, code, mate_code, near_codes, windows
     )
+    mate_near_code, product = lax.optimization_barrier((mate_near_code, product))
     terms, mate_sum, far_sum = push_away(
-        held, product, other, away_select, windows if halves else []
+        held, product, other, away_select, mate_near_code, windows if halves else []
     )
     mate_came = to_mate(mate_sum)
     far_came = to_far(far_sum)
-    own_sum, near_sum = push_home(terms, home_select, mate_came)
+    own_sum, near_sum = push_home(terms, home, mate_came)
     near_came = to_near(near_sum)
     down_check = (
         own_sum + (far_came.astype(jnp.float32) + near_came.astype(jnp.float32))

time: 34 us -> 33.1 us (0.974)
  waiting for transfers between devices: 10.2 us -> 8.54 us
  Pallas kernels: 9.36 us -> 10.1 us
    ppermute x3, waiting for transfers between devices: 1.17 us -> 0.01 us  [to_mate(): return lax.ppermute(value, 'tile', pairs)]
    ppermute x2, waiting for transfers between devices: 3.94 us -> 2.92 us  [to_near(): lax.ppermute(value, 'tile', [(a, b) for a, b in pairs if 0 <= b < count])]
    pallas_call x1, Pallas kernels: 3.92 us -> 4.48 us  [prepare(): pl.pallas_call(functools.partial(prepare_kernel, windows), out_shape=[jax...]
    ppermute x2, starting transfers between devices: 6.44 us -> 6.04 us  [to_near(): lax.ppermute(value, 'tile', [(a, b) for a, b in pairs if 0 <= b < count])]
  transfers between devices with their start and end apart: 9 -> 9, of which waited for: 5 -> 3; matrix products, arithmetic and copies ran while one was open for 0% -> 0% of each run, Pallas kernels for 18% -> 21%
where the time goes in v6:
time: 33.1 us; the launch traced here: 32.9 us
  starting transfers between devices  13.3 us (40%)
  Pallas kernels  10.1 us (31%)
  waiting for transfers between devices  8.54 us (26%)
  other arithmetic  0.75 us (2%)
    ppermute x2, starting transfers between devices, to_near(): lax.ppermute(value, 'tile', [(a, b) for a, b in pairs if 0 <= b < count])  6.04 us
    pallas_call x1, Pallas kernels, prepare(): pl.pallas_call(functools.partial(prepare_kernel, windows), out_shape=[jax...  4.48 us
    ppermute x3, waiting for transfers between devices, across_sub(): return lax.ppermute(shard, 'sub', [(0, 1), (1, 0)])  4.38 us
    ppermute x3, starting transfers between devices, across_sub(): return lax.ppermute(shard, 'sub', [(0, 1), (1, 0)])  3.44 us
    ppermute x1, starting transfers between devices, to_far(): lax.ppermute(value, 'tile', [(a, b) for a, b in pairs if 0 <= b < count])  3.26 us
    ppermute x2, waiting for transfers between devices, to_near(): lax.ppermute(value, 'tile', [(a, b) for a, b in pairs if 0 <= b < count])  2.92 us
    pallas_call x1, Pallas kernels, push_away(): pl.pallas_call(functools.partial(push_away_kernel, windows), out_shape=[j...  2.18 us
    pallas_call x1, Pallas kernels, stage(): pl.pallas_call(functools.partial(stage_kernel, windows), out_shape=[jax.S...  1.51 us
  transfers between devices with their start and end apart: 9, of which 3 were waited for; matrix products, arithmetic and copies ran while one was open for 0% of the time, Pallas kernels for 21%

profile of v6, /device:TPU:8, one launch (start us, length us, event | category | flops | bytes accessed | tf_op | source)
XLA Modules:
  0.0 32.9 jit_solution(718884356941166451)
XLA Ops:
  0.0 0.7 %bitcast_select_fusion.code_ref = s32[8,128]{1,0:T(8,128)S(1)} fusion(s32[128,8]{0,1:T(8,128)} %param.11, s32[128,8]{0,1:T(8,128)} %param.12, s32[128]{0:T(128)} %param.13), kind=kLoop, calls=%fused_computation.2 | loop fusion | flops 4096 | bytes 12800 | tf_op jit(solution)/shard_map/jit(_where)/select_n | solution.py:352
  0.7 0.0 collective-permute-start
  0.7 1.6 %collective-permute-start.1 = (bf16[444,128]{1,0:T(8,128)(2,1)}, bf16[444,128]{1,0:T(8,128)(2,1)S(1)}, u32[]{:S(2)}, u32[]{:S(2)}) collective-permute-start(bf16[444,128]{1,0:T(8,128)(2,1)} %own_ref.1), channel_id=1, source_target_pairs={{0,1},{1,0},{2,3},{3,2},{4,5},{5,4},{6,7},{7,6},{8,9},{9,8},{10,11... | collective-permute-start | bytes 341000 | tf_op jit(solution)/shard_map/ppermute | solution.py:20
  2.3 0.0 collective-permute-done.mate_ref
  2.3 3.1 %collective-permute-start.2 = (s32[16,128]{1,0:T(8,128)S(1)}, s32[16,128]{1,0:T(8,128)S(1)}, u32[]{:S(2)}, u32[]{:S(2)}) collective-permute-start(s32[16,128]{1,0:T(8,128)S(1)} %pad_add_fusion), channel_id=1, source_target_pairs={{2,4},{4,2},{6,8},{8,6},{10,12},{12,10},{14,16},{16,14},{18,20},{2... | collective-permute-start | bytes 24584 | tf_op jit(solution)/shard_map/ppermute | solution.py:32
  5.4 1.5 %stage.1 = (bf16[444,888]{1,0:T(8,128)(2,1)S(1)}, f32[444,128]{1,0:T(8,128)S(1)}) custom-call(bf16[444,888]{1,0:T(8,128)(2,1)} %matrix_ref.2, bf16[444,128]{1,0:T(8,128)(2,1)} %own_ref.1), custom_call_target="tpu_custom_call" | custom-call | flops 100933632 | bytes 1577088 | tf_op jit(solution)/shard_map/stage/pallas_call | solution.py:82
  6.9 0.0 collective-permute-done.1.other_ref
  6.9 0.3 rest.2.own_ref
  7.2 1.2 %collective-permute-start.4 = (bf16[444,128]{1,0:T(8,128)(2,1)S(1)}, bf16[444,128]{1,0:T(8,128)(2,1)S(1)}, u32[]{:S(2)}, u32[]{:S(2)}) collective-permute-start(bf16[444,128]{1,0:T(8,128)(2,1)S(1)} %rest.2.own_ref), channel_id=1, source_target_pairs={{0,1},{1,0},{2,3},{3,2},{4,5},{5,4},{6,7},{7,6},{8,9},{9,8},{10,11... | collective-permute-start | bytes 341000 | tf_op jit(solution)/shard_map/ppermute | solution.py:20
  8.4 0.0 collective-permute-done.2.near_ref
  8.4 0.2 collective-permute-start.3
  8.5 4.5 %prepare.1 = (bf16[444,8,888]{2,1,0:T(8,128)(2,1)S(1)}, f32[3552,128]{1,0:T(8,128)S(1)}, bf16[1024,256]{1,0:T(8,128)(2,1)S(1)}, bf16[1024,256]{1,0:T(8,128)(2,1)S(1)}) custom-call(bf16[444,8,888]{2,1,0:T(8,128)(2,1)} %bitcast.3, bf16[444,128]{1,0:T(8,128)(2,1)S(1)} %rest.2.own_ref, s32[8,128]{1,0:T(8,128)S(1)} %bitcast_select_fusion.code_ref, ...), custom_call_target="tpu_custom_call" | custom-call | flops 4294967296 | tf_op jit(solution)/shard_map/prepare/pallas_call | solution.py:228
  13.0 0.0 copy-start
  13.0 0.0 collective-permute-done.3.code_ref
  13.1 0.0 collective-permute-done.4.other_ref
  13.1 2.2 %push_away.1 = (bf16[444,1024]{1,0:T(8,128)(2,1)S(1)}, bf16[444,256]{1,0:T(8,128)(2,1)S(1)}, bf16[444,128]{1,0:T(8,128)(2,1)S(1)}) custom-call(bf16[444,8,888]{2,1,0:T(8,128)(2,1)S(1)} %get-tuple-element.26.held_ref, f32[3552,128]{1,0:T(8,128)S(1)} %get-tuple-element.28.product_ref, bf16[444,128]{1,0:T(8,128)(2,1)S(1)} %collective-permute-done.4.other_ref, ...), custom_call_target="tpu_custom_call" | custom-call | flops 814743552 | bytes 6308352 | tf_op jit(solution)/shard_map/push_away/pallas_call | solution.py:295
  15.3 0.4 %collective-permute-start.5 = (bf16[444,256]{1,0:T(8,128)(2,1)S(1)}, bf16[444,256]{1,0:T(8,128)(2,1)S(1)}, u32[]{:S(2)}, u32[]{:S(2)}) collective-permute-start(bf16[444,256]{1,0:T(8,128)(2,1)S(1)} %get-tuple-element.33), channel_id=1, source_target_pairs={{0,2},{2,0},{4,6},{6,4},{8,10},{10,8},{12,14},{14,12},{16,18},{18,... | collective-permute-start | bytes 681992 | tf_op jit(solution)/shard_map/ppermute | solution.py:26
  15.7 3.3 %collective-permute-start.6 = (bf16[444,128]{1,0:T(8,128)(2,1)S(1)}, bf16[444,128]{1,0:T(8,128)(2,1)S(1)}, u32[]{:S(2)}, u32[]{:S(2)}) collective-permute-start(bf16[444,128]{1,0:T(8,128)(2,1)S(1)} %get-tuple-element.35), channel_id=1, source_target_pairs={{2,6},{4,0},{6,10},{8,4},{10,14},{12,8},{14,18},{16,12},{18,22},{2... | collective-permute-start | bytes 341000 | tf_op jit(solution)/shard_map/ppermute | solution.py:38
  18.9 0.0 collective-permute-done.5.came_ref
  18.9 0.4 %push_home.1 = (f32[444,128]{1,0:T(8,128)S(1)}, bf16[444,128]{1,0:T(8,128)(2,1)S(1)}) custom-call(bf16[444,1024]{1,0:T(8,128)(2,1)S(1)} %get-tuple-element.31.terms_ref, bf16[1024,256]{1,0:T(8,128)(2,1)S(1)} %get-tuple-element.32.select_ref, bf16[444,256]{1,0:T(8,128)(2,1)S(1)} %collective-permute-done.5.came_ref), custom_call_target="tpu_custom_call" | custom-call | flops 232783872 | bytes 1818624 | tf_op jit(solution)/shard_map/push_home/pallas_call | solution.py:330
  19.4 3.0 %collective-permute-start.7 = (bf16[444,128]{1,0:T(8,128)(2,1)S(1)}, bf16[444,128]{1,0:T(8,128)(2,1)S(1)}, u32[]{:S(2)}, u32[]{:S(2)}) collective-permute-start(bf16[444,128]{1,0:T(8,128)(2,1)S(1)} %get-tuple-element.36), channel_id=1, source_target_pairs={{2,4},{4,2},{6,8},{8,6},{10,12},{12,10},{14,16},{16,14},{18,20},{2... | collective-permute-start | bytes 341000 | tf_op jit(solution)/shard_map/ppermute | solution.py:32
  22.3 1.2 %collective-permute-done.6 = bf16[444,128]{1,0:T(8,128)(2,1)S(1)} collective-permute-done((bf16[444,128]{1,0:T(8,128)(2,1)S(1)}, bf16[444,128]{1,0:T(8,128)(2,1)S(1)}, u32[]{:S(2)}, u32[]{:S(2)}) %collective-permute-start.6) | collective-permute-done | bytes 113696 | tf_op jit(solution)/shard_map/ppermute | solution.py:38
  23.6 2.9 %collective-permute-done.7 = bf16[444,128]{1,0:T(8,128)(2,1)S(1)} collective-permute-done((bf16[444,128]{1,0:T(8,128)(2,1)S(1)}, bf16[444,128]{1,0:T(8,128)(2,1)S(1)}, u32[]{:S(2)}, u32[]{:S(2)}) %collective-permute-start.7) | collective-permute-done | bytes 113696 | tf_op jit(solution)/shard_map/ppermute | solution.py:32
  26.5 0.7 %collective-permute-start.8 = (bf16[444,128]{1,0:T(8,128)(2,1)S(1)}, bf16[444,128]{1,0:T(8,128)(2,1)S(1)}, u32[]{:S(2)}, u32[]{:S(2)}) collective-permute-start(bf16[444,128]{1,0:T(8,128)(2,1)S(1)} %add_convert_fusion.own_ref), channel_id=1, source_target_pairs={{0,1},{1,0},{2,3},{3,2},{4,5},{5,4},{6,7},{7,6},{8,9},{9,8},{10,11... | collective-permute-start | bytes 341000 | tf_op jit(solution)/shard_map/ppermute | solution.py:20
  27.2 0.0 copy-done
  27.2 0.3 first.1.part_ref
  27.5 4.4 %collective-permute-done.8.other_ref = bf16[444,128]{1,0:T(8,128)(2,1)S(1)} collective-permute-done((bf16[444,128]{1,0:T(8,128)(2,1)S(1)}, bf16[444,128]{1,0:T(8,128)(2,1)S(1)}, u32[]{:S(2)}, u32[]{:S(2)}) %collective-permute-start.8) | collective-permute-done | bytes 113696 | tf_op jit(solution)/shard_map/ppermute | solution.py:20
  31.9 1.0 %rest.3 = bf16[444,128]{1,0:T(8,128)(2,1)} custom-call(bf16[444,888]{1,0:T(8,128)(2,1)S(1)} %copy-done, f32[444,128]{1,0:T(8,128)S(1)} %first.1.part_ref, bf16[444,128]{1,0:T(8,128)(2,1)S(1)} %collective-permute-done.8.other_ref), custom_call_target="tpu_custom_call" | custom-call | flops 58195968 | bytes 454656 | tf_op jit(solution)/shard_map/rest/pallas_call | solution.py:150
  (3 shorter events, 0.0 us)
Async XLA Ops:
  0.7 1.6 %collective-permute-start = (s32[8,128]{1,0:T(8,128)S(1)}, s32[8,128]{1,0:T(8,128)S(1)}, u32[]{:S(2)}, u32[]{:S(2)}) collective-permute-start(s32[8,128]{1,0:T(8,128)S(1)} %bitcast_select_fusion.code_ref), channel_id=1, source_target_pairs={{0,2},{2,0},{4,6},{6,4},{8,10},{10,8},{12,14},{14,12},{16,18},{18,... | collective-permute-start | bytes 12296 | tf_op jit(solution)/shard_map/ppermute | solution.py:26
  0.7 6.2 %collective-permute-start.1 = (bf16[444,128]{1,0:T(8,128)(2,1)}, bf16[444,128]{1,0:T(8,128)(2,1)S(1)}, u32[]{:S(2)}, u32[]{:S(2)}) collective-permute-start(bf16[444,128]{1,0:T(8,128)(2,1)} %own_ref.1), channel_id=1, source_target_pairs={{0,1},{1,0},{2,3},{3,2},{4,5},{5,4},{6,7},{7,6},{8,9},{9,8},{10,11... | collective-permute-start | bytes 341000 | tf_op jit(solution)/shard_map/ppermute | solution.py:20
  2.3 6.1 %collective-permute-start.2 = (s32[16,128]{1,0:T(8,128)S(1)}, s32[16,128]{1,0:T(8,128)S(1)}, u32[]{:S(2)}, u32[]{:S(2)}) collective-permute-start(s32[16,128]{1,0:T(8,128)S(1)} %pad_add_fusion), channel_id=1, source_target_pairs={{2,4},{4,2},{6,8},{8,6},{10,12},{12,10},{14,16},{16,14},{18,20},{2... | collective-permute-start | bytes 24584 | tf_op jit(solution)/shard_map/ppermute | solution.py:32
  7.2 5.9 %collective-permute-start.4 = (bf16[444,128]{1,0:T(8,128)(2,1)S(1)}, bf16[444,128]{1,0:T(8,128)(2,1)S(1)}, u32[]{:S(2)}, u32[]{:S(2)}) collective-permute-start(bf16[444,128]{1,0:T(8,128)(2,1)S(1)} %rest.2.own_ref), channel_id=1, source_target_pairs={{0,1},{1,0},{2,3},{3,2},{4,5},{5,4},{6,7},{7,6},{8,9},{9,8},{10,11... | collective-permute-start | bytes 341000 | tf_op jit(solution)/shard_map/ppermute | solution.py:20
  8.4 4.7 %collective-permute-start.3 = (s32[8,128]{1,0:T(8,128)S(1)}, s32[8,128]{1,0:T(8,128)S(1)}, u32[]{:S(2)}, u32[]{:S(2)}) collective-permute-start(s32[8,128]{1,0:T(8,128)S(1)} %slice.3), channel_id=1, source_target_pairs={{0,2},{2,0},{4,6},{6,4},{8,10},{10,8},{12,14},{14,12},{16,18},{18,... | collective-permute-start | bytes 12296 | tf_op jit(solution)/shard_map/ppermute | solution.py:26
  13.0 14.2 %copy-start = (bf16[444,888]{1,0:T(8,128)(2,1)S(1)}, bf16[444,888]{1,0:T(8,128)(2,1)}, u32[]{:S(2)}) copy-start(bf16[444,888]{1,0:T(8,128)(2,1)} %matrix_ref.4) | copy-start | bytes 2365636
  15.3 3.7 %collective-permute-start.5 = (bf16[444,256]{1,0:T(8,128)(2,1)S(1)}, bf16[444,256]{1,0:T(8,128)(2,1)S(1)}, u32[]{:S(2)}, u32[]{:S(2)}) collective-permute-start(bf16[444,256]{1,0:T(8,128)(2,1)S(1)} %get-tuple-element.33), channel_id=1, source_target_pairs={{0,2},{2,0},{4,6},{6,4},{8,10},{10,8},{12,14},{14,12},{16,18},{18,... | collective-permute-start | bytes 681992 | tf_op jit(solution)/shard_map/ppermute | solution.py:26
  15.7 7.9 %collective-permute-start.6 = (bf16[444,128]{1,0:T(8,128)(2,1)S(1)}, bf16[444,128]{1,0:T(8,128)(2,1)S(1)}, u32[]{:S(2)}, u32[]{:S(2)}) collective-permute-start(bf16[444,128]{1,0:T(8,128)(2,1)S(1)} %get-tuple-element.35), channel_id=1, source_target_pairs={{2,6},{4,0},{6,10},{8,4},{10,14},{12,8},{14,18},{16,12},{18,22},{2... | collective-permute-start | bytes 341000 | tf_op jit(solution)/shard_map/ppermute | solution.py:38
  19.4 7.1 %collective-permute-start.7 = (bf16[444,128]{1,0:T(8,128)(2,1)S(1)}, bf16[444,128]{1,0:T(8,128)(2,1)S(1)}, u32[]{:S(2)}, u32[]{:S(2)}) collective-permute-start(bf16[444,128]{1,0:T(8,128)(2,1)S(1)} %get-tuple-element.36), channel_id=1, source_target_pairs={{2,4},{4,2},{6,8},{8,6},{10,12},{12,10},{14,16},{16,14},{18,20},{2... | collective-permute-start | bytes 341000 | tf_op jit(solution)/shard_map/ppermute | solution.py:32
  26.5 5.4 %collective-permute-start.8 = (bf16[444,128]{1,0:T(8,128)(2,1)S(1)}, bf16[444,128]{1,0:T(8,128)(2,1)S(1)}, u32[]{:S(2)}, u32[]{:S(2)}) collective-permute-start(bf16[444,128]{1,0:T(8,128)(2,1)S(1)} %add_convert_fusion.own_ref), channel_id=1, source_target_pairs={{0,1},{1,0},{2,3},{3,2},{4,5},{5,4},{6,7},{7,6},{8,9},{9,8},{10,11... | collective-permute-start | bytes 341000 | tf_op jit(solution)/shard_map/ppermute | solution.py:20

commit v7 on v6

--- a/solution.py
+++ b/solution.py
@@ -11,8 +11,6 @@
 CLASS_SHIFT = 10
 CHUNK = 112
 LANES = 128
-LOAD = 56
-IN_FLIGHT = 3
 WHOLE = pl.BlockSpec(memory_space=pltpu.VMEM)
 
 
@@ -185,15 +183,32 @@
 ):
     rows, classes, _ = translate_ref.shape
     entries, cells = code_ref.shape
-    parts = chunks(rows, LOAD)
-    copies = []
-    for i, (start, size) in enumerate(parts):
-        part = pl.ds(start, size)
-        copies.append(
-            pltpu.make_async_copy(translate_ref.at[part], held_ref.at[part], sems.at[i])
-        )
-    for copy in copies[:IN_FLIGHT]:
-        copy.start()
+    depth = translate_ref.shape[2]
+    parts = chunks(rows, CHUNK)
+
+    def load(low, high, semaphore):
+        copies = []
+        for i, (start, size) in enumerate(parts):
+            where = (pl.ds(start, size), slice(None), pl.ds(low, high - low))
+            copies.append(
+                pltpu.make_async_copy(
+                    translate_ref.at[where], held_ref.at[where], sems.at[semaphore, i]
+                )
+            )
+        return copies
+
+    def on_window(run):
+        for index, window in enumerate(windows):
+            if len(windows) == 1:
+                run(*window)
+            else:
+                pl.when(lax.axis_index("sub") == index)(functools.partial(run, *window))
+
+    def begin(low, high, offset):
+        for copy in load(low, high, 0):
+            copy.start()
+
+    on_window(begin)
 
     step = away()
     build_select(code_ref[...], REACH * cells, home_ref, 0, classes)
@@ -201,23 +216,28 @@
     build_select(mate_ref[...], (REACH + step) * cells, away_ref, 0, classes)
     build_select(near_ref[entries:, :], (REACH - 2 * step) * cells, away_ref, cells, classes)
 
-    for index, (low, high, offset) in enumerate(windows):
-        def run(low=low, high=high, offset=offset):
-            pad_into(padded, offset, own_ref)
-            right = padded[: high - low, :].astype(jnp.bfloat16)
-            for i, (start, size) in enumerate(parts):
-                copies[i].wait()
-                if i + IN_FLIGHT < len(parts):
-                    copies[i + IN_FLIGHT].start()
-                left = held_ref[start : start + size, :, low:high]
-                product_ref[start * classes : (start + size) * classes, :] = jnp.dot(
-                    left.reshape(size * classes, high - low), right,
-                    preferred_element_type=jnp.float32,
-                )
-        if len(windows) == 1:
-            run()
-        else:
-            pl.when(lax.axis_index("sub") == index)(run)
+    def run(low, high, offset):
+        first_copies = load(low, high, 0)
+        other_copies = []
+        for left, right in ((0, low), (high, depth)):
+            if left < right:
+                other_copies += load(left, right, 1)
+        pad_into(padded, offset, own_ref)
+        equivalent = padded[: high - low, :].astype(jnp.bfloat16)
+        for copy in first_copies:
+            copy.wait()
+        for copy in other_copies:
+            copy.start()
+        for start, size in parts:
+            matrix = held_ref[start : start + size, :, low:high]
+            product_ref[start * classes : (start + size) * classes, :] = jnp.dot(
+                matrix.reshape(size * classes, high - low), equivalent,
+                preferred_element_type=jnp.float32,
+            )
+        for copy in other_copies:
+            copy.wait()
+
+    on_window(run)
 
 
 def prepare(operators, own, code, mate_code, near_codes, windows):
@@ -237,7 +257,7 @@
         out_specs=[WHOLE] * 4,
         scratch_shapes=[
             pltpu.VMEM((span, cells), jnp.float32),
-            pltpu.SemaphoreType.DMA((len(chunks(rows, LOAD)),)),
+            pltpu.SemaphoreType.DMA((2, len(chunks(rows, CHUNK)))),
         ],
         cost_estimate=pl.CostEstimate(flops=1 << 32, bytes_accessed=0, transcendentals=0),
         compiler_params=pltpu.CompilerParams(vmem_limit_bytes=32 << 20),

time: 33.1 us -> 32.8 us (level)
  Pallas kernels: 10.1 us -> 9.47 us
  starting transfers between devices: 13.3 us -> 13.8 us
    pallas_call x1, Pallas kernels: 4.48 us -> 3.81 us  [prepare(): pl.pallas_call(functools.partial(prepare_kernel, windows), out_shape=[jax...]
    ppermute x3, starting transfers between devices: 3.44 us -> 3.88 us  [across_sub(): return lax.ppermute(shard, 'sub', [(0, 1), (1, 0)])]
    ppermute x3, starting transfers between devices: 0.58 us -> 0.24 us  [to_mate(): return lax.ppermute(value, 'tile', pairs)]
  transfers between devices with their start and end apart: 9 -> 9, of which waited for: 3 -> 4; matrix products, arithmetic and copies ran while one was open for 0% -> 0% of each run, Pallas kernels for 21% -> 19%
where the time goes in v7:
time: 32.8 us; the launch traced here: 32.6 us
  starting transfers between devices  13.8 us (42%)
  Pallas kernels  9.47 us (29%)
  waiting for transfers between devices  8.48 us (26%)
  other arithmetic  0.75 us (2%)
    ppermute x2, starting transfers between devices, to_near(): lax.ppermute(value, 'tile', [(a, b) for a, b in pairs if 0 <= b < count])  6.32 us
    ppermute x3, waiting for transfers between devices, across_sub(): return lax.ppermute(shard, 'sub', [(0, 1), (1, 0)])  4.6 us
    ppermute x3, starting transfers between devices, across_sub(): return lax.ppermute(shard, 'sub', [(0, 1), (1, 0)])  3.88 us
    pallas_call x1, Pallas kernels, prepare(): pl.pallas_call(functools.partial(prepare_kernel, windows), out_shape=[jax...  3.81 us
    ppermute x1, starting transfers between devices, to_far(): lax.ppermute(value, 'tile', [(a, b) for a, b in pairs if 0 <= b < count])  3.31 us
    ppermute x2, waiting for transfers between devices, to_near(): lax.ppermute(value, 'tile', [(a, b) for a, b in pairs if 0 <= b < count])  2.96 us
    pallas_call x1, Pallas kernels, push_away(): pl.pallas_call(functools.partial(push_away_kernel, windows), out_shape=[j...  2.18 us
    pallas_call x1, Pallas kernels, stage(): pl.pallas_call(functools.partial(stage_kernel, windows), out_shape=[jax.S...  1.51 us
  transfers between devices with their start and end apart: 9, of which 4 were waited for; matrix products, arithmetic and copies ran while one was open for 0% of the time, Pallas kernels for 19%

profile of v7, /device:TPU:8, one launch (start us, length us, event | category | flops | bytes accessed | tf_op | source)
XLA Modules:
  0.0 32.6 jit_solution(13006187048529572854)
XLA Ops:
  0.0 0.7 %bitcast_select_fusion.code_ref = s32[8,128]{1,0:T(8,128)S(1)} fusion(s32[128,8]{0,1:T(8,128)} %param.11, s32[128,8]{0,1:T(8,128)} %param.12, s32[128]{0:T(128)} %param.13), kind=kLoop, calls=%fused_computation.2 | loop fusion | flops 4096 | bytes 12800 | tf_op jit(solution)/shard_map/jit(_where)/select_n | solution.py:372
  0.7 0.0 collective-permute-start
  0.7 1.6 %collective-permute-start.1 = (bf16[444,128]{1,0:T(8,128)(2,1)}, bf16[444,128]{1,0:T(8,128)(2,1)S(1)}, u32[]{:S(2)}, u32[]{:S(2)}) collective-permute-start(bf16[444,128]{1,0:T(8,128)(2,1)} %own_ref.1), channel_id=1, source_target_pairs={{0,1},{1,0},{2,3},{3,2},{4,5},{5,4},{6,7},{7,6},{8,9},{9,8},{10,11... | collective-permute-start | bytes 341000 | tf_op jit(solution)/shard_map/ppermute | solution.py:18
  2.3 0.0 collective-permute-done.mate_ref
  2.3 3.1 %collective-permute-start.2 = (s32[16,128]{1,0:T(8,128)S(1)}, s32[16,128]{1,0:T(8,128)S(1)}, u32[]{:S(2)}, u32[]{:S(2)}) collective-permute-start(s32[16,128]{1,0:T(8,128)S(1)} %pad_add_fusion), channel_id=1, source_target_pairs={{2,4},{4,2},{6,8},{8,6},{10,12},{12,10},{14,16},{16,14},{18,20},{2... | collective-permute-start | bytes 24584 | tf_op jit(solution)/shard_map/ppermute | solution.py:30
  5.4 1.5 %stage.1 = (bf16[444,888]{1,0:T(8,128)(2,1)S(1)}, f32[444,128]{1,0:T(8,128)S(1)}) custom-call(bf16[444,888]{1,0:T(8,128)(2,1)} %matrix_ref.2, bf16[444,128]{1,0:T(8,128)(2,1)} %own_ref.1), custom_call_target="tpu_custom_call" | custom-call | flops 100933632 | bytes 1577088 | tf_op jit(solution)/shard_map/stage/pallas_call | solution.py:80
  6.9 0.0 collective-permute-done.1.other_ref
  6.9 0.3 rest.2.own_ref
  7.2 1.2 %collective-permute-start.4 = (bf16[444,128]{1,0:T(8,128)(2,1)S(1)}, bf16[444,128]{1,0:T(8,128)(2,1)S(1)}, u32[]{:S(2)}, u32[]{:S(2)}) collective-permute-start(bf16[444,128]{1,0:T(8,128)(2,1)S(1)} %rest.2.own_ref), channel_id=1, source_target_pairs={{0,1},{1,0},{2,3},{3,2},{4,5},{5,4},{6,7},{7,6},{8,9},{9,8},{10,11... | collective-permute-start | bytes 341000 | tf_op jit(solution)/shard_map/ppermute | solution.py:18
  8.4 0.0 collective-permute-done.2.near_ref
  8.4 0.2 collective-permute-start.3
  8.5 3.8 %prepare.1 = (bf16[444,8,888]{2,1,0:T(8,128)(2,1)S(1)}, f32[3552,128]{1,0:T(8,128)S(1)}, bf16[1024,256]{1,0:T(8,128)(2,1)S(1)}, bf16[1024,256]{1,0:T(8,128)(2,1)S(1)}) custom-call(bf16[444,8,888]{2,1,0:T(8,128)(2,1)} %bitcast.3, bf16[444,128]{1,0:T(8,128)(2,1)S(1)} %rest.2.own_ref, s32[8,128]{1,0:T(8,128)S(1)} %bitcast_select_fusion.code_ref, ...), custom_call_target="tpu_custom_call" | custom-call | flops 4294967296 | tf_op jit(solution)/shard_map/prepare/pallas_call | solution.py:248
  12.4 0.0 copy-start
  12.4 0.0 collective-permute-done.3.code_ref
  12.4 0.4 %collective-permute-done.4.other_ref = bf16[444,128]{1,0:T(8,128)(2,1)S(1)} collective-permute-done((bf16[444,128]{1,0:T(8,128)(2,1)S(1)}, bf16[444,128]{1,0:T(8,128)(2,1)S(1)}, u32[]{:S(2)}, u32[]{:S(2)}) %collective-permute-start.4) | collective-permute-done | bytes 113696 | tf_op jit(solution)/shard_map/ppermute | solution.py:18
  12.8 2.2 %push_away.1 = (bf16[444,1024]{1,0:T(8,128)(2,1)S(1)}, bf16[444,256]{1,0:T(8,128)(2,1)S(1)}, bf16[444,128]{1,0:T(8,128)(2,1)S(1)}) custom-call(bf16[444,8,888]{2,1,0:T(8,128)(2,1)S(1)} %get-tuple-element.26.held_ref, f32[3552,128]{1,0:T(8,128)S(1)} %get-tuple-element.28.product_ref, bf16[444,128]{1,0:T(8,128)(2,1)S(1)} %collective-permute-done.4.other_ref, ...), custom_call_target="tpu_custom_call" | custom-call | flops 814743552 | bytes 6308352 | tf_op jit(solution)/shard_map/push_away/pallas_call | solution.py:315
  15.0 0.1 collective-permute-start.5
  15.0 3.3 %collective-permute-start.6 = (bf16[444,128]{1,0:T(8,128)(2,1)S(1)}, bf16[444,128]{1,0:T(8,128)(2,1)S(1)}, u32[]{:S(2)}, u32[]{:S(2)}) collective-permute-start(bf16[444,128]{1,0:T(8,128)(2,1)S(1)} %get-tuple-element.35), channel_id=1, source_target_pairs={{2,6},{4,0},{6,10},{8,4},{10,14},{12,8},{14,18},{16,12},{18,22},{2... | collective-permute-start | bytes 341000 | tf_op jit(solution)/shard_map/ppermute | solution.py:36
  18.4 0.0 collective-permute-done.5.came_ref
  18.4 0.4 %push_home.1 = (f32[444,128]{1,0:T(8,128)S(1)}, bf16[444,128]{1,0:T(8,128)(2,1)S(1)}) custom-call(bf16[444,1024]{1,0:T(8,128)(2,1)S(1)} %get-tuple-element.31.terms_ref, bf16[1024,256]{1,0:T(8,128)(2,1)S(1)} %get-tuple-element.32.select_ref, bf16[444,256]{1,0:T(8,128)(2,1)S(1)} %collective-permute-done.5.came_ref), custom_call_target="tpu_custom_call" | custom-call | flops 232783872 | bytes 1818624 | tf_op jit(solution)/shard_map/push_home/pallas_call | solution.py:350
  18.8 3.2 %collective-permute-start.7 = (bf16[444,128]{1,0:T(8,128)(2,1)S(1)}, bf16[444,128]{1,0:T(8,128)(2,1)S(1)}, u32[]{:S(2)}, u32[]{:S(2)}) collective-permute-start(bf16[444,128]{1,0:T(8,128)(2,1)S(1)} %get-tuple-element.36), channel_id=1, source_target_pairs={{2,4},{4,2},{6,8},{8,6},{10,12},{12,10},{14,16},{16,14},{18,20},{2... | collective-permute-start | bytes 341000 | tf_op jit(solution)/shard_map/ppermute | solution.py:30
  22.0 0.9 %collective-permute-done.6 = bf16[444,128]{1,0:T(8,128)(2,1)S(1)} collective-permute-done((bf16[444,128]{1,0:T(8,128)(2,1)S(1)}, bf16[444,128]{1,0:T(8,128)(2,1)S(1)}, u32[]{:S(2)}, u32[]{:S(2)}) %collective-permute-start.6) | collective-permute-done | bytes 113696 | tf_op jit(solution)/shard_map/ppermute | solution.py:36
  23.0 3.0 %collective-permute-done.7 = bf16[444,128]{1,0:T(8,128)(2,1)S(1)} collective-permute-done((bf16[444,128]{1,0:T(8,128)(2,1)S(1)}, bf16[444,128]{1,0:T(8,128)(2,1)S(1)}, u32[]{:S(2)}, u32[]{:S(2)}) %collective-permute-start.7) | collective-permute-done | bytes 113696 | tf_op jit(solution)/shard_map/ppermute | solution.py:30
  26.0 1.2 %collective-permute-start.8 = (bf16[444,128]{1,0:T(8,128)(2,1)S(1)}, bf16[444,128]{1,0:T(8,128)(2,1)S(1)}, u32[]{:S(2)}, u32[]{:S(2)}) collective-permute-start(bf16[444,128]{1,0:T(8,128)(2,1)S(1)} %add_convert_fusion.own_ref), channel_id=1, source_target_pairs={{0,1},{1,0},{2,3},{3,2},{4,5},{5,4},{6,7},{7,6},{8,9},{9,8},{10,11... | collective-permute-start | bytes 341000 | tf_op jit(solution)/shard_map/ppermute | solution.py:18
  27.1 0.0 copy-done
  27.1 0.3 first.1.part_ref
  27.4 4.2 %collective-permute-done.8.other_ref = bf16[444,128]{1,0:T(8,128)(2,1)S(1)} collective-permute-done((bf16[444,128]{1,0:T(8,128)(2,1)S(1)}, bf16[444,128]{1,0:T(8,128)(2,1)S(1)}, u32[]{:S(2)}, u32[]{:S(2)}) %collective-permute-start.8) | collective-permute-done | bytes 113696 | tf_op jit(solution)/shard_map/ppermute | solution.py:18
  31.6 1.0 %rest.3 = bf16[444,128]{1,0:T(8,128)(2,1)} custom-call(bf16[444,888]{1,0:T(8,128)(2,1)S(1)} %copy-done, f32[444,128]{1,0:T(8,128)S(1)} %first.1.part_ref, bf16[444,128]{1,0:T(8,128)(2,1)S(1)} %collective-permute-done.8.other_ref), custom_call_target="tpu_custom_call" | custom-call | flops 58195968 | bytes 454656 | tf_op jit(solution)/shard_map/rest/pallas_call | solution.py:148
  (3 shorter events, 0.0 us)
Async XLA Ops:
  0.7 1.6 %collective-permute-start = (s32[8,128]{1,0:T(8,128)S(1)}, s32[8,128]{1,0:T(8,128)S(1)}, u32[]{:S(2)}, u32[]{:S(2)}) collective-permute-start(s32[8,128]{1,0:T(8,128)S(1)} %bitcast_select_fusion.code_ref), channel_id=1, source_target_pairs={{0,2},{2,0},{4,6},{6,4},{8,10},{10,8},{12,14},{14,12},{16,18},{18,... | collective-permute-start | bytes 12296 | tf_op jit(solution)/shard_map/ppermute | solution.py:24
  0.7 6.2 %collective-permute-start.1 = (bf16[444,128]{1,0:T(8,128)(2,1)}, bf16[444,128]{1,0:T(8,128)(2,1)S(1)}, u32[]{:S(2)}, u32[]{:S(2)}) collective-permute-start(bf16[444,128]{1,0:T(8,128)(2,1)} %own_ref.1), channel_id=1, source_target_pairs={{0,1},{1,0},{2,3},{3,2},{4,5},{5,4},{6,7},{7,6},{8,9},{9,8},{10,11... | collective-permute-start | bytes 341000 | tf_op jit(solution)/shard_map/ppermute | solution.py:18
  2.3 6.1 %collective-permute-start.2 = (s32[16,128]{1,0:T(8,128)S(1)}, s32[16,128]{1,0:T(8,128)S(1)}, u32[]{:S(2)}, u32[]{:S(2)}) collective-permute-start(s32[16,128]{1,0:T(8,128)S(1)} %pad_add_fusion), channel_id=1, source_target_pairs={{2,4},{4,2},{6,8},{8,6},{10,12},{12,10},{14,16},{16,14},{18,20},{2... | collective-permute-start | bytes 24584 | tf_op jit(solution)/shard_map/ppermute | solution.py:30
  7.2 5.6 %collective-permute-start.4 = (bf16[444,128]{1,0:T(8,128)(2,1)S(1)}, bf16[444,128]{1,0:T(8,128)(2,1)S(1)}, u32[]{:S(2)}, u32[]{:S(2)}) collective-permute-start(bf16[444,128]{1,0:T(8,128)(2,1)S(1)} %rest.2.own_ref), channel_id=1, source_target_pairs={{0,1},{1,0},{2,3},{3,2},{4,5},{5,4},{6,7},{7,6},{8,9},{9,8},{10,11... | collective-permute-start | bytes 341000 | tf_op jit(solution)/shard_map/ppermute | solution.py:18
  8.4 4.0 %collective-permute-start.3 = (s32[8,128]{1,0:T(8,128)S(1)}, s32[8,128]{1,0:T(8,128)S(1)}, u32[]{:S(2)}, u32[]{:S(2)}) collective-permute-start(s32[8,128]{1,0:T(8,128)S(1)} %slice.3), channel_id=1, source_target_pairs={{0,2},{2,0},{4,6},{6,4},{8,10},{10,8},{12,14},{14,12},{16,18},{18,... | collective-permute-start | bytes 12296 | tf_op jit(solution)/shard_map/ppermute | solution.py:24
  12.4 14.8 %copy-start = (bf16[444,888]{1,0:T(8,128)(2,1)S(1)}, bf16[444,888]{1,0:T(8,128)(2,1)}, u32[]{:S(2)}) copy-start(bf16[444,888]{1,0:T(8,128)(2,1)} %matrix_ref.4) | copy-start | bytes 2365636
  15.0 3.4 %collective-permute-start.5 = (bf16[444,256]{1,0:T(8,128)(2,1)S(1)}, bf16[444,256]{1,0:T(8,128)(2,1)S(1)}, u32[]{:S(2)}, u32[]{:S(2)}) collective-permute-start(bf16[444,256]{1,0:T(8,128)(2,1)S(1)} %get-tuple-element.33), channel_id=1, source_target_pairs={{0,2},{2,0},{4,6},{6,4},{8,10},{10,8},{12,14},{14,12},{16,18},{18,... | collective-permute-start | bytes 681992 | tf_op jit(solution)/shard_map/ppermute | solution.py:24
  15.0 7.9 %collective-permute-start.6 = (bf16[444,128]{1,0:T(8,128)(2,1)S(1)}, bf16[444,128]{1,0:T(8,128)(2,1)S(1)}, u32[]{:S(2)}, u32[]{:S(2)}) collective-permute-start(bf16[444,128]{1,0:T(8,128)(2,1)S(1)} %get-tuple-element.35), channel_id=1, source_target_pairs={{2,6},{4,0},{6,10},{8,4},{10,14},{12,8},{14,18},{16,12},{18,22},{2... | collective-permute-start | bytes 341000 | tf_op jit(solution)/shard_map/ppermute | solution.py:36
  18.8 7.1 %collective-permute-start.7 = (bf16[444,128]{1,0:T(8,128)(2,1)S(1)}, bf16[444,128]{1,0:T(8,128)(2,1)S(1)}, u32[]{:S(2)}, u32[]{:S(2)}) collective-permute-start(bf16[444,128]{1,0:T(8,128)(2,1)S(1)} %get-tuple-element.36), channel_id=1, source_target_pairs={{2,4},{4,2},{6,8},{8,6},{10,12},{12,10},{14,16},{16,14},{18,20},{2... | collective-permute-start | bytes 341000 | tf_op jit(solution)/shard_map/ppermute | solution.py:30
  26.0 5.7 %collective-permute-start.8 = (bf16[444,128]{1,0:T(8,128)(2,1)S(1)}, bf16[444,128]{1,0:T(8,128)(2,1)S(1)}, u32[]{:S(2)}, u32[]{:S(2)}) collective-permute-start(bf16[444,128]{1,0:T(8,128)(2,1)S(1)} %add_convert_fusion.own_ref), channel_id=1, source_target_pairs={{0,1},{1,0},{2,3},{3,2},{4,5},{5,4},{6,7},{7,6},{8,9},{9,8},{10,11... | collective-permute-start | bytes 341000 | tf_op jit(solution)/shard_map/ppermute | solution.py:18

commit v8 on v7

--- a/solution.py
+++ b/solution.py
@@ -59,43 +59,6 @@
     for i, ref in enumerate(refs):
         rows, cells = ref.shape
         padded[offset : offset + rows, i * cells : (i + 1) * cells] = ref[...].astype(padded.dtype)
-
-
-def stage_kernel(windows, matrix_ref, own_ref, held_ref, part_ref, own_held, padded, sems):
-    copies = [
-        pltpu.make_async_copy(own_ref, own_held, sems.at[0]),
-        pltpu.make_async_copy(matrix_ref, held_ref, sems.at[1]),
-    ]
-    for copy in copies:
-        copy.start()
-    for copy in copies:
-        copy.wait()
-    first_kernel(windows, held_ref, own_held, part_ref, padded)
-
-
-def stage(matrix, own, windows):
-    rows, depth = matrix.shape
-    cells = own.shape[1]
-    span = max(high - low for low, high, _ in windows)
-    return pl.pallas_call(
-        functools.partial(stage_kernel, windows),
-        out_shape=[
-            jax.ShapeDtypeStruct(matrix.shape, matrix.dtype),
-            jax.ShapeDtypeStruct((rows, cells), jnp.float32),
-        ],
-        in_specs=[pl.BlockSpec(memory_space=pltpu.HBM)] * 2,
-        out_specs=[WHOLE] * 2,
-        scratch_shapes=[
-            pltpu.VMEM(own.shape, own.dtype),
-            pltpu.VMEM((span, cells), jnp.float32),
-            pltpu.SemaphoreType.DMA((2,)),
-        ],
-        cost_estimate=pl.CostEstimate(
-            flops=2 * rows * depth * cells, bytes_accessed=4 * matrix.size, transcendentals=0
-        ),
-        compiler_params=pltpu.CompilerParams(vmem_limit_bytes=24 << 20),
-        name="stage",
-    )(*[pltpu.with_memory_space_constraint(x, pltpu.HBM) for x in (matrix, own)])
 
 
 def first_kernel(windows, matrix_ref, own_ref, out_ref, padded):
@@ -177,25 +140,47 @@
             out_ref[row : row + band, column : column + cells] = totals[k]
 
 
+def window_copies(translate_ref, held_ref, sems, low, high):
+    copies = []
+    for i, (start, size) in enumerate(chunks(translate_ref.shape[0], CHUNK)):
+        where = (pl.ds(start, size), slice(None), pl.ds(low, high - low))
+        copies.append(
+            pltpu.make_async_copy(translate_ref.at[where], held_ref.at[where], sems.at[i])
+        )
+    return copies
+
+
+def load_kernel(windows, translate_ref, held_ref, sems):
+    for index, (low, high, _) in enumerate(windows):
+        def run(low=low, high=high):
+            copies = window_copies(translate_ref, held_ref, sems, low, high)
+            for copy in copies:
+                copy.start()
+            for copy in copies:
+                copy.wait()
+        pl.when(lax.axis_index("sub") != index)(run)
+
+
+def load(operators, windows):
+    rows = operators.shape[0]
+    return pl.pallas_call(
+        functools.partial(load_kernel, windows),
+        out_shape=jax.ShapeDtypeStruct(operators.shape, jnp.bfloat16),
+        in_specs=[pl.BlockSpec(memory_space=pltpu.HBM)],
+        out_specs=WHOLE,
+        scratch_shapes=[pltpu.SemaphoreType.DMA((len(chunks(rows, CHUNK)),))],
+        cost_estimate=pl.CostEstimate(flops=1 << 30, bytes_accessed=0, transcendentals=0),
+        compiler_params=pltpu.CompilerParams(vmem_limit_bytes=16 << 20),
+        name="load",
+    )(pltpu.with_memory_space_constraint(operators, pltpu.HBM))
+
+
 def prepare_kernel(
     windows, translate_ref, own_ref, code_ref, mate_ref, near_ref,
-    held_ref, product_ref, home_ref, away_ref, padded, sems,
+    product_ref, home_ref, away_ref, held, padded, sems,
 ):
     rows, classes, _ = translate_ref.shape
     entries, cells = code_ref.shape
-    depth = translate_ref.shape[2]
-    parts = chunks(rows, CHUNK)
-
-    def load(low, high, semaphore):
-        copies = []
-        for i, (start, size) in enumerate(parts):
-            where = (pl.ds(start, size), slice(None), pl.ds(low, high - low))
-            copies.append(
-                pltpu.make_async_copy(
-                    translate_ref.at[where], held_ref.at[where], sems.at[semaphore, i]
-                )
-            )
-        return copies
 
     def on_window(run):
         for index, window in enumerate(windows):
@@ -205,7 +190,7 @@
                 pl.when(lax.axis_index("sub") == index)(functools.partial(run, *window))
 
     def begin(low, high, offset):
-        for copy in load(low, high, 0):
+        for copy in window_copies(translate_ref, held, sems, low, high):
             copy.start()
 
     on_window(begin)
@@ -217,25 +202,16 @@
     build_select(near_ref[entries:, :], (REACH - 2 * step) * cells, away_ref, cells, classes)
 
     def run(low, high, offset):
-        first_copies = load(low, high, 0)
-        other_copies = []
-        for left, right in ((0, low), (high, depth)):
-            if left < right:
-                other_copies += load(left, right, 1)
         pad_into(padded, offset, own_ref)
         equivalent = padded[: high - low, :].astype(jnp.bfloat16)
-        for copy in first_copies:
+        copies = window_copies(translate_ref, held, sems, low, high)
+        for copy, (start, size) in zip(copies, chunks(rows, CHUNK)):
             copy.wait()
-        for copy in other_copies:
-            copy.start()
-        for start, size in parts:
-            matrix = held_ref[start : start + size, :, low:high]
+            matrix = held[start : start + size, :, low:high]
             product_ref[start * classes : (start + size) * classes, :] = jnp.dot(
                 matrix.reshape(size * classes, high - low), equivalent,
                 preferred_element_type=jnp.float32,
             )
-        for copy in other_copies:
-            copy.wait()
 
     on_window(run)
 
@@ -248,16 +224,16 @@
     return pl.pallas_call(
         functools.partial(prepare_kernel, windows),
         out_shape=[
-            jax.ShapeDtypeStruct((rows, classes, depth), jnp.bfloat16),
             jax.ShapeDtypeStruct((rows * classes, cells), jnp.float32),
             select,
             select,
         ],
         in_specs=[pl.BlockSpec(memory_space=pltpu.HBM)] + [WHOLE] * 4,
-        out_specs=[WHOLE] * 4,
+        out_specs=[WHOLE] * 3,
         scratch_shapes=[
+            pltpu.VMEM(operators.shape, jnp.bfloat16),
             pltpu.VMEM((span, cells), jnp.float32),
-            pltpu.SemaphoreType.DMA((2, len(chunks(rows, CHUNK)))),
+            pltpu.SemaphoreType.DMA((len(chunks(rows, CHUNK)),)),
         ],
         cost_estimate=pl.CostEstimate(flops=1 << 32, bytes_accessed=0, transcendentals=0),
         compiler_params=pltpu.CompilerParams(vmem_limit_bytes=32 << 20),
@@ -378,23 +354,26 @@
     if halves:
         windows = half_windows(rows, depth, 2)
         other_check = across_sub(up_check)
-        staged, mate_code = lax.optimization_barrier((up_inverse, mate_code))
-        up_held, part = stage(staged, up_check, windows)
-        equivalent = rest(up_held, part, other_check, windows)
-        other = across_sub(equivalent)
+        check = jnp.where(
+            lax.axis_index("sub") == 0,
+            jnp.concatenate([up_check, other_check], axis=0),
+            jnp.concatenate([other_check, up_check], axis=0),
+        )
+        check = lax.optimization_barrier((check, mate_code))[0]
     else:
         windows = [(0, depth, 0)]
-        equivalent = lax.all_gather(
-            jnp.dot(
-                up_inverse, lax.all_gather(up_check, "sub", axis=0, tiled=True),
-                preferred_element_type=jnp.float32,
-            ).astype(jnp.bfloat16),
-            "sub", axis=0, tiled=True,
-        )
-        other = equivalent
-    near_codes, _ = lax.optimization_barrier((near_codes, equivalent))
+        check = lax.all_gather(up_check, "sub", axis=0, tiled=True)
+    equivalent = jnp.dot(up_inverse, check, preferred_element_type=jnp.float32)
+    equivalent = equivalent.astype(jnp.bfloat16)
+    if halves:
+        other = across_sub(equivalent)
+        held = load(lax.optimization_barrier((operators, equivalent))[0], windows)
+    else:
+        equivalent = lax.all_gather(equivalent, "sub", axis=0, tiled=True)
+        other, held = equivalent, operators
+    near_codes, _, _ = lax.optimization_barrier((near_codes, equivalent, held))
     mate_near_code = to_mate(near_codes[:entries])
-    held, product, home, away_select = prepare(
+    product, home, away_select = prepare(
         operators, equivalent, code, mate_code, near_codes, windows
     )
     mate_near_code, product = lax.optimization_barrier((mate_near_code, product))

time: 32.8 us -> 35.5 us (1.082)
  waiting for transfers between devices: 8.48 us -> 9.78 us
  other arithmetic: 0.75 us -> 1.89 us
  matrix products: 0 us -> 0.38 us
    select_n x0 -> x1, other arithmetic: none -> 1.07 us  [shards(): jnp.where(lax.axis_index('sub') == 0, jnp.concatenate([up_check, other_ch...]
    ppermute x3, waiting for transfers between devices: 4.6 us -> 5.44 us  [across_sub(): return lax.ppermute(shard, 'sub', [(0, 1), (1, 0)])]
    pallas_call x1, Pallas kernels: 1.51 us -> 2.04 us  [load(): pl.pallas_call(functools.partial(load_kernel, windows), out_shape=jax.Sha...]
    ppermute x2, starting transfers between devices: 6.32 us -> 5.85 us  [to_near(): lax.ppermute(value, 'tile', [(a, b) for a, b in pairs if 0 <= b < count])]
    ppermute x1, waiting for transfers between devices: 0.91 us -> 1.33 us  [to_far(): lax.ppermute(value, 'tile', [(a, b) for a, b in pairs if 0 <= b < count])]
    ppermute x3, starting transfers between devices: 0.24 us -> 0.63 us  [to_mate(): return lax.ppermute(value, 'tile', pairs)]
    dot_general x0 -> x1, matrix products: none -> 0.38 us  [shards(): equivalent = jnp.dot(up_inverse, check, preferred_element_type=jnp.float32)]
    pallas_call x2 -> x1, Pallas kernels: 1.27 us -> 0.95 us  [rest(): pl.pallas_call(functools.partial(rest_kernel, windows), out_shape=jax.Sha...]
  transfers between devices with their start and end apart: 9 -> 9, of which waited for: 4 -> 4; matrix products, arithmetic and copies ran while one was open for 0% -> 4% of each run, Pallas kernels for 19% -> 18%
where the time goes in v8:
time: 35.5 us; the launch traced here: 35.3 us
  starting transfers between devices  13.5 us (38%)
  waiting for transfers between devices  9.78 us (28%)
  Pallas kernels  9.56 us (27%)
  other arithmetic  1.89 us (5%)
  matrix products  0.38 us (1%)
    ppermute x2, starting transfers between devices, to_near(): lax.ppermute(value, 'tile', [(a, b) for a, b in pairs if 0 <= b < count])  5.85 us
    ppermute x3, waiting for transfers between devices, across_sub(): return lax.ppermute(shard, 'sub', [(0, 1), (1, 0)])  5.44 us
    ppermute x3, starting transfers between devices, across_sub(): return lax.ppermute(shard, 'sub', [(0, 1), (1, 0)])  3.7 us
    pallas_call x1, Pallas kernels, prepare(): pl.pallas_call(functools.partial(prepare_kernel, windows), out_shape=[jax...  3.69 us
    ppermute x1, starting transfers between devices, to_far(): lax.ppermute(value, 'tile', [(a, b) for a, b in pairs if 0 <= b < count])  3.31 us
    ppermute x2, waiting for transfers between devices, to_near(): lax.ppermute(value, 'tile', [(a, b) for a, b in pairs if 0 <= b < count])  3 us
    pallas_call x1, Pallas kernels, push_away(): pl.pallas_call(functools.partial(push_away_kernel, windows), out_shape=[j...  2.18 us
    pallas_call x1, Pallas kernels, load(): pl.pallas_call(functools.partial(load_kernel, windows), out_shape=jax.Sha...  2.04 us
  transfers between devices with their start and end apart: 9, of which 4 were waited for; matrix products, arithmetic and copies ran while one was open for 4% of the time, Pallas kernels for 18%

profile of v8, /device:TPU:8, one launch (start us, length us, event | category | flops | bytes accessed | tf_op | source)
XLA Modules:
  0.0 35.3 jit_solution(156977654717766879)
XLA Ops:
  0.0 0.0 copy-start
  0.0 0.8 %bitcast_select_fusion.code_ref = s32[8,128]{1,0:T(8,128)S(1)} fusion(s32[128,8]{0,1:T(8,128)} %param.11, s32[128,8]{0,1:T(8,128)} %param.12, s32[128]{0:T(128)} %param.13), kind=kLoop, calls=%fused_computation.5 | loop fusion | flops 4096 | bytes 12800 | tf_op jit(solution)/shard_map/jit(_where)/select_n | solution.py:348
  0.8 0.0 collective-permute-start.1
  0.8 1.6 %collective-permute-start = (bf16[444,128]{1,0:T(8,128)(2,1)}, bf16[444,128]{1,0:T(8,128)(2,1)S(1)}, u32[]{:S(2)}, u32[]{:S(2)}) collective-permute-start(bf16[444,128]{1,0:T(8,128)(2,1)} %param.7), channel_id=1, source_target_pairs={{0,1},{1,0},{2,3},{3,2},{4,5},{5,4},{6,7},{7,6},{8,9},{9,8},{10,11... | collective-permute-start | bytes 341000 | tf_op jit(solution)/shard_map/ppermute | solution.py:18
  2.3 0.0 collective-permute-done.1.mate_ref
  2.3 3.1 %collective-permute-start.2 = (s32[16,128]{1,0:T(8,128)S(1)}, s32[16,128]{1,0:T(8,128)S(1)}, u32[]{:S(2)}, u32[]{:S(2)}) collective-permute-start(s32[16,128]{1,0:T(8,128)S(1)} %pad_add_fusion), channel_id=1, source_target_pairs={{2,4},{4,2},{6,8},{8,6},{10,12},{12,10},{14,16},{16,14},{18,20},{2... | collective-permute-start | bytes 24584 | tf_op jit(solution)/shard_map/ppermute | solution.py:30
  5.4 1.1 %collective-permute-done = bf16[444,128]{1,0:T(8,128)(2,1)S(1)} collective-permute-done((bf16[444,128]{1,0:T(8,128)(2,1)}, bf16[444,128]{1,0:T(8,128)(2,1)S(1)}, u32[]{:S(2)}, u32[]{:S(2)}) %collective-permute-start) | collective-permute-done | bytes 113696 | tf_op jit(solution)/shard_map/ppermute | solution.py:18
  6.6 1.1 %maximum_select_fusion = bf16[888,128]{1,0:T(8,128)(2,1)S(1)} fusion(bf16[444,128]{1,0:T(8,128)(2,1)S(1)} %collective-permute-done, bf16[444,128]{1,0:T(8,128)(2,1)} %param.7, pred[]{:T(512)S(6)} %eq.3), kind=kLoop, calls=%fused_computation.3 | loop fusion | flops 1022976 | bytes 454657 | tf_op jit(solution)/shard_map/jit(_where)/select_n | solution.py:357
  7.6 0.0 copy-done
  7.6 0.4 %fusion.own_ref = bf16[444,128]{1,0:T(8,128)(2,1)S(1)} fusion(bf16[888,128]{1,0:T(8,128)(2,1)S(1)} %maximum_select_fusion, bf16[444,888]{1,0:T(8,128)(2,1)S(1)} %copy-done), kind=kOutput, calls=%fused_computation.1 | convolution fusion | flops 100990464 | bytes 1129536 | tf_op jit(solution)/shard_map/dot_general | solution.py:366
  8.0 1.6 %collective-permute-start.4 = (bf16[444,128]{1,0:T(8,128)(2,1)S(1)}, bf16[444,128]{1,0:T(8,128)(2,1)S(1)}, u32[]{:S(2)}, u32[]{:S(2)}) collective-permute-start(bf16[444,128]{1,0:T(8,128)(2,1)S(1)} %fusion.own_ref), channel_id=1, source_target_pairs={{0,1},{1,0},{2,3},{3,2},{4,5},{5,4},{6,7},{7,6},{8,9},{9,8},{10,11... | collective-permute-start | bytes 341000 | tf_op jit(solution)/shard_map/ppermute | solution.py:18
  9.6 2.0 %load.1.held_ref = bf16[444,8,888]{2,1,0:T(8,128)(2,1)S(1)} custom-call(bf16[444,8,888]{2,1,0:T(8,128)(2,1)} %bitcast.7), custom_call_target="tpu_custom_call" | custom-call | flops 1073741824 | tf_op jit(solution)/shard_map/load/pallas_call | solution.py:166
  11.6 0.0 collective-permute-done.2.near_ref
  11.6 0.1 collective-permute-start.3
  11.7 3.7 %prepare.1 = (f32[3552,128]{1,0:T(8,128)S(1)}, bf16[1024,256]{1,0:T(8,128)(2,1)S(1)}, bf16[1024,256]{1,0:T(8,128)(2,1)S(1)}) custom-call(bf16[444,8,888]{2,1,0:T(8,128)(2,1)} %bitcast.8, bf16[444,128]{1,0:T(8,128)(2,1)S(1)} %fusion.own_ref, s32[8,128]{1,0:T(8,128)S(1)} %bitcast_select_fusion.code_ref, s32[8,128]{1,0:T(8,128)S(1)} %collective-permute-done.1.mate_ref, ...), custom_call_target="tpu_custom_call" | custom-call | flops 4294967296 | tf_op jit(solution)/shard_map/prepare/pallas_call | solution.py:224
  15.4 0.0 copy-start.1
  15.4 0.0 collective-permute-done.3.code_ref
  15.4 0.0 collective-permute-done.4.other_ref
  15.5 2.2 %push_away.1 = (bf16[444,1024]{1,0:T(8,128)(2,1)S(1)}, bf16[444,256]{1,0:T(8,128)(2,1)S(1)}, bf16[444,128]{1,0:T(8,128)(2,1)S(1)}) custom-call(bf16[444,8,888]{2,1,0:T(8,128)(2,1)S(1)} %load.1.held_ref, f32[3552,128]{1,0:T(8,128)S(1)} %get-tuple-element.22.product_ref, bf16[444,128]{1,0:T(8,128)(2,1)S(1)} %collective-permute-done.4.other_ref, ...), custom_call_target="tpu_custom_call" | custom-call | flops 814743552 | bytes 6308352 | tf_op jit(solution)/shard_map/push_away/pallas_call | solution.py:291
  17.6 0.6 %collective-permute-start.5 = (bf16[444,256]{1,0:T(8,128)(2,1)S(1)}, bf16[444,256]{1,0:T(8,128)(2,1)S(1)}, u32[]{:S(2)}, u32[]{:S(2)}) collective-permute-start(bf16[444,256]{1,0:T(8,128)(2,1)S(1)} %get-tuple-element.27), channel_id=1, source_target_pairs={{0,2},{2,0},{4,6},{6,4},{8,10},{10,8},{12,14},{14,12},{16,18},{18,... | collective-permute-start | bytes 681992 | tf_op jit(solution)/shard_map/ppermute | solution.py:24
  18.2 3.3 %collective-permute-start.6 = (bf16[444,128]{1,0:T(8,128)(2,1)S(1)}, bf16[444,128]{1,0:T(8,128)(2,1)S(1)}, u32[]{:S(2)}, u32[]{:S(2)}) collective-permute-start(bf16[444,128]{1,0:T(8,128)(2,1)S(1)} %get-tuple-element.29), channel_id=1, source_target_pairs={{2,6},{4,0},{6,10},{8,4},{10,14},{12,8},{14,18},{16,12},{18,22},{2... | collective-permute-start | bytes 341000 | tf_op jit(solution)/shard_map/ppermute | solution.py:36
  21.5 0.0 collective-permute-done.5.came_ref
  21.5 0.4 %push_home.1 = (f32[444,128]{1,0:T(8,128)S(1)}, bf16[444,128]{1,0:T(8,128)(2,1)S(1)}) custom-call(bf16[444,1024]{1,0:T(8,128)(2,1)S(1)} %get-tuple-element.25.terms_ref, bf16[1024,256]{1,0:T(8,128)(2,1)S(1)} %get-tuple-element.26.select_ref, bf16[444,256]{1,0:T(8,128)(2,1)S(1)} %collective-permute-done.5.came_ref), custom_call_target="tpu_custom_call" | custom-call | flops 232783872 | bytes 1818624 | tf_op jit(solution)/shard_map/push_home/pallas_call | solution.py:326
  21.9 2.8 %collective-permute-start.7 = (bf16[444,128]{1,0:T(8,128)(2,1)S(1)}, bf16[444,128]{1,0:T(8,128)(2,1)S(1)}, u32[]{:S(2)}, u32[]{:S(2)}) collective-permute-start(bf16[444,128]{1,0:T(8,128)(2,1)S(1)} %get-tuple-element.30), channel_id=1, source_target_pairs={{2,4},{4,2},{6,8},{8,6},{10,12},{12,10},{14,16},{16,14},{18,20},{2... | collective-permute-start | bytes 341000 | tf_op jit(solution)/shard_map/ppermute | solution.py:30
  24.7 1.3 %collective-permute-done.6 = bf16[444,128]{1,0:T(8,128)(2,1)S(1)} collective-permute-done((bf16[444,128]{1,0:T(8,128)(2,1)S(1)}, bf16[444,128]{1,0:T(8,128)(2,1)S(1)}, u32[]{:S(2)}, u32[]{:S(2)}) %collective-permute-start.6) | collective-permute-done | bytes 113696 | tf_op jit(solution)/shard_map/ppermute | solution.py:36
  26.1 3.0 %collective-permute-done.7 = bf16[444,128]{1,0:T(8,128)(2,1)S(1)} collective-permute-done((bf16[444,128]{1,0:T(8,128)(2,1)S(1)}, bf16[444,128]{1,0:T(8,128)(2,1)S(1)}, u32[]{:S(2)}, u32[]{:S(2)}) %collective-permute-start.7) | collective-permute-done | bytes 113696 | tf_op jit(solution)/shard_map/ppermute | solution.py:30
  29.1 0.6 %collective-permute-start.8 = (bf16[444,128]{1,0:T(8,128)(2,1)S(1)}, bf16[444,128]{1,0:T(8,128)(2,1)S(1)}, u32[]{:S(2)}, u32[]{:S(2)}) collective-permute-start(bf16[444,128]{1,0:T(8,128)(2,1)S(1)} %add_convert_fusion.own_ref), channel_id=1, source_target_pairs={{0,1},{1,0},{2,3},{3,2},{4,5},{5,4},{6,7},{7,6},{8,9},{9,8},{10,11... | collective-permute-start | bytes 341000 | tf_op jit(solution)/shard_map/ppermute | solution.py:18
  29.7 0.0 copy-done.1
  29.7 0.3 first.1.part_ref
  30.0 4.3 %collective-permute-done.8.other_ref = bf16[444,128]{1,0:T(8,128)(2,1)S(1)} collective-permute-done((bf16[444,128]{1,0:T(8,128)(2,1)S(1)}, bf16[444,128]{1,0:T(8,128)(2,1)S(1)}, u32[]{:S(2)}, u32[]{:S(2)}) %collective-permute-start.8) | collective-permute-done | bytes 113696 | tf_op jit(solution)/shard_map/ppermute | solution.py:18
  34.3 1.0 %rest.1 = bf16[444,128]{1,0:T(8,128)(2,1)} custom-call(bf16[444,888]{1,0:T(8,128)(2,1)S(1)} %copy-done.1, f32[444,128]{1,0:T(8,128)S(1)} %first.1.part_ref, bf16[444,128]{1,0:T(8,128)(2,1)S(1)} %collective-permute-done.8.other_ref), custom_call_target="tpu_custom_call" | custom-call | flops 58195968 | bytes 454656 | tf_op jit(solution)/shard_map/rest/pallas_call | solution.py:111
  (3 shorter events, 0.0 us)
Async XLA Ops:
  0.0 7.6 %copy-start = (bf16[444,888]{1,0:T(8,128)(2,1)S(1)}, bf16[444,888]{1,0:T(8,128)(2,1)}, u32[]{:S(2)}) copy-start(bf16[444,888]{1,0:T(8,128)(2,1)} %param.8) | copy-start | bytes 2365636
  0.8 1.6 %collective-permute-start.1 = (s32[8,128]{1,0:T(8,128)S(1)}, s32[8,128]{1,0:T(8,128)S(1)}, u32[]{:S(2)}, u32[]{:S(2)}) collective-permute-start(s32[8,128]{1,0:T(8,128)S(1)} %bitcast_select_fusion.code_ref), channel_id=1, source_target_pairs={{0,2},{2,0},{4,6},{6,4},{8,10},{10,8},{12,14},{14,12},{16,18},{18,... | collective-permute-start | bytes 12296 | tf_op jit(solution)/shard_map/ppermute | solution.py:24
  0.8 5.8 %collective-permute-start = (bf16[444,128]{1,0:T(8,128)(2,1)}, bf16[444,128]{1,0:T(8,128)(2,1)S(1)}, u32[]{:S(2)}, u32[]{:S(2)}) collective-permute-start(bf16[444,128]{1,0:T(8,128)(2,1)} %param.7), channel_id=1, source_target_pairs={{0,1},{1,0},{2,3},{3,2},{4,5},{5,4},{6,7},{7,6},{8,9},{9,8},{10,11... | collective-permute-start | bytes 341000 | tf_op jit(solution)/shard_map/ppermute | solution.py:18
  2.3 9.3 %collective-permute-start.2 = (s32[16,128]{1,0:T(8,128)S(1)}, s32[16,128]{1,0:T(8,128)S(1)}, u32[]{:S(2)}, u32[]{:S(2)}) collective-permute-start(s32[16,128]{1,0:T(8,128)S(1)} %pad_add_fusion), channel_id=1, source_target_pairs={{2,4},{4,2},{6,8},{8,6},{10,12},{12,10},{14,16},{16,14},{18,20},{2... | collective-permute-start | bytes 24584 | tf_op jit(solution)/shard_map/ppermute | solution.py:30
  8.0 7.4 %collective-permute-start.4 = (bf16[444,128]{1,0:T(8,128)(2,1)S(1)}, bf16[444,128]{1,0:T(8,128)(2,1)S(1)}, u32[]{:S(2)}, u32[]{:S(2)}) collective-permute-start(bf16[444,128]{1,0:T(8,128)(2,1)S(1)} %fusion.own_ref), channel_id=1, source_target_pairs={{0,1},{1,0},{2,3},{3,2},{4,5},{5,4},{6,7},{7,6},{8,9},{9,8},{10,11... | collective-permute-start | bytes 341000 | tf_op jit(solution)/shard_map/ppermute | solution.py:18
  11.6 3.8 %collective-permute-start.3 = (s32[8,128]{1,0:T(8,128)S(1)}, s32[8,128]{1,0:T(8,128)S(1)}, u32[]{:S(2)}, u32[]{:S(2)}) collective-permute-start(s32[8,128]{1,0:T(8,128)S(1)} %slice.3), channel_id=1, source_target_pairs={{0,2},{2,0},{4,6},{6,4},{8,10},{10,8},{12,14},{14,12},{16,18},{18,... | collective-permute-start | bytes 12296 | tf_op jit(solution)/shard_map/ppermute | solution.py:24
  15.4 14.3 %copy-start.1 = (bf16[444,888]{1,0:T(8,128)(2,1)S(1)}, bf16[444,888]{1,0:T(8,128)(2,1)}, u32[]{:S(2)}) copy-start(bf16[444,888]{1,0:T(8,128)(2,1)} %matrix_ref.3) | copy-start | bytes 2365636
  17.6 3.9 %collective-permute-start.5 = (bf16[444,256]{1,0:T(8,128)(2,1)S(1)}, bf16[444,256]{1,0:T(8,128)(2,1)S(1)}, u32[]{:S(2)}, u32[]{:S(2)}) collective-permute-start(bf16[444,256]{1,0:T(8,128)(2,1)S(1)} %get-tuple-element.27), channel_id=1, source_target_pairs={{0,2},{2,0},{4,6},{6,4},{8,10},{10,8},{12,14},{14,12},{16,18},{18,... | collective-permute-start | bytes 681992 | tf_op jit(solution)/shard_map/ppermute | solution.py:24
  18.2 7.9 %collective-permute-start.6 = (bf16[444,128]{1,0:T(8,128)(2,1)S(1)}, bf16[444,128]{1,0:T(8,128)(2,1)S(1)}, u32[]{:S(2)}, u32[]{:S(2)}) collective-permute-start(bf16[444,128]{1,0:T(8,128)(2,1)S(1)} %get-tuple-element.29), channel_id=1, source_target_pairs={{2,6},{4,0},{6,10},{8,4},{10,14},{12,8},{14,18},{16,12},{18,22},{2... | collective-permute-start | bytes 341000 | tf_op jit(solution)/shard_map/ppermute | solution.py:36
  21.9 7.1 %collective-permute-start.7 = (bf16[444,128]{1,0:T(8,128)(2,1)S(1)}, bf16[444,128]{1,0:T(8,128)(2,1)S(1)}, u32[]{:S(2)}, u32[]{:S(2)}) collective-permute-start(bf16[444,128]{1,0:T(8,128)(2,1)S(1)} %get-tuple-element.30), channel_id=1, source_target_pairs={{2,4},{4,2},{6,8},{8,6},{10,12},{12,10},{14,16},{16,14},{18,20},{2... | collective-permute-start | bytes 341000 | tf_op jit(solution)/shard_map/ppermute | solution.py:30
  29.1 5.2 %collective-permute-start.8 = (bf16[444,128]{1,0:T(8,128)(2,1)S(1)}, bf16[444,128]{1,0:T(8,128)(2,1)S(1)}, u32[]{:S(2)}, u32[]{:S(2)}) collective-permute-start(bf16[444,128]{1,0:T(8,128)(2,1)S(1)} %add_convert_fusion.own_ref), channel_id=1, source_target_pairs={{0,1},{1,0},{2,3},{3,2},{4,5},{5,4},{6,7},{7,6},{8,9},{9,8},{10,11... | collective-permute-start | bytes 341000 | tf_op jit(solution)/shard_map/ppermute | solution.py:18

commit v9 on v5

--- a/solution.py
+++ b/solution.py
@@ -11,7 +11,6 @@
 CLASS_SHIFT = 10
 CHUNK = 112
 LANES = 128
-PREPARE = 1 << 32
 WHOLE = pl.BlockSpec(memory_space=pltpu.VMEM)
 
 
@@ -51,8 +50,8 @@
     return windows
 
 
-def chunks(rows):
-    return [(start, min(CHUNK, rows - start)) for start in range(0, rows, CHUNK)]
+def chunks(rows, size):
+    return [(start, min(size, rows - start)) for start in range(0, rows, size)]
 
 
 def pad_into(padded, offset, *refs):
@@ -60,6 +59,68 @@
     for i, ref in enumerate(refs):
         rows, cells = ref.shape
         padded[offset : offset + rows, i * cells : (i + 1) * cells] = ref[...].astype(padded.dtype)
+
+
+def code_kernel(slot_ref, class_ref, count_ref, code_ref, slots, classes, counts, sems):
+    copies = [
+        pltpu.make_async_copy(source, target, sems.at[i])
+        for i, (source, target) in enumerate(
+            ((slot_ref, slots), (class_ref, classes), (count_ref, counts))
+        )
+    ]
+    for copy in copies:
+        copy.start()
+    for copy in copies:
+        copy.wait()
+    entry = lax.broadcasted_iota(jnp.int32, code_ref.shape, 0)
+    code_ref[...] = jnp.where(
+        entry < counts[...], (classes[...] << CLASS_SHIFT) + slots[...], -1
+    )
+
+
+def coded(list_slot, list_class, list_count):
+    operands = (list_slot.T, list_class.T, list_count[None, :])
+    return pl.pallas_call(
+        code_kernel,
+        out_shape=jax.ShapeDtypeStruct(operands[0].shape, jnp.int32),
+        in_specs=[pl.BlockSpec(memory_space=pltpu.HBM)] * 3,
+        out_specs=WHOLE,
+        scratch_shapes=[pltpu.VMEM(x.shape, x.dtype) for x in operands]
+        + [pltpu.SemaphoreType.DMA((3,))],
+        cost_estimate=pl.CostEstimate(flops=1 << 33, bytes_accessed=0, transcendentals=0),
+        compiler_params=pltpu.CompilerParams(vmem_limit_bytes=4 << 20),
+        name="code",
+    )(*[pltpu.with_memory_space_constraint(x, pltpu.HBM) for x in operands])
+
+
+def joined_kernel(matrix_ref, own_ref, other_ref, out_ref, joined):
+    rows = own_ref.shape[0]
+    halves = [slice(0, rows), slice(rows, 2 * rows)]
+    for index in range(2):
+        def place(index=index):
+            joined[halves[index], :] = own_ref[...].astype(jnp.float32)
+            joined[halves[1 - index], :] = other_ref[...].astype(jnp.float32)
+        pl.when(lax.axis_index("sub") == index)(place)
+    out_ref[...] = jnp.dot(
+        matrix_ref[...], joined[...].astype(jnp.bfloat16), preferred_element_type=jnp.float32
+    ).astype(jnp.bfloat16)
+
+
+def joined_product(matrix, own, other):
+    rows, depth = matrix.shape
+    cells = own.shape[1]
+    return pl.pallas_call(
+        joined_kernel,
+        out_shape=jax.ShapeDtypeStruct((rows, cells), jnp.bfloat16),
+        in_specs=[WHOLE] * 3,
+        out_specs=WHOLE,
+        scratch_shapes=[pltpu.VMEM((depth, cells), jnp.float32)],
+        cost_estimate=pl.CostEstimate(
+            flops=2 * rows * depth * cells, bytes_accessed=2 * rows * depth, transcendentals=0
+        ),
+        compiler_params=pltpu.CompilerParams(vmem_limit_bytes=8 << 20),
+        name="joined",
+    )(matrix, own, other)
 
 
 def first_kernel(windows, matrix_ref, own_ref, out_ref, padded):
@@ -123,7 +184,7 @@
     )(matrix, part, other)
 
 
-def build_select(code, base, out_ref, classes):
+def build_select(code, base, out_ref, column, classes):
     entries, cells = code.shape
     slots = (code & ((1 << CLASS_SHIFT) - 1)) - base
     kinds = code >> CLASS_SHIFT
@@ -137,32 +198,25 @@
                 used = jnp.where(kinds[entry : entry + 1, :] == k, 1.0, 0.0).astype(jnp.bfloat16)
                 totals[k] = totals[k] + hit * used
         for k in range(classes):
-            out_ref[k * cells + low : k * cells + low + band, :] = totals[k]
+            row = k * cells + low
+            out_ref[row : row + band, column : column + cells] = totals[k]
 
 
 def prepare_kernel(
-    windows, translate_ref, own_ref, code_ref, mate_ref,
-    held_ref, product_ref, home_ref, mate_select_ref, padded, sems,
+    windows, operators_ref, own_ref, code_ref, mate_ref,
+    product_ref, home_ref, mate_select_ref, padded,
 ):
-    rows, classes, _ = translate_ref.shape
+    rows, classes, _ = operators_ref.shape
     cells = code_ref.shape[1]
-    copies = []
-    for i, (start, size) in enumerate(chunks(rows)):
-        part = pl.ds(start, size)
-        copy = pltpu.make_async_copy(translate_ref.at[part], held_ref.at[part], sems.at[i])
-        copy.start()
-        copies.append(copy)
-
-    build_select(code_ref[...], REACH * cells, home_ref, classes)
-    build_select(mate_ref[...], (REACH + away()) * cells, mate_select_ref, classes)
+    build_select(code_ref[...], REACH * cells, home_ref, 0, classes)
+    build_select(mate_ref[...], (REACH + away()) * cells, mate_select_ref, 0, classes)
 
     for index, (low, high, offset) in enumerate(windows):
         def run(low=low, high=high, offset=offset):
             pad_into(padded, offset, own_ref)
             right = padded[: high - low, :].astype(jnp.bfloat16)
-            for copy, (start, size) in zip(copies, chunks(rows)):
-                copy.wait()
-                left = held_ref[start : start + size, :, low:high]
+            for start, size in chunks(rows, CHUNK):
+                left = operators_ref[start : start + size, :, low:high]
                 product_ref[start * classes : (start + size) * classes, :] = jnp.dot(
                     left.reshape(size * classes, high - low), right,
                     preferred_element_type=jnp.float32,
@@ -181,29 +235,23 @@
     return pl.pallas_call(
         functools.partial(prepare_kernel, windows),
         out_shape=[
-            jax.ShapeDtypeStruct((rows, classes, depth), jnp.bfloat16),
-            jax.ShapeDtypeStruct((rows * classes, cells), jnp.float32),
-            select,
-            select,
+            jax.ShapeDtypeStruct((rows * classes, cells), jnp.float32), select, select,
         ],
-        in_specs=[pl.BlockSpec(memory_space=pltpu.HBM)] + [WHOLE] * 3,
-        out_specs=[WHOLE] * 4,
-        scratch_shapes=[
-            pltpu.VMEM((span, cells), jnp.float32),
-            pltpu.SemaphoreType.DMA((len(chunks(rows)),)),
-        ],
-        cost_estimate=pl.CostEstimate(flops=PREPARE, bytes_accessed=0, transcendentals=0),
-        compiler_params=pltpu.CompilerParams(vmem_limit_bytes=32 << 20),
+        in_specs=[WHOLE] * 4,
+        out_specs=[WHOLE] * 3,
+        scratch_shapes=[pltpu.VMEM((span, cells), jnp.float32)],
+        cost_estimate=pl.CostEstimate(flops=1 << 32, bytes_accessed=0, transcendentals=0),
+        compiler_params=pltpu.CompilerParams(vmem_limit_bytes=24 << 20),
         name="prepare",
-    )(pltpu.with_memory_space_constraint(operators, pltpu.HBM), own, code, mate_code)
+    )(operators, own, code, mate_code)
 
 
 def select_kernel(near_ref, near_select_ref, far_select_ref):
     entries, cells = near_ref.shape[0] // 2, near_ref.shape[1]
     classes = near_select_ref.shape[0] // cells
     step = away()
-    build_select(near_ref[:entries, :], (REACH - step) * cells, near_select_ref, classes)
-    build_select(near_ref[entries:, :], (REACH - 2 * step) * cells, far_select_ref, classes)
+    build_select(near_ref[:entries, :], (REACH - step) * cells, near_select_ref, 0, classes)
+    build_select(near_ref[entries:, :], (REACH - 2 * step) * cells, far_select_ref, 0, classes)
 
 
 def selections(near_codes, classes):
@@ -214,7 +262,7 @@
         out_shape=[select, select],
         in_specs=[WHOLE],
         out_specs=[WHOLE] * 2,
-        cost_estimate=pl.CostEstimate(flops=PREPARE, bytes_accessed=0, transcendentals=0),
+        cost_estimate=pl.CostEstimate(flops=1 << 29, bytes_accessed=0, transcendentals=0),
         compiler_params=pltpu.CompilerParams(vmem_limit_bytes=8 << 20),
         name="selections",
     )(near_codes)
@@ -226,7 +274,7 @@
 ):
     rows, classes, _ = held_ref.shape
     cells = far_ref.shape[1]
-    build_select(code_ref[...], (REACH + 2 * away()) * cells, select, classes)
+    build_select(code_ref[...], (REACH + 2 * away()) * cells, select, 0, classes)
 
     def part_classes(source, start, size):
         for k in range(classes):
@@ -237,7 +285,7 @@
         def run(low=low, high=high, offset=offset):
             pad_into(padded, offset, other_ref)
             right = padded[: high - low, :].astype(jnp.bfloat16)
-            for start, size in chunks(rows):
+            for start, size in chunks(rows, CHUNK):
                 left = held_ref[start : start + size, :, low:high]
                 part = slice(start * classes, (start + size) * classes)
                 product[part, :] = product_ref[part, :] + jnp.dot(
@@ -248,15 +296,15 @@
         pl.when(lax.axis_index("sub") != index)(run)
 
     if not windows:
-        for start, size in chunks(rows):
+        for start, size in chunks(rows, CHUNK):
             part_classes(product_ref, start, size)
 
-    for ref, column, chosen in (
-        (mate_ref, 0, mate_select_ref), (far_ref, 0, far_select_ref), (mate_ref, cells, select)
-    ):
-        ref[:, column : column + cells] = jnp.dot(
-            terms_ref[...], chosen[...], preferred_element_type=jnp.float32
-        ).astype(jnp.bfloat16)
+    terms = terms_ref[...]
+    chosen = jnp.concatenate([mate_select_ref[...], far_select_ref[...], select[...]], axis=1)
+    total = jnp.dot(terms, chosen, preferred_element_type=jnp.float32).astype(jnp.bfloat16)
+    mate_ref[:, :cells] = total[:, :cells]
+    far_ref[...] = total[:, cells : 2 * cells]
+    mate_ref[:, cells:] = total[:, 2 * cells :]
 
 
 def push_away(held, product, other, mate_select, far_select, code, windows):
@@ -289,14 +337,11 @@
 
 def push_home_kernel(terms_ref, home_ref, near_select_ref, came_ref, own_ref, near_ref):
     cells = near_ref.shape[1]
-    terms = terms_ref[...]
-    near_ref[...] = (
-        jnp.dot(terms, near_select_ref[...], preferred_element_type=jnp.float32)
-        + came_ref[:, cells:].astype(jnp.float32)
-    ).astype(jnp.bfloat16)
-    own_ref[...] = jnp.dot(
-        terms, home_ref[...], preferred_element_type=jnp.float32
-    ) + came_ref[:, :cells].astype(jnp.float32)
+    chosen = jnp.concatenate([home_ref[...], near_select_ref[...]], axis=1)
+    total = jnp.dot(terms_ref[...], chosen, preferred_element_type=jnp.float32)
+    total = total + came_ref[...].astype(jnp.float32)
+    own_ref[...] = total[:, :cells]
+    near_ref[...] = total[:, cells:].astype(jnp.bfloat16)
 
 
 def push_home(terms, home, near_select, came):
@@ -323,37 +368,32 @@
     cells, entries = list_slot.shape
     halves = lax.axis_size("sub") == 2
 
-    active = lax.broadcasted_iota(jnp.int32, (entries, cells), 0) < list_count[None, :]
-    code = jnp.where(active, (list_class.T << CLASS_SHIFT) + list_slot.T, -1)
-    operators = jnp.transpose(translate, (1, 0, 2))
+    code = coded(list_slot, list_class, list_count)
     mate_code = to_mate(code)
     near_codes = to_near(jnp.concatenate([code, mate_code], axis=0))
 
     operators = jnp.transpose(translate, (1, 0, 2))
     if halves:
         windows = half_windows(rows, depth, 2)
-        mine = lax.axis_index("sub") * rows
-        check = lax.dynamic_update_slice(
-            jnp.zeros((depth, cells), up_check.dtype), up_check, (mine, 0)
-        )
-        check, mate_code = lax.optimization_barrier((check, mate_code))
-        check = lax.dynamic_update_slice(check, across_sub(up_check), (rows - mine, 0))
+        own_check = lax.optimization_barrier((up_check, mate_code))[0]
+        equivalent = joined_product(up_inverse, own_check, across_sub(up_check))
+        other = across_sub(equivalent)
     else:
         windows = [(0, depth, 0)]
-        check = lax.all_gather(up_check, "sub", axis=0, tiled=True)
-    equivalent = jnp.dot(up_inverse, check, preferred_element_type=jnp.float32)
-    equivalent = equivalent.astype(jnp.bfloat16)
-    if halves:
-        other = across_sub(equivalent)
-    else:
-        equivalent = lax.all_gather(equivalent, "sub", axis=0, tiled=True)
+        equivalent = lax.all_gather(
+            jnp.dot(
+                up_inverse, lax.all_gather(up_check, "sub", axis=0, tiled=True),
+                preferred_element_type=jnp.float32,
+            ).astype(jnp.bfloat16),
+            "sub", axis=0, tiled=True,
+        )
         other = equivalent
-    held, product, home, mate_select = prepare(operators, equivalent, code, mate_code, windows)
+    product, home, mate_select = prepare(operators, equivalent, code, mate_code, windows)
     near_codes, product = lax.optimization_barrier((near_codes, product))
     near_select, far_select = selections(near_codes, classes)
-    mate_near_code = to_mate(near_codes[:entries])
     terms, mate_sum, far_sum = push_away(
-        held, product, other, mate_select, far_select, mate_near_code, windows if halves else []
+        operators, product, other, mate_select, far_select, to_mate(near_codes[:entries]),
+        windows if halves else [],
     )
     mate_came = to_mate(mate_sum)
     far_came = to_far(far_sum)

time: 35.2 us -> 31.8 us (0.903)
  local copies, waits for them, and re-layouts: 1.95 us -> 0.02 us
  Pallas kernels: 8.68 us -> 7.13 us
  starting transfers between devices: 13.5 us -> 14.5 us
  other arithmetic: 0.83 us -> 0.05 us
  matrix products: 0.38 us -> 0 us
    pallas_call x1, Pallas kernels: 3.92 us -> 1.55 us  [prepare(): pl.pallas_call(functools.partial(prepare_kernel, windows), out_shape=[jax...]
    dynamic_update_slice x2 -> x0, local copies, waits for them, and re-layouts: 1.9 us -> none  [the longest x1 1.5 us: shards(): lax.dynamic_update_slice(jnp.zeros((depth, cells), up_check.dtype), up_ch...]
    pallas_call x0 -> x2, Pallas kernels: none -> 1.3 us  [the longest x1 0.88 us: coded(): pl.pallas_call(code_kernel, out_shape=jax.ShapeDtypeStruct(operands[0].sh...]
    ppermute x3, starting transfers between devices: 3.71 us -> 4.66 us  [across_sub(): return lax.ppermute(shard, 'sub', [(0, 1), (1, 0)])]
    select_n x1 -> x0, other arithmetic: 0.78 us -> none  [shards(): code = jnp.where(active, (list_class.T << CLASS_SHIFT) + list_slot.T, -1)]
    ppermute x3, waiting for transfers between devices: 4.77 us -> 5.21 us  [across_sub(): return lax.ppermute(shard, 'sub', [(0, 1), (1, 0)])]
    dot_general x1 -> x0, matrix products: 0.38 us -> none  [shards(): equivalent = jnp.dot(up_inverse, check, preferred_element_type=jnp.float32)]
  transfers between devices with their start and end apart: 9 -> 9, of which waited for: 4 -> 6; matrix products, arithmetic and copies ran while one was open for 7% -> 0% of each run, Pallas kernels for 15% -> 10%
where the time goes in v9:
time: 31.8 us; the launch traced here: 31.6 us
  starting transfers between devices  14.5 us (46%)
  waiting for transfers between devices  9.78 us (31%)
  Pallas kernels  7.13 us (22%)
    ppermute x2, starting transfers between devices, to_near(): lax.ppermute(value, 'tile', [(a, b) for a, b in pairs if 0 <= b < count])  6.3 us
    ppermute x3, waiting for transfers between devices, across_sub(): return lax.ppermute(shard, 'sub', [(0, 1), (1, 0)])  5.21 us
    ppermute x3, starting transfers between devices, across_sub(): return lax.ppermute(shard, 'sub', [(0, 1), (1, 0)])  4.66 us
    ppermute x1, starting transfers between devices, to_far(): lax.ppermute(value, 'tile', [(a, b) for a, b in pairs if 0 <= b < count])  3.32 us
    ppermute x2, waiting for transfers between devices, to_near(): lax.ppermute(value, 'tile', [(a, b) for a, b in pairs if 0 <= b < count])  2.96 us
    pallas_call x1, Pallas kernels, push_away(): pl.pallas_call(functools.partial(push_away_kernel, windows), out_shape=[j...  2.18 us
    pallas_call x1, Pallas kernels, prepare(): pl.pallas_call(functools.partial(prepare_kernel, windows), out_shape=[jax...  1.55 us
    pallas_call x1, Pallas kernels, rest(): pl.pallas_call(functools.partial(rest_kernel, windows), out_shape=jax.Sha...  0.95 us
  transfers between devices with their start and end apart: 9, of which 6 were waited for; matrix products, arithmetic and copies ran while one was open for 0% of the time, Pallas kernels for 10%

profile of v9, /device:TPU:8, one launch (start us, length us, event | category | flops | bytes accessed | tf_op | source)
XLA Modules:
  0.0 31.6 jit_solution(17762778231193669374)
XLA Ops:
  0.0 0.0 copy-start.3
  0.0 0.0 copy-start.2
  0.0 0.0 copy-start
  0.0 0.9 %code.1.code_ref = s32[8,128]{1,0:T(8,128)S(1)} custom-call(s32[8,128]{1,0:T(8,128)} %bitcast.6, s32[8,128]{1,0:T(8,128)} %bitcast.7, s32[1,128]{1,0:T(1,128)} %bitcast.8), custom_call_target="tpu_custom_call" | custom-call | flops 8589934592 | tf_op jit(solution)/shard_map/code/pallas_call | solution.py:83
  0.9 0.1 collective-permute-start
  1.0 0.0 copy-done.3
  1.0 1.6 %collective-permute-start.2 = (bf16[444,128]{1,0:T(8,128)(2,1)S(1)}, bf16[444,128]{1,0:T(8,128)(2,1)S(1)}, u32[]{:S(2)}, u32[]{:S(2)}) collective-permute-start(bf16[444,128]{1,0:T(8,128)(2,1)S(1)} %copy-done.3), channel_id=1, source_target_pairs={{0,1},{1,0},{2,3},{3,2},{4,5},{5,4},{6,7},{7,6},{8,9},{9,8},{10,11... | collective-permute-start | bytes 341000 | tf_op jit(solution)/shard_map/ppermute | solution.py:18
  2.5 0.0 collective-permute-done.mate_ref
  2.6 3.1 %collective-permute-start.1 = (s32[16,128]{1,0:T(8,128)S(1)}, s32[16,128]{1,0:T(8,128)S(1)}, u32[]{:S(2)}, u32[]{:S(2)}) collective-permute-start(s32[16,128]{1,0:T(8,128)S(1)} %pad_add_fusion), channel_id=1, source_target_pairs={{2,4},{4,2},{6,8},{8,6},{10,12},{12,10},{14,16},{16,14},{18,20},{2... | collective-permute-start | bytes 24584 | tf_op jit(solution)/shard_map/ppermute | solution.py:30
  5.6 0.9 %collective-permute-done.2.other_ref = bf16[444,128]{1,0:T(8,128)(2,1)S(1)} collective-permute-done((bf16[444,128]{1,0:T(8,128)(2,1)S(1)}, bf16[444,128]{1,0:T(8,128)(2,1)S(1)}, u32[]{:S(2)}, u32[]{:S(2)}) %collective-permute-start.2) | collective-permute-done | bytes 113696 | tf_op jit(solution)/shard_map/ppermute | solution.py:18
  6.5 0.0 copy-done.2
  6.5 0.4 %joined.1.own_ref = bf16[444,128]{1,0:T(8,128)(2,1)S(1)} custom-call(bf16[444,888]{1,0:T(8,128)(2,1)S(1)} %copy-done.2, bf16[444,128]{1,0:T(8,128)(2,1)S(1)} %copy-done.3, bf16[444,128]{1,0:T(8,128)(2,1)S(1)} %collective-permute-done.2.other_ref), custom_call_target="tpu_custom_call" | custom-call | flops 100933632 | bytes 788544 | tf_op jit(solution)/shard_map/joined/pallas_call | solution.py:112
  7.0 1.6 %collective-permute-start.3 = (bf16[444,128]{1,0:T(8,128)(2,1)S(1)}, bf16[444,128]{1,0:T(8,128)(2,1)S(1)}, u32[]{:S(2)}, u32[]{:S(2)}) collective-permute-start(bf16[444,128]{1,0:T(8,128)(2,1)S(1)} %joined.1.own_ref), channel_id=1, source_target_pairs={{0,1},{1,0},{2,3},{3,2},{4,5},{5,4},{6,7},{7,6},{8,9},{9,8},{10,11... | collective-permute-start | bytes 341000 | tf_op jit(solution)/shard_map/ppermute | solution.py:18
  8.5 0.0 copy-done
  8.5 1.6 %prepare.1 = (f32[3552,128]{1,0:T(8,128)S(1)}, bf16[1024,128]{1,0:T(8,128)(2,1)S(1)}, bf16[1024,128]{1,0:T(8,128)(2,1)S(1)}) custom-call(bf16[444,8,888]{2,1,0:T(8,128)(2,1)S(1)} %bitcast.4, bf16[444,128]{1,0:T(8,128)(2,1)S(1)} %joined.1.own_ref, s32[8,128]{1,0:T(8,128)S(1)} %code.1.code_ref, s32[8,128]{1,0:T(8,128)S(1)} %collective-permute-done.mate_ref), custom_call_target="tpu_custom_call" | custom-call | flops 4294967296 | tf_op jit(solution)/shard_map/prepare/pallas_call | solution.py:235
  10.1 0.0 collective-permute-done.1.near_ref
  10.1 0.0 copy-start.1
  10.1 0.1 collective-permute-start.4
  10.2 0.5 %selections.1 = (bf16[1024,128]{1,0:T(8,128)(2,1)S(1)}, bf16[1024,128]{1,0:T(8,128)(2,1)S(1)}) custom-call(s32[16,128]{1,0:T(8,128)S(1)} %collective-permute-done.1.near_ref), custom_call_target="tpu_custom_call" | custom-call | flops 536870912 | tf_op jit(solution)/shard_map/selections/pallas_call | solution.py:260
  10.7 0.7 %collective-permute-done.4.code_ref = s32[8,128]{1,0:T(8,128)S(1)} collective-permute-done((s32[8,128]{1,0:T(8,128)S(1)}, s32[8,128]{1,0:T(8,128)S(1)}, u32[]{:S(2)}, u32[]{:S(2)}) %collective-permute-start.4) | collective-permute-done | bytes 4128 | tf_op jit(solution)/shard_map/ppermute | solution.py:24
  11.4 0.5 %collective-permute-done.3.other_ref = bf16[444,128]{1,0:T(8,128)(2,1)S(1)} collective-permute-done((bf16[444,128]{1,0:T(8,128)(2,1)S(1)}, bf16[444,128]{1,0:T(8,128)(2,1)S(1)}, u32[]{:S(2)}, u32[]{:S(2)}) %collective-permute-start.3) | collective-permute-done | bytes 113696 | tf_op jit(solution)/shard_map/ppermute | solution.py:18
  11.8 2.2 %push_away.1 = (bf16[444,1024]{1,0:T(8,128)(2,1)S(1)}, bf16[444,256]{1,0:T(8,128)(2,1)S(1)}, bf16[444,128]{1,0:T(8,128)(2,1)S(1)}) custom-call(bf16[444,8,888]{2,1,0:T(8,128)(2,1)S(1)} %bitcast.5, f32[3552,128]{1,0:T(8,128)S(1)} %get-tuple-element.20.product_ref, bf16[444,128]{1,0:T(8,128)(2,1)S(1)} %collective-permute-done.3.other_ref, ...), custom_call_target="tpu_custom_call" | custom-call | flops 814743552 | bytes 6308352 | tf_op jit(solution)/shard_map/push_away/pallas_call | solution.py:314
  14.0 0.1 collective-permute-start.5
  14.1 3.3 %collective-permute-start.6 = (bf16[444,128]{1,0:T(8,128)(2,1)S(1)}, bf16[444,128]{1,0:T(8,128)(2,1)S(1)}, u32[]{:S(2)}, u32[]{:S(2)}) collective-permute-start(bf16[444,128]{1,0:T(8,128)(2,1)S(1)} %get-tuple-element.29), channel_id=1, source_target_pairs={{2,6},{4,0},{6,10},{8,4},{10,14},{12,8},{14,18},{16,12},{18,22},{2... | collective-permute-start | bytes 341000 | tf_op jit(solution)/shard_map/ppermute | solution.py:36
  17.4 0.0 collective-permute-done.5.came_ref
  17.4 0.4 %push_home.1 = (f32[444,128]{1,0:T(8,128)S(1)}, bf16[444,128]{1,0:T(8,128)(2,1)S(1)}) custom-call(bf16[444,1024]{1,0:T(8,128)(2,1)S(1)} %get-tuple-element.24.terms_ref, bf16[1024,128]{1,0:T(8,128)(2,1)S(1)} %get-tuple-element.25.home_ref, bf16[1024,128]{1,0:T(8,128)(2,1)S(1)} %get-tuple-element.26.near_select_ref, ...), custom_call_target="tpu_custom_call" | custom-call | flops 232783872 | bytes 1818624 | tf_op jit(solution)/shard_map/push_home/pallas_call | solution.py:350
  17.8 3.2 %collective-permute-start.7 = (bf16[444,128]{1,0:T(8,128)(2,1)S(1)}, bf16[444,128]{1,0:T(8,128)(2,1)S(1)}, u32[]{:S(2)}, u32[]{:S(2)}) collective-permute-start(bf16[444,128]{1,0:T(8,128)(2,1)S(1)} %get-tuple-element.30), channel_id=1, source_target_pairs={{2,4},{4,2},{6,8},{8,6},{10,12},{12,10},{14,16},{16,14},{18,20},{2... | collective-permute-start | bytes 341000 | tf_op jit(solution)/shard_map/ppermute | solution.py:30
  21.1 0.9 %collective-permute-done.6 = bf16[444,128]{1,0:T(8,128)(2,1)S(1)} collective-permute-done((bf16[444,128]{1,0:T(8,128)(2,1)S(1)}, bf16[444,128]{1,0:T(8,128)(2,1)S(1)}, u32[]{:S(2)}, u32[]{:S(2)}) %collective-permute-start.6) | collective-permute-done | bytes 113696 | tf_op jit(solution)/shard_map/ppermute | solution.py:36
  22.0 3.0 %collective-permute-done.7 = bf16[444,128]{1,0:T(8,128)(2,1)S(1)} collective-permute-done((bf16[444,128]{1,0:T(8,128)(2,1)S(1)}, bf16[444,128]{1,0:T(8,128)(2,1)S(1)}, u32[]{:S(2)}, u32[]{:S(2)}) %collective-permute-start.7) | collective-permute-done | bytes 113696 | tf_op jit(solution)/shard_map/ppermute | solution.py:30
  25.0 1.6 %collective-permute-start.8 = (bf16[444,128]{1,0:T(8,128)(2,1)S(1)}, bf16[444,128]{1,0:T(8,128)(2,1)S(1)}, u32[]{:S(2)}, u32[]{:S(2)}) collective-permute-start(bf16[444,128]{1,0:T(8,128)(2,1)S(1)} %add_convert_fusion.own_ref), channel_id=1, source_target_pairs={{0,1},{1,0},{2,3},{3,2},{4,5},{5,4},{6,7},{7,6},{8,9},{9,8},{10,11... | collective-permute-start | bytes 341000 | tf_op jit(solution)/shard_map/ppermute | solution.py:18
  26.6 0.0 copy-done.1
  26.6 0.3 first.1.part_ref
  26.9 3.8 %collective-permute-done.8.other_ref = bf16[444,128]{1,0:T(8,128)(2,1)S(1)} collective-permute-done((bf16[444,128]{1,0:T(8,128)(2,1)S(1)}, bf16[444,128]{1,0:T(8,128)(2,1)S(1)}, u32[]{:S(2)}, u32[]{:S(2)}) %collective-permute-start.8) | collective-permute-done | bytes 113696 | tf_op jit(solution)/shard_map/ppermute | solution.py:18
  30.7 1.0 %rest.1 = bf16[444,128]{1,0:T(8,128)(2,1)} custom-call(bf16[444,888]{1,0:T(8,128)(2,1)S(1)} %copy-done.1, f32[444,128]{1,0:T(8,128)S(1)} %first.1.part_ref, bf16[444,128]{1,0:T(8,128)(2,1)S(1)} %collective-permute-done.8.other_ref), custom_call_target="tpu_custom_call" | custom-call | flops 58195968 | bytes 454656 | tf_op jit(solution)/shard_map/rest/pallas_call | solution.py:173
  (3 shorter events, 0.1 us)
Async XLA Ops:
  0.0 1.0 %copy-start.3 = (bf16[444,128]{1,0:T(8,128)(2,1)S(1)}, bf16[444,128]{1,0:T(8,128)(2,1)}, u32[]{:S(2)}) copy-start(bf16[444,128]{1,0:T(8,128)(2,1)} %own_ref) | copy-start | bytes 340996
  0.0 6.5 %copy-start.2 = (bf16[444,888]{1,0:T(8,128)(2,1)S(1)}, bf16[444,888]{1,0:T(8,128)(2,1)}, u32[]{:S(2)}) copy-start(bf16[444,888]{1,0:T(8,128)(2,1)} %matrix_ref.3) | copy-start | bytes 2365636
  0.0 8.5 %copy-start = (bf16[8,444,888]{2,0,1:T(8,128)(2,1)S(1)}, bf16[8,444,888]{2,0,1:T(8,128)(2,1)}, u32[]{:S(2)}) copy-start(bf16[8,444,888]{2,0,1:T(8,128)(2,1)} %param.9) | copy-start | bytes 18925060
  0.9 1.6 %collective-permute-start = (s32[8,128]{1,0:T(8,128)S(1)}, s32[8,128]{1,0:T(8,128)S(1)}, u32[]{:S(2)}, u32[]{:S(2)}) collective-permute-start(s32[8,128]{1,0:T(8,128)S(1)} %code.1.code_ref), channel_id=1, source_target_pairs={{0,2},{2,0},{4,6},{6,4},{8,10},{10,8},{12,14},{14,12},{16,18},{18,... | collective-permute-start | bytes 12296 | tf_op jit(solution)/shard_map/ppermute | solution.py:24
  1.0 5.6 %collective-permute-start.2 = (bf16[444,128]{1,0:T(8,128)(2,1)S(1)}, bf16[444,128]{1,0:T(8,128)(2,1)S(1)}, u32[]{:S(2)}, u32[]{:S(2)}) collective-permute-start(bf16[444,128]{1,0:T(8,128)(2,1)S(1)} %copy-done.3), channel_id=1, source_target_pairs={{0,1},{1,0},{2,3},{3,2},{4,5},{5,4},{6,7},{7,6},{8,9},{9,8},{10,11... | collective-permute-start | bytes 341000 | tf_op jit(solution)/shard_map/ppermute | solution.py:18
  2.6 7.5 %collective-permute-start.1 = (s32[16,128]{1,0:T(8,128)S(1)}, s32[16,128]{1,0:T(8,128)S(1)}, u32[]{:S(2)}, u32[]{:S(2)}) collective-permute-start(s32[16,128]{1,0:T(8,128)S(1)} %pad_add_fusion), channel_id=1, source_target_pairs={{2,4},{4,2},{6,8},{8,6},{10,12},{12,10},{14,16},{16,14},{18,20},{2... | collective-permute-start | bytes 24584 | tf_op jit(solution)/shard_map/ppermute | solution.py:30
  7.0 4.9 %collective-permute-start.3 = (bf16[444,128]{1,0:T(8,128)(2,1)S(1)}, bf16[444,128]{1,0:T(8,128)(2,1)S(1)}, u32[]{:S(2)}, u32[]{:S(2)}) collective-permute-start(bf16[444,128]{1,0:T(8,128)(2,1)S(1)} %joined.1.own_ref), channel_id=1, source_target_pairs={{0,1},{1,0},{2,3},{3,2},{4,5},{5,4},{6,7},{7,6},{8,9},{9,8},{10,11... | collective-permute-start | bytes 341000 | tf_op jit(solution)/shard_map/ppermute | solution.py:18
  10.1 16.5 %copy-start.1 = (bf16[444,888]{1,0:T(8,128)(2,1)S(1)}, bf16[444,888]{1,0:T(8,128)(2,1)}, u32[]{:S(2)}) copy-start(bf16[444,888]{1,0:T(8,128)(2,1)} %matrix_ref.5) | copy-start | bytes 2365636
  10.1 1.2 %collective-permute-start.4 = (s32[8,128]{1,0:T(8,128)S(1)}, s32[8,128]{1,0:T(8,128)S(1)}, u32[]{:S(2)}, u32[]{:S(2)}) collective-permute-start(s32[8,128]{1,0:T(8,128)S(1)} %slice.3), channel_id=1, source_target_pairs={{0,2},{2,0},{4,6},{6,4},{8,10},{10,8},{12,14},{14,12},{16,18},{18,... | collective-permute-start | bytes 12296 | tf_op jit(solution)/shard_map/ppermute | solution.py:24
  14.0 3.4 %collective-permute-start.5 = (bf16[444,256]{1,0:T(8,128)(2,1)S(1)}, bf16[444,256]{1,0:T(8,128)(2,1)S(1)}, u32[]{:S(2)}, u32[]{:S(2)}) collective-permute-start(bf16[444,256]{1,0:T(8,128)(2,1)S(1)} %get-tuple-element.27), channel_id=1, source_target_pairs={{0,2},{2,0},{4,6},{6,4},{8,10},{10,8},{12,14},{14,12},{16,18},{18,... | collective-permute-start | bytes 681992 | tf_op jit(solution)/shard_map/ppermute | solution.py:24
  14.1 7.9 %collective-permute-start.6 = (bf16[444,128]{1,0:T(8,128)(2,1)S(1)}, bf16[444,128]{1,0:T(8,128)(2,1)S(1)}, u32[]{:S(2)}, u32[]{:S(2)}) collective-permute-start(bf16[444,128]{1,0:T(8,128)(2,1)S(1)} %get-tuple-element.29), channel_id=1, source_target_pairs={{2,6},{4,0},{6,10},{8,4},{10,14},{12,8},{14,18},{16,12},{18,22},{2... | collective-permute-start | bytes 341000 | tf_op jit(solution)/shard_map/ppermute | solution.py:36
  17.8 7.1 %collective-permute-start.7 = (bf16[444,128]{1,0:T(8,128)(2,1)S(1)}, bf16[444,128]{1,0:T(8,128)(2,1)S(1)}, u32[]{:S(2)}, u32[]{:S(2)}) collective-permute-start(bf16[444,128]{1,0:T(8,128)(2,1)S(1)} %get-tuple-element.30), channel_id=1, source_target_pairs={{2,4},{4,2},{6,8},{8,6},{10,12},{12,10},{14,16},{16,14},{18,20},{2... | collective-permute-start | bytes 341000 | tf_op jit(solution)/shard_map/ppermute | solution.py:30
  25.0 5.7 %collective-permute-start.8 = (bf16[444,128]{1,0:T(8,128)(2,1)S(1)}, bf16[444,128]{1,0:T(8,128)(2,1)S(1)}, u32[]{:S(2)}, u32[]{:S(2)}) collective-permute-start(bf16[444,128]{1,0:T(8,128)(2,1)S(1)} %add_convert_fusion.own_ref), channel_id=1, source_target_pairs={{0,1},{1,0},{2,3},{3,2},{4,5},{5,4},{6,7},{7,6},{8,9},{9,8},{10,11... | collective-permute-start | bytes 341000 | tf_op jit(solution)/shard_map/ppermute | solution.py:18

commit v10 on v9

--- a/solution.py
+++ b/solution.py
@@ -34,6 +34,26 @@
     count = lax.axis_size("tile")
     pairs = [(t, t + 4 * (t % 2) - 2) for t in range(count)]
     return lax.ppermute(value, "tile", [(a, b) for a, b in pairs if 0 <= b < count])
+
+
+def near_or_mates_far(value):
+    count = lax.axis_size("tile")
+    pairs = []
+    for t in range(count):
+        step = 2 * (t % 2) - 1
+        for index, target in ((0, t + step), (1, t - 3 * step)):
+            if 0 <= target < count:
+                pairs.append((2 * t + index, 2 * target + index))
+    return lax.ppermute(value, ("tile", "sub"), pairs)
+
+
+def crosswise(value):
+    count = lax.axis_size("tile")
+    pairs = [
+        (2 * t + index, 2 * (t ^ 1) + 1 - index)
+        for t in range(count) for index in range(2) if t ^ 1 < count
+    ]
+    return lax.ppermute(value, ("tile", "sub"), pairs)
 
 
 def away():
@@ -203,21 +223,20 @@
 
 
 def prepare_kernel(
-    windows, operators_ref, own_ref, code_ref, mate_ref,
-    product_ref, home_ref, mate_select_ref, padded,
+    windows, part, distance, operators_ref, own_ref, code_ref, product_ref, select_ref, padded
 ):
-    rows, classes, _ = operators_ref.shape
-    cells = code_ref.shape[1]
-    build_select(code_ref[...], REACH * cells, home_ref, 0, classes)
-    build_select(mate_ref[...], (REACH + away()) * cells, mate_select_ref, 0, classes)
+    classes = operators_ref.shape[1]
+    cells = own_ref.shape[1]
+    build_select(code_ref[...], (REACH + distance * away()) * cells, select_ref, 0, classes)
 
     for index, (low, high, offset) in enumerate(windows):
         def run(low=low, high=high, offset=offset):
             pad_into(padded, offset, own_ref)
             right = padded[: high - low, :].astype(jnp.bfloat16)
-            for start, size in chunks(rows, CHUNK):
+            for start, size in part:
                 left = operators_ref[start : start + size, :, low:high]
-                product_ref[start * classes : (start + size) * classes, :] = jnp.dot(
+                row = (start - part[0][0]) * classes
+                product_ref[row : row + size * classes, :] = jnp.dot(
                     left.reshape(size * classes, high - low), right,
                     preferred_element_type=jnp.float32,
                 )
@@ -227,54 +246,73 @@
             pl.when(lax.axis_index("sub") == index)(run)
 
 
-def prepare(operators, own, code, mate_code, windows):
-    rows, classes, depth = operators.shape
-    cells = code.shape[1]
+def prepare(operators, own, code, windows, part, distance):
+    classes = operators.shape[1]
+    cells = own.shape[1]
     span = max(high - low for low, high, _ in windows)
-    select = jax.ShapeDtypeStruct((classes * cells, cells), jnp.bfloat16)
-    return pl.pallas_call(
-        functools.partial(prepare_kernel, windows),
+    rows = sum(size for _, size in part)
+    return pl.pallas_call(
+        functools.partial(prepare_kernel, windows, part, distance),
         out_shape=[
-            jax.ShapeDtypeStruct((rows * classes, cells), jnp.float32), select, select,
+            jax.ShapeDtypeStruct((rows * classes, cells), jnp.float32),
+            jax.ShapeDtypeStruct((classes * cells, cells), jnp.bfloat16),
         ],
-        in_specs=[WHOLE] * 4,
-        out_specs=[WHOLE] * 3,
+        in_specs=[WHOLE] * 3,
+        out_specs=[WHOLE] * 2,
         scratch_shapes=[pltpu.VMEM((span, cells), jnp.float32)],
         cost_estimate=pl.CostEstimate(flops=1 << 32, bytes_accessed=0, transcendentals=0),
         compiler_params=pltpu.CompilerParams(vmem_limit_bytes=24 << 20),
         name="prepare",
-    )(operators, own, code, mate_code)
-
-
-def select_kernel(near_ref, near_select_ref, far_select_ref):
-    entries, cells = near_ref.shape[0] // 2, near_ref.shape[1]
+    )(operators, own, code)
+
+
+def select_kernel(
+    halves, got_ref, crossed_ref, swapped_ref, near_select_ref, far_select_ref, mate_near_ref
+):
+    entries, cells = got_ref.shape
     classes = near_select_ref.shape[0] // cells
     step = away()
-    build_select(near_ref[:entries, :], (REACH - step) * cells, near_select_ref, 0, classes)
-    build_select(near_ref[entries:, :], (REACH - 2 * step) * cells, far_select_ref, 0, classes)
-
-
-def selections(near_codes, classes):
-    cells = near_codes.shape[1]
+    got, crossed = got_ref[...], crossed_ref[...]
+    low, high = swapped_ref[:entries, :], swapped_ref[entries:, :]
+    near, far, mate_near = got, crossed, low
+    if halves:
+        first = lax.axis_index("sub") == 0
+        near = jnp.where(first, near, high)
+        far = jnp.where(first, far, low)
+        mate_near = jnp.where(first, mate_near, crossed)
+    build_select(near, (REACH - step) * cells, near_select_ref, 0, classes)
+    build_select(far, (REACH - 2 * step) * cells, far_select_ref, 0, classes)
+    build_select(mate_near, (REACH + 2 * step) * cells, mate_near_ref, 0, classes)
+
+
+def selections(got, crossed, swapped, classes, halves):
+    cells = got.shape[1]
     select = jax.ShapeDtypeStruct((classes * cells, cells), jnp.bfloat16)
     return pl.pallas_call(
-        select_kernel,
-        out_shape=[select, select],
-        in_specs=[WHOLE],
-        out_specs=[WHOLE] * 2,
-        cost_estimate=pl.CostEstimate(flops=1 << 29, bytes_accessed=0, transcendentals=0),
+        functools.partial(select_kernel, halves),
+        out_shape=[select] * 3,
+        in_specs=[WHOLE] * 3,
+        out_specs=[WHOLE] * 3,
+        cost_estimate=pl.CostEstimate(flops=1 << 20, bytes_accessed=0, transcendentals=0),
         compiler_params=pltpu.CompilerParams(vmem_limit_bytes=8 << 20),
         name="selections",
-    )(near_codes)
+    )(got, crossed, swapped)
 
 
 def push_away_kernel(
-    windows, held_ref, product_ref, other_ref, mate_select_ref, far_select_ref, code_ref,
-    terms_ref, mate_ref, far_ref, padded, product, select,
+    windows, held_ref, low_ref, high_ref, other_ref,
+    mate_select_ref, far_select_ref, mate_near_ref,
+    terms_ref, mate_ref, far_ref, padded, product,
 ):
     rows, classes, _ = held_ref.shape
     cells = far_ref.shape[1]
-    build_select(code_ref[...], (REACH + 2 * away()) * cells, select, 0, classes)
+    split = low_ref.shape[0]
+
+    def own_half(start, size):
+        if start * classes < split:
+            return low_ref[start * classes : (start + size) * classes, :]
+        row = start * classes - split
+        return high_ref[row : row + size * classes, :]
 
     def part_classes(source, start, size):
         for k in range(classes):
@@ -288,7 +326,7 @@
             for start, size in chunks(rows, CHUNK):
                 left = held_ref[start : start + size, :, low:high]
                 part = slice(start * classes, (start + size) * classes)
-                product[part, :] = product_ref[part, :] + jnp.dot(
+                product[part, :] = own_half(start, size) + jnp.dot(
                     left.reshape(size * classes, high - low), right,
                     preferred_element_type=jnp.float32,
                 )
@@ -297,17 +335,18 @@
 
     if not windows:
         for start, size in chunks(rows, CHUNK):
-            part_classes(product_ref, start, size)
+            product[start * classes : (start + size) * classes, :] = own_half(start, size)
+            part_classes(product, start, size)
 
     terms = terms_ref[...]
-    chosen = jnp.concatenate([mate_select_ref[...], far_select_ref[...], select[...]], axis=1)
+    chosen = jnp.concatenate([mate_select_ref[...], far_select_ref[...], mate_near_ref[...]], axis=1)
     total = jnp.dot(terms, chosen, preferred_element_type=jnp.float32).astype(jnp.bfloat16)
     mate_ref[:, :cells] = total[:, :cells]
     far_ref[...] = total[:, cells : 2 * cells]
     mate_ref[:, cells:] = total[:, 2 * cells :]
 
 
-def push_away(held, product, other, mate_select, far_select, code, windows):
+def push_away(held, low, high, other, mate_select, far_select, mate_near, windows):
     rows, classes, depth = held.shape
     cells = other.shape[1]
     span = max([high - low for low, high, _ in windows], default=LANES)
@@ -318,12 +357,11 @@
             jax.ShapeDtypeStruct((rows, 2 * cells), jnp.bfloat16),
             jax.ShapeDtypeStruct((rows, cells), jnp.bfloat16),
         ],
-        in_specs=[WHOLE] * 6,
+        in_specs=[WHOLE] * 7,
         out_specs=[WHOLE] * 3,
         scratch_shapes=[
             pltpu.VMEM((span, cells), jnp.float32),
             pltpu.VMEM((rows * classes, cells), jnp.float32),
-            pltpu.VMEM((classes * cells, cells), jnp.bfloat16),
         ],
         cost_estimate=pl.CostEstimate(
             flops=2 * rows * classes * cells * (span + 3 * cells),
@@ -332,7 +370,7 @@
         ),
         compiler_params=pltpu.CompilerParams(vmem_limit_bytes=32 << 20),
         name="push_away",
-    )(held, product, other, mate_select, far_select, code)
+    )(held, low, high, other, mate_select, far_select, mate_near)
 
 
 def push_home_kernel(terms_ref, home_ref, near_select_ref, came_ref, own_ref, near_ref):
@@ -370,14 +408,15 @@
 
     code = coded(list_slot, list_class, list_count)
     mate_code = to_mate(code)
-    near_codes = to_near(jnp.concatenate([code, mate_code], axis=0))
 
     operators = jnp.transpose(translate, (1, 0, 2))
     if halves:
         windows = half_windows(rows, depth, 2)
-        own_check = lax.optimization_barrier((up_check, mate_code))[0]
-        equivalent = joined_product(up_inverse, own_check, across_sub(up_check))
+        got = near_or_mates_far(code)
+        equivalent = joined_product(up_inverse, up_check, across_sub(up_check))
         other = across_sub(equivalent)
+        got, _ = lax.optimization_barrier((got, equivalent))
+        crossed = crosswise(got)
     else:
         windows = [(0, depth, 0)]
         equivalent = lax.all_gather(
@@ -388,11 +427,19 @@
             "sub", axis=0, tiled=True,
         )
         other = equivalent
-    product, home, mate_select = prepare(operators, equivalent, code, mate_code, windows)
-    near_codes, product = lax.optimization_barrier((near_codes, product))
-    near_select, far_select = selections(near_codes, classes)
+        near_codes = to_near(jnp.concatenate([code, mate_code], axis=0))
+        got, crossed = near_codes[:entries], near_codes[entries:]
+
+    parts = chunks(rows, CHUNK)
+    half = pl.cdiv(len(parts), 2)
+    low, home = prepare(operators, equivalent, code, windows, parts[:half], 0)
+    crossed, low = lax.optimization_barrier((crossed, low))
+    swapped = to_mate(jnp.concatenate([got, crossed], axis=0))
+    high, mate_select = prepare(operators, equivalent, mate_code, windows, parts[half:], 1)
+    swapped, high = lax.optimization_barrier((swapped, high))
+    near_select, far_select, mate_near = selections(got, crossed, swapped, classes, halves)
     terms, mate_sum, far_sum = push_away(
-        operators, product, other, mate_select, far_select, to_mate(near_codes[:entries]),
+        operators, low, high, other, mate_select, far_select, mate_near,
         windows if halves else [],
     )
     mate_came = to_mate(mate_sum)

time: 31.8 us -> 33.3 us (1.047)
  waiting for transfers between devices: 9.78 us -> 11.8 us
  starting transfers between devices: 14.5 us -> 13.9 us
    ppermute x0 -> x2, starting transfers between devices: none -> 4.03 us  [the longest x1 3.53 us: near_or_mates_far(): return lax.ppermute(value, ('tile', 'sub'), pairs)]
    ppermute x2 -> x1, starting transfers between devices: 6.3 us -> 3.06 us  [to_near(): lax.ppermute(value, 'tile', [(a, b) for a, b in pairs if 0 <= b < count])]
    ppermute x0 -> x2, waiting for transfers between devices: none -> 3.15 us  [the longest x1 1.78 us: crosswise(): return lax.ppermute(value, ('tile', 'sub'), pairs)]
    ppermute x3, starting transfers between devices: 4.66 us -> 2.82 us  [across_sub(): return lax.ppermute(shard, 'sub', [(0, 1), (1, 0)])]
    ppermute x3, waiting for transfers between devices: 0.69 us -> 0.01 us  [to_mate(): return lax.ppermute(value, 'tile', pairs)]
    ppermute x3, waiting for transfers between devices: 5.21 us -> 4.54 us  [across_sub(): return lax.ppermute(shard, 'sub', [(0, 1), (1, 0)])]
    ppermute x3, starting transfers between devices: 0.21 us -> 0.73 us  [to_mate(): return lax.ppermute(value, 'tile', pairs)]
    pallas_call x2 -> x3, Pallas kernels: 2.01 us -> 2.39 us  [the longest x2 1.71 us: prepare(): pl.pallas_call(functools.partial(prepare_kernel, windows, part, distance)...]
  transfers between devices with their start and end apart: 9 -> 10, of which waited for: 6 -> 5; matrix products, arithmetic and copies ran while one was open for 0% -> 0% of each run, Pallas kernels for 10% -> 13%
where the time goes in v10:
time: 33.3 us; the launch traced here: 33.1 us
  starting transfers between devices  13.9 us (42%)
  waiting for transfers between devices  11.8 us (35%)
  Pallas kernels  7.3 us (22%)
    ppermute x3, waiting for transfers between devices, across_sub(): return lax.ppermute(shard, 'sub', [(0, 1), (1, 0)])  4.54 us
    ppermute x1, starting transfers between devices, near_or_mates_far(): return lax.ppermute(value, ('tile', 'sub'), pairs)  3.53 us
    ppermute x1, starting transfers between devices, to_far(): lax.ppermute(value, 'tile', [(a, b) for a, b in pairs if 0 <= b < count])  3.23 us
    ppermute x1, starting transfers between devices, to_near(): lax.ppermute(value, 'tile', [(a, b) for a, b in pairs if 0 <= b < count])  3.06 us
    ppermute x1, waiting for transfers between devices, to_near(): lax.ppermute(value, 'tile', [(a, b) for a, b in pairs if 0 <= b < count])  2.88 us
    ppermute x3, starting transfers between devices, across_sub(): return lax.ppermute(shard, 'sub', [(0, 1), (1, 0)])  2.82 us
    pallas_call x1, Pallas kernels, push_away(): pl.pallas_call(functools.partial(push_away_kernel, windows), out_shape=[j...  1.96 us
    ppermute x1, waiting for transfers between devices, crosswise(): return lax.ppermute(value, ('tile', 'sub'), pairs)  1.78 us
  transfers between devices with their start and end apart: 10, of which 5 were waited for; matrix products, arithmetic and copies ran while one was open for 0% of the time, Pallas kernels for 13%

profile of v10, /device:TPU:8, one launch (start us, length us, event | category | flops | bytes accessed | tf_op | source)
XLA Modules:
  0.0 33.1 jit_solution(13940701985261782713)
XLA Ops:
  0.0 1.5 %collective-permute-start.1 = (bf16[444,128]{1,0:T(8,128)(2,1)}, bf16[444,128]{1,0:T(8,128)(2,1)S(1)}, u32[]{:S(2)}, u32[]{:S(2)}) collective-permute-start(bf16[444,128]{1,0:T(8,128)(2,1)} %own_ref.1), channel_id=1, source_target_pairs={{0,1},{1,0},{2,3},{3,2},{4,5},{5,4},{6,7},{7,6},{8,9},{9,8},{10,11... | collective-permute-start | bytes 341000 | tf_op jit(solution)/shard_map/ppermute | solution.py:18
  1.5 0.0 copy-start.2
  1.5 0.0 copy-start.3
  1.5 0.0 copy-start
  1.5 0.9 %code.1.code_ref = s32[8,128]{1,0:T(8,128)S(1)} custom-call(s32[8,128]{1,0:T(8,128)} %bitcast.7, s32[8,128]{1,0:T(8,128)} %bitcast.8, s32[1,128]{1,0:T(1,128)} %bitcast.9), custom_call_target="tpu_custom_call" | custom-call | flops 8589934592 | tf_op jit(solution)/shard_map/code/pallas_call | solution.py:103
  2.4 0.1 collective-permute-start.4
  2.5 3.5 %collective-permute-start = (s32[8,128]{1,0:T(8,128)S(1)}, s32[8,128]{1,0:T(8,128)S(1)}, u32[]{:S(2)}, u32[]{:S(2)}) collective-permute-start(s32[8,128]{1,0:T(8,128)S(1)} %code.1.code_ref), channel_id=1, source_target_pairs={{1,7},{2,4},{4,2},{5,11},{6,8},{7,1},{8,6},{9,15},{10,12},{11,5},{... | collective-permute-start | bytes 12296 | tf_op jit(solution)/shard_map/ppermute | solution.py:47
  6.0 0.0 collective-permute-done.1.other_ref
  6.0 0.0 copy-done.2
  6.0 0.0 copy-done.3
  6.0 0.4 %joined.1.own_ref = bf16[444,128]{1,0:T(8,128)(2,1)S(1)} custom-call(bf16[444,888]{1,0:T(8,128)(2,1)S(1)} %copy-done.2, bf16[444,128]{1,0:T(8,128)(2,1)S(1)} %copy-done.3, bf16[444,128]{1,0:T(8,128)(2,1)S(1)} %collective-permute-done.1.other_ref), custom_call_target="tpu_custom_call" | custom-call | flops 100933632 | bytes 788544 | tf_op jit(solution)/shard_map/joined/pallas_call | solution.py:132
  6.5 0.7 %collective-permute-start.5 = (bf16[444,128]{1,0:T(8,128)(2,1)S(1)}, bf16[444,128]{1,0:T(8,128)(2,1)S(1)}, u32[]{:S(2)}, u32[]{:S(2)}) collective-permute-start(bf16[444,128]{1,0:T(8,128)(2,1)S(1)} %joined.1.own_ref), channel_id=1, source_target_pairs={{0,1},{1,0},{2,3},{3,2},{4,5},{5,4},{6,7},{7,6},{8,9},{9,8},{10,11... | collective-permute-start | bytes 341000 | tf_op jit(solution)/shard_map/ppermute | solution.py:18
  7.2 1.4 %collective-permute-done.got_ref = s32[8,128]{1,0:T(8,128)S(1)} collective-permute-done((s32[8,128]{1,0:T(8,128)S(1)}, s32[8,128]{1,0:T(8,128)S(1)}, u32[]{:S(2)}, u32[]{:S(2)}) %collective-permute-start) | collective-permute-done | bytes 4128 | tf_op jit(solution)/shard_map/ppermute | solution.py:47
  8.6 0.5 %collective-permute-start.2 = (s32[8,128]{1,0:T(8,128)S(1)}, s32[8,128]{1,0:T(8,128)S(1)}, u32[]{:S(2)}, u32[]{:S(2)}) collective-permute-start(s32[8,128]{1,0:T(8,128)S(1)} %collective-permute-done.got_ref), channel_id=1, source_target_pairs={{0,3},{1,2},{2,1},{3,0},{4,7},{5,6},{6,5},{7,4},{8,11},{9,10},{10,... | collective-permute-start | bytes 12296 | tf_op jit(solution)/shard_map/ppermute | solution.py:56
  9.1 0.0 copy-done
  9.1 0.9 %prepare.2 = (f32[1792,128]{1,0:T(8,128)S(1)}, bf16[1024,128]{1,0:T(8,128)(2,1)S(1)}) custom-call(bf16[444,8,888]{2,1,0:T(8,128)(2,1)S(1)} %bitcast.4, bf16[444,128]{1,0:T(8,128)(2,1)S(1)} %joined.1.own_ref, s32[8,128]{1,0:T(8,128)S(1)} %code.1.code_ref), custom_call_target="tpu_custom_call" | custom-call | flops 4294967296 | tf_op jit(solution)/shard_map/prepare/pallas_call | solution.py:254
  9.9 1.8 %collective-permute-done.2.crossed_ref = s32[8,128]{1,0:T(8,128)S(1)} collective-permute-done((s32[8,128]{1,0:T(8,128)S(1)}, s32[8,128]{1,0:T(8,128)S(1)}, u32[]{:S(2)}, u32[]{:S(2)}) %collective-permute-start.2) | collective-permute-done | bytes 4128 | tf_op jit(solution)/shard_map/ppermute | solution.py:56
  11.7 0.3 collective-permute-start.3
  12.0 0.0 collective-permute-done.4.code_ref
  12.0 0.9 %prepare.3 = (f32[1760,128]{1,0:T(8,128)S(1)}, bf16[1024,128]{1,0:T(8,128)(2,1)S(1)}) custom-call(bf16[444,8,888]{2,1,0:T(8,128)(2,1)S(1)} %bitcast.5, bf16[444,128]{1,0:T(8,128)(2,1)S(1)} %joined.1.own_ref, s32[8,128]{1,0:T(8,128)S(1)} %collective-permute-done.4.code_ref), custom_call_target="tpu_custom_call" | custom-call | flops 4294967296 | tf_op jit(solution)/shard_map/prepare/pallas_call | solution.py:254
  12.9 0.0 copy-start.1
  12.9 0.0 collective-permute-done.3.swapped_ref
  12.9 0.7 %selections.1 = (bf16[1024,128]{1,0:T(8,128)(2,1)S(1)}, bf16[1024,128]{1,0:T(8,128)(2,1)S(1)}, bf16[1024,128]{1,0:T(8,128)(2,1)S(1)}) custom-call(s32[8,128]{1,0:T(8,128)S(1)} %collective-permute-done.got_ref, s32[8,128]{1,0:T(8,128)S(1)} %collective-permute-done.2.crossed_ref, s32[16,128]{1,0:T(8,128)S(1)} %collective-permute-done.3.swapped_ref), custom_call_target="tpu_custom_call" | custom-call | flops 1048576 | tf_op jit(solution)/shard_map/selections/pallas_call | solution.py:291
  13.6 0.0 collective-permute-done.5.other_ref
  13.6 2.0 %push_away.1 = (bf16[444,1024]{1,0:T(8,128)(2,1)S(1)}, bf16[444,256]{1,0:T(8,128)(2,1)S(1)}, bf16[444,128]{1,0:T(8,128)(2,1)S(1)}) custom-call(bf16[444,8,888]{2,1,0:T(8,128)(2,1)S(1)} %bitcast.6, f32[1792,128]{1,0:T(8,128)S(1)} %get-tuple-element.24.low_ref, f32[1760,128]{1,0:T(8,128)S(1)} %get-tuple-element.27.high_ref, ...), custom_call_target="tpu_custom_call" | custom-call | flops 814743552 | bytes 6308352 | tf_op jit(solution)/shard_map/push_away/pallas_call | solution.py:353
  15.6 0.3 %collective-permute-start.6 = (bf16[444,256]{1,0:T(8,128)(2,1)S(1)}, bf16[444,256]{1,0:T(8,128)(2,1)S(1)}, u32[]{:S(2)}, u32[]{:S(2)}) collective-permute-start(bf16[444,256]{1,0:T(8,128)(2,1)S(1)} %get-tuple-element.35), channel_id=1, source_target_pairs={{0,2},{2,0},{4,6},{6,4},{8,10},{10,8},{12,14},{14,12},{16,18},{18,... | collective-permute-start | bytes 681992 | tf_op jit(solution)/shard_map/ppermute | solution.py:24
  15.9 3.2 %collective-permute-start.7 = (bf16[444,128]{1,0:T(8,128)(2,1)S(1)}, bf16[444,128]{1,0:T(8,128)(2,1)S(1)}, u32[]{:S(2)}, u32[]{:S(2)}) collective-permute-start(bf16[444,128]{1,0:T(8,128)(2,1)S(1)} %get-tuple-element.37), channel_id=1, source_target_pairs={{2,6},{4,0},{6,10},{8,4},{10,14},{12,8},{14,18},{16,12},{18,22},{2... | collective-permute-start | bytes 341000 | tf_op jit(solution)/shard_map/ppermute | solution.py:36
  19.2 0.0 collective-permute-done.6.came_ref
  19.2 0.4 %push_home.1 = (f32[444,128]{1,0:T(8,128)S(1)}, bf16[444,128]{1,0:T(8,128)(2,1)S(1)}) custom-call(bf16[444,1024]{1,0:T(8,128)(2,1)S(1)} %get-tuple-element.32.terms_ref, bf16[1024,128]{1,0:T(8,128)(2,1)S(1)} %get-tuple-element.33.home_ref, bf16[1024,128]{1,0:T(8,128)(2,1)S(1)} %get-tuple-element.34.near_select_ref, ...), custom_call_target="tpu_custom_call" | custom-call | flops 232783872 | bytes 1818624 | tf_op jit(solution)/shard_map/push_home/pallas_call | solution.py:388
  19.6 3.1 %collective-permute-start.8 = (bf16[444,128]{1,0:T(8,128)(2,1)S(1)}, bf16[444,128]{1,0:T(8,128)(2,1)S(1)}, u32[]{:S(2)}, u32[]{:S(2)}) collective-permute-start(bf16[444,128]{1,0:T(8,128)(2,1)S(1)} %get-tuple-element.38), channel_id=1, source_target_pairs={{2,4},{4,2},{6,8},{8,6},{10,12},{12,10},{14,16},{16,14},{18,20},{2... | collective-permute-start | bytes 341000 | tf_op jit(solution)/shard_map/ppermute | solution.py:30
  22.6 1.2 %collective-permute-done.7 = bf16[444,128]{1,0:T(8,128)(2,1)S(1)} collective-permute-done((bf16[444,128]{1,0:T(8,128)(2,1)S(1)}, bf16[444,128]{1,0:T(8,128)(2,1)S(1)}, u32[]{:S(2)}, u32[]{:S(2)}) %collective-permute-start.7) | collective-permute-done | bytes 113696 | tf_op jit(solution)/shard_map/ppermute | solution.py:36
  23.8 2.9 %collective-permute-done.8 = bf16[444,128]{1,0:T(8,128)(2,1)S(1)} collective-permute-done((bf16[444,128]{1,0:T(8,128)(2,1)S(1)}, bf16[444,128]{1,0:T(8,128)(2,1)S(1)}, u32[]{:S(2)}, u32[]{:S(2)}) %collective-permute-start.8) | collective-permute-done | bytes 113696 | tf_op jit(solution)/shard_map/ppermute | solution.py:30
  26.8 0.6 %collective-permute-start.9 = (bf16[444,128]{1,0:T(8,128)(2,1)S(1)}, bf16[444,128]{1,0:T(8,128)(2,1)S(1)}, u32[]{:S(2)}, u32[]{:S(2)}) collective-permute-start(bf16[444,128]{1,0:T(8,128)(2,1)S(1)} %add_convert_fusion.own_ref), channel_id=1, source_target_pairs={{0,1},{1,0},{2,3},{3,2},{4,5},{5,4},{6,7},{7,6},{8,9},{9,8},{10,11... | collective-permute-start | bytes 341000 | tf_op jit(solution)/shard_map/ppermute | solution.py:18
  27.4 0.0 copy-done.1
  27.4 0.3 first.1.part_ref
  27.7 4.5 %collective-permute-done.9.other_ref = bf16[444,128]{1,0:T(8,128)(2,1)S(1)} collective-permute-done((bf16[444,128]{1,0:T(8,128)(2,1)S(1)}, bf16[444,128]{1,0:T(8,128)(2,1)S(1)}, u32[]{:S(2)}, u32[]{:S(2)}) %collective-permute-start.9) | collective-permute-done | bytes 113696 | tf_op jit(solution)/shard_map/ppermute | solution.py:18
  32.2 1.0 %rest.1 = bf16[444,128]{1,0:T(8,128)(2,1)} custom-call(bf16[444,888]{1,0:T(8,128)(2,1)S(1)} %copy-done.1, f32[444,128]{1,0:T(8,128)S(1)} %first.1.part_ref, bf16[444,128]{1,0:T(8,128)(2,1)S(1)} %collective-permute-done.9.other_ref), custom_call_target="tpu_custom_call" | custom-call | flops 58195968 | bytes 454656 | tf_op jit(solution)/shard_map/rest/pallas_call | solution.py:193
  (2 shorter events, 0.1 us)
Async XLA Ops:
  0.0 6.0 %collective-permute-start.1 = (bf16[444,128]{1,0:T(8,128)(2,1)}, bf16[444,128]{1,0:T(8,128)(2,1)S(1)}, u32[]{:S(2)}, u32[]{:S(2)}) collective-permute-start(bf16[444,128]{1,0:T(8,128)(2,1)} %own_ref.1), channel_id=1, source_target_pairs={{0,1},{1,0},{2,3},{3,2},{4,5},{5,4},{6,7},{7,6},{8,9},{9,8},{10,11... | collective-permute-start | bytes 341000 | tf_op jit(solution)/shard_map/ppermute | solution.py:18
  1.5 4.5 %copy-start.2 = (bf16[444,888]{1,0:T(8,128)(2,1)S(1)}, bf16[444,888]{1,0:T(8,128)(2,1)}, u32[]{:S(2)}) copy-start(bf16[444,888]{1,0:T(8,128)(2,1)} %matrix_ref.3) | copy-start | bytes 2365636
  1.5 4.5 %copy-start.3 = (bf16[444,128]{1,0:T(8,128)(2,1)S(1)}, bf16[444,128]{1,0:T(8,128)(2,1)}, u32[]{:S(2)}) copy-start(bf16[444,128]{1,0:T(8,128)(2,1)} %own_ref.1) | copy-start | bytes 340996
  1.5 7.6 %copy-start = (bf16[8,444,888]{2,0,1:T(8,128)(2,1)S(1)}, bf16[8,444,888]{2,0,1:T(8,128)(2,1)}, u32[]{:S(2)}) copy-start(bf16[8,444,888]{2,0,1:T(8,128)(2,1)} %param.9) | copy-start | bytes 18925060
  2.4 9.6 %collective-permute-start.4 = (s32[8,128]{1,0:T(8,128)S(1)}, s32[8,128]{1,0:T(8,128)S(1)}, u32[]{:S(2)}, u32[]{:S(2)}) collective-permute-start(s32[8,128]{1,0:T(8,128)S(1)} %code.1.code_ref), channel_id=1, source_target_pairs={{0,2},{2,0},{4,6},{6,4},{8,10},{10,8},{12,14},{14,12},{16,18},{18,... | collective-permute-start | bytes 12296 | tf_op jit(solution)/shard_map/ppermute | solution.py:24
  2.5 6.1 %collective-permute-start = (s32[8,128]{1,0:T(8,128)S(1)}, s32[8,128]{1,0:T(8,128)S(1)}, u32[]{:S(2)}, u32[]{:S(2)}) collective-permute-start(s32[8,128]{1,0:T(8,128)S(1)} %code.1.code_ref), channel_id=1, source_target_pairs={{1,7},{2,4},{4,2},{5,11},{6,8},{7,1},{8,6},{9,15},{10,12},{11,5},{... | collective-permute-start | bytes 12296 | tf_op jit(solution)/shard_map/ppermute | solution.py:47
  6.5 7.1 %collective-permute-start.5 = (bf16[444,128]{1,0:T(8,128)(2,1)S(1)}, bf16[444,128]{1,0:T(8,128)(2,1)S(1)}, u32[]{:S(2)}, u32[]{:S(2)}) collective-permute-start(bf16[444,128]{1,0:T(8,128)(2,1)S(1)} %joined.1.own_ref), channel_id=1, source_target_pairs={{0,1},{1,0},{2,3},{3,2},{4,5},{5,4},{6,7},{7,6},{8,9},{9,8},{10,11... | collective-permute-start | bytes 341000 | tf_op jit(solution)/shard_map/ppermute | solution.py:18
  8.6 3.1 %collective-permute-start.2 = (s32[8,128]{1,0:T(8,128)S(1)}, s32[8,128]{1,0:T(8,128)S(1)}, u32[]{:S(2)}, u32[]{:S(2)}) collective-permute-start(s32[8,128]{1,0:T(8,128)S(1)} %collective-permute-done.got_ref), channel_id=1, source_target_pairs={{0,3},{1,2},{2,1},{3,0},{4,7},{5,6},{6,5},{7,4},{8,11},{9,10},{10,... | collective-permute-start | bytes 12296 | tf_op jit(solution)/shard_map/ppermute | solution.py:56
  11.7 1.2 %collective-permute-start.3 = (s32[16,128]{1,0:T(8,128)S(1)}, s32[16,128]{1,0:T(8,128)S(1)}, u32[]{:S(2)}, u32[]{:S(2)}) collective-permute-start(s32[16,128]{1,0:T(8,128)S(1)} %pad_add_fusion), channel_id=1, source_target_pairs={{0,2},{2,0},{4,6},{6,4},{8,10},{10,8},{12,14},{14,12},{16,18},{18,... | collective-permute-start | bytes 24584 | tf_op jit(solution)/shard_map/ppermute | solution.py:24
  12.9 14.5 %copy-start.1 = (bf16[444,888]{1,0:T(8,128)(2,1)S(1)}, bf16[444,888]{1,0:T(8,128)(2,1)}, u32[]{:S(2)}) copy-start(bf16[444,888]{1,0:T(8,128)(2,1)} %matrix_ref.5) | copy-start | bytes 2365636
  15.6 3.6 %collective-permute-start.6 = (bf16[444,256]{1,0:T(8,128)(2,1)S(1)}, bf16[444,256]{1,0:T(8,128)(2,1)S(1)}, u32[]{:S(2)}, u32[]{:S(2)}) collective-permute-start(bf16[444,256]{1,0:T(8,128)(2,1)S(1)} %get-tuple-element.35), channel_id=1, source_target_pairs={{0,2},{2,0},{4,6},{6,4},{8,10},{10,8},{12,14},{14,12},{16,18},{18,... | collective-permute-start | bytes 681992 | tf_op jit(solution)/shard_map/ppermute | solution.py:24
  15.9 7.9 %collective-permute-start.7 = (bf16[444,128]{1,0:T(8,128)(2,1)S(1)}, bf16[444,128]{1,0:T(8,128)(2,1)S(1)}, u32[]{:S(2)}, u32[]{:S(2)}) collective-permute-start(bf16[444,128]{1,0:T(8,128)(2,1)S(1)} %get-tuple-element.37), channel_id=1, source_target_pairs={{2,6},{4,0},{6,10},{8,4},{10,14},{12,8},{14,18},{16,12},{18,22},{2... | collective-permute-start | bytes 341000 | tf_op jit(solution)/shard_map/ppermute | solution.py:36
  19.6 7.1 %collective-permute-start.8 = (bf16[444,128]{1,0:T(8,128)(2,1)S(1)}, bf16[444,128]{1,0:T(8,128)(2,1)S(1)}, u32[]{:S(2)}, u32[]{:S(2)}) collective-permute-start(bf16[444,128]{1,0:T(8,128)(2,1)S(1)} %get-tuple-element.38), channel_id=1, source_target_pairs={{2,4},{4,2},{6,8},{8,6},{10,12},{12,10},{14,16},{16,14},{18,20},{2... | collective-permute-start | bytes 341000 | tf_op jit(solution)/shard_map/ppermute | solution.py:30
  26.8 5.4 %collective-permute-start.9 = (bf16[444,128]{1,0:T(8,128)(2,1)S(1)}, bf16[444,128]{1,0:T(8,128)(2,1)S(1)}, u32[]{:S(2)}, u32[]{:S(2)}) collective-permute-start(bf16[444,128]{1,0:T(8,128)(2,1)S(1)} %add_convert_fusion.own_ref), channel_id=1, source_target_pairs={{0,1},{1,0},{2,3},{3,2},{4,5},{5,4},{6,7},{7,6},{8,9},{9,8},{10,11... | collective-permute-start | bytes 341000 | tf_op jit(solution)/shard_map/ppermute | solution.py:18

commit v11 on v10

--- a/solution.py
+++ b/solution.py
@@ -34,26 +34,6 @@
     count = lax.axis_size("tile")
     pairs = [(t, t + 4 * (t % 2) - 2) for t in range(count)]
     return lax.ppermute(value, "tile", [(a, b) for a, b in pairs if 0 <= b < count])
-
-
-def near_or_mates_far(value):
-    count = lax.axis_size("tile")
-    pairs = []
-    for t in range(count):
-        step = 2 * (t % 2) - 1
-        for index, target in ((0, t + step), (1, t - 3 * step)):
-            if 0 <= target < count:
-                pairs.append((2 * t + index, 2 * target + index))
-    return lax.ppermute(value, ("tile", "sub"), pairs)
-
-
-def crosswise(value):
-    count = lax.axis_size("tile")
-    pairs = [
-        (2 * t + index, 2 * (t ^ 1) + 1 - index)
-        for t in range(count) for index in range(2) if t ^ 1 < count
-    ]
-    return lax.ppermute(value, ("tile", "sub"), pairs)
 
 
 def away():
@@ -79,38 +59,6 @@
     for i, ref in enumerate(refs):
         rows, cells = ref.shape
         padded[offset : offset + rows, i * cells : (i + 1) * cells] = ref[...].astype(padded.dtype)
-
-
-def code_kernel(slot_ref, class_ref, count_ref, code_ref, slots, classes, counts, sems):
-    copies = [
-        pltpu.make_async_copy(source, target, sems.at[i])
-        for i, (source, target) in enumerate(
-            ((slot_ref, slots), (class_ref, classes), (count_ref, counts))
-        )
-    ]
-    for copy in copies:
-        copy.start()
-    for copy in copies:
-        copy.wait()
-    entry = lax.broadcasted_iota(jnp.int32, code_ref.shape, 0)
-    code_ref[...] = jnp.where(
-        entry < counts[...], (classes[...] << CLASS_SHIFT) + slots[...], -1
-    )
-
-
-def coded(list_slot, list_class, list_count):
-    operands = (list_slot.T, list_class.T, list_count[None, :])
-    return pl.pallas_call(
-        code_kernel,
-        out_shape=jax.ShapeDtypeStruct(operands[0].shape, jnp.int32),
-        in_specs=[pl.BlockSpec(memory_space=pltpu.HBM)] * 3,
-        out_specs=WHOLE,
-        scratch_shapes=[pltpu.VMEM(x.shape, x.dtype) for x in operands]
-        + [pltpu.SemaphoreType.DMA((3,))],
-        cost_estimate=pl.CostEstimate(flops=1 << 33, bytes_accessed=0, transcendentals=0),
-        compiler_params=pltpu.CompilerParams(vmem_limit_bytes=4 << 20),
-        name="code",
-    )(*[pltpu.with_memory_space_constraint(x, pltpu.HBM) for x in operands])
 
 
 def joined_kernel(matrix_ref, own_ref, other_ref, out_ref, joined):
@@ -223,11 +171,9 @@
 
 
 def prepare_kernel(
-    windows, part, distance, operators_ref, own_ref, code_ref, product_ref, select_ref, padded
+    windows, part, operators_ref, own_ref, product_ref, padded
 ):
     classes = operators_ref.shape[1]
-    cells = own_ref.shape[1]
-    build_select(code_ref[...], (REACH + distance * away()) * cells, select_ref, 0, classes)
 
     for index, (low, high, offset) in enumerate(windows):
         def run(low=low, high=high, offset=offset):
@@ -246,57 +192,64 @@
             pl.when(lax.axis_index("sub") == index)(run)
 
 
-def prepare(operators, own, code, windows, part, distance):
+def prepare(operators, own, windows, part):
     classes = operators.shape[1]
     cells = own.shape[1]
     span = max(high - low for low, high, _ in windows)
     rows = sum(size for _, size in part)
     return pl.pallas_call(
-        functools.partial(prepare_kernel, windows, part, distance),
-        out_shape=[
-            jax.ShapeDtypeStruct((rows * classes, cells), jnp.float32),
-            jax.ShapeDtypeStruct((classes * cells, cells), jnp.bfloat16),
-        ],
-        in_specs=[WHOLE] * 3,
-        out_specs=[WHOLE] * 2,
+        functools.partial(prepare_kernel, windows, part),
+        out_shape=jax.ShapeDtypeStruct((rows * classes, cells), jnp.float32),
+        in_specs=[WHOLE] * 2,
+        out_specs=WHOLE,
         scratch_shapes=[pltpu.VMEM((span, cells), jnp.float32)],
         cost_estimate=pl.CostEstimate(flops=1 << 32, bytes_accessed=0, transcendentals=0),
         compiler_params=pltpu.CompilerParams(vmem_limit_bytes=24 << 20),
         name="prepare",
-    )(operators, own, code)
-
-
-def select_kernel(
-    halves, got_ref, crossed_ref, swapped_ref, near_select_ref, far_select_ref, mate_near_ref
-):
-    entries, cells = got_ref.shape
-    classes = near_select_ref.shape[0] // cells
+    )(operators, own)
+
+
+def home_kernel(code_ref, out_ref):
+    cells = code_ref.shape[1]
+    build_select(code_ref[...], REACH * cells, out_ref, 0, out_ref.shape[0] // cells)
+
+
+def home_selection(code, classes):
+    cells = code.shape[1]
+    return pl.pallas_call(
+        home_kernel,
+        out_shape=jax.ShapeDtypeStruct((classes * cells, cells), jnp.bfloat16),
+        in_specs=[WHOLE],
+        out_specs=WHOLE,
+        cost_estimate=pl.CostEstimate(flops=1 << 31, bytes_accessed=0, transcendentals=0),
+        compiler_params=pltpu.CompilerParams(vmem_limit_bytes=8 << 20),
+        name="home",
+    )(code)
+
+
+def select_kernel(mate_ref, near_ref, mate_near_ref, *select_refs):
+    entries, cells = mate_ref.shape
     step = away()
-    got, crossed = got_ref[...], crossed_ref[...]
-    low, high = swapped_ref[:entries, :], swapped_ref[entries:, :]
-    near, far, mate_near = got, crossed, low
-    if halves:
-        first = lax.axis_index("sub") == 0
-        near = jnp.where(first, near, high)
-        far = jnp.where(first, far, low)
-        mate_near = jnp.where(first, mate_near, crossed)
-    build_select(near, (REACH - step) * cells, near_select_ref, 0, classes)
-    build_select(far, (REACH - 2 * step) * cells, far_select_ref, 0, classes)
-    build_select(mate_near, (REACH + 2 * step) * cells, mate_near_ref, 0, classes)
-
-
-def selections(got, crossed, swapped, classes, halves):
-    cells = got.shape[1]
+    for ref, code, distance in zip(
+        select_refs,
+        (mate_ref[...], near_ref[:entries, :], near_ref[entries:, :], mate_near_ref[...]),
+        (-step, step, 2 * step, -2 * step),
+    ):
+        build_select(code, (REACH - distance) * cells, ref, 0, ref.shape[0] // cells)
+
+
+def selections(mate_code, near_codes, mate_near_code, classes):
+    cells = mate_code.shape[1]
     select = jax.ShapeDtypeStruct((classes * cells, cells), jnp.bfloat16)
     return pl.pallas_call(
-        functools.partial(select_kernel, halves),
-        out_shape=[select] * 3,
+        select_kernel,
+        out_shape=[select] * 4,
         in_specs=[WHOLE] * 3,
-        out_specs=[WHOLE] * 3,
+        out_specs=[WHOLE] * 4,
         cost_estimate=pl.CostEstimate(flops=1 << 20, bytes_accessed=0, transcendentals=0),
         compiler_params=pltpu.CompilerParams(vmem_limit_bytes=8 << 20),
         name="selections",
-    )(got, crossed, swapped)
+    )(mate_code, near_codes, mate_near_code)
 
 
 def push_away_kernel(
@@ -406,17 +359,16 @@
     cells, entries = list_slot.shape
     halves = lax.axis_size("sub") == 2
 
-    code = coded(list_slot, list_class, list_count)
-    mate_code = to_mate(code)
+    active = lax.broadcasted_iota(jnp.int32, (entries, cells), 0) < list_count[None, :]
+    code = jnp.where(active, (list_class.T << CLASS_SHIFT) + list_slot.T, -1)
+    mate_code, home = lax.optimization_barrier((to_mate(code), home_selection(code, classes)))
+    near_codes = to_near(jnp.concatenate([code, mate_code], axis=0))
 
     operators = jnp.transpose(translate, (1, 0, 2))
     if halves:
         windows = half_windows(rows, depth, 2)
-        got = near_or_mates_far(code)
         equivalent = joined_product(up_inverse, up_check, across_sub(up_check))
         other = across_sub(equivalent)
-        got, _ = lax.optimization_barrier((got, equivalent))
-        crossed = crosswise(got)
     else:
         windows = [(0, depth, 0)]
         equivalent = lax.all_gather(
@@ -427,17 +379,17 @@
             "sub", axis=0, tiled=True,
         )
         other = equivalent
-        near_codes = to_near(jnp.concatenate([code, mate_code], axis=0))
-        got, crossed = near_codes[:entries], near_codes[entries:]
 
     parts = chunks(rows, CHUNK)
     half = pl.cdiv(len(parts), 2)
-    low, home = prepare(operators, equivalent, code, windows, parts[:half], 0)
-    crossed, low = lax.optimization_barrier((crossed, low))
-    swapped = to_mate(jnp.concatenate([got, crossed], axis=0))
-    high, mate_select = prepare(operators, equivalent, mate_code, windows, parts[half:], 1)
-    swapped, high = lax.optimization_barrier((swapped, high))
-    near_select, far_select, mate_near = selections(got, crossed, swapped, classes, halves)
+    low = prepare(operators, equivalent, windows, parts[:half])
+    near_codes, low = lax.optimization_barrier((near_codes, low))
+    mate_near_code = to_mate(near_codes[:entries])
+    high = prepare(operators, equivalent, windows, parts[half:])
+    mate_near_code, high = lax.optimization_barrier((mate_near_code, high))
+    mate_select, near_select, far_select, mate_near = selections(
+        mate_code, near_codes, mate_near_code, classes
+    )
     terms, mate_sum, far_sum = push_away(
         operators, low, high, other, mate_select, far_select, mate_near,
         windows if halves else [],

time: 33.3 us -> 31.7 us (0.952)
  waiting for transfers between devices: 11.8 us -> 9.55 us
  Pallas kernels: 7.3 us -> 6.4 us
  other arithmetic: 0.05 us -> 0.9 us
  starting transfers between devices: 13.9 us -> 14.5 us
    ppermute x2 -> x0, starting transfers between devices: 4.03 us -> none  [the longest x1 3.53 us: near_or_mates_far(): return lax.ppermute(value, ('tile', 'sub'), pairs)]
    ppermute x1 -> x2, starting transfers between devices: 3.06 us -> 6.33 us  [to_near(): lax.ppermute(value, 'tile', [(a, b) for a, b in pairs if 0 <= b < count])]
    ppermute x2 -> x0, waiting for transfers between devices: 3.15 us -> none  [the longest x1 1.78 us: crosswise(): return lax.ppermute(value, ('tile', 'sub'), pairs)]
    ppermute x3, starting transfers between devices: 2.82 us -> 4.67 us  [across_sub(): return lax.ppermute(shard, 'sub', [(0, 1), (1, 0)])]
    pallas_call x4, Pallas kernels: 3.27 us -> 2.4 us  [the longest x2 1.27 us: prepare(): pl.pallas_call(functools.partial(prepare_kernel, windows, part), out_shap...]
    select_n x0 -> x1, other arithmetic: none -> 0.86 us  [shards(): code = jnp.where(active, (list_class.T << CLASS_SHIFT) + list_slot.T, -1)]
    ppermute x3, waiting for transfers between devices: 4.54 us -> 5.19 us  [across_sub(): return lax.ppermute(shard, 'sub', [(0, 1), (1, 0)])]
    ppermute x3, starting transfers between devices: 0.73 us -> 0.14 us  [to_mate(): return lax.ppermute(value, 'tile', pairs)]
  transfers between devices with their start and end apart: 10 -> 9, of which waited for: 5 -> 6; matrix products, arithmetic and copies ran while one was open for 0% -> 0% of each run, Pallas kernels for 13% -> 11%
where the time goes in v11:
time: 31.7 us; the launch traced here: 31.5 us
  starting transfers between devices  14.5 us (46%)
  waiting for transfers between devices  9.55 us (30%)
  Pallas kernels  6.4 us (20%)
  other arithmetic  0.9 us (3%)
    ppermute x2, starting transfers between devices, to_near(): lax.ppermute(value, 'tile', [(a, b) for a, b in pairs if 0 <= b < count])  6.33 us
    ppermute x3, waiting for transfers between devices, across_sub(): return lax.ppermute(shard, 'sub', [(0, 1), (1, 0)])  5.19 us
    ppermute x3, starting transfers between devices, across_sub(): return lax.ppermute(shard, 'sub', [(0, 1), (1, 0)])  4.67 us
    ppermute x1, starting transfers between devices, to_far(): lax.ppermute(value, 'tile', [(a, b) for a, b in pairs if 0 <= b < count])  3.31 us
    ppermute x2, waiting for transfers between devices, to_near(): lax.ppermute(value, 'tile', [(a, b) for a, b in pairs if 0 <= b < count])  2.95 us
    pallas_call x1, Pallas kernels, push_away(): pl.pallas_call(functools.partial(push_away_kernel, windows), out_shape=[j...  1.95 us
    pallas_call x2, Pallas kernels, prepare(): pl.pallas_call(functools.partial(prepare_kernel, windows, part), out_shap...  1.27 us
    pallas_call x1, Pallas kernels, rest(): pl.pallas_call(functools.partial(rest_kernel, windows), out_shape=jax.Sha...  0.95 us
  transfers between devices with their start and end apart: 9, of which 6 were waited for; matrix products, arithmetic and copies ran while one was open for 0% of the time, Pallas kernels for 11%

profile of v11, /device:TPU:8, one launch (start us, length us, event | category | flops | bytes accessed | tf_op | source)
XLA Modules:
  0.0 31.5 jit_solution(4092590075630997878)
XLA Ops:
  0.0 0.0 copy-start.3
  0.0 0.0 copy-start.2
  0.0 0.0 copy-start
  0.0 0.9 %bitcast_select_fusion.code_ref = s32[8,128]{1,0:T(8,128)S(1)} fusion(s32[128,8]{0,1:T(8,128)} %param.11, s32[128,8]{0,1:T(8,128)} %param.12, s32[128]{0:T(128)} %param.13), kind=kLoop, calls=%fused_computation.2 | loop fusion | flops 4096 | bytes 12800 | tf_op jit(solution)/shard_map/jit(_where)/select_n | solution.py:363
  0.9 0.0 collective-permute-start
  0.9 1.6 %collective-permute-start.2 = (bf16[444,128]{1,0:T(8,128)(2,1)}, bf16[444,128]{1,0:T(8,128)(2,1)S(1)}, u32[]{:S(2)}, u32[]{:S(2)}) collective-permute-start(bf16[444,128]{1,0:T(8,128)(2,1)} %own_ref.1), channel_id=1, source_target_pairs={{0,1},{1,0},{2,3},{3,2},{4,5},{5,4},{6,7},{7,6},{8,9},{9,8},{10,11... | collective-permute-start | bytes 341000 | tf_op jit(solution)/shard_map/ppermute | solution.py:18
  2.4 0.2 home.1.home_ref
  2.7 0.0 collective-permute-done.mate_ref
  2.7 3.1 %collective-permute-start.1 = (s32[16,128]{1,0:T(8,128)S(1)}, s32[16,128]{1,0:T(8,128)S(1)}, u32[]{:S(2)}, u32[]{:S(2)}) collective-permute-start(s32[16,128]{1,0:T(8,128)S(1)} %pad_add_fusion), channel_id=1, source_target_pairs={{2,4},{4,2},{6,8},{8,6},{10,12},{12,10},{14,16},{16,14},{18,20},{2... | collective-permute-start | bytes 24584 | tf_op jit(solution)/shard_map/ppermute | solution.py:30
  5.8 0.9 %collective-permute-done.2.other_ref = bf16[444,128]{1,0:T(8,128)(2,1)S(1)} collective-permute-done((bf16[444,128]{1,0:T(8,128)(2,1)}, bf16[444,128]{1,0:T(8,128)(2,1)S(1)}, u32[]{:S(2)}, u32[]{:S(2)}) %collective-permute-start.2) | collective-permute-done | bytes 113696 | tf_op jit(solution)/shard_map/ppermute | solution.py:18
  6.6 0.0 copy-done.3
  6.6 0.0 copy-done.2
  6.6 0.4 %joined.1.own_ref = bf16[444,128]{1,0:T(8,128)(2,1)S(1)} custom-call(bf16[444,888]{1,0:T(8,128)(2,1)S(1)} %copy-done.2, bf16[444,128]{1,0:T(8,128)(2,1)S(1)} %copy-done.3, bf16[444,128]{1,0:T(8,128)(2,1)S(1)} %collective-permute-done.2.other_ref), custom_call_target="tpu_custom_call" | custom-call | flops 100933632 | bytes 788544 | tf_op jit(solution)/shard_map/joined/pallas_call | solution.py:80
  7.1 1.6 %collective-permute-start.4 = (bf16[444,128]{1,0:T(8,128)(2,1)S(1)}, bf16[444,128]{1,0:T(8,128)(2,1)S(1)}, u32[]{:S(2)}, u32[]{:S(2)}) collective-permute-start(bf16[444,128]{1,0:T(8,128)(2,1)S(1)} %joined.1.own_ref), channel_id=1, source_target_pairs={{0,1},{1,0},{2,3},{3,2},{4,5},{5,4},{6,7},{7,6},{8,9},{9,8},{10,11... | collective-permute-start | bytes 341000 | tf_op jit(solution)/shard_map/ppermute | solution.py:18
  8.6 0.0 copy-done
  8.6 0.6 %prepare.2.low_ref = f32[1792,128]{1,0:T(8,128)S(1)} custom-call(bf16[444,8,888]{2,1,0:T(8,128)(2,1)S(1)} %bitcast.3, bf16[444,128]{1,0:T(8,128)(2,1)S(1)} %joined.1.own_ref), custom_call_target="tpu_custom_call" | custom-call | flops 4294967296 | tf_op jit(solution)/shard_map/prepare/pallas_call | solution.py:200
  9.3 0.0 collective-permute-done.1.near_ref
  9.3 0.1 collective-permute-start.3
  9.4 0.6 %prepare.3.high_ref = f32[1760,128]{1,0:T(8,128)S(1)} custom-call(bf16[444,8,888]{2,1,0:T(8,128)(2,1)S(1)} %bitcast.4, bf16[444,128]{1,0:T(8,128)(2,1)S(1)} %joined.1.own_ref), custom_call_target="tpu_custom_call" | custom-call | flops 4294967296 | tf_op jit(solution)/shard_map/prepare/pallas_call | solution.py:200
  10.0 0.0 copy-start.1
  10.0 0.5 %collective-permute-done.3.mate_near_ref = s32[8,128]{1,0:T(8,128)S(1)} collective-permute-done((s32[8,128]{1,0:T(8,128)S(1)}, s32[8,128]{1,0:T(8,128)S(1)}, u32[]{:S(2)}, u32[]{:S(2)}) %collective-permute-start.3) | collective-permute-done | bytes 4128 | tf_op jit(solution)/shard_map/ppermute | solution.py:24
  10.5 0.9 %selections.1 = (bf16[1024,128]{1,0:T(8,128)(2,1)S(1)}, bf16[1024,128]{1,0:T(8,128)(2,1)S(1)}, bf16[1024,128]{1,0:T(8,128)(2,1)S(1)}, bf16[1024,128]{1,0:T(8,128)(2,1)S(1)}) custom-call(s32[8,128]{1,0:T(8,128)S(1)} %collective-permute-done.mate_ref, s32[16,128]{1,0:T(8,128)S(1)} %collective-permute-done.1.near_ref, ...), custom_call_target="tpu_custom_call" | custom-call | flops 1048576 | tf_op jit(solution)/shard_map/selections/pallas_call | solution.py:244
  11.4 0.5 %collective-permute-done.4.other_ref = bf16[444,128]{1,0:T(8,128)(2,1)S(1)} collective-permute-done((bf16[444,128]{1,0:T(8,128)(2,1)S(1)}, bf16[444,128]{1,0:T(8,128)(2,1)S(1)}, u32[]{:S(2)}, u32[]{:S(2)}) %collective-permute-start.4) | collective-permute-done | bytes 113696 | tf_op jit(solution)/shard_map/ppermute | solution.py:18
  11.9 1.9 %push_away.1 = (bf16[444,1024]{1,0:T(8,128)(2,1)S(1)}, bf16[444,256]{1,0:T(8,128)(2,1)S(1)}, bf16[444,128]{1,0:T(8,128)(2,1)S(1)}) custom-call(bf16[444,8,888]{2,1,0:T(8,128)(2,1)S(1)} %bitcast.5, f32[1792,128]{1,0:T(8,128)S(1)} %prepare.2.low_ref, f32[1760,128]{1,0:T(8,128)S(1)} %prepare.3.high_ref, bf16[444,128]{1,0:T(8,128)(2,1)S(1)} %collective-permute-done.4.other_ref, ...), custom_call_target="tpu_custom_call" | custom-call | flops 814743552 | bytes 6308352 | tf_op jit(solution)/shard_map/push_away/pallas_call | solution.py:306
  13.9 0.1 collective-permute-start.5
  14.0 3.3 %collective-permute-start.6 = (bf16[444,128]{1,0:T(8,128)(2,1)S(1)}, bf16[444,128]{1,0:T(8,128)(2,1)S(1)}, u32[]{:S(2)}, u32[]{:S(2)}) collective-permute-start(bf16[444,128]{1,0:T(8,128)(2,1)S(1)} %get-tuple-element.33), channel_id=1, source_target_pairs={{2,6},{4,0},{6,10},{8,4},{10,14},{12,8},{14,18},{16,12},{18,22},{2... | collective-permute-start | bytes 341000 | tf_op jit(solution)/shard_map/ppermute | solution.py:36
  17.3 0.0 collective-permute-done.5.came_ref
  17.3 0.4 %push_home.1 = (f32[444,128]{1,0:T(8,128)S(1)}, bf16[444,128]{1,0:T(8,128)(2,1)S(1)}) custom-call(bf16[444,1024]{1,0:T(8,128)(2,1)S(1)} %get-tuple-element.28.terms_ref, bf16[1024,128]{1,0:T(8,128)(2,1)S(1)} %home.1.home_ref, bf16[1024,128]{1,0:T(8,128)(2,1)S(1)} %get-tuple-element.30.near_select_ref, bf16[444,256]{1,0:T(8,128)(2,1)S(1)} %collective-permute-done.5.came_ref), custom_call_target="tpu_custom_call" | custom-call | flops 232783872 | bytes 1818624 | tf_op jit(solution)/shard_map/push_home/pallas_call | solution.py:341
  17.7 3.2 %collective-permute-start.7 = (bf16[444,128]{1,0:T(8,128)(2,1)S(1)}, bf16[444,128]{1,0:T(8,128)(2,1)S(1)}, u32[]{:S(2)}, u32[]{:S(2)}) collective-permute-start(bf16[444,128]{1,0:T(8,128)(2,1)S(1)} %get-tuple-element.34), channel_id=1, source_target_pairs={{2,4},{4,2},{6,8},{8,6},{10,12},{12,10},{14,16},{16,14},{18,20},{2... | collective-permute-start | bytes 341000 | tf_op jit(solution)/shard_map/ppermute | solution.py:30
  21.0 0.9 %collective-permute-done.6 = bf16[444,128]{1,0:T(8,128)(2,1)S(1)} collective-permute-done((bf16[444,128]{1,0:T(8,128)(2,1)S(1)}, bf16[444,128]{1,0:T(8,128)(2,1)S(1)}, u32[]{:S(2)}, u32[]{:S(2)}) %collective-permute-start.6) | collective-permute-done | bytes 113696 | tf_op jit(solution)/shard_map/ppermute | solution.py:36
  21.9 2.9 %collective-permute-done.7 = bf16[444,128]{1,0:T(8,128)(2,1)S(1)} collective-permute-done((bf16[444,128]{1,0:T(8,128)(2,1)S(1)}, bf16[444,128]{1,0:T(8,128)(2,1)S(1)}, u32[]{:S(2)}, u32[]{:S(2)}) %collective-permute-start.7) | collective-permute-done | bytes 113696 | tf_op jit(solution)/shard_map/ppermute | solution.py:30
  24.9 1.6 %collective-permute-start.8 = (bf16[444,128]{1,0:T(8,128)(2,1)S(1)}, bf16[444,128]{1,0:T(8,128)(2,1)S(1)}, u32[]{:S(2)}, u32[]{:S(2)}) collective-permute-start(bf16[444,128]{1,0:T(8,128)(2,1)S(1)} %add_convert_fusion.own_ref), channel_id=1, source_target_pairs={{0,1},{1,0},{2,3},{3,2},{4,5},{5,4},{6,7},{7,6},{8,9},{9,8},{10,11... | collective-permute-start | bytes 341000 | tf_op jit(solution)/shard_map/ppermute | solution.py:18
  26.4 0.0 copy-done.1
  26.4 0.3 first.1.part_ref
  26.7 3.8 %collective-permute-done.8.other_ref = bf16[444,128]{1,0:T(8,128)(2,1)S(1)} collective-permute-done((bf16[444,128]{1,0:T(8,128)(2,1)S(1)}, bf16[444,128]{1,0:T(8,128)(2,1)S(1)}, u32[]{:S(2)}, u32[]{:S(2)}) %collective-permute-start.8) | collective-permute-done | bytes 113696 | tf_op jit(solution)/shard_map/ppermute | solution.py:18
  30.5 1.0 %rest.1 = bf16[444,128]{1,0:T(8,128)(2,1)} custom-call(bf16[444,888]{1,0:T(8,128)(2,1)S(1)} %copy-done.1, f32[444,128]{1,0:T(8,128)S(1)} %first.1.part_ref, bf16[444,128]{1,0:T(8,128)(2,1)S(1)} %collective-permute-done.8.other_ref), custom_call_target="tpu_custom_call" | custom-call | flops 58195968 | bytes 454656 | tf_op jit(solution)/shard_map/rest/pallas_call | solution.py:141
  (3 shorter events, 0.0 us)
Async XLA Ops:
  0.0 6.6 %copy-start.3 = (bf16[444,128]{1,0:T(8,128)(2,1)S(1)}, bf16[444,128]{1,0:T(8,128)(2,1)}, u32[]{:S(2)}) copy-start(bf16[444,128]{1,0:T(8,128)(2,1)} %own_ref.1) | copy-start | bytes 340996
  0.0 6.6 %copy-start.2 = (bf16[444,888]{1,0:T(8,128)(2,1)S(1)}, bf16[444,888]{1,0:T(8,128)(2,1)}, u32[]{:S(2)}) copy-start(bf16[444,888]{1,0:T(8,128)(2,1)} %matrix_ref.3) | copy-start | bytes 2365636
  0.0 8.6 %copy-start = (bf16[8,444,888]{2,0,1:T(8,128)(2,1)S(1)}, bf16[8,444,888]{2,0,1:T(8,128)(2,1)}, u32[]{:S(2)}) copy-start(bf16[8,444,888]{2,0,1:T(8,128)(2,1)} %param.9) | copy-start | bytes 18925060
  0.9 1.8 %collective-permute-start = (s32[8,128]{1,0:T(8,128)S(1)}, s32[8,128]{1,0:T(8,128)S(1)}, u32[]{:S(2)}, u32[]{:S(2)}) collective-permute-start(s32[8,128]{1,0:T(8,128)S(1)} %bitcast_select_fusion.code_ref), channel_id=1, source_target_pairs={{0,2},{2,0},{4,6},{6,4},{8,10},{10,8},{12,14},{14,12},{16,18},{18,... | collective-permute-start | bytes 12296 | tf_op jit(solution)/shard_map/ppermute | solution.py:24
  0.9 5.8 %collective-permute-start.2 = (bf16[444,128]{1,0:T(8,128)(2,1)}, bf16[444,128]{1,0:T(8,128)(2,1)S(1)}, u32[]{:S(2)}, u32[]{:S(2)}) collective-permute-start(bf16[444,128]{1,0:T(8,128)(2,1)} %own_ref.1), channel_id=1, source_target_pairs={{0,1},{1,0},{2,3},{3,2},{4,5},{5,4},{6,7},{7,6},{8,9},{9,8},{10,11... | collective-permute-start | bytes 341000 | tf_op jit(solution)/shard_map/ppermute | solution.py:18
  2.7 6.6 %collective-permute-start.1 = (s32[16,128]{1,0:T(8,128)S(1)}, s32[16,128]{1,0:T(8,128)S(1)}, u32[]{:S(2)}, u32[]{:S(2)}) collective-permute-start(s32[16,128]{1,0:T(8,128)S(1)} %pad_add_fusion), channel_id=1, source_target_pairs={{2,4},{4,2},{6,8},{8,6},{10,12},{12,10},{14,16},{16,14},{18,20},{2... | collective-permute-start | bytes 24584 | tf_op jit(solution)/shard_map/ppermute | solution.py:30
  7.1 4.9 %collective-permute-start.4 = (bf16[444,128]{1,0:T(8,128)(2,1)S(1)}, bf16[444,128]{1,0:T(8,128)(2,1)S(1)}, u32[]{:S(2)}, u32[]{:S(2)}) collective-permute-start(bf16[444,128]{1,0:T(8,128)(2,1)S(1)} %joined.1.own_ref), channel_id=1, source_target_pairs={{0,1},{1,0},{2,3},{3,2},{4,5},{5,4},{6,7},{7,6},{8,9},{9,8},{10,11... | collective-permute-start | bytes 341000 | tf_op jit(solution)/shard_map/ppermute | solution.py:18
  9.3 1.2 %collective-permute-start.3 = (s32[8,128]{1,0:T(8,128)S(1)}, s32[8,128]{1,0:T(8,128)S(1)}, u32[]{:S(2)}, u32[]{:S(2)}) collective-permute-start(s32[8,128]{1,0:T(8,128)S(1)} %slice.3), channel_id=1, source_target_pairs={{0,2},{2,0},{4,6},{6,4},{8,10},{10,8},{12,14},{14,12},{16,18},{18,... | collective-permute-start | bytes 12296 | tf_op jit(solution)/shard_map/ppermute | solution.py:24
  10.0 16.4 %copy-start.1 = (bf16[444,888]{1,0:T(8,128)(2,1)S(1)}, bf16[444,888]{1,0:T(8,128)(2,1)}, u32[]{:S(2)}) copy-start(bf16[444,888]{1,0:T(8,128)(2,1)} %matrix_ref.5) | copy-start | bytes 2365636
  13.9 3.4 %collective-permute-start.5 = (bf16[444,256]{1,0:T(8,128)(2,1)S(1)}, bf16[444,256]{1,0:T(8,128)(2,1)S(1)}, u32[]{:S(2)}, u32[]{:S(2)}) collective-permute-start(bf16[444,256]{1,0:T(8,128)(2,1)S(1)} %get-tuple-element.31), channel_id=1, source_target_pairs={{0,2},{2,0},{4,6},{6,4},{8,10},{10,8},{12,14},{14,12},{16,18},{18,... | collective-permute-start | bytes 681992 | tf_op jit(solution)/shard_map/ppermute | solution.py:24
  14.0 7.9 %collective-permute-start.6 = (bf16[444,128]{1,0:T(8,128)(2,1)S(1)}, bf16[444,128]{1,0:T(8,128)(2,1)S(1)}, u32[]{:S(2)}, u32[]{:S(2)}) collective-permute-start(bf16[444,128]{1,0:T(8,128)(2,1)S(1)} %get-tuple-element.33), channel_id=1, source_target_pairs={{2,6},{4,0},{6,10},{8,4},{10,14},{12,8},{14,18},{16,12},{18,22},{2... | collective-permute-start | bytes 341000 | tf_op jit(solution)/shard_map/ppermute | solution.py:36
  17.7 7.1 %collective-permute-start.7 = (bf16[444,128]{1,0:T(8,128)(2,1)S(1)}, bf16[444,128]{1,0:T(8,128)(2,1)S(1)}, u32[]{:S(2)}, u32[]{:S(2)}) collective-permute-start(bf16[444,128]{1,0:T(8,128)(2,1)S(1)} %get-tuple-element.34), channel_id=1, source_target_pairs={{2,4},{4,2},{6,8},{8,6},{10,12},{12,10},{14,16},{16,14},{18,20},{2... | collective-permute-start | bytes 341000 | tf_op jit(solution)/shard_map/ppermute | solution.py:30
  24.9 5.7 %collective-permute-start.8 = (bf16[444,128]{1,0:T(8,128)(2,1)S(1)}, bf16[444,128]{1,0:T(8,128)(2,1)S(1)}, u32[]{:S(2)}, u32[]{:S(2)}) collective-permute-start(bf16[444,128]{1,0:T(8,128)(2,1)S(1)} %add_convert_fusion.own_ref), channel_id=1, source_target_pairs={{0,1},{1,0},{2,3},{3,2},{4,5},{5,4},{6,7},{7,6},{8,9},{9,8},{10,11... | collective-permute-start | bytes 341000 | tf_op jit(solution)/shard_map/ppermute | solution.py:18

commit v12 on v11

--- a/solution.py
+++ b/solution.py
@@ -28,6 +28,16 @@
     count = lax.axis_size("tile")
     pairs = [(t, t + 2 * (t % 2) - 1) for t in range(count)]
     return lax.ppermute(value, "tile", [(a, b) for a, b in pairs if 0 <= b < count])
+
+
+def to_near_crosswise(value):
+    count = lax.axis_size("tile")
+    pairs = []
+    for t in range(count):
+        target = t + 2 * (t % 2) - 1
+        if 0 <= target < count:
+            pairs += [(2 * t + index, 2 * target + 1 - index) for index in range(2)]
+    return lax.ppermute(value, ("tile", "sub"), pairs)
 
 
 def to_far(value):
@@ -398,11 +408,19 @@
     far_came = to_far(far_sum)
     own_sum, near_sum = push_home(terms, home, near_select, mate_came)
     near_came = to_near(near_sum)
-    down_check = (
-        own_sum + (far_came.astype(jnp.float32) + near_came.astype(jnp.float32))
-    ).astype(jnp.bfloat16)
     if halves:
-        other_down = across_sub(down_check)
+        near_crossed = to_near_crosswise(near_sum)
+        far_came, _ = lax.optimization_barrier((far_came, near_sum))
+    base = own_sum + far_came.astype(jnp.float32)
+    if halves:
+        half_base = base.astype(jnp.bfloat16)
+        near_came, _ = lax.optimization_barrier((near_came, half_base))
+        other_base = across_sub(half_base)
+    down_check = (base + near_came.astype(jnp.float32)).astype(jnp.bfloat16)
+    if halves:
+        other_down = (
+            other_base.astype(jnp.float32) + near_crossed.astype(jnp.float32)
+        ).astype(jnp.bfloat16)
         return rest(down_inverse, first(down_inverse, down_check, windows), other_down, windows)
     return jnp.dot(
         down_inverse, lax.all_gather(down_check, "sub", axis=0, tiled=True),

time: 31.7 us -> 31.3 us (0.987)
  waiting for transfers between devices: 9.55 us -> 5.8 us
  starting transfers between devices: 14.5 us -> 17.6 us
    ppermute x0 -> x1, starting transfers between devices: none -> 4.17 us  [to_near_crosswise(): return lax.ppermute(value, ('tile', 'sub'), pairs)]
    ppermute x3, waiting for transfers between devices: 5.19 us -> 2.15 us  [across_sub(): return lax.ppermute(shard, 'sub', [(0, 1), (1, 0)])]
    ppermute x3, starting transfers between devices: 4.67 us -> 3.7 us  [across_sub(): return lax.ppermute(shard, 'sub', [(0, 1), (1, 0)])]
    ppermute x1, waiting for transfers between devices: 0.92 us -> 0.01 us  [to_far(): lax.ppermute(value, 'tile', [(a, b) for a, b in pairs if 0 <= b < count])]
  transfers between devices with their start and end apart: 9 -> 10, of which waited for: 6 -> 5; matrix products, arithmetic and copies ran while one was open for 0% -> 0% of each run, Pallas kernels for 11% -> 11%
where the time goes in v12:
time: 31.3 us; the launch traced here: 31 us
  starting transfers between devices  17.6 us (56%)
  Pallas kernels  6.42 us (21%)
  waiting for transfers between devices  5.8 us (19%)
  other arithmetic  0.97 us (3%)
    ppermute x2, starting transfers between devices, to_near(): lax.ppermute(value, 'tile', [(a, b) for a, b in pairs if 0 <= b < count])  6.32 us
    ppermute x1, starting transfers between devices, to_near_crosswise(): return lax.ppermute(value, ('tile', 'sub'), pairs)  4.17 us
    ppermute x3, starting transfers between devices, across_sub(): return lax.ppermute(shard, 'sub', [(0, 1), (1, 0)])  3.7 us
    ppermute x1, starting transfers between devices, to_far(): lax.ppermute(value, 'tile', [(a, b) for a, b in pairs if 0 <= b < count])  3.31 us
    ppermute x2, waiting for transfers between devices, to_near(): lax.ppermute(value, 'tile', [(a, b) for a, b in pairs if 0 <= b < count])  3.15 us
    ppermute x3, waiting for transfers between devices, across_sub(): return lax.ppermute(shard, 'sub', [(0, 1), (1, 0)])  2.15 us
    pallas_call x1, Pallas kernels, push_away(): pl.pallas_call(functools.partial(push_away_kernel, windows), out_shape=[j...  1.95 us
    pallas_call x2, Pallas kernels, prepare(): pl.pallas_call(functools.partial(prepare_kernel, windows, part), out_shap...  1.27 us
  transfers between devices with their start and end apart: 10, of which 5 were waited for; matrix products, arithmetic and copies ran while one was open for 0% of the time, Pallas kernels for 11%

profile of v12, /device:TPU:8, one launch (start us, length us, event | category | flops | bytes accessed | tf_op | source)
XLA Modules:
  0.0 31.0 jit_solution(4714313844458457142)
XLA Ops:
  0.0 0.0 copy-start.3
  0.0 0.0 copy-start.2
  0.0 0.0 copy-start
  0.0 0.9 %bitcast_select_fusion.code_ref = s32[8,128]{1,0:T(8,128)S(1)} fusion(s32[128,8]{0,1:T(8,128)} %param.11, s32[128,8]{0,1:T(8,128)} %param.12, s32[128]{0:T(128)} %param.13), kind=kLoop, calls=%fused_computation.5 | loop fusion | flops 4096 | bytes 12800 | tf_op jit(solution)/shard_map/jit(_where)/select_n | solution.py:373
  0.9 0.0 collective-permute-start
  0.9 1.6 %collective-permute-start.2 = (bf16[444,128]{1,0:T(8,128)(2,1)}, bf16[444,128]{1,0:T(8,128)(2,1)S(1)}, u32[]{:S(2)}, u32[]{:S(2)}) collective-permute-start(bf16[444,128]{1,0:T(8,128)(2,1)} %own_ref.1), channel_id=1, source_target_pairs={{0,1},{1,0},{2,3},{3,2},{4,5},{5,4},{6,7},{7,6},{8,9},{9,8},{10,11... | collective-permute-start | bytes 341000 | tf_op jit(solution)/shard_map/ppermute | solution.py:18
  2.4 0.2 home.1.home_ref
  2.7 0.0 collective-permute-done.mate_ref
  2.7 3.1 %collective-permute-start.1 = (s32[16,128]{1,0:T(8,128)S(1)}, s32[16,128]{1,0:T(8,128)S(1)}, u32[]{:S(2)}, u32[]{:S(2)}) collective-permute-start(s32[16,128]{1,0:T(8,128)S(1)} %pad_add_fusion), channel_id=1, source_target_pairs={{2,4},{4,2},{6,8},{8,6},{10,12},{12,10},{14,16},{16,14},{18,20},{2... | collective-permute-start | bytes 24584 | tf_op jit(solution)/shard_map/ppermute | solution.py:30
  5.8 0.9 %collective-permute-done.2.other_ref = bf16[444,128]{1,0:T(8,128)(2,1)S(1)} collective-permute-done((bf16[444,128]{1,0:T(8,128)(2,1)}, bf16[444,128]{1,0:T(8,128)(2,1)S(1)}, u32[]{:S(2)}, u32[]{:S(2)}) %collective-permute-start.2) | collective-permute-done | bytes 113696 | tf_op jit(solution)/shard_map/ppermute | solution.py:18
  6.6 0.0 copy-done.3
  6.6 0.0 copy-done.2
  6.6 0.4 %joined.1.own_ref = bf16[444,128]{1,0:T(8,128)(2,1)S(1)} custom-call(bf16[444,888]{1,0:T(8,128)(2,1)S(1)} %copy-done.2, bf16[444,128]{1,0:T(8,128)(2,1)S(1)} %copy-done.3, bf16[444,128]{1,0:T(8,128)(2,1)S(1)} %collective-permute-done.2.other_ref), custom_call_target="tpu_custom_call" | custom-call | flops 100933632 | bytes 788544 | tf_op jit(solution)/shard_map/joined/pallas_call | solution.py:90
  7.1 1.6 %collective-permute-start.4 = (bf16[444,128]{1,0:T(8,128)(2,1)S(1)}, bf16[444,128]{1,0:T(8,128)(2,1)S(1)}, u32[]{:S(2)}, u32[]{:S(2)}) collective-permute-start(bf16[444,128]{1,0:T(8,128)(2,1)S(1)} %joined.1.own_ref), channel_id=1, source_target_pairs={{0,1},{1,0},{2,3},{3,2},{4,5},{5,4},{6,7},{7,6},{8,9},{9,8},{10,11... | collective-permute-start | bytes 341000 | tf_op jit(solution)/shard_map/ppermute | solution.py:18
  8.6 0.0 copy-done
  8.6 0.6 %prepare.2.low_ref = f32[1792,128]{1,0:T(8,128)S(1)} custom-call(bf16[444,8,888]{2,1,0:T(8,128)(2,1)S(1)} %bitcast.3, bf16[444,128]{1,0:T(8,128)(2,1)S(1)} %joined.1.own_ref), custom_call_target="tpu_custom_call" | custom-call | flops 4294967296 | tf_op jit(solution)/shard_map/prepare/pallas_call | solution.py:210
  9.3 0.0 collective-permute-done.1.near_ref
  9.3 0.1 collective-permute-start.3
  9.4 0.6 %prepare.3.high_ref = f32[1760,128]{1,0:T(8,128)S(1)} custom-call(bf16[444,8,888]{2,1,0:T(8,128)(2,1)S(1)} %bitcast.4, bf16[444,128]{1,0:T(8,128)(2,1)S(1)} %joined.1.own_ref), custom_call_target="tpu_custom_call" | custom-call | flops 4294967296 | tf_op jit(solution)/shard_map/prepare/pallas_call | solution.py:210
  10.0 0.0 copy-start.1
  10.0 0.5 %collective-permute-done.3.mate_near_ref = s32[8,128]{1,0:T(8,128)S(1)} collective-permute-done((s32[8,128]{1,0:T(8,128)S(1)}, s32[8,128]{1,0:T(8,128)S(1)}, u32[]{:S(2)}, u32[]{:S(2)}) %collective-permute-start.3) | collective-permute-done | bytes 4128 | tf_op jit(solution)/shard_map/ppermute | solution.py:24
  10.5 0.9 %selections.1 = (bf16[1024,128]{1,0:T(8,128)(2,1)S(1)}, bf16[1024,128]{1,0:T(8,128)(2,1)S(1)}, bf16[1024,128]{1,0:T(8,128)(2,1)S(1)}, bf16[1024,128]{1,0:T(8,128)(2,1)S(1)}) custom-call(s32[8,128]{1,0:T(8,128)S(1)} %collective-permute-done.mate_ref, s32[16,128]{1,0:T(8,128)S(1)} %collective-permute-done.1.near_ref, ...), custom_call_target="tpu_custom_call" | custom-call | flops 1048576 | tf_op jit(solution)/shard_map/selections/pallas_call | solution.py:254
  11.4 0.5 %collective-permute-done.4.other_ref = bf16[444,128]{1,0:T(8,128)(2,1)S(1)} collective-permute-done((bf16[444,128]{1,0:T(8,128)(2,1)S(1)}, bf16[444,128]{1,0:T(8,128)(2,1)S(1)}, u32[]{:S(2)}, u32[]{:S(2)}) %collective-permute-start.4) | collective-permute-done | bytes 113696 | tf_op jit(solution)/shard_map/ppermute | solution.py:18
  11.9 1.9 %push_away.1 = (bf16[444,1024]{1,0:T(8,128)(2,1)S(1)}, bf16[444,256]{1,0:T(8,128)(2,1)S(1)}, bf16[444,128]{1,0:T(8,128)(2,1)S(1)}) custom-call(bf16[444,8,888]{2,1,0:T(8,128)(2,1)S(1)} %bitcast.5, f32[1792,128]{1,0:T(8,128)S(1)} %prepare.2.low_ref, f32[1760,128]{1,0:T(8,128)S(1)} %prepare.3.high_ref, bf16[444,128]{1,0:T(8,128)(2,1)S(1)} %collective-permute-done.4.other_ref, ...), custom_call_target="tpu_custom_call" | custom-call | flops 814743552 | bytes 6308352 | tf_op jit(solution)/shard_map/push_away/pallas_call | solution.py:316
  13.9 0.1 collective-permute-start.5
  14.0 3.3 %collective-permute-start.6 = (bf16[444,128]{1,0:T(8,128)(2,1)S(1)}, bf16[444,128]{1,0:T(8,128)(2,1)S(1)}, u32[]{:S(2)}, u32[]{:S(2)}) collective-permute-start(bf16[444,128]{1,0:T(8,128)(2,1)S(1)} %get-tuple-element.35), channel_id=1, source_target_pairs={{2,6},{4,0},{6,10},{8,4},{10,14},{12,8},{14,18},{16,12},{18,22},{2... | collective-permute-start | bytes 341000 | tf_op jit(solution)/shard_map/ppermute | solution.py:46
  17.3 0.0 collective-permute-done.5.came_ref
  17.3 0.4 %push_home.1 = (f32[444,128]{1,0:T(8,128)S(1)}, bf16[444,128]{1,0:T(8,128)(2,1)S(1)}) custom-call(bf16[444,1024]{1,0:T(8,128)(2,1)S(1)} %get-tuple-element.30.terms_ref, bf16[1024,128]{1,0:T(8,128)(2,1)S(1)} %home.1.home_ref, bf16[1024,128]{1,0:T(8,128)(2,1)S(1)} %get-tuple-element.32.near_select_ref, bf16[444,256]{1,0:T(8,128)(2,1)S(1)} %collective-permute-done.5.came_ref), custom_call_target="tpu_custom_call" | custom-call | flops 232783872 | bytes 1818624 | tf_op jit(solution)/shard_map/push_home/pallas_call | solution.py:351
  17.7 4.2 %collective-permute-start.9 = (bf16[444,128]{1,0:T(8,128)(2,1)S(1)}, bf16[444,128]{1,0:T(8,128)(2,1)S(1)}, u32[]{:S(2)}, u32[]{:S(2)}) collective-permute-start(bf16[444,128]{1,0:T(8,128)(2,1)S(1)} %get-tuple-element.36), channel_id=1, source_target_pairs={{2,5},{3,4},{4,3},{5,2},{6,9},{7,8},{8,7},{9,6},{10,13},{11,12},{1... | collective-permute-start | bytes 341000 | tf_op jit(solution)/shard_map/ppermute | solution.py:40
  21.9 3.2 %collective-permute-start.7 = (bf16[444,128]{1,0:T(8,128)(2,1)S(1)}, bf16[444,128]{1,0:T(8,128)(2,1)S(1)}, u32[]{:S(2)}, u32[]{:S(2)}) collective-permute-start(bf16[444,128]{1,0:T(8,128)(2,1)S(1)} %get-tuple-element.36), channel_id=1, source_target_pairs={{2,4},{4,2},{6,8},{8,6},{10,12},{12,10},{14,16},{16,14},{18,20},{2... | collective-permute-start | bytes 341000 | tf_op jit(solution)/shard_map/ppermute | solution.py:30
  25.1 0.0 collective-permute-done.6
  25.2 0.6 %collective-permute-start.8 = (bf16[444,128]{1,0:T(8,128)(2,1)S(1)}, bf16[444,128]{1,0:T(8,128)(2,1)S(1)}, u32[]{:S(2)}, u32[]{:S(2)}) collective-permute-start(bf16[444,128]{1,0:T(8,128)(2,1)S(1)} %fusion), channel_id=1, source_target_pairs={{0,1},{1,0},{2,3},{3,2},{4,5},{5,4},{6,7},{7,6},{8,9},{9,8},{10,11... | collective-permute-start | bytes 341000 | tf_op jit(solution)/shard_map/ppermute | solution.py:18
  25.8 3.1 %collective-permute-done.7 = bf16[444,128]{1,0:T(8,128)(2,1)S(1)} collective-permute-done((bf16[444,128]{1,0:T(8,128)(2,1)S(1)}, bf16[444,128]{1,0:T(8,128)(2,1)S(1)}, u32[]{:S(2)}, u32[]{:S(2)}) %collective-permute-start.7) | collective-permute-done | bytes 113696 | tf_op jit(solution)/shard_map/ppermute | solution.py:30
  28.9 0.0 copy-done.1
  29.0 0.3 first.1.part_ref
  29.3 0.8 %collective-permute-done.8 = bf16[444,128]{1,0:T(8,128)(2,1)S(1)} collective-permute-done((bf16[444,128]{1,0:T(8,128)(2,1)S(1)}, bf16[444,128]{1,0:T(8,128)(2,1)S(1)}, u32[]{:S(2)}, u32[]{:S(2)}) %collective-permute-start.8) | collective-permute-done | bytes 113696 | tf_op jit(solution)/shard_map/ppermute | solution.py:18
  30.0 0.0 collective-permute-done.9
  30.1 1.0 %rest.1 = bf16[444,128]{1,0:T(8,128)(2,1)} custom-call(bf16[444,888]{1,0:T(8,128)(2,1)S(1)} %copy-done.1, f32[444,128]{1,0:T(8,128)S(1)} %first.1.part_ref, bf16[444,128]{1,0:T(8,128)(2,1)S(1)} %add_convert_fusion.other_ref), custom_call_target="tpu_custom_call" | custom-call | flops 58195968 | bytes 454656 | tf_op jit(solution)/shard_map/rest/pallas_call | solution.py:151
  (5 shorter events, 0.1 us)
Async XLA Ops:
  0.0 6.6 %copy-start.3 = (bf16[444,128]{1,0:T(8,128)(2,1)S(1)}, bf16[444,128]{1,0:T(8,128)(2,1)}, u32[]{:S(2)}) copy-start(bf16[444,128]{1,0:T(8,128)(2,1)} %own_ref.1) | copy-start | bytes 340996
  0.0 6.6 %copy-start.2 = (bf16[444,888]{1,0:T(8,128)(2,1)S(1)}, bf16[444,888]{1,0:T(8,128)(2,1)}, u32[]{:S(2)}) copy-start(bf16[444,888]{1,0:T(8,128)(2,1)} %matrix_ref.3) | copy-start | bytes 2365636
  0.0 8.6 %copy-start = (bf16[8,444,888]{2,0,1:T(8,128)(2,1)S(1)}, bf16[8,444,888]{2,0,1:T(8,128)(2,1)}, u32[]{:S(2)}) copy-start(bf16[8,444,888]{2,0,1:T(8,128)(2,1)} %param.9) | copy-start | bytes 18925060
  0.9 1.8 %collective-permute-start = (s32[8,128]{1,0:T(8,128)S(1)}, s32[8,128]{1,0:T(8,128)S(1)}, u32[]{:S(2)}, u32[]{:S(2)}) collective-permute-start(s32[8,128]{1,0:T(8,128)S(1)} %bitcast_select_fusion.code_ref), channel_id=1, source_target_pairs={{0,2},{2,0},{4,6},{6,4},{8,10},{10,8},{12,14},{14,12},{16,18},{18,... | collective-permute-start | bytes 12296 | tf_op jit(solution)/shard_map/ppermute | solution.py:24
  0.9 5.8 %collective-permute-start.2 = (bf16[444,128]{1,0:T(8,128)(2,1)}, bf16[444,128]{1,0:T(8,128)(2,1)S(1)}, u32[]{:S(2)}, u32[]{:S(2)}) collective-permute-start(bf16[444,128]{1,0:T(8,128)(2,1)} %own_ref.1), channel_id=1, source_target_pairs={{0,1},{1,0},{2,3},{3,2},{4,5},{5,4},{6,7},{7,6},{8,9},{9,8},{10,11... | collective-permute-start | bytes 341000 | tf_op jit(solution)/shard_map/ppermute | solution.py:18
  2.7 6.6 %collective-permute-start.1 = (s32[16,128]{1,0:T(8,128)S(1)}, s32[16,128]{1,0:T(8,128)S(1)}, u32[]{:S(2)}, u32[]{:S(2)}) collective-permute-start(s32[16,128]{1,0:T(8,128)S(1)} %pad_add_fusion), channel_id=1, source_target_pairs={{2,4},{4,2},{6,8},{8,6},{10,12},{12,10},{14,16},{16,14},{18,20},{2... | collective-permute-start | bytes 24584 | tf_op jit(solution)/shard_map/ppermute | solution.py:30
  7.1 4.9 %collective-permute-start.4 = (bf16[444,128]{1,0:T(8,128)(2,1)S(1)}, bf16[444,128]{1,0:T(8,128)(2,1)S(1)}, u32[]{:S(2)}, u32[]{:S(2)}) collective-permute-start(bf16[444,128]{1,0:T(8,128)(2,1)S(1)} %joined.1.own_ref), channel_id=1, source_target_pairs={{0,1},{1,0},{2,3},{3,2},{4,5},{5,4},{6,7},{7,6},{8,9},{9,8},{10,11... | collective-permute-start | bytes 341000 | tf_op jit(solution)/shard_map/ppermute | solution.py:18
  9.3 1.2 %collective-permute-start.3 = (s32[8,128]{1,0:T(8,128)S(1)}, s32[8,128]{1,0:T(8,128)S(1)}, u32[]{:S(2)}, u32[]{:S(2)}) collective-permute-start(s32[8,128]{1,0:T(8,128)S(1)} %slice.3), channel_id=1, source_target_pairs={{0,2},{2,0},{4,6},{6,4},{8,10},{10,8},{12,14},{14,12},{16,18},{18,... | collective-permute-start | bytes 12296 | tf_op jit(solution)/shard_map/ppermute | solution.py:24
  10.0 18.9 %copy-start.1 = (bf16[444,888]{1,0:T(8,128)(2,1)S(1)}, bf16[444,888]{1,0:T(8,128)(2,1)}, u32[]{:S(2)}) copy-start(bf16[444,888]{1,0:T(8,128)(2,1)} %matrix_ref.5) | copy-start | bytes 2365636
  13.9 3.4 %collective-permute-start.5 = (bf16[444,256]{1,0:T(8,128)(2,1)S(1)}, bf16[444,256]{1,0:T(8,128)(2,1)S(1)}, u32[]{:S(2)}, u32[]{:S(2)}) collective-permute-start(bf16[444,256]{1,0:T(8,128)(2,1)S(1)} %get-tuple-element.33), channel_id=1, source_target_pairs={{0,2},{2,0},{4,6},{6,4},{8,10},{10,8},{12,14},{14,12},{16,18},{18,... | collective-permute-start | bytes 681992 | tf_op jit(solution)/shard_map/ppermute | solution.py:24
  14.0 11.2 %collective-permute-start.6 = (bf16[444,128]{1,0:T(8,128)(2,1)S(1)}, bf16[444,128]{1,0:T(8,128)(2,1)S(1)}, u32[]{:S(2)}, u32[]{:S(2)}) collective-permute-start(bf16[444,128]{1,0:T(8,128)(2,1)S(1)} %get-tuple-element.35), channel_id=1, source_target_pairs={{2,6},{4,0},{6,10},{8,4},{10,14},{12,8},{14,18},{16,12},{18,22},{2... | collective-permute-start | bytes 341000 | tf_op jit(solution)/shard_map/ppermute | solution.py:46
  17.7 12.3 %collective-permute-start.9 = (bf16[444,128]{1,0:T(8,128)(2,1)S(1)}, bf16[444,128]{1,0:T(8,128)(2,1)S(1)}, u32[]{:S(2)}, u32[]{:S(2)}) collective-permute-start(bf16[444,128]{1,0:T(8,128)(2,1)S(1)} %get-tuple-element.36), channel_id=1, source_target_pairs={{2,5},{3,4},{4,3},{5,2},{6,9},{7,8},{8,7},{9,6},{10,13},{11,12},{1... | collective-permute-start | bytes 341000 | tf_op jit(solution)/shard_map/ppermute | solution.py:40
  21.9 7.0 %collective-permute-start.7 = (bf16[444,128]{1,0:T(8,128)(2,1)S(1)}, bf16[444,128]{1,0:T(8,128)(2,1)S(1)}, u32[]{:S(2)}, u32[]{:S(2)}) collective-permute-start(bf16[444,128]{1,0:T(8,128)(2,1)S(1)} %get-tuple-element.36), channel_id=1, source_target_pairs={{2,4},{4,2},{6,8},{8,6},{10,12},{12,10},{14,16},{16,14},{18,20},{2... | collective-permute-start | bytes 341000 | tf_op jit(solution)/shard_map/ppermute | solution.py:30
  25.2 4.9 %collective-permute-start.8 = (bf16[444,128]{1,0:T(8,128)(2,1)S(1)}, bf16[444,128]{1,0:T(8,128)(2,1)S(1)}, u32[]{:S(2)}, u32[]{:S(2)}) collective-permute-start(bf16[444,128]{1,0:T(8,128)(2,1)S(1)} %fusion), channel_id=1, source_target_pairs={{0,1},{1,0},{2,3},{3,2},{4,5},{5,4},{6,7},{7,6},{8,9},{9,8},{10,11... | collective-permute-start | bytes 341000 | tf_op jit(solution)/shard_map/ppermute | solution.py:18

commit v13 on v12

--- a/solution.py
+++ b/solution.py
@@ -99,67 +99,6 @@
         compiler_params=pltpu.CompilerParams(vmem_limit_bytes=8 << 20),
         name="joined",
     )(matrix, own, other)
-
-
-def first_kernel(windows, matrix_ref, own_ref, out_ref, padded):
-    for index, (low, high, offset) in enumerate(windows):
-        def run(low=low, high=high, offset=offset):
-            pad_into(padded, offset, own_ref)
-            out_ref[...] = jnp.dot(
-                matrix_ref[:, low:high], padded[: high - low, :].astype(jnp.bfloat16),
-                preferred_element_type=jnp.float32,
-            )
-        pl.when(lax.axis_index("sub") == index)(run)
-
-
-def first(matrix, own, windows):
-    rows, depth = matrix.shape
-    cells = own.shape[1]
-    span = max(high - low for low, high, _ in windows)
-    return pl.pallas_call(
-        functools.partial(first_kernel, windows),
-        out_shape=jax.ShapeDtypeStruct((rows, cells), jnp.float32),
-        in_specs=[WHOLE] * 2,
-        out_specs=WHOLE,
-        scratch_shapes=[pltpu.VMEM((span, cells), jnp.float32)],
-        cost_estimate=pl.CostEstimate(
-            flops=2 * rows * depth * cells, bytes_accessed=4 * rows * depth, transcendentals=0
-        ),
-        compiler_params=pltpu.CompilerParams(vmem_limit_bytes=16 << 20),
-        name="first",
-    )(matrix, own)
-
-
-def rest_kernel(windows, matrix_ref, part_ref, other_ref, out_ref, padded):
-    for index, (low, high, offset) in enumerate(windows):
-        def run(low=low, high=high, offset=offset):
-            pad_into(padded, offset, other_ref)
-            out_ref[...] = (
-                part_ref[...]
-                + jnp.dot(
-                    matrix_ref[:, low:high], padded[: high - low, :].astype(jnp.bfloat16),
-                    preferred_element_type=jnp.float32,
-                )
-            ).astype(jnp.bfloat16)
-        pl.when(lax.axis_index("sub") != index)(run)
-
-
-def rest(matrix, part, other, windows):
-    rows, depth = matrix.shape
-    cells = other.shape[1]
-    span = max(high - low for low, high, _ in windows)
-    return pl.pallas_call(
-        functools.partial(rest_kernel, windows),
-        out_shape=jax.ShapeDtypeStruct((rows, cells), jnp.bfloat16),
-        in_specs=[WHOLE] * 3,
-        out_specs=WHOLE,
-        scratch_shapes=[pltpu.VMEM((span, cells), jnp.float32)],
-        cost_estimate=pl.CostEstimate(
-            flops=2 * rows * span * cells, bytes_accessed=2 * rows * span, transcendentals=0
-        ),
-        compiler_params=pltpu.CompilerParams(vmem_limit_bytes=16 << 20),
-        name="rest",
-    )(matrix, part, other)
 
 
 def build_select(code, base, out_ref, column, classes):
@@ -421,7 +360,7 @@
         other_down = (
             other_base.astype(jnp.float32) + near_crossed.astype(jnp.float32)
         ).astype(jnp.bfloat16)
-        return rest(down_inverse, first(down_inverse, down_check, windows), other_down, windows)
+        return joined_product(down_inverse, down_check, other_down)
     return jnp.dot(
         down_inverse, lax.all_gather(down_check, "sub", axis=0, tiled=True),
         preferred_element_type=jnp.float32,

time: 31.3 us -> 31.3 us (level)
    pallas_call x2 -> x0, Pallas kernels: 1.26 us -> none  [the longest x1 0.97 us: rest(): pl.pallas_call(functools.partial(rest_kernel, windows), out_shape=jax.Sha...]
    pallas_call x1 -> x2, Pallas kernels: 0.41 us -> 1.48 us  [joined_product(): pl.pallas_call(joined_kernel, out_shape=jax.ShapeDtypeStruct((rows, cells...]
  transfers between devices with their start and end apart: 10 -> 10, of which waited for: 5 -> 5; matrix products, arithmetic and copies ran while one was open for 0% -> 0% of each run, Pallas kernels for 11% -> 10%
where the time goes in v13:
time: 31.3 us; the launch traced here: 31.1 us
  starting transfers between devices  17.6 us (56%)
  Pallas kernels  6.23 us (20%)
  waiting for transfers between devices  6.1 us (19%)
  other arithmetic  0.97 us (3%)
    ppermute x2, starting transfers between devices, to_near(): lax.ppermute(value, 'tile', [(a, b) for a, b in pairs if 0 <= b < count])  6.32 us
    ppermute x1, starting transfers between devices, to_near_crosswise(): return lax.ppermute(value, ('tile', 'sub'), pairs)  4.17 us
    ppermute x3, starting transfers between devices, across_sub(): return lax.ppermute(shard, 'sub', [(0, 1), (1, 0)])  3.7 us
    ppermute x1, starting transfers between devices, to_far(): lax.ppermute(value, 'tile', [(a, b) for a, b in pairs if 0 <= b < count])  3.32 us
    ppermute x2, waiting for transfers between devices, to_near(): lax.ppermute(value, 'tile', [(a, b) for a, b in pairs if 0 <= b < count])  3.15 us
    ppermute x3, waiting for transfers between devices, across_sub(): return lax.ppermute(shard, 'sub', [(0, 1), (1, 0)])  2.45 us
    pallas_call x1, Pallas kernels, push_away(): pl.pallas_call(functools.partial(push_away_kernel, windows), out_shape=[j...  1.94 us
    pallas_call x2, Pallas kernels, joined_product(): pl.pallas_call(joined_kernel, out_shape=jax.ShapeDtypeStruct((rows, cells...  1.48 us
  transfers between devices with their start and end apart: 10, of which 5 were waited for; matrix products, arithmetic and copies ran while one was open for 0% of the time, Pallas kernels for 10%

profile of v13, /device:TPU:8, one launch (start us, length us, event | category | flops | bytes accessed | tf_op | source)
XLA Modules:
  0.0 31.1 jit_solution(4311218511572964864)
XLA Ops:
  0.0 0.0 copy-start.3
  0.0 0.0 copy-start.1
  0.0 0.0 copy-start
  0.0 0.9 %bitcast_select_fusion.code_ref = s32[8,128]{1,0:T(8,128)S(1)} fusion(s32[128,8]{0,1:T(8,128)} %param.11, s32[128,8]{0,1:T(8,128)} %param.12, s32[128]{0:T(128)} %param.13), kind=kLoop, calls=%fused_computation.5 | loop fusion | flops 4096 | bytes 12800 | tf_op jit(solution)/shard_map/jit(_where)/select_n | solution.py:312
  0.9 0.0 collective-permute-start
  0.9 1.6 %collective-permute-start.2 = (bf16[444,128]{1,0:T(8,128)(2,1)}, bf16[444,128]{1,0:T(8,128)(2,1)S(1)}, u32[]{:S(2)}, u32[]{:S(2)}) collective-permute-start(bf16[444,128]{1,0:T(8,128)(2,1)} %own_ref.1), channel_id=1, source_target_pairs={{0,1},{1,0},{2,3},{3,2},{4,5},{5,4},{6,7},{7,6},{8,9},{9,8},{10,11... | collective-permute-start | bytes 341000 | tf_op jit(solution)/shard_map/ppermute | solution.py:18
  2.4 0.2 home.1.home_ref
  2.7 0.0 collective-permute-done.mate_ref
  2.7 3.1 %collective-permute-start.1 = (s32[16,128]{1,0:T(8,128)S(1)}, s32[16,128]{1,0:T(8,128)S(1)}, u32[]{:S(2)}, u32[]{:S(2)}) collective-permute-start(s32[16,128]{1,0:T(8,128)S(1)} %pad_add_fusion), channel_id=1, source_target_pairs={{2,4},{4,2},{6,8},{8,6},{10,12},{12,10},{14,16},{16,14},{18,20},{2... | collective-permute-start | bytes 24584 | tf_op jit(solution)/shard_map/ppermute | solution.py:30
  5.8 0.9 %collective-permute-done.2.other_ref = bf16[444,128]{1,0:T(8,128)(2,1)S(1)} collective-permute-done((bf16[444,128]{1,0:T(8,128)(2,1)}, bf16[444,128]{1,0:T(8,128)(2,1)S(1)}, u32[]{:S(2)}, u32[]{:S(2)}) %collective-permute-start.2) | collective-permute-done | bytes 113696 | tf_op jit(solution)/shard_map/ppermute | solution.py:18
  6.6 0.0 copy-done.3
  6.6 0.0 copy-done.1
  6.6 0.4 %joined.2.own_ref = bf16[444,128]{1,0:T(8,128)(2,1)S(1)} custom-call(bf16[444,888]{1,0:T(8,128)(2,1)S(1)} %copy-done.1, bf16[444,128]{1,0:T(8,128)(2,1)S(1)} %copy-done.3, bf16[444,128]{1,0:T(8,128)(2,1)S(1)} %collective-permute-done.2.other_ref), custom_call_target="tpu_custom_call" | custom-call | flops 100933632 | bytes 788544 | tf_op jit(solution)/shard_map/joined/pallas_call | solution.py:90
  7.1 1.6 %collective-permute-start.4 = (bf16[444,128]{1,0:T(8,128)(2,1)S(1)}, bf16[444,128]{1,0:T(8,128)(2,1)S(1)}, u32[]{:S(2)}, u32[]{:S(2)}) collective-permute-start(bf16[444,128]{1,0:T(8,128)(2,1)S(1)} %joined.2.own_ref), channel_id=1, source_target_pairs={{0,1},{1,0},{2,3},{3,2},{4,5},{5,4},{6,7},{7,6},{8,9},{9,8},{10,11... | collective-permute-start | bytes 341000 | tf_op jit(solution)/shard_map/ppermute | solution.py:18
  8.6 0.0 copy-done
  8.6 0.6 %prepare.2.low_ref = f32[1792,128]{1,0:T(8,128)S(1)} custom-call(bf16[444,8,888]{2,1,0:T(8,128)(2,1)S(1)} %bitcast.3, bf16[444,128]{1,0:T(8,128)(2,1)S(1)} %joined.2.own_ref), custom_call_target="tpu_custom_call" | custom-call | flops 4294967296 | tf_op jit(solution)/shard_map/prepare/pallas_call | solution.py:149
  9.3 0.0 collective-permute-done.1.near_ref
  9.3 0.1 collective-permute-start.3
  9.4 0.6 %prepare.3.high_ref = f32[1760,128]{1,0:T(8,128)S(1)} custom-call(bf16[444,8,888]{2,1,0:T(8,128)(2,1)S(1)} %bitcast.4, bf16[444,128]{1,0:T(8,128)(2,1)S(1)} %joined.2.own_ref), custom_call_target="tpu_custom_call" | custom-call | flops 4294967296 | tf_op jit(solution)/shard_map/prepare/pallas_call | solution.py:149
  10.0 0.0 copy-start.2
  10.0 0.5 %collective-permute-done.3.mate_near_ref = s32[8,128]{1,0:T(8,128)S(1)} collective-permute-done((s32[8,128]{1,0:T(8,128)S(1)}, s32[8,128]{1,0:T(8,128)S(1)}, u32[]{:S(2)}, u32[]{:S(2)}) %collective-permute-start.3) | collective-permute-done | bytes 4128 | tf_op jit(solution)/shard_map/ppermute | solution.py:24
  10.5 0.9 %selections.1 = (bf16[1024,128]{1,0:T(8,128)(2,1)S(1)}, bf16[1024,128]{1,0:T(8,128)(2,1)S(1)}, bf16[1024,128]{1,0:T(8,128)(2,1)S(1)}, bf16[1024,128]{1,0:T(8,128)(2,1)S(1)}) custom-call(s32[8,128]{1,0:T(8,128)S(1)} %collective-permute-done.mate_ref, s32[16,128]{1,0:T(8,128)S(1)} %collective-permute-done.1.near_ref, ...), custom_call_target="tpu_custom_call" | custom-call | flops 1048576 | tf_op jit(solution)/shard_map/selections/pallas_call | solution.py:193
  11.4 0.5 %collective-permute-done.4.other_ref = bf16[444,128]{1,0:T(8,128)(2,1)S(1)} collective-permute-done((bf16[444,128]{1,0:T(8,128)(2,1)S(1)}, bf16[444,128]{1,0:T(8,128)(2,1)S(1)}, u32[]{:S(2)}, u32[]{:S(2)}) %collective-permute-start.4) | collective-permute-done | bytes 113696 | tf_op jit(solution)/shard_map/ppermute | solution.py:18
  11.9 1.9 %push_away.1 = (bf16[444,1024]{1,0:T(8,128)(2,1)S(1)}, bf16[444,256]{1,0:T(8,128)(2,1)S(1)}, bf16[444,128]{1,0:T(8,128)(2,1)S(1)}) custom-call(bf16[444,8,888]{2,1,0:T(8,128)(2,1)S(1)} %bitcast.5, f32[1792,128]{1,0:T(8,128)S(1)} %prepare.2.low_ref, f32[1760,128]{1,0:T(8,128)S(1)} %prepare.3.high_ref, bf16[444,128]{1,0:T(8,128)(2,1)S(1)} %collective-permute-done.4.other_ref, ...), custom_call_target="tpu_custom_call" | custom-call | flops 814743552 | bytes 6308352 | tf_op jit(solution)/shard_map/push_away/pallas_call | solution.py:255
  13.9 0.1 collective-permute-start.5
  14.0 3.3 %collective-permute-start.6 = (bf16[444,128]{1,0:T(8,128)(2,1)S(1)}, bf16[444,128]{1,0:T(8,128)(2,1)S(1)}, u32[]{:S(2)}, u32[]{:S(2)}) collective-permute-start(bf16[444,128]{1,0:T(8,128)(2,1)S(1)} %get-tuple-element.35), channel_id=1, source_target_pairs={{2,6},{4,0},{6,10},{8,4},{10,14},{12,8},{14,18},{16,12},{18,22},{2... | collective-permute-start | bytes 341000 | tf_op jit(solution)/shard_map/ppermute | solution.py:46
  17.3 0.0 collective-permute-done.5.came_ref
  17.3 0.4 %push_home.1 = (f32[444,128]{1,0:T(8,128)S(1)}, bf16[444,128]{1,0:T(8,128)(2,1)S(1)}) custom-call(bf16[444,1024]{1,0:T(8,128)(2,1)S(1)} %get-tuple-element.30.terms_ref, bf16[1024,128]{1,0:T(8,128)(2,1)S(1)} %home.1.home_ref, bf16[1024,128]{1,0:T(8,128)(2,1)S(1)} %get-tuple-element.32.near_select_ref, bf16[444,256]{1,0:T(8,128)(2,1)S(1)} %collective-permute-done.5.came_ref), custom_call_target="tpu_custom_call" | custom-call | flops 232783872 | bytes 1818624 | tf_op jit(solution)/shard_map/push_home/pallas_call | solution.py:290
  17.7 4.2 %collective-permute-start.9 = (bf16[444,128]{1,0:T(8,128)(2,1)S(1)}, bf16[444,128]{1,0:T(8,128)(2,1)S(1)}, u32[]{:S(2)}, u32[]{:S(2)}) collective-permute-start(bf16[444,128]{1,0:T(8,128)(2,1)S(1)} %get-tuple-element.36), channel_id=1, source_target_pairs={{2,5},{3,4},{4,3},{5,2},{6,9},{7,8},{8,7},{9,6},{10,13},{11,12},{1... | collective-permute-start | bytes 341000 | tf_op jit(solution)/shard_map/ppermute | solution.py:40
  21.9 3.2 %collective-permute-start.7 = (bf16[444,128]{1,0:T(8,128)(2,1)S(1)}, bf16[444,128]{1,0:T(8,128)(2,1)S(1)}, u32[]{:S(2)}, u32[]{:S(2)}) collective-permute-start(bf16[444,128]{1,0:T(8,128)(2,1)S(1)} %get-tuple-element.36), channel_id=1, source_target_pairs={{2,4},{4,2},{6,8},{8,6},{10,12},{12,10},{14,16},{16,14},{18,20},{2... | collective-permute-start | bytes 341000 | tf_op jit(solution)/shard_map/ppermute | solution.py:30
  25.1 0.0 collective-permute-done.6
  25.2 0.6 %collective-permute-start.8 = (bf16[444,128]{1,0:T(8,128)(2,1)S(1)}, bf16[444,128]{1,0:T(8,128)(2,1)S(1)}, u32[]{:S(2)}, u32[]{:S(2)}) collective-permute-start(bf16[444,128]{1,0:T(8,128)(2,1)S(1)} %fusion), channel_id=1, source_target_pairs={{0,1},{1,0},{2,3},{3,2},{4,5},{5,4},{6,7},{7,6},{8,9},{9,8},{10,11... | collective-permute-start | bytes 341000 | tf_op jit(solution)/shard_map/ppermute | solution.py:18
  25.8 3.1 %collective-permute-done.7 = bf16[444,128]{1,0:T(8,128)(2,1)S(1)} collective-permute-done((bf16[444,128]{1,0:T(8,128)(2,1)S(1)}, bf16[444,128]{1,0:T(8,128)(2,1)S(1)}, u32[]{:S(2)}, u32[]{:S(2)}) %collective-permute-start.7) | collective-permute-done | bytes 113696 | tf_op jit(solution)/shard_map/ppermute | solution.py:30
  28.9 1.1 %collective-permute-done.8 = bf16[444,128]{1,0:T(8,128)(2,1)S(1)} collective-permute-done((bf16[444,128]{1,0:T(8,128)(2,1)S(1)}, bf16[444,128]{1,0:T(8,128)(2,1)S(1)}, u32[]{:S(2)}, u32[]{:S(2)}) %collective-permute-start.8) | collective-permute-done | bytes 113696 | tf_op jit(solution)/shard_map/ppermute | solution.py:18
  30.0 0.0 collective-permute-done.9
  30.1 0.0 copy-done.2
  30.1 1.1 %joined.3 = bf16[444,128]{1,0:T(8,128)(2,1)} custom-call(bf16[444,888]{1,0:T(8,128)(2,1)S(1)} %copy-done.2, bf16[444,128]{1,0:T(8,128)(2,1)S(1)} %add_convert_fusion.1.own_ref, bf16[444,128]{1,0:T(8,128)(2,1)S(1)} %add_convert_fusion.other_ref), custom_call_target="tpu_custom_call" | custom-call | flops 100933632 | bytes 788544 | tf_op jit(solution)/shard_map/joined/pallas_call | solution.py:90
  (5 shorter events, 0.1 us)
Async XLA Ops:
  0.0 6.6 %copy-start.3 = (bf16[444,128]{1,0:T(8,128)(2,1)S(1)}, bf16[444,128]{1,0:T(8,128)(2,1)}, u32[]{:S(2)}) copy-start(bf16[444,128]{1,0:T(8,128)(2,1)} %own_ref.1) | copy-start | bytes 340996
  0.0 6.6 %copy-start.1 = (bf16[444,888]{1,0:T(8,128)(2,1)S(1)}, bf16[444,888]{1,0:T(8,128)(2,1)}, u32[]{:S(2)}) copy-start(bf16[444,888]{1,0:T(8,128)(2,1)} %matrix_ref.2) | copy-start | bytes 2365636
  0.0 8.6 %copy-start = (bf16[8,444,888]{2,0,1:T(8,128)(2,1)S(1)}, bf16[8,444,888]{2,0,1:T(8,128)(2,1)}, u32[]{:S(2)}) copy-start(bf16[8,444,888]{2,0,1:T(8,128)(2,1)} %param.9) | copy-start | bytes 18925060
  0.9 1.8 %collective-permute-start = (s32[8,128]{1,0:T(8,128)S(1)}, s32[8,128]{1,0:T(8,128)S(1)}, u32[]{:S(2)}, u32[]{:S(2)}) collective-permute-start(s32[8,128]{1,0:T(8,128)S(1)} %bitcast_select_fusion.code_ref), channel_id=1, source_target_pairs={{0,2},{2,0},{4,6},{6,4},{8,10},{10,8},{12,14},{14,12},{16,18},{18,... | collective-permute-start | bytes 12296 | tf_op jit(solution)/shard_map/ppermute | solution.py:24
  0.9 5.8 %collective-permute-start.2 = (bf16[444,128]{1,0:T(8,128)(2,1)}, bf16[444,128]{1,0:T(8,128)(2,1)S(1)}, u32[]{:S(2)}, u32[]{:S(2)}) collective-permute-start(bf16[444,128]{1,0:T(8,128)(2,1)} %own_ref.1), channel_id=1, source_target_pairs={{0,1},{1,0},{2,3},{3,2},{4,5},{5,4},{6,7},{7,6},{8,9},{9,8},{10,11... | collective-permute-start | bytes 341000 | tf_op jit(solution)/shard_map/ppermute | solution.py:18
  2.7 6.6 %collective-permute-start.1 = (s32[16,128]{1,0:T(8,128)S(1)}, s32[16,128]{1,0:T(8,128)S(1)}, u32[]{:S(2)}, u32[]{:S(2)}) collective-permute-start(s32[16,128]{1,0:T(8,128)S(1)} %pad_add_fusion), channel_id=1, source_target_pairs={{2,4},{4,2},{6,8},{8,6},{10,12},{12,10},{14,16},{16,14},{18,20},{2... | collective-permute-start | bytes 24584 | tf_op jit(solution)/shard_map/ppermute | solution.py:30
  7.1 4.9 %collective-permute-start.4 = (bf16[444,128]{1,0:T(8,128)(2,1)S(1)}, bf16[444,128]{1,0:T(8,128)(2,1)S(1)}, u32[]{:S(2)}, u32[]{:S(2)}) collective-permute-start(bf16[444,128]{1,0:T(8,128)(2,1)S(1)} %joined.2.own_ref), channel_id=1, source_target_pairs={{0,1},{1,0},{2,3},{3,2},{4,5},{5,4},{6,7},{7,6},{8,9},{9,8},{10,11... | collective-permute-start | bytes 341000 | tf_op jit(solution)/shard_map/ppermute | solution.py:18
  9.3 1.2 %collective-permute-start.3 = (s32[8,128]{1,0:T(8,128)S(1)}, s32[8,128]{1,0:T(8,128)S(1)}, u32[]{:S(2)}, u32[]{:S(2)}) collective-permute-start(s32[8,128]{1,0:T(8,128)S(1)} %slice.3), channel_id=1, source_target_pairs={{0,2},{2,0},{4,6},{6,4},{8,10},{10,8},{12,14},{14,12},{16,18},{18,... | collective-permute-start | bytes 12296 | tf_op jit(solution)/shard_map/ppermute | solution.py:24
  10.0 20.0 %copy-start.2 = (bf16[444,888]{1,0:T(8,128)(2,1)S(1)}, bf16[444,888]{1,0:T(8,128)(2,1)}, u32[]{:S(2)}) copy-start(bf16[444,888]{1,0:T(8,128)(2,1)} %matrix_ref.3) | copy-start | bytes 2365636
  13.9 3.4 %collective-permute-start.5 = (bf16[444,256]{1,0:T(8,128)(2,1)S(1)}, bf16[444,256]{1,0:T(8,128)(2,1)S(1)}, u32[]{:S(2)}, u32[]{:S(2)}) collective-permute-start(bf16[444,256]{1,0:T(8,128)(2,1)S(1)} %get-tuple-element.33), channel_id=1, source_target_pairs={{0,2},{2,0},{4,6},{6,4},{8,10},{10,8},{12,14},{14,12},{16,18},{18,... | collective-permute-start | bytes 681992 | tf_op jit(solution)/shard_map/ppermute | solution.py:24
  14.0 11.2 %collective-permute-start.6 = (bf16[444,128]{1,0:T(8,128)(2,1)S(1)}, bf16[444,128]{1,0:T(8,128)(2,1)S(1)}, u32[]{:S(2)}, u32[]{:S(2)}) collective-permute-start(bf16[444,128]{1,0:T(8,128)(2,1)S(1)} %get-tuple-element.35), channel_id=1, source_target_pairs={{2,6},{4,0},{6,10},{8,4},{10,14},{12,8},{14,18},{16,12},{18,22},{2... | collective-permute-start | bytes 341000 | tf_op jit(solution)/shard_map/ppermute | solution.py:46
  17.7 12.3 %collective-permute-start.9 = (bf16[444,128]{1,0:T(8,128)(2,1)S(1)}, bf16[444,128]{1,0:T(8,128)(2,1)S(1)}, u32[]{:S(2)}, u32[]{:S(2)}) collective-permute-start(bf16[444,128]{1,0:T(8,128)(2,1)S(1)} %get-tuple-element.36), channel_id=1, source_target_pairs={{2,5},{3,4},{4,3},{5,2},{6,9},{7,8},{8,7},{9,6},{10,13},{11,12},{1... | collective-permute-start | bytes 341000 | tf_op jit(solution)/shard_map/ppermute | solution.py:40
  21.9 7.0 %collective-permute-start.7 = (bf16[444,128]{1,0:T(8,128)(2,1)S(1)}, bf16[444,128]{1,0:T(8,128)(2,1)S(1)}, u32[]{:S(2)}, u32[]{:S(2)}) collective-permute-start(bf16[444,128]{1,0:T(8,128)(2,1)S(1)} %get-tuple-element.36), channel_id=1, source_target_pairs={{2,4},{4,2},{6,8},{8,6},{10,12},{12,10},{14,16},{16,14},{18,20},{2... | collective-permute-start | bytes 341000 | tf_op jit(solution)/shard_map/ppermute | solution.py:30
  25.2 4.9 %collective-permute-start.8 = (bf16[444,128]{1,0:T(8,128)(2,1)S(1)}, bf16[444,128]{1,0:T(8,128)(2,1)S(1)}, u32[]{:S(2)}, u32[]{:S(2)}) collective-permute-start(bf16[444,128]{1,0:T(8,128)(2,1)S(1)} %fusion), channel_id=1, source_target_pairs={{0,1},{1,0},{2,3},{3,2},{4,5},{5,4},{6,7},{7,6},{8,9},{9,8},{10,11... | collective-permute-start | bytes 341000 | tf_op jit(solution)/shard_map/ppermute | solution.py:18

commit v14 on v13

--- a/solution.py
+++ b/solution.py
@@ -308,6 +308,10 @@
     cells, entries = list_slot.shape
     halves = lax.axis_size("sub") == 2
 
+    if halves:
+        other_check = across_sub(up_check)
+        list_slot, up_check = lax.optimization_barrier((list_slot, up_check))
+
     active = lax.broadcasted_iota(jnp.int32, (entries, cells), 0) < list_count[None, :]
     code = jnp.where(active, (list_class.T << CLASS_SHIFT) + list_slot.T, -1)
     mate_code, home = lax.optimization_barrier((to_mate(code), home_selection(code, classes)))
@@ -316,7 +320,7 @@
     operators = jnp.transpose(translate, (1, 0, 2))
     if halves:
         windows = half_windows(rows, depth, 2)
-        equivalent = joined_product(up_inverse, up_check, across_sub(up_check))
+        equivalent = joined_product(up_inverse, up_check, other_check)
         other = across_sub(equivalent)
     else:
         windows = [(0, depth, 0)]

time: 31.3 us -> 31.1 us (level)
  starting transfers between devices: 17.6 us -> 15.5 us
  waiting for transfers between devices: 6.1 us -> 7.65 us
  other arithmetic: 0.97 us -> 1.35 us
    ppermute x2, waiting for transfers between devices: 3.15 us -> 4.21 us  [to_near(): lax.ppermute(value, 'tile', [(a, b) for a, b in pairs if 0 <= b < count])]
    ppermute x3, waiting for transfers between devices: 0.49 us -> 1.45 us  [to_mate(): return lax.ppermute(value, 'tile', pairs)]
    ppermute x1, starting transfers between devices: 3.32 us -> 2.46 us  [to_far(): lax.ppermute(value, 'tile', [(a, b) for a, b in pairs if 0 <= b < count])]
    ppermute x3, starting transfers between devices: 3.7 us -> 3.19 us  [across_sub(): return lax.ppermute(shard, 'sub', [(0, 1), (1, 0)])]
    ppermute x3, waiting for transfers between devices: 2.45 us -> 1.98 us  [across_sub(): return lax.ppermute(shard, 'sub', [(0, 1), (1, 0)])]
    select_n x1, other arithmetic: 0.86 us -> 1.25 us  [shards(): code = jnp.where(active, (list_class.T << CLASS_SHIFT) + list_slot.T, -1)]
    ppermute x2, starting transfers between devices: 6.32 us -> 5.96 us  [to_near(): lax.ppermute(value, 'tile', [(a, b) for a, b in pairs if 0 <= b < count])]
    ppermute x1, starting transfers between devices: 4.17 us -> 3.82 us  [to_near_crosswise(): return lax.ppermute(value, ('tile', 'sub'), pairs)]
  transfers between devices with their start and end apart: 10 -> 10, of which waited for: 5 -> 6; matrix products, arithmetic and copies ran while one was open for 0% -> 4% of each run, Pallas kernels for 10% -> 10%
where the time goes in v14:
time: 31.1 us; the launch traced here: 30.9 us
  starting transfers between devices  15.5 us (50%)
  waiting for transfers between devices  7.65 us (25%)
  Pallas kernels  6.24 us (20%)
  other arithmetic  1.35 us (4%)
    ppermute x2, starting transfers between devices, to_near(): lax.ppermute(value, 'tile', [(a, b) for a, b in pairs if 0 <= b < count])  5.96 us
    ppermute x2, waiting for transfers between devices, to_near(): lax.ppermute(value, 'tile', [(a, b) for a, b in pairs if 0 <= b < count])  4.21 us
    ppermute x1, starting transfers between devices, to_near_crosswise(): return lax.ppermute(value, ('tile', 'sub'), pairs)  3.82 us
    ppermute x3, starting transfers between devices, across_sub(): return lax.ppermute(shard, 'sub', [(0, 1), (1, 0)])  3.19 us
    ppermute x1, starting transfers between devices, to_far(): lax.ppermute(value, 'tile', [(a, b) for a, b in pairs if 0 <= b < count])  2.46 us
    ppermute x3, waiting for transfers between devices, across_sub(): return lax.ppermute(shard, 'sub', [(0, 1), (1, 0)])  1.98 us
    pallas_call x1, Pallas kernels, push_away(): pl.pallas_call(functools.partial(push_away_kernel, windows), out_shape=[j...  1.94 us
    pallas_call x2, Pallas kernels, joined_product(): pl.pallas_call(joined_kernel, out_shape=jax.ShapeDtypeStruct((rows, cells...  1.49 us
  transfers between devices with their start and end apart: 10, of which 6 were waited for; matrix products, arithmetic and copies ran while one was open for 4% of the time, Pallas kernels for 10%

profile of v14, /device:TPU:8, one launch (start us, length us, event | category | flops | bytes accessed | tf_op | source)
XLA Modules:
  0.0 30.9 jit_solution(13327067369939637885)
XLA Ops:
  0.0 0.0 copy-start.3
  0.0 0.0 copy-start.1
  0.0 0.0 copy-start
  0.0 1.6 %collective-permute-start.2 = (bf16[444,128]{1,0:T(8,128)(2,1)}, bf16[444,128]{1,0:T(8,128)(2,1)S(1)}, u32[]{:S(2)}, u32[]{:S(2)}) collective-permute-start(bf16[444,128]{1,0:T(8,128)(2,1)} %own_ref), channel_id=1, source_target_pairs={{0,1},{1,0},{2,3},{3,2},{4,5},{5,4},{6,7},{7,6},{8,9},{9,8},{10,11... | collective-permute-start | bytes 341000 | tf_op jit(solution)/shard_map/ppermute | solution.py:18
  1.6 1.2 %bitcast_select_fusion.code_ref = s32[8,128]{1,0:T(8,128)S(1)} fusion(s32[128,8]{0,1:T(8,128)} %param.11, s32[128,8]{0,1:T(8,128)} %param.12, s32[128]{0:T(128)} %param.13), kind=kLoop, calls=%fused_computation.5 | loop fusion | flops 4096 | bytes 12800 | tf_op jit(solution)/shard_map/jit(_where)/select_n | solution.py:316
  2.8 0.0 collective-permute-start
  2.8 0.2 home.1.home_ref
  3.0 0.9 %collective-permute-done.mate_ref = s32[8,128]{1,0:T(8,128)S(1)} collective-permute-done((s32[8,128]{1,0:T(8,128)S(1)}, s32[8,128]{1,0:T(8,128)S(1)}, u32[]{:S(2)}, u32[]{:S(2)}) %collective-permute-start) | collective-permute-done | bytes 4128 | tf_op jit(solution)/shard_map/ppermute | solution.py:24
  4.0 3.1 %collective-permute-start.1 = (s32[16,128]{1,0:T(8,128)S(1)}, s32[16,128]{1,0:T(8,128)S(1)}, u32[]{:S(2)}, u32[]{:S(2)}) collective-permute-start(s32[16,128]{1,0:T(8,128)S(1)} %pad_add_fusion), channel_id=1, source_target_pairs={{2,4},{4,2},{6,8},{8,6},{10,12},{12,10},{14,16},{16,14},{18,20},{2... | collective-permute-start | bytes 24584 | tf_op jit(solution)/shard_map/ppermute | solution.py:30
  7.1 0.0 collective-permute-done.2.other_ref
  7.1 0.0 copy-done.3
  7.1 0.0 copy-done.1
  7.1 0.4 %joined.2.own_ref = bf16[444,128]{1,0:T(8,128)(2,1)S(1)} custom-call(bf16[444,888]{1,0:T(8,128)(2,1)S(1)} %copy-done.1, bf16[444,128]{1,0:T(8,128)(2,1)S(1)} %copy-done.3, bf16[444,128]{1,0:T(8,128)(2,1)S(1)} %collective-permute-done.2.other_ref), custom_call_target="tpu_custom_call" | custom-call | flops 100933632 | bytes 788544 | tf_op jit(solution)/shard_map/joined/pallas_call | solution.py:90
  7.5 0.3 %collective-permute-start.4 = (bf16[444,128]{1,0:T(8,128)(2,1)S(1)}, bf16[444,128]{1,0:T(8,128)(2,1)S(1)}, u32[]{:S(2)}, u32[]{:S(2)}) collective-permute-start(bf16[444,128]{1,0:T(8,128)(2,1)S(1)} %joined.2.own_ref), channel_id=1, source_target_pairs={{0,1},{1,0},{2,3},{3,2},{4,5},{5,4},{6,7},{7,6},{8,9},{9,8},{10,11... | collective-permute-start | bytes 341000 | tf_op jit(solution)/shard_map/ppermute | solution.py:18
  7.9 0.0 copy-done
  7.9 0.6 %prepare.2.low_ref = f32[1792,128]{1,0:T(8,128)S(1)} custom-call(bf16[444,8,888]{2,1,0:T(8,128)(2,1)S(1)} %bitcast.3, bf16[444,128]{1,0:T(8,128)(2,1)S(1)} %joined.2.own_ref), custom_call_target="tpu_custom_call" | custom-call | flops 4294967296 | tf_op jit(solution)/shard_map/prepare/pallas_call | solution.py:149
  8.5 1.3 %collective-permute-done.1.near_ref = s32[16,128]{1,0:T(8,128)S(1)} collective-permute-done((s32[16,128]{1,0:T(8,128)S(1)}, s32[16,128]{1,0:T(8,128)S(1)}, u32[]{:S(2)}, u32[]{:S(2)}) %collective-permute-start.1) | collective-permute-done | bytes 8224 | tf_op jit(solution)/shard_map/ppermute | solution.py:30
  9.8 0.0 collective-permute-start.3
  9.8 0.6 %prepare.3.high_ref = f32[1760,128]{1,0:T(8,128)S(1)} custom-call(bf16[444,8,888]{2,1,0:T(8,128)(2,1)S(1)} %bitcast.4, bf16[444,128]{1,0:T(8,128)(2,1)S(1)} %joined.2.own_ref), custom_call_target="tpu_custom_call" | custom-call | flops 4294967296 | tf_op jit(solution)/shard_map/prepare/pallas_call | solution.py:149
  10.5 0.0 copy-start.2
  10.5 0.5 %collective-permute-done.3.mate_near_ref = s32[8,128]{1,0:T(8,128)S(1)} collective-permute-done((s32[8,128]{1,0:T(8,128)S(1)}, s32[8,128]{1,0:T(8,128)S(1)}, u32[]{:S(2)}, u32[]{:S(2)}) %collective-permute-start.3) | collective-permute-done | bytes 4128 | tf_op jit(solution)/shard_map/ppermute | solution.py:24
  11.0 0.9 %selections.1 = (bf16[1024,128]{1,0:T(8,128)(2,1)S(1)}, bf16[1024,128]{1,0:T(8,128)(2,1)S(1)}, bf16[1024,128]{1,0:T(8,128)(2,1)S(1)}, bf16[1024,128]{1,0:T(8,128)(2,1)S(1)}) custom-call(s32[8,128]{1,0:T(8,128)S(1)} %collective-permute-done.mate_ref, s32[16,128]{1,0:T(8,128)S(1)} %collective-permute-done.1.near_ref, ...), custom_call_target="tpu_custom_call" | custom-call | flops 1048576 | tf_op jit(solution)/shard_map/selections/pallas_call | solution.py:193
  11.9 1.2 %collective-permute-done.4.other_ref = bf16[444,128]{1,0:T(8,128)(2,1)S(1)} collective-permute-done((bf16[444,128]{1,0:T(8,128)(2,1)S(1)}, bf16[444,128]{1,0:T(8,128)(2,1)S(1)}, u32[]{:S(2)}, u32[]{:S(2)}) %collective-permute-start.4) | collective-permute-done | bytes 113696 | tf_op jit(solution)/shard_map/ppermute | solution.py:18
  13.1 1.9 %push_away.1 = (bf16[444,1024]{1,0:T(8,128)(2,1)S(1)}, bf16[444,256]{1,0:T(8,128)(2,1)S(1)}, bf16[444,128]{1,0:T(8,128)(2,1)S(1)}) custom-call(bf16[444,8,888]{2,1,0:T(8,128)(2,1)S(1)} %bitcast.5, f32[1792,128]{1,0:T(8,128)S(1)} %prepare.2.low_ref, f32[1760,128]{1,0:T(8,128)S(1)} %prepare.3.high_ref, bf16[444,128]{1,0:T(8,128)(2,1)S(1)} %collective-permute-done.4.other_ref, ...), custom_call_target="tpu_custom_call" | custom-call | flops 814743552 | bytes 6308352 | tf_op jit(solution)/shard_map/push_away/pallas_call | solution.py:255
  15.1 0.1 collective-permute-start.5
  15.1 2.5 %collective-permute-start.6 = (bf16[444,128]{1,0:T(8,128)(2,1)S(1)}, bf16[444,128]{1,0:T(8,128)(2,1)S(1)}, u32[]{:S(2)}, u32[]{:S(2)}) collective-permute-start(bf16[444,128]{1,0:T(8,128)(2,1)S(1)} %get-tuple-element.39), channel_id=1, source_target_pairs={{2,6},{4,0},{6,10},{8,4},{10,14},{12,8},{14,18},{16,12},{18,22},{2... | collective-permute-start | bytes 341000 | tf_op jit(solution)/shard_map/ppermute | solution.py:46
  17.6 0.0 collective-permute-done.5.came_ref
  17.6 0.4 %push_home.1 = (f32[444,128]{1,0:T(8,128)S(1)}, bf16[444,128]{1,0:T(8,128)(2,1)S(1)}) custom-call(bf16[444,1024]{1,0:T(8,128)(2,1)S(1)} %get-tuple-element.34.terms_ref, bf16[1024,128]{1,0:T(8,128)(2,1)S(1)} %home.1.home_ref, bf16[1024,128]{1,0:T(8,128)(2,1)S(1)} %get-tuple-element.36.near_select_ref, bf16[444,256]{1,0:T(8,128)(2,1)S(1)} %collective-permute-done.5.came_ref), custom_call_target="tpu_custom_call" | custom-call | flops 232783872 | bytes 1818624 | tf_op jit(solution)/shard_map/push_home/pallas_call | solution.py:290
  18.0 3.8 %collective-permute-start.9 = (bf16[444,128]{1,0:T(8,128)(2,1)S(1)}, bf16[444,128]{1,0:T(8,128)(2,1)S(1)}, u32[]{:S(2)}, u32[]{:S(2)}) collective-permute-start(bf16[444,128]{1,0:T(8,128)(2,1)S(1)} %get-tuple-element.40), channel_id=1, source_target_pairs={{2,5},{3,4},{4,3},{5,2},{6,9},{7,8},{8,7},{9,6},{10,13},{11,12},{1... | collective-permute-start | bytes 341000 | tf_op jit(solution)/shard_map/ppermute | solution.py:40
  21.9 2.9 %collective-permute-start.7 = (bf16[444,128]{1,0:T(8,128)(2,1)S(1)}, bf16[444,128]{1,0:T(8,128)(2,1)S(1)}, u32[]{:S(2)}, u32[]{:S(2)}) collective-permute-start(bf16[444,128]{1,0:T(8,128)(2,1)S(1)} %get-tuple-element.40), channel_id=1, source_target_pairs={{2,4},{4,2},{6,8},{8,6},{10,12},{12,10},{14,16},{16,14},{18,20},{2... | collective-permute-start | bytes 341000 | tf_op jit(solution)/shard_map/ppermute | solution.py:30
  24.7 0.0 collective-permute-done.6
  24.8 1.3 %collective-permute-start.8 = (bf16[444,128]{1,0:T(8,128)(2,1)S(1)}, bf16[444,128]{1,0:T(8,128)(2,1)S(1)}, u32[]{:S(2)}, u32[]{:S(2)}) collective-permute-start(bf16[444,128]{1,0:T(8,128)(2,1)S(1)} %fusion), channel_id=1, source_target_pairs={{0,1},{1,0},{2,3},{3,2},{4,5},{5,4},{6,7},{7,6},{8,9},{9,8},{10,11... | collective-permute-start | bytes 341000 | tf_op jit(solution)/shard_map/ppermute | solution.py:18
  26.1 2.9 %collective-permute-done.7 = bf16[444,128]{1,0:T(8,128)(2,1)S(1)} collective-permute-done((bf16[444,128]{1,0:T(8,128)(2,1)S(1)}, bf16[444,128]{1,0:T(8,128)(2,1)S(1)}, u32[]{:S(2)}, u32[]{:S(2)}) %collective-permute-start.7) | collective-permute-done | bytes 113696 | tf_op jit(solution)/shard_map/ppermute | solution.py:30
  29.0 0.8 %collective-permute-done.8 = bf16[444,128]{1,0:T(8,128)(2,1)S(1)} collective-permute-done((bf16[444,128]{1,0:T(8,128)(2,1)S(1)}, bf16[444,128]{1,0:T(8,128)(2,1)S(1)}, u32[]{:S(2)}, u32[]{:S(2)}) %collective-permute-start.8) | collective-permute-done | bytes 113696 | tf_op jit(solution)/shard_map/ppermute | solution.py:18
  29.8 0.0 collective-permute-done.9
  29.8 0.0 copy-done.2
  29.9 1.1 %joined.3 = bf16[444,128]{1,0:T(8,128)(2,1)} custom-call(bf16[444,888]{1,0:T(8,128)(2,1)S(1)} %copy-done.2, bf16[444,128]{1,0:T(8,128)(2,1)S(1)} %add_convert_fusion.1.own_ref, bf16[444,128]{1,0:T(8,128)(2,1)S(1)} %add_convert_fusion.other_ref), custom_call_target="tpu_custom_call" | custom-call | flops 100933632 | bytes 788544 | tf_op jit(solution)/shard_map/joined/pallas_call | solution.py:90
  (5 shorter events, 0.1 us)
Async XLA Ops:
  0.0 7.1 %copy-start.3 = (bf16[444,128]{1,0:T(8,128)(2,1)S(1)}, bf16[444,128]{1,0:T(8,128)(2,1)}, u32[]{:S(2)}) copy-start(bf16[444,128]{1,0:T(8,128)(2,1)} %own_ref) | copy-start | bytes 340996
  0.0 7.1 %copy-start.1 = (bf16[444,888]{1,0:T(8,128)(2,1)S(1)}, bf16[444,888]{1,0:T(8,128)(2,1)}, u32[]{:S(2)}) copy-start(bf16[444,888]{1,0:T(8,128)(2,1)} %matrix_ref.2) | copy-start | bytes 2365636
  0.0 7.9 %copy-start = (bf16[8,444,888]{2,0,1:T(8,128)(2,1)S(1)}, bf16[8,444,888]{2,0,1:T(8,128)(2,1)}, u32[]{:S(2)}) copy-start(bf16[8,444,888]{2,0,1:T(8,128)(2,1)} %param.9) | copy-start | bytes 18925060
  0.0 7.1 %collective-permute-start.2 = (bf16[444,128]{1,0:T(8,128)(2,1)}, bf16[444,128]{1,0:T(8,128)(2,1)S(1)}, u32[]{:S(2)}, u32[]{:S(2)}) collective-permute-start(bf16[444,128]{1,0:T(8,128)(2,1)} %own_ref), channel_id=1, source_target_pairs={{0,1},{1,0},{2,3},{3,2},{4,5},{5,4},{6,7},{7,6},{8,9},{9,8},{10,11... | collective-permute-start | bytes 341000 | tf_op jit(solution)/shard_map/ppermute | solution.py:18
  2.8 1.2 %collective-permute-start = (s32[8,128]{1,0:T(8,128)S(1)}, s32[8,128]{1,0:T(8,128)S(1)}, u32[]{:S(2)}, u32[]{:S(2)}) collective-permute-start(s32[8,128]{1,0:T(8,128)S(1)} %bitcast_select_fusion.code_ref), channel_id=1, source_target_pairs={{0,2},{2,0},{4,6},{6,4},{8,10},{10,8},{12,14},{14,12},{16,18},{18,... | collective-permute-start | bytes 12296 | tf_op jit(solution)/shard_map/ppermute | solution.py:24
  4.0 5.9 %collective-permute-start.1 = (s32[16,128]{1,0:T(8,128)S(1)}, s32[16,128]{1,0:T(8,128)S(1)}, u32[]{:S(2)}, u32[]{:S(2)}) collective-permute-start(s32[16,128]{1,0:T(8,128)S(1)} %pad_add_fusion), channel_id=1, source_target_pairs={{2,4},{4,2},{6,8},{8,6},{10,12},{12,10},{14,16},{16,14},{18,20},{2... | collective-permute-start | bytes 24584 | tf_op jit(solution)/shard_map/ppermute | solution.py:30
  7.5 5.6 %collective-permute-start.4 = (bf16[444,128]{1,0:T(8,128)(2,1)S(1)}, bf16[444,128]{1,0:T(8,128)(2,1)S(1)}, u32[]{:S(2)}, u32[]{:S(2)}) collective-permute-start(bf16[444,128]{1,0:T(8,128)(2,1)S(1)} %joined.2.own_ref), channel_id=1, source_target_pairs={{0,1},{1,0},{2,3},{3,2},{4,5},{5,4},{6,7},{7,6},{8,9},{9,8},{10,11... | collective-permute-start | bytes 341000 | tf_op jit(solution)/shard_map/ppermute | solution.py:18
  9.8 1.2 %collective-permute-start.3 = (s32[8,128]{1,0:T(8,128)S(1)}, s32[8,128]{1,0:T(8,128)S(1)}, u32[]{:S(2)}, u32[]{:S(2)}) collective-permute-start(s32[8,128]{1,0:T(8,128)S(1)} %slice.3), channel_id=1, source_target_pairs={{0,2},{2,0},{4,6},{6,4},{8,10},{10,8},{12,14},{14,12},{16,18},{18,... | collective-permute-start | bytes 12296 | tf_op jit(solution)/shard_map/ppermute | solution.py:24
  10.5 19.4 %copy-start.2 = (bf16[444,888]{1,0:T(8,128)(2,1)S(1)}, bf16[444,888]{1,0:T(8,128)(2,1)}, u32[]{:S(2)}) copy-start(bf16[444,888]{1,0:T(8,128)(2,1)} %matrix_ref.3) | copy-start | bytes 2365636
  15.1 2.5 %collective-permute-start.5 = (bf16[444,256]{1,0:T(8,128)(2,1)S(1)}, bf16[444,256]{1,0:T(8,128)(2,1)S(1)}, u32[]{:S(2)}, u32[]{:S(2)}) collective-permute-start(bf16[444,256]{1,0:T(8,128)(2,1)S(1)} %get-tuple-element.37), channel_id=1, source_target_pairs={{0,2},{2,0},{4,6},{6,4},{8,10},{10,8},{12,14},{14,12},{16,18},{18,... | collective-permute-start | bytes 681992 | tf_op jit(solution)/shard_map/ppermute | solution.py:24
  15.1 9.6 %collective-permute-start.6 = (bf16[444,128]{1,0:T(8,128)(2,1)S(1)}, bf16[444,128]{1,0:T(8,128)(2,1)S(1)}, u32[]{:S(2)}, u32[]{:S(2)}) collective-permute-start(bf16[444,128]{1,0:T(8,128)(2,1)S(1)} %get-tuple-element.39), channel_id=1, source_target_pairs={{2,6},{4,0},{6,10},{8,4},{10,14},{12,8},{14,18},{16,12},{18,22},{2... | collective-permute-start | bytes 341000 | tf_op jit(solution)/shard_map/ppermute | solution.py:46
  18.0 11.8 %collective-permute-start.9 = (bf16[444,128]{1,0:T(8,128)(2,1)S(1)}, bf16[444,128]{1,0:T(8,128)(2,1)S(1)}, u32[]{:S(2)}, u32[]{:S(2)}) collective-permute-start(bf16[444,128]{1,0:T(8,128)(2,1)S(1)} %get-tuple-element.40), channel_id=1, source_target_pairs={{2,5},{3,4},{4,3},{5,2},{6,9},{7,8},{8,7},{9,6},{10,13},{11,12},{1... | collective-permute-start | bytes 341000 | tf_op jit(solution)/shard_map/ppermute | solution.py:40
  21.9 7.1 %collective-permute-start.7 = (bf16[444,128]{1,0:T(8,128)(2,1)S(1)}, bf16[444,128]{1,0:T(8,128)(2,1)S(1)}, u32[]{:S(2)}, u32[]{:S(2)}) collective-permute-start(bf16[444,128]{1,0:T(8,128)(2,1)S(1)} %get-tuple-element.40), channel_id=1, source_target_pairs={{2,4},{4,2},{6,8},{8,6},{10,12},{12,10},{14,16},{16,14},{18,20},{2... | collective-permute-start | bytes 341000 | tf_op jit(solution)/shard_map/ppermute | solution.py:30
  24.8 5.0 %collective-permute-start.8 = (bf16[444,128]{1,0:T(8,128)(2,1)S(1)}, bf16[444,128]{1,0:T(8,128)(2,1)S(1)}, u32[]{:S(2)}, u32[]{:S(2)}) collective-permute-start(bf16[444,128]{1,0:T(8,128)(2,1)S(1)} %fusion), channel_id=1, source_target_pairs={{0,1},{1,0},{2,3},{3,2},{4,5},{5,4},{6,7},{7,6},{8,9},{9,8},{10,11... | collective-permute-start | bytes 341000 | tf_op jit(solution)/shard_map/ppermute | solution.py:18

commit v15 on v14

--- a/solution.py
+++ b/solution.py
@@ -275,32 +275,27 @@
     )(held, low, high, other, mate_select, far_select, mate_near)
 
 
-def push_home_kernel(terms_ref, home_ref, near_select_ref, came_ref, own_ref, near_ref):
-    cells = near_ref.shape[1]
-    chosen = jnp.concatenate([home_ref[...], near_select_ref[...]], axis=1)
-    total = jnp.dot(terms_ref[...], chosen, preferred_element_type=jnp.float32)
-    total = total + came_ref[...].astype(jnp.float32)
-    own_ref[...] = total[:, :cells]
-    near_ref[...] = total[:, cells:].astype(jnp.bfloat16)
-
-
-def push_home(terms, home, near_select, came):
+def push_home_kernel(column, terms_ref, select_ref, came_ref, out_ref):
+    cells = out_ref.shape[1]
+    total = jnp.dot(terms_ref[...], select_ref[...], preferred_element_type=jnp.float32)
+    came = came_ref[:, column * cells : (column + 1) * cells]
+    out_ref[...] = (total + came.astype(jnp.float32)).astype(out_ref.dtype)
+
+
+def push_home(terms, select, came, column, dtype):
     rows = terms.shape[0]
-    cells = home.shape[1]
-    return pl.pallas_call(
-        push_home_kernel,
-        out_shape=[
-            jax.ShapeDtypeStruct((rows, cells), jnp.float32),
-            jax.ShapeDtypeStruct((rows, cells), jnp.bfloat16),
-        ],
-        in_specs=[WHOLE] * 4,
-        out_specs=[WHOLE] * 2,
+    cells = select.shape[1]
+    return pl.pallas_call(
+        functools.partial(push_home_kernel, column),
+        out_shape=jax.ShapeDtypeStruct((rows, cells), dtype),
+        in_specs=[WHOLE] * 3,
+        out_specs=WHOLE,
         cost_estimate=pl.CostEstimate(
-            flops=2 * terms.size * 2 * cells, bytes_accessed=4 * terms.size, transcendentals=0
+            flops=2 * terms.size * cells, bytes_accessed=4 * terms.size, transcendentals=0
         ),
         compiler_params=pltpu.CompilerParams(vmem_limit_bytes=16 << 20),
         name="push_home",
-    )(terms, home, near_select, came)
+    )(terms, select, came)
 
 
 def shards(up_check, up_inverse, translate, down_inverse, list_slot, list_class, list_count):
@@ -349,7 +344,9 @@
     )
     mate_came = to_mate(mate_sum)
     far_came = to_far(far_sum)
-    own_sum, near_sum = push_home(terms, home, near_select, mate_came)
+    near_sum = push_home(terms, near_select, mate_came, 1, jnp.bfloat16)
+    terms, near_sum = lax.optimization_barrier((terms, near_sum))
+    own_sum = push_home(terms, home, mate_came, 0, jnp.float32)
     near_came = to_near(near_sum)
     if halves:
         near_crossed = to_near_crosswise(near_sum)

time: 31.1 us -> 31.4 us (level)
  Pallas kernels: 6.24 us -> 6.64 us
    ppermute x2, waiting for transfers between devices: 4.21 us -> 3.8 us  [to_near(): lax.ppermute(value, 'tile', [(a, b) for a, b in pairs if 0 <= b < count])]
    pallas_call x1 -> x2, Pallas kernels: 0.41 us -> 0.81 us  [push_home(): pl.pallas_call(functools.partial(push_home_kernel, column), out_shape=jax...]
  transfers between devices with their start and end apart: 10 -> 10, of which waited for: 6 -> 6; matrix products, arithmetic and copies ran while one was open for 4% -> 4% of each run, Pallas kernels for 10% -> 12%
where the time goes in v15:
time: 31.4 us; the launch traced here: 31.2 us
  starting transfers between devices  15.5 us (49%)
  waiting for transfers between devices  7.5 us (24%)
  Pallas kernels  6.64 us (21%)
  other arithmetic  1.35 us (4%)
    ppermute x2, starting transfers between devices, to_near(): lax.ppermute(value, 'tile', [(a, b) for a, b in pairs if 0 <= b < count])  5.95 us
    ppermute x1, starting transfers between devices, to_near_crosswise(): return lax.ppermute(value, ('tile', 'sub'), pairs)  3.82 us
    ppermute x2, waiting for transfers between devices, to_near(): lax.ppermute(value, 'tile', [(a, b) for a, b in pairs if 0 <= b < count])  3.8 us
    ppermute x3, starting transfers between devices, across_sub(): return lax.ppermute(shard, 'sub', [(0, 1), (1, 0)])  3.19 us
    ppermute x1, starting transfers between devices, to_far(): lax.ppermute(value, 'tile', [(a, b) for a, b in pairs if 0 <= b < count])  2.45 us
    ppermute x3, waiting for transfers between devices, across_sub(): return lax.ppermute(shard, 'sub', [(0, 1), (1, 0)])  2.23 us
    pallas_call x1, Pallas kernels, push_away(): pl.pallas_call(functools.partial(push_away_kernel, windows), out_shape=[j...  1.95 us
    pallas_call x2, Pallas kernels, joined_product(): pl.pallas_call(joined_kernel, out_shape=jax.ShapeDtypeStruct((rows, cells...  1.49 us
  transfers between devices with their start and end apart: 10, of which 6 were waited for; matrix products, arithmetic and copies ran while one was open for 4% of the time, Pallas kernels for 12%

profile of v15, /device:TPU:8, one launch (start us, length us, event | category | flops | bytes accessed | tf_op | source)
XLA Modules:
  0.0 31.2 jit_solution(7401273377339414257)
XLA Ops:
  0.0 0.0 copy-start.3
  0.0 0.0 copy-start.1
  0.0 0.0 copy-start
  0.0 1.6 %collective-permute-start.2 = (bf16[444,128]{1,0:T(8,128)(2,1)}, bf16[444,128]{1,0:T(8,128)(2,1)S(1)}, u32[]{:S(2)}, u32[]{:S(2)}) collective-permute-start(bf16[444,128]{1,0:T(8,128)(2,1)} %own_ref), channel_id=1, source_target_pairs={{0,1},{1,0},{2,3},{3,2},{4,5},{5,4},{6,7},{7,6},{8,9},{9,8},{10,11... | collective-permute-start | bytes 341000 | tf_op jit(solution)/shard_map/ppermute | solution.py:18
  1.6 1.2 %bitcast_select_fusion.code_ref = s32[8,128]{1,0:T(8,128)S(1)} fusion(s32[128,8]{0,1:T(8,128)} %param.11, s32[128,8]{0,1:T(8,128)} %param.12, s32[128]{0:T(128)} %param.13), kind=kLoop, calls=%fused_computation.5 | loop fusion | flops 4096 | bytes 12800 | tf_op jit(solution)/shard_map/jit(_where)/select_n | solution.py:311
  2.8 0.0 collective-permute-start
  2.8 0.2 home.1.select_ref
  3.0 0.9 %collective-permute-done.mate_ref = s32[8,128]{1,0:T(8,128)S(1)} collective-permute-done((s32[8,128]{1,0:T(8,128)S(1)}, s32[8,128]{1,0:T(8,128)S(1)}, u32[]{:S(2)}, u32[]{:S(2)}) %collective-permute-start) | collective-permute-done | bytes 4128 | tf_op jit(solution)/shard_map/ppermute | solution.py:24
  4.0 3.1 %collective-permute-start.1 = (s32[16,128]{1,0:T(8,128)S(1)}, s32[16,128]{1,0:T(8,128)S(1)}, u32[]{:S(2)}, u32[]{:S(2)}) collective-permute-start(s32[16,128]{1,0:T(8,128)S(1)} %pad_add_fusion), channel_id=1, source_target_pairs={{2,4},{4,2},{6,8},{8,6},{10,12},{12,10},{14,16},{16,14},{18,20},{2... | collective-permute-start | bytes 24584 | tf_op jit(solution)/shard_map/ppermute | solution.py:30
  7.1 0.0 collective-permute-done.2.other_ref
  7.1 0.0 copy-done.3
  7.1 0.0 copy-done.1
  7.1 0.4 %joined.2.own_ref = bf16[444,128]{1,0:T(8,128)(2,1)S(1)} custom-call(bf16[444,888]{1,0:T(8,128)(2,1)S(1)} %copy-done.1, bf16[444,128]{1,0:T(8,128)(2,1)S(1)} %copy-done.3, bf16[444,128]{1,0:T(8,128)(2,1)S(1)} %collective-permute-done.2.other_ref), custom_call_target="tpu_custom_call" | custom-call | flops 100933632 | bytes 788544 | tf_op jit(solution)/shard_map/joined/pallas_call | solution.py:90
  7.5 0.3 %collective-permute-start.4 = (bf16[444,128]{1,0:T(8,128)(2,1)S(1)}, bf16[444,128]{1,0:T(8,128)(2,1)S(1)}, u32[]{:S(2)}, u32[]{:S(2)}) collective-permute-start(bf16[444,128]{1,0:T(8,128)(2,1)S(1)} %joined.2.own_ref), channel_id=1, source_target_pairs={{0,1},{1,0},{2,3},{3,2},{4,5},{5,4},{6,7},{7,6},{8,9},{9,8},{10,11... | collective-permute-start | bytes 341000 | tf_op jit(solution)/shard_map/ppermute | solution.py:18
  7.9 0.0 copy-done
  7.9 0.6 %prepare.2.low_ref = f32[1792,128]{1,0:T(8,128)S(1)} custom-call(bf16[444,8,888]{2,1,0:T(8,128)(2,1)S(1)} %bitcast.3, bf16[444,128]{1,0:T(8,128)(2,1)S(1)} %joined.2.own_ref), custom_call_target="tpu_custom_call" | custom-call | flops 4294967296 | tf_op jit(solution)/shard_map/prepare/pallas_call | solution.py:149
  8.5 1.3 %collective-permute-done.1.near_ref = s32[16,128]{1,0:T(8,128)S(1)} collective-permute-done((s32[16,128]{1,0:T(8,128)S(1)}, s32[16,128]{1,0:T(8,128)S(1)}, u32[]{:S(2)}, u32[]{:S(2)}) %collective-permute-start.1) | collective-permute-done | bytes 8224 | tf_op jit(solution)/shard_map/ppermute | solution.py:30
  9.8 0.0 collective-permute-start.3
  9.8 0.6 %prepare.3.high_ref = f32[1760,128]{1,0:T(8,128)S(1)} custom-call(bf16[444,8,888]{2,1,0:T(8,128)(2,1)S(1)} %bitcast.4, bf16[444,128]{1,0:T(8,128)(2,1)S(1)} %joined.2.own_ref), custom_call_target="tpu_custom_call" | custom-call | flops 4294967296 | tf_op jit(solution)/shard_map/prepare/pallas_call | solution.py:149
  10.5 0.5 %collective-permute-done.3.mate_near_ref = s32[8,128]{1,0:T(8,128)S(1)} collective-permute-done((s32[8,128]{1,0:T(8,128)S(1)}, s32[8,128]{1,0:T(8,128)S(1)}, u32[]{:S(2)}, u32[]{:S(2)}) %collective-permute-start.3) | collective-permute-done | bytes 4128 | tf_op jit(solution)/shard_map/ppermute | solution.py:24
  11.0 0.9 %selections.1 = (bf16[1024,128]{1,0:T(8,128)(2,1)S(1)}, bf16[1024,128]{1,0:T(8,128)(2,1)S(1)}, bf16[1024,128]{1,0:T(8,128)(2,1)S(1)}, bf16[1024,128]{1,0:T(8,128)(2,1)S(1)}) custom-call(s32[8,128]{1,0:T(8,128)S(1)} %collective-permute-done.mate_ref, s32[16,128]{1,0:T(8,128)S(1)} %collective-permute-done.1.near_ref, ...), custom_call_target="tpu_custom_call" | custom-call | flops 1048576 | tf_op jit(solution)/shard_map/selections/pallas_call | solution.py:193
  11.9 1.2 %collective-permute-done.4.other_ref = bf16[444,128]{1,0:T(8,128)(2,1)S(1)} collective-permute-done((bf16[444,128]{1,0:T(8,128)(2,1)S(1)}, bf16[444,128]{1,0:T(8,128)(2,1)S(1)}, u32[]{:S(2)}, u32[]{:S(2)}) %collective-permute-start.4) | collective-permute-done | bytes 113696 | tf_op jit(solution)/shard_map/ppermute | solution.py:18
  13.1 0.0 copy-start.2
  13.1 1.9 %push_away.1 = (bf16[444,1024]{1,0:T(8,128)(2,1)S(1)}, bf16[444,256]{1,0:T(8,128)(2,1)S(1)}, bf16[444,128]{1,0:T(8,128)(2,1)S(1)}) custom-call(bf16[444,8,888]{2,1,0:T(8,128)(2,1)S(1)} %bitcast.5, f32[1792,128]{1,0:T(8,128)S(1)} %prepare.2.low_ref, f32[1760,128]{1,0:T(8,128)S(1)} %prepare.3.high_ref, bf16[444,128]{1,0:T(8,128)(2,1)S(1)} %collective-permute-done.4.other_ref, ...), custom_call_target="tpu_custom_call" | custom-call | flops 814743552 | bytes 6308352 | tf_op jit(solution)/shard_map/push_away/pallas_call | solution.py:255
  15.1 0.1 collective-permute-start.5
  15.1 2.5 %collective-permute-start.6 = (bf16[444,128]{1,0:T(8,128)(2,1)S(1)}, bf16[444,128]{1,0:T(8,128)(2,1)S(1)}, u32[]{:S(2)}, u32[]{:S(2)}) collective-permute-start(bf16[444,128]{1,0:T(8,128)(2,1)S(1)} %get-tuple-element.39), channel_id=1, source_target_pairs={{2,6},{4,0},{6,10},{8,4},{10,14},{12,8},{14,18},{16,12},{18,22},{2... | collective-permute-start | bytes 341000 | tf_op jit(solution)/shard_map/ppermute | solution.py:46
  17.6 0.0 collective-permute-done.5.came_ref
  17.6 0.4 %push_home.2 = bf16[444,128]{1,0:T(8,128)(2,1)S(1)} custom-call(bf16[444,1024]{1,0:T(8,128)(2,1)S(1)} %get-tuple-element.37.terms_ref, bf16[1024,128]{1,0:T(8,128)(2,1)S(1)} %get-tuple-element.35.select_ref, bf16[444,256]{1,0:T(8,128)(2,1)S(1)} %collective-permute-done.5.came_ref), custom_call_target="tpu_custom_call" | custom-call | flops 116391936 | bytes 1818624 | tf_op jit(solution)/shard_map/push_home/pallas_call | solution.py:288
  18.0 3.8 %collective-permute-start.9 = (bf16[444,128]{1,0:T(8,128)(2,1)S(1)}, bf16[444,128]{1,0:T(8,128)(2,1)S(1)}, u32[]{:S(2)}, u32[]{:S(2)}) collective-permute-start(bf16[444,128]{1,0:T(8,128)(2,1)S(1)} %push_home.2), channel_id=1, source_target_pairs={{2,5},{3,4},{4,3},{5,2},{6,9},{7,8},{8,7},{9,6},{10,13},{11,12},{1... | collective-permute-start | bytes 341000 | tf_op jit(solution)/shard_map/ppermute | solution.py:40
  21.8 2.9 %collective-permute-start.7 = (bf16[444,128]{1,0:T(8,128)(2,1)S(1)}, bf16[444,128]{1,0:T(8,128)(2,1)S(1)}, u32[]{:S(2)}, u32[]{:S(2)}) collective-permute-start(bf16[444,128]{1,0:T(8,128)(2,1)S(1)} %push_home.2), channel_id=1, source_target_pairs={{2,4},{4,2},{6,8},{8,6},{10,12},{12,10},{14,16},{16,14},{18,20},{2... | collective-permute-start | bytes 341000 | tf_op jit(solution)/shard_map/ppermute | solution.py:30
  24.7 0.0 collective-permute-done.6
  24.7 0.4 %push_home.3 = f32[444,128]{1,0:T(8,128)S(1)} custom-call(bf16[444,1024]{1,0:T(8,128)(2,1)S(1)} %get-tuple-element.37.terms_ref, bf16[1024,128]{1,0:T(8,128)(2,1)S(1)} %home.1.select_ref, bf16[444,256]{1,0:T(8,128)(2,1)S(1)} %collective-permute-done.5.came_ref), custom_call_target="tpu_custom_call" | custom-call | flops 116391936 | bytes 1818624 | tf_op jit(solution)/shard_map/push_home/pallas_call | solution.py:288
  25.2 1.3 %collective-permute-start.8 = (bf16[444,128]{1,0:T(8,128)(2,1)S(1)}, bf16[444,128]{1,0:T(8,128)(2,1)S(1)}, u32[]{:S(2)}, u32[]{:S(2)}) collective-permute-start(bf16[444,128]{1,0:T(8,128)(2,1)S(1)} %fusion), channel_id=1, source_target_pairs={{0,1},{1,0},{2,3},{3,2},{4,5},{5,4},{6,7},{7,6},{8,9},{9,8},{10,11... | collective-permute-start | bytes 341000 | tf_op jit(solution)/shard_map/ppermute | solution.py:18
  26.5 2.5 %collective-permute-done.7 = bf16[444,128]{1,0:T(8,128)(2,1)S(1)} collective-permute-done((bf16[444,128]{1,0:T(8,128)(2,1)S(1)}, bf16[444,128]{1,0:T(8,128)(2,1)S(1)}, u32[]{:S(2)}, u32[]{:S(2)}) %collective-permute-start.7) | collective-permute-done | bytes 113696 | tf_op jit(solution)/shard_map/ppermute | solution.py:30
  29.0 1.0 %collective-permute-done.8 = bf16[444,128]{1,0:T(8,128)(2,1)S(1)} collective-permute-done((bf16[444,128]{1,0:T(8,128)(2,1)S(1)}, bf16[444,128]{1,0:T(8,128)(2,1)S(1)}, u32[]{:S(2)}, u32[]{:S(2)}) %collective-permute-start.8) | collective-permute-done | bytes 113696 | tf_op jit(solution)/shard_map/ppermute | solution.py:18
  30.1 0.0 collective-permute-done.9
  30.1 0.0 copy-done.2
  30.1 1.1 %joined.3 = bf16[444,128]{1,0:T(8,128)(2,1)} custom-call(bf16[444,888]{1,0:T(8,128)(2,1)S(1)} %copy-done.2, bf16[444,128]{1,0:T(8,128)(2,1)S(1)} %add_convert_fusion.1.own_ref, bf16[444,128]{1,0:T(8,128)(2,1)S(1)} %add_convert_fusion.other_ref), custom_call_target="tpu_custom_call" | custom-call | flops 100933632 | bytes 788544 | tf_op jit(solution)/shard_map/joined/pallas_call | solution.py:90
  (5 shorter events, 0.1 us)
Async XLA Ops:
  0.0 7.1 %copy-start.3 = (bf16[444,128]{1,0:T(8,128)(2,1)S(1)}, bf16[444,128]{1,0:T(8,128)(2,1)}, u32[]{:S(2)}) copy-start(bf16[444,128]{1,0:T(8,128)(2,1)} %own_ref) | copy-start | bytes 340996
  0.0 7.1 %copy-start.1 = (bf16[444,888]{1,0:T(8,128)(2,1)S(1)}, bf16[444,888]{1,0:T(8,128)(2,1)}, u32[]{:S(2)}) copy-start(bf16[444,888]{1,0:T(8,128)(2,1)} %matrix_ref.2) | copy-start | bytes 2365636
  0.0 7.9 %copy-start = (bf16[8,444,888]{2,0,1:T(8,128)(2,1)S(1)}, bf16[8,444,888]{2,0,1:T(8,128)(2,1)}, u32[]{:S(2)}) copy-start(bf16[8,444,888]{2,0,1:T(8,128)(2,1)} %param.9) | copy-start | bytes 18925060
  0.0 7.1 %collective-permute-start.2 = (bf16[444,128]{1,0:T(8,128)(2,1)}, bf16[444,128]{1,0:T(8,128)(2,1)S(1)}, u32[]{:S(2)}, u32[]{:S(2)}) collective-permute-start(bf16[444,128]{1,0:T(8,128)(2,1)} %own_ref), channel_id=1, source_target_pairs={{0,1},{1,0},{2,3},{3,2},{4,5},{5,4},{6,7},{7,6},{8,9},{9,8},{10,11... | collective-permute-start | bytes 341000 | tf_op jit(solution)/shard_map/ppermute | solution.py:18
  2.8 1.2 %collective-permute-start = (s32[8,128]{1,0:T(8,128)S(1)}, s32[8,128]{1,0:T(8,128)S(1)}, u32[]{:S(2)}, u32[]{:S(2)}) collective-permute-start(s32[8,128]{1,0:T(8,128)S(1)} %bitcast_select_fusion.code_ref), channel_id=1, source_target_pairs={{0,2},{2,0},{4,6},{6,4},{8,10},{10,8},{12,14},{14,12},{16,18},{18,... | collective-permute-start | bytes 12296 | tf_op jit(solution)/shard_map/ppermute | solution.py:24
  4.0 5.9 %collective-permute-start.1 = (s32[16,128]{1,0:T(8,128)S(1)}, s32[16,128]{1,0:T(8,128)S(1)}, u32[]{:S(2)}, u32[]{:S(2)}) collective-permute-start(s32[16,128]{1,0:T(8,128)S(1)} %pad_add_fusion), channel_id=1, source_target_pairs={{2,4},{4,2},{6,8},{8,6},{10,12},{12,10},{14,16},{16,14},{18,20},{2... | collective-permute-start | bytes 24584 | tf_op jit(solution)/shard_map/ppermute | solution.py:30
  7.5 5.6 %collective-permute-start.4 = (bf16[444,128]{1,0:T(8,128)(2,1)S(1)}, bf16[444,128]{1,0:T(8,128)(2,1)S(1)}, u32[]{:S(2)}, u32[]{:S(2)}) collective-permute-start(bf16[444,128]{1,0:T(8,128)(2,1)S(1)} %joined.2.own_ref), channel_id=1, source_target_pairs={{0,1},{1,0},{2,3},{3,2},{4,5},{5,4},{6,7},{7,6},{8,9},{9,8},{10,11... | collective-permute-start | bytes 341000 | tf_op jit(solution)/shard_map/ppermute | solution.py:18
  9.8 1.2 %collective-permute-start.3 = (s32[8,128]{1,0:T(8,128)S(1)}, s32[8,128]{1,0:T(8,128)S(1)}, u32[]{:S(2)}, u32[]{:S(2)}) collective-permute-start(s32[8,128]{1,0:T(8,128)S(1)} %slice.3), channel_id=1, source_target_pairs={{0,2},{2,0},{4,6},{6,4},{8,10},{10,8},{12,14},{14,12},{16,18},{18,... | collective-permute-start | bytes 12296 | tf_op jit(solution)/shard_map/ppermute | solution.py:24
  13.1 17.0 %copy-start.2 = (bf16[444,888]{1,0:T(8,128)(2,1)S(1)}, bf16[444,888]{1,0:T(8,128)(2,1)}, u32[]{:S(2)}) copy-start(bf16[444,888]{1,0:T(8,128)(2,1)} %matrix_ref.3) | copy-start | bytes 2365636
  15.1 2.5 %collective-permute-start.5 = (bf16[444,256]{1,0:T(8,128)(2,1)S(1)}, bf16[444,256]{1,0:T(8,128)(2,1)S(1)}, u32[]{:S(2)}, u32[]{:S(2)}) collective-permute-start(bf16[444,256]{1,0:T(8,128)(2,1)S(1)} %get-tuple-element.36), channel_id=1, source_target_pairs={{0,2},{2,0},{4,6},{6,4},{8,10},{10,8},{12,14},{14,12},{16,18},{18,... | collective-permute-start | bytes 681992 | tf_op jit(solution)/shard_map/ppermute | solution.py:24
  15.1 9.6 %collective-permute-start.6 = (bf16[444,128]{1,0:T(8,128)(2,1)S(1)}, bf16[444,128]{1,0:T(8,128)(2,1)S(1)}, u32[]{:S(2)}, u32[]{:S(2)}) collective-permute-start(bf16[444,128]{1,0:T(8,128)(2,1)S(1)} %get-tuple-element.39), channel_id=1, source_target_pairs={{2,6},{4,0},{6,10},{8,4},{10,14},{12,8},{14,18},{16,12},{18,22},{2... | collective-permute-start | bytes 341000 | tf_op jit(solution)/shard_map/ppermute | solution.py:46
  18.0 12.0 %collective-permute-start.9 = (bf16[444,128]{1,0:T(8,128)(2,1)S(1)}, bf16[444,128]{1,0:T(8,128)(2,1)S(1)}, u32[]{:S(2)}, u32[]{:S(2)}) collective-permute-start(bf16[444,128]{1,0:T(8,128)(2,1)S(1)} %push_home.2), channel_id=1, source_target_pairs={{2,5},{3,4},{4,3},{5,2},{6,9},{7,8},{8,7},{9,6},{10,13},{11,12},{1... | collective-permute-start | bytes 341000 | tf_op jit(solution)/shard_map/ppermute | solution.py:40
  21.8 7.1 %collective-permute-start.7 = (bf16[444,128]{1,0:T(8,128)(2,1)S(1)}, bf16[444,128]{1,0:T(8,128)(2,1)S(1)}, u32[]{:S(2)}, u32[]{:S(2)}) collective-permute-start(bf16[444,128]{1,0:T(8,128)(2,1)S(1)} %push_home.2), channel_id=1, source_target_pairs={{2,4},{4,2},{6,8},{8,6},{10,12},{12,10},{14,16},{16,14},{18,20},{2... | collective-permute-start | bytes 341000 | tf_op jit(solution)/shard_map/ppermute | solution.py:30
  25.2 4.9 %collective-permute-start.8 = (bf16[444,128]{1,0:T(8,128)(2,1)S(1)}, bf16[444,128]{1,0:T(8,128)(2,1)S(1)}, u32[]{:S(2)}, u32[]{:S(2)}) collective-permute-start(bf16[444,128]{1,0:T(8,128)(2,1)S(1)} %fusion), channel_id=1, source_target_pairs={{0,1},{1,0},{2,3},{3,2},{4,5},{5,4},{6,7},{7,6},{8,9},{9,8},{10,11... | collective-permute-start | bytes 341000 | tf_op jit(solution)/shard_map/ppermute | solution.py:18

commit v16 on v12

--- a/solution.py
+++ b/solution.py
@@ -369,6 +369,10 @@
     cells, entries = list_slot.shape
     halves = lax.axis_size("sub") == 2
 
+    if halves:
+        other_check = across_sub(up_check)
+        list_slot, up_check = lax.optimization_barrier((list_slot, up_check))
+
     active = lax.broadcasted_iota(jnp.int32, (entries, cells), 0) < list_count[None, :]
     code = jnp.where(active, (list_class.T << CLASS_SHIFT) + list_slot.T, -1)
     mate_code, home = lax.optimization_barrier((to_mate(code), home_selection(code, classes)))
@@ -377,7 +381,7 @@
     operators = jnp.transpose(translate, (1, 0, 2))
     if halves:
         windows = half_windows(rows, depth, 2)
-        equivalent = joined_product(up_inverse, up_check, across_sub(up_check))
+        equivalent = joined_product(up_inverse, up_check, other_check)
         other = across_sub(equivalent)
     else:
         windows = [(0, depth, 0)]

time: 31.3 us -> 31.2 us (level)
  starting transfers between devices: 17.6 us -> 15.5 us
  waiting for transfers between devices: 5.8 us -> 7.35 us
  other arithmetic: 0.97 us -> 1.35 us
    ppermute x2, waiting for transfers between devices: 3.15 us -> 4.21 us  [to_near(): lax.ppermute(value, 'tile', [(a, b) for a, b in pairs if 0 <= b < count])]
    ppermute x3, waiting for transfers between devices: 0.49 us -> 1.45 us  [to_mate(): return lax.ppermute(value, 'tile', pairs)]
    ppermute x1, starting transfers between devices: 3.31 us -> 2.46 us  [to_far(): lax.ppermute(value, 'tile', [(a, b) for a, b in pairs if 0 <= b < count])]
    ppermute x3, starting transfers between devices: 3.7 us -> 3.19 us  [across_sub(): return lax.ppermute(shard, 'sub', [(0, 1), (1, 0)])]
    ppermute x3, waiting for transfers between devices: 2.15 us -> 1.68 us  [across_sub(): return lax.ppermute(shard, 'sub', [(0, 1), (1, 0)])]
    select_n x1, other arithmetic: 0.86 us -> 1.25 us  [shards(): code = jnp.where(active, (list_class.T << CLASS_SHIFT) + list_slot.T, -1)]
    ppermute x2, starting transfers between devices: 6.32 us -> 5.96 us  [to_near(): lax.ppermute(value, 'tile', [(a, b) for a, b in pairs if 0 <= b < count])]
    ppermute x1, starting transfers between devices: 4.17 us -> 3.82 us  [to_near_crosswise(): return lax.ppermute(value, ('tile', 'sub'), pairs)]
  transfers between devices with their start and end apart: 10 -> 10, of which waited for: 5 -> 6; matrix products, arithmetic and copies ran while one was open for 0% -> 4% of each run, Pallas kernels for 11% -> 11%
where the time goes in v16:
time: 31.2 us; the launch traced here: 30.8 us
  starting transfers between devices  15.5 us (50%)
  waiting for transfers between devices  7.35 us (24%)
  Pallas kernels  6.42 us (21%)
  other arithmetic  1.35 us (4%)
    ppermute x2, starting transfers between devices, to_near(): lax.ppermute(value, 'tile', [(a, b) for a, b in pairs if 0 <= b < count])  5.96 us
    ppermute x2, waiting for transfers between devices, to_near(): lax.ppermute(value, 'tile', [(a, b) for a, b in pairs if 0 <= b < count])  4.21 us
    ppermute x1, starting transfers between devices, to_near_crosswise(): return lax.ppermute(value, ('tile', 'sub'), pairs)  3.82 us
    ppermute x3, starting transfers between devices, across_sub(): return lax.ppermute(shard, 'sub', [(0, 1), (1, 0)])  3.19 us
    ppermute x1, starting transfers between devices, to_far(): lax.ppermute(value, 'tile', [(a, b) for a, b in pairs if 0 <= b < count])  2.46 us
    pallas_call x1, Pallas kernels, push_away(): pl.pallas_call(functools.partial(push_away_kernel, windows), out_shape=[j...  1.94 us
    ppermute x3, waiting for transfers between devices, across_sub(): return lax.ppermute(shard, 'sub', [(0, 1), (1, 0)])  1.68 us
    ppermute x3, waiting for transfers between devices, to_mate(): return lax.ppermute(value, 'tile', pairs)  1.45 us
  transfers between devices with their start and end apart: 10, of which 6 were waited for; matrix products, arithmetic and copies ran while one was open for 4% of the time, Pallas kernels for 11%

profile of v16, /device:TPU:8, one launch (start us, length us, event | category | flops | bytes accessed | tf_op | source)
XLA Modules:
  0.0 30.8 jit_solution(15307421234361273781)
XLA Ops:
  0.0 0.0 copy-start.3
  0.0 0.0 copy-start.2
  0.0 0.0 copy-start
  0.0 1.6 %collective-permute-start.2 = (bf16[444,128]{1,0:T(8,128)(2,1)}, bf16[444,128]{1,0:T(8,128)(2,1)S(1)}, u32[]{:S(2)}, u32[]{:S(2)}) collective-permute-start(bf16[444,128]{1,0:T(8,128)(2,1)} %own_ref), channel_id=1, source_target_pairs={{0,1},{1,0},{2,3},{3,2},{4,5},{5,4},{6,7},{7,6},{8,9},{9,8},{10,11... | collective-permute-start | bytes 341000 | tf_op jit(solution)/shard_map/ppermute | solution.py:18
  1.6 1.2 %bitcast_select_fusion.code_ref = s32[8,128]{1,0:T(8,128)S(1)} fusion(s32[128,8]{0,1:T(8,128)} %param.11, s32[128,8]{0,1:T(8,128)} %param.12, s32[128]{0:T(128)} %param.13), kind=kLoop, calls=%fused_computation.5 | loop fusion | flops 4096 | bytes 12800 | tf_op jit(solution)/shard_map/jit(_where)/select_n | solution.py:377
  2.8 0.0 collective-permute-start
  2.8 0.2 home.1.home_ref
  3.0 0.9 %collective-permute-done.mate_ref = s32[8,128]{1,0:T(8,128)S(1)} collective-permute-done((s32[8,128]{1,0:T(8,128)S(1)}, s32[8,128]{1,0:T(8,128)S(1)}, u32[]{:S(2)}, u32[]{:S(2)}) %collective-permute-start) | collective-permute-done | bytes 4128 | tf_op jit(solution)/shard_map/ppermute | solution.py:24
  4.0 3.1 %collective-permute-start.1 = (s32[16,128]{1,0:T(8,128)S(1)}, s32[16,128]{1,0:T(8,128)S(1)}, u32[]{:S(2)}, u32[]{:S(2)}) collective-permute-start(s32[16,128]{1,0:T(8,128)S(1)} %pad_add_fusion), channel_id=1, source_target_pairs={{2,4},{4,2},{6,8},{8,6},{10,12},{12,10},{14,16},{16,14},{18,20},{2... | collective-permute-start | bytes 24584 | tf_op jit(solution)/shard_map/ppermute | solution.py:30
  7.1 0.0 collective-permute-done.2.other_ref
  7.1 0.0 copy-done.3
  7.1 0.0 copy-done.2
  7.1 0.4 %joined.1.own_ref = bf16[444,128]{1,0:T(8,128)(2,1)S(1)} custom-call(bf16[444,888]{1,0:T(8,128)(2,1)S(1)} %copy-done.2, bf16[444,128]{1,0:T(8,128)(2,1)S(1)} %copy-done.3, bf16[444,128]{1,0:T(8,128)(2,1)S(1)} %collective-permute-done.2.other_ref), custom_call_target="tpu_custom_call" | custom-call | flops 100933632 | bytes 788544 | tf_op jit(solution)/shard_map/joined/pallas_call | solution.py:90
  7.5 0.3 %collective-permute-start.4 = (bf16[444,128]{1,0:T(8,128)(2,1)S(1)}, bf16[444,128]{1,0:T(8,128)(2,1)S(1)}, u32[]{:S(2)}, u32[]{:S(2)}) collective-permute-start(bf16[444,128]{1,0:T(8,128)(2,1)S(1)} %joined.1.own_ref), channel_id=1, source_target_pairs={{0,1},{1,0},{2,3},{3,2},{4,5},{5,4},{6,7},{7,6},{8,9},{9,8},{10,11... | collective-permute-start | bytes 341000 | tf_op jit(solution)/shard_map/ppermute | solution.py:18
  7.9 0.0 copy-done
  7.9 0.6 %prepare.2.low_ref = f32[1792,128]{1,0:T(8,128)S(1)} custom-call(bf16[444,8,888]{2,1,0:T(8,128)(2,1)S(1)} %bitcast.3, bf16[444,128]{1,0:T(8,128)(2,1)S(1)} %joined.1.own_ref), custom_call_target="tpu_custom_call" | custom-call | flops 4294967296 | tf_op jit(solution)/shard_map/prepare/pallas_call | solution.py:210
  8.5 1.3 %collective-permute-done.1.near_ref = s32[16,128]{1,0:T(8,128)S(1)} collective-permute-done((s32[16,128]{1,0:T(8,128)S(1)}, s32[16,128]{1,0:T(8,128)S(1)}, u32[]{:S(2)}, u32[]{:S(2)}) %collective-permute-start.1) | collective-permute-done | bytes 8224 | tf_op jit(solution)/shard_map/ppermute | solution.py:30
  9.8 0.0 collective-permute-start.3
  9.8 0.6 %prepare.3.high_ref = f32[1760,128]{1,0:T(8,128)S(1)} custom-call(bf16[444,8,888]{2,1,0:T(8,128)(2,1)S(1)} %bitcast.4, bf16[444,128]{1,0:T(8,128)(2,1)S(1)} %joined.1.own_ref), custom_call_target="tpu_custom_call" | custom-call | flops 4294967296 | tf_op jit(solution)/shard_map/prepare/pallas_call | solution.py:210
  10.5 0.0 copy-start.1
  10.5 0.5 %collective-permute-done.3.mate_near_ref = s32[8,128]{1,0:T(8,128)S(1)} collective-permute-done((s32[8,128]{1,0:T(8,128)S(1)}, s32[8,128]{1,0:T(8,128)S(1)}, u32[]{:S(2)}, u32[]{:S(2)}) %collective-permute-start.3) | collective-permute-done | bytes 4128 | tf_op jit(solution)/shard_map/ppermute | solution.py:24
  11.0 0.9 %selections.1 = (bf16[1024,128]{1,0:T(8,128)(2,1)S(1)}, bf16[1024,128]{1,0:T(8,128)(2,1)S(1)}, bf16[1024,128]{1,0:T(8,128)(2,1)S(1)}, bf16[1024,128]{1,0:T(8,128)(2,1)S(1)}) custom-call(s32[8,128]{1,0:T(8,128)S(1)} %collective-permute-done.mate_ref, s32[16,128]{1,0:T(8,128)S(1)} %collective-permute-done.1.near_ref, ...), custom_call_target="tpu_custom_call" | custom-call | flops 1048576 | tf_op jit(solution)/shard_map/selections/pallas_call | solution.py:254
  11.9 1.2 %collective-permute-done.4.other_ref = bf16[444,128]{1,0:T(8,128)(2,1)S(1)} collective-permute-done((bf16[444,128]{1,0:T(8,128)(2,1)S(1)}, bf16[444,128]{1,0:T(8,128)(2,1)S(1)}, u32[]{:S(2)}, u32[]{:S(2)}) %collective-permute-start.4) | collective-permute-done | bytes 113696 | tf_op jit(solution)/shard_map/ppermute | solution.py:18
  13.1 1.9 %push_away.1 = (bf16[444,1024]{1,0:T(8,128)(2,1)S(1)}, bf16[444,256]{1,0:T(8,128)(2,1)S(1)}, bf16[444,128]{1,0:T(8,128)(2,1)S(1)}) custom-call(bf16[444,8,888]{2,1,0:T(8,128)(2,1)S(1)} %bitcast.5, f32[1792,128]{1,0:T(8,128)S(1)} %prepare.2.low_ref, f32[1760,128]{1,0:T(8,128)S(1)} %prepare.3.high_ref, bf16[444,128]{1,0:T(8,128)(2,1)S(1)} %collective-permute-done.4.other_ref, ...), custom_call_target="tpu_custom_call" | custom-call | flops 814743552 | bytes 6308352 | tf_op jit(solution)/shard_map/push_away/pallas_call | solution.py:316
  15.1 0.1 collective-permute-start.5
  15.1 2.5 %collective-permute-start.6 = (bf16[444,128]{1,0:T(8,128)(2,1)S(1)}, bf16[444,128]{1,0:T(8,128)(2,1)S(1)}, u32[]{:S(2)}, u32[]{:S(2)}) collective-permute-start(bf16[444,128]{1,0:T(8,128)(2,1)S(1)} %get-tuple-element.39), channel_id=1, source_target_pairs={{2,6},{4,0},{6,10},{8,4},{10,14},{12,8},{14,18},{16,12},{18,22},{2... | collective-permute-start | bytes 341000 | tf_op jit(solution)/shard_map/ppermute | solution.py:46
  17.6 0.0 collective-permute-done.5.came_ref
  17.6 0.4 %push_home.1 = (f32[444,128]{1,0:T(8,128)S(1)}, bf16[444,128]{1,0:T(8,128)(2,1)S(1)}) custom-call(bf16[444,1024]{1,0:T(8,128)(2,1)S(1)} %get-tuple-element.34.terms_ref, bf16[1024,128]{1,0:T(8,128)(2,1)S(1)} %home.1.home_ref, bf16[1024,128]{1,0:T(8,128)(2,1)S(1)} %get-tuple-element.36.near_select_ref, bf16[444,256]{1,0:T(8,128)(2,1)S(1)} %collective-permute-done.5.came_ref), custom_call_target="tpu_custom_call" | custom-call | flops 232783872 | bytes 1818624 | tf_op jit(solution)/shard_map/push_home/pallas_call | solution.py:351
  18.0 3.8 %collective-permute-start.9 = (bf16[444,128]{1,0:T(8,128)(2,1)S(1)}, bf16[444,128]{1,0:T(8,128)(2,1)S(1)}, u32[]{:S(2)}, u32[]{:S(2)}) collective-permute-start(bf16[444,128]{1,0:T(8,128)(2,1)S(1)} %get-tuple-element.40), channel_id=1, source_target_pairs={{2,5},{3,4},{4,3},{5,2},{6,9},{7,8},{8,7},{9,6},{10,13},{11,12},{1... | collective-permute-start | bytes 341000 | tf_op jit(solution)/shard_map/ppermute | solution.py:40
  21.9 2.9 %collective-permute-start.7 = (bf16[444,128]{1,0:T(8,128)(2,1)S(1)}, bf16[444,128]{1,0:T(8,128)(2,1)S(1)}, u32[]{:S(2)}, u32[]{:S(2)}) collective-permute-start(bf16[444,128]{1,0:T(8,128)(2,1)S(1)} %get-tuple-element.40), channel_id=1, source_target_pairs={{2,4},{4,2},{6,8},{8,6},{10,12},{12,10},{14,16},{16,14},{18,20},{2... | collective-permute-start | bytes 341000 | tf_op jit(solution)/shard_map/ppermute | solution.py:30
  24.7 0.0 collective-permute-done.6
  24.8 1.3 %collective-permute-start.8 = (bf16[444,128]{1,0:T(8,128)(2,1)S(1)}, bf16[444,128]{1,0:T(8,128)(2,1)S(1)}, u32[]{:S(2)}, u32[]{:S(2)}) collective-permute-start(bf16[444,128]{1,0:T(8,128)(2,1)S(1)} %fusion), channel_id=1, source_target_pairs={{0,1},{1,0},{2,3},{3,2},{4,5},{5,4},{6,7},{7,6},{8,9},{9,8},{10,11... | collective-permute-start | bytes 341000 | tf_op jit(solution)/shard_map/ppermute | solution.py:18
  26.1 2.9 %collective-permute-done.7 = bf16[444,128]{1,0:T(8,128)(2,1)S(1)} collective-permute-done((bf16[444,128]{1,0:T(8,128)(2,1)S(1)}, bf16[444,128]{1,0:T(8,128)(2,1)S(1)}, u32[]{:S(2)}, u32[]{:S(2)}) %collective-permute-start.7) | collective-permute-done | bytes 113696 | tf_op jit(solution)/shard_map/ppermute | solution.py:30
  29.0 0.0 copy-done.1
  29.0 0.3 first.1.part_ref
  29.3 0.5 %collective-permute-done.8 = bf16[444,128]{1,0:T(8,128)(2,1)S(1)} collective-permute-done((bf16[444,128]{1,0:T(8,128)(2,1)S(1)}, bf16[444,128]{1,0:T(8,128)(2,1)S(1)}, u32[]{:S(2)}, u32[]{:S(2)}) %collective-permute-start.8) | collective-permute-done | bytes 113696 | tf_op jit(solution)/shard_map/ppermute | solution.py:18
  29.8 0.0 collective-permute-done.9
  29.8 1.0 %rest.1 = bf16[444,128]{1,0:T(8,128)(2,1)} custom-call(bf16[444,888]{1,0:T(8,128)(2,1)S(1)} %copy-done.1, f32[444,128]{1,0:T(8,128)S(1)} %first.1.part_ref, bf16[444,128]{1,0:T(8,128)(2,1)S(1)} %add_convert_fusion.other_ref), custom_call_target="tpu_custom_call" | custom-call | flops 58195968 | bytes 454656 | tf_op jit(solution)/shard_map/rest/pallas_call | solution.py:151
  (5 shorter events, 0.1 us)
Async XLA Ops:
  0.0 7.1 %copy-start.3 = (bf16[444,128]{1,0:T(8,128)(2,1)S(1)}, bf16[444,128]{1,0:T(8,128)(2,1)}, u32[]{:S(2)}) copy-start(bf16[444,128]{1,0:T(8,128)(2,1)} %own_ref) | copy-start | bytes 340996
  0.0 7.1 %copy-start.2 = (bf16[444,888]{1,0:T(8,128)(2,1)S(1)}, bf16[444,888]{1,0:T(8,128)(2,1)}, u32[]{:S(2)}) copy-start(bf16[444,888]{1,0:T(8,128)(2,1)} %matrix_ref.3) | copy-start | bytes 2365636
  0.0 7.9 %copy-start = (bf16[8,444,888]{2,0,1:T(8,128)(2,1)S(1)}, bf16[8,444,888]{2,0,1:T(8,128)(2,1)}, u32[]{:S(2)}) copy-start(bf16[8,444,888]{2,0,1:T(8,128)(2,1)} %param.9) | copy-start | bytes 18925060
  0.0 7.1 %collective-permute-start.2 = (bf16[444,128]{1,0:T(8,128)(2,1)}, bf16[444,128]{1,0:T(8,128)(2,1)S(1)}, u32[]{:S(2)}, u32[]{:S(2)}) collective-permute-start(bf16[444,128]{1,0:T(8,128)(2,1)} %own_ref), channel_id=1, source_target_pairs={{0,1},{1,0},{2,3},{3,2},{4,5},{5,4},{6,7},{7,6},{8,9},{9,8},{10,11... | collective-permute-start | bytes 341000 | tf_op jit(solution)/shard_map/ppermute | solution.py:18
  2.8 1.2 %collective-permute-start = (s32[8,128]{1,0:T(8,128)S(1)}, s32[8,128]{1,0:T(8,128)S(1)}, u32[]{:S(2)}, u32[]{:S(2)}) collective-permute-start(s32[8,128]{1,0:T(8,128)S(1)} %bitcast_select_fusion.code_ref), channel_id=1, source_target_pairs={{0,2},{2,0},{4,6},{6,4},{8,10},{10,8},{12,14},{14,12},{16,18},{18,... | collective-permute-start | bytes 12296 | tf_op jit(solution)/shard_map/ppermute | solution.py:24
  4.0 5.9 %collective-permute-start.1 = (s32[16,128]{1,0:T(8,128)S(1)}, s32[16,128]{1,0:T(8,128)S(1)}, u32[]{:S(2)}, u32[]{:S(2)}) collective-permute-start(s32[16,128]{1,0:T(8,128)S(1)} %pad_add_fusion), channel_id=1, source_target_pairs={{2,4},{4,2},{6,8},{8,6},{10,12},{12,10},{14,16},{16,14},{18,20},{2... | collective-permute-start | bytes 24584 | tf_op jit(solution)/shard_map/ppermute | solution.py:30
  7.5 5.6 %collective-permute-start.4 = (bf16[444,128]{1,0:T(8,128)(2,1)S(1)}, bf16[444,128]{1,0:T(8,128)(2,1)S(1)}, u32[]{:S(2)}, u32[]{:S(2)}) collective-permute-start(bf16[444,128]{1,0:T(8,128)(2,1)S(1)} %joined.1.own_ref), channel_id=1, source_target_pairs={{0,1},{1,0},{2,3},{3,2},{4,5},{5,4},{6,7},{7,6},{8,9},{9,8},{10,11... | collective-permute-start | bytes 341000 | tf_op jit(solution)/shard_map/ppermute | solution.py:18
  9.8 1.2 %collective-permute-start.3 = (s32[8,128]{1,0:T(8,128)S(1)}, s32[8,128]{1,0:T(8,128)S(1)}, u32[]{:S(2)}, u32[]{:S(2)}) collective-permute-start(s32[8,128]{1,0:T(8,128)S(1)} %slice.3), channel_id=1, source_target_pairs={{0,2},{2,0},{4,6},{6,4},{8,10},{10,8},{12,14},{14,12},{16,18},{18,... | collective-permute-start | bytes 12296 | tf_op jit(solution)/shard_map/ppermute | solution.py:24
  10.5 18.5 %copy-start.1 = (bf16[444,888]{1,0:T(8,128)(2,1)S(1)}, bf16[444,888]{1,0:T(8,128)(2,1)}, u32[]{:S(2)}) copy-start(bf16[444,888]{1,0:T(8,128)(2,1)} %matrix_ref.5) | copy-start | bytes 2365636
  15.1 2.5 %collective-permute-start.5 = (bf16[444,256]{1,0:T(8,128)(2,1)S(1)}, bf16[444,256]{1,0:T(8,128)(2,1)S(1)}, u32[]{:S(2)}, u32[]{:S(2)}) collective-permute-start(bf16[444,256]{1,0:T(8,128)(2,1)S(1)} %get-tuple-element.37), channel_id=1, source_target_pairs={{0,2},{2,0},{4,6},{6,4},{8,10},{10,8},{12,14},{14,12},{16,18},{18,... | collective-permute-start | bytes 681992 | tf_op jit(solution)/shard_map/ppermute | solution.py:24
  15.1 9.6 %collective-permute-start.6 = (bf16[444,128]{1,0:T(8,128)(2,1)S(1)}, bf16[444,128]{1,0:T(8,128)(2,1)S(1)}, u32[]{:S(2)}, u32[]{:S(2)}) collective-permute-start(bf16[444,128]{1,0:T(8,128)(2,1)S(1)} %get-tuple-element.39), channel_id=1, source_target_pairs={{2,6},{4,0},{6,10},{8,4},{10,14},{12,8},{14,18},{16,12},{18,22},{2... | collective-permute-start | bytes 341000 | tf_op jit(solution)/shard_map/ppermute | solution.py:46
  18.0 11.8 %collective-permute-start.9 = (bf16[444,128]{1,0:T(8,128)(2,1)S(1)}, bf16[444,128]{1,0:T(8,128)(2,1)S(1)}, u32[]{:S(2)}, u32[]{:S(2)}) collective-permute-start(bf16[444,128]{1,0:T(8,128)(2,1)S(1)} %get-tuple-element.40), channel_id=1, source_target_pairs={{2,5},{3,4},{4,3},{5,2},{6,9},{7,8},{8,7},{9,6},{10,13},{11,12},{1... | collective-permute-start | bytes 341000 | tf_op jit(solution)/shard_map/ppermute | solution.py:40
  21.9 7.1 %collective-permute-start.7 = (bf16[444,128]{1,0:T(8,128)(2,1)S(1)}, bf16[444,128]{1,0:T(8,128)(2,1)S(1)}, u32[]{:S(2)}, u32[]{:S(2)}) collective-permute-start(bf16[444,128]{1,0:T(8,128)(2,1)S(1)} %get-tuple-element.40), channel_id=1, source_target_pairs={{2,4},{4,2},{6,8},{8,6},{10,12},{12,10},{14,16},{16,14},{18,20},{2... | collective-permute-start | bytes 341000 | tf_op jit(solution)/shard_map/ppermute | solution.py:30
  24.8 5.0 %collective-permute-start.8 = (bf16[444,128]{1,0:T(8,128)(2,1)S(1)}, bf16[444,128]{1,0:T(8,128)(2,1)S(1)}, u32[]{:S(2)}, u32[]{:S(2)}) collective-permute-start(bf16[444,128]{1,0:T(8,128)(2,1)S(1)} %fusion), channel_id=1, source_target_pairs={{0,1},{1,0},{2,3},{3,2},{4,5},{5,4},{6,7},{7,6},{8,9},{9,8},{10,11... | collective-permute-start | bytes 341000 | tf_op jit(solution)/shard_map/ppermute | solution.py:18
